TPU v7x, 32 devices: a whole 2x2x4 slice. The times are simulated.
32 devices in a mesh: sp: 16 (over z, y, x), fl: 2 (over core).
Axes of the slice: x: 2, y: 2, z: 4, core: 2. Of those that a mesh axis runs over, the one named last changes fastest.
Arguments:
- volume: bfloat16 [16, 64, 16, 24, 512], P('sp'), may hold values from -6 to 6
- kernel_three: bfloat16 [128, 1728], P('fl'), may hold values from -0.15625 to 0.15625
- gain_three: float32 [128], P('fl'), may hold values from 0.1 to 1.9
- shift_three: float32 [128], P('fl'), may hold values from -0.5 to 0.5
- kernel_four: bfloat16 [256, 3456], P('fl'), may hold values from -0.109375 to 0.109375
- gain_four: float32 [256], P('fl'), may hold values from 0.1 to 1.9
- shift_four: float32 [256], P('fl'), may hold values from -0.5 to 0.5
Outputs:
- deep_features: bfloat16 [16, 256, 4, 6, 128], P('sp', 'fl')
All inputs are finite; a program needn't handle non-finite values.
Results may differ from a plain program's by a relative error of at most 0.0048.
Values may be sent and summed in bfloat16 or wider, within the bound.
No kernel may reach another device: no remote copies, remote signals or barrier semaphores. Data moves between devices by JAX's collectives and lax.ppermute only.
A program may use at most 320 MiB of HBM per device.

v0:
```python
import jax
import jax.numpy as jnp
from jax import lax
from jax.sharding import PartitionSpec as P


def passed_along(value, axis, steps):
    count = lax.axis_size(axis)
    initial, last = (max(0, -steps), min(count, count - steps))
    return lax.ppermute(value, axis, [(source, source + steps) for source in range(initial, last)])


def convolve(slab, kernel, strides, pads):
    return lax.conv_general_dilated(
        slab[None],
        kernel,
        strides,
        pads,
        dimension_numbers=("NCDHW", "OIDHW", "NCDHW"),
        preferred_element_type=jnp.float32,
    )[0]


def activate(conv_out, gain, shift):
    return jax.nn.relu(conv_out * gain[:, None, None, None] + shift[:, None, None, None]).astype(
        jnp.bfloat16
    )


def layer_three(field, weights, first_row):
    planes = field.shape[1]
    rows = field.shape[2]
    prior = passed_along(field[:, planes - 1 :], "sp", 8)
    extended = jnp.concatenate([prior, field], 1)
    rim_rows = passed_along(extended[:, :, rows - 1 :], "sp", 1)
    rim_rows = jnp.where(first_row, jnp.zeros_like(rim_rows), rim_rows)
    extended = jnp.concatenate([rim_rows, extended], 2)
    return convolve(extended, weights, (2, 2, 2), ((0, 0), (0, 0), (1, 1)))


def layer_four(field, weights, first_row):
    planes = field.shape[1]
    rows = field.shape[2]
    prior = passed_along(field[:, planes - 1 :], "sp", 8)
    extended = jnp.concatenate([prior, field], 1)
    rim_rows = passed_along(extended[:, :, rows - 1 :], "sp", 1)
    rim_rows = jnp.where(first_row, jnp.zeros_like(rim_rows), rim_rows)
    extended = jnp.concatenate([rim_rows, extended], 2)
    return convolve(extended, weights, (2, 2, 2), ((0, 0), (0, 0), (1, 1)))


def shards(volume, kernel_three, gain_three, shift_three, kernel_four, gain_four, shift_four):
    field = volume[0]
    in_chan = field.shape[0]
    first_row = lax.axis_index("sp") % 8 == 0
    weights_three = kernel_three.reshape(kernel_three.shape[0], in_chan, 3, 3, 3)
    third_half = activate(layer_three(field, weights_three, first_row), gain_three, shift_three)
    third = lax.all_gather(third_half, "fl", axis=0, tiled=True)
    weights_four = kernel_four.reshape(kernel_four.shape[0], third.shape[0], 3, 3, 3)
    fourth = activate(layer_four(third, weights_four, first_row), gain_four, shift_four)
    return fourth[None]


def solution(mesh):
    return jax.shard_map(
        shards,
        mesh=mesh,
        in_specs=(
            P("sp", None, None, None, None),
            P("fl", None),
            P("fl"),
            P("fl"),
            P("fl", None),
            P("fl"),
            P("fl"),
        ),
        out_specs=P("sp", "fl", None, None, None),
        check_vma=False,
    )
```

profile of v0, /device:TPU:25, one launch (start us, length us, event | category | flops | bytes accessed | tf_op | source)
XLA Modules:
  0.0 628.8 jit_solution(18353077463602228957)
XLA Ops:
  6.5 0.0 all-gather.2.cloned.1.call-start
  6.5 22.6 %copy.67 = bf16[1,64,16,24,512]{4,1,3,2,0:T(8,128)(2,1)S(1)} copy(bf16[1,64,16,24,512]{4,3,2,1,0:T(8,128)(2,1)} %param.7) | data formatting | bytes 50331648 | tf_op args[0]
  29.2 0.1 slice.20
  29.3 0.0 copy-start.5
  29.3 1.4 collective-permute-start
  30.7 71.4 %collective-permute-done = bf16[64,1,24,512]{3,0,2,1:T(8,128)(2,1)S(1)} collective-permute-done((bf16[64,1,24,512]{3,0,2,1:T(8,128)(2,1)S(1)}, bf16[64,1,24,512]{3,0,2,1:T(8,128)(2,1)S(1)}, u32[]{:S(2)}, u32[]{:S(2)}) %collective-permute-start) | collective-permute-done | bytes 1572896 | tf_op jit(solution)/shard_map/ppermute | solution.py:10
  102.1 1.2 pad_maximum_fusion
  103.3 3.1 collective-permute-start.1
  106.5 0.3 copy.44
  106.7 1.1 reshape.10
  107.8 25.0 %collective-permute-done.1 = bf16[64,17,1,512]{3,0,2,1:T(8,128)(2,1)S(1)} collective-permute-done((bf16[64,17,1,512]{3,0,2,1:T(8,128)(2,1)}, bf16[64,17,1,512]{3,0,2,1:T(8,128)(2,1)S(1)}, u32[]{:S(2)}, u32[]{:S(2)}) %collective-permute-start.1) | collective-permute-done | bytes 1114144 | tf_op jit(solution)/shard_map/ppermute | solution.py:10
  132.8 0.1 broadcast_select_fusion
  132.9 18.5 %maximum_bitcast_fusion = bf16[64,17,25,1,512]{4,0,2,1,3:T(8,128)(2,1)} fusion(bf16[64,16,24,512]{3,0,2,1:T(8,128)(2,1)} %bitcast.45, bf16[64,1,24,512]{3,0,2,1:T(8,128)(2,1)S(1)} %collective-permute-done, bf16[64,17,1,512]{3,0,2,1:T(8,128)(2,1)S(1)} %broadcast_select_fusion), kind=kLoop, calls=%fused_computation.6 | loop fusion | flops 27852800 | bytes 55705600 | tf_op jit(solution)/shard_map/broadcast_in_dim | solution.py:15
  151.4 21.3 %pad = bf16[64,17,25,1,528]{4,0,2,1,3:T(8,128)(2,1)} pad(bf16[64,17,25,1,512]{4,0,2,1,3:T(8,128)(2,1)} %maximum_bitcast_fusion, bf16[]{:T(256)} %constant.26.clone.1), padding=0_0x0_0x0_0x0_0x1_15 | pad | bytes 56576000 | tf_op jit(solution)/shard_map/broadcast_in_dim | solution.py:15
  172.7 83.7 %reshape.14 = bf16[64,17,25,1,8,66]{5,4,0,2,1,3:T(8,128)(2,1)} reshape(bf16[64,17,25,1,528]{4,0,2,1,3:T(8,128)(2,1)} %pad) | data formatting | bytes 57446400 | tf_op jit(solution)/shard_map/conv_general_dilated | solution.py:14
  256.4 85.9 %copy.43 = bf16[64,17,25,1,8,66]{0,4,5,2,1,3:T(8,128)(2,1)} copy(bf16[64,17,25,1,8,66]{5,4,0,2,1,3:T(8,128)(2,1)} %reshape.14) | data formatting | bytes 57446400 | tf_op jit(solution)/shard_map/conv_general_dilated | solution.py:14
  342.3 1.9 slice.21
  344.2 76.7 %fusion.7 = f32[8,12,8,33,64]{4,2,3,1,0:T(8,128)} fusion(bf16[64,17,25,1,7,2]{0,4,5,2,1,3:T(8,128)(2,1)S(1)} %slice.21, bf16[64,17,25,1,8,66]{0,4,5,2,1,3:T(8,128)(2,1)} %copy.43, pred[8,33]{0,1:T(8,128)(4,1)S(1)} %copy-done.10, bf16[64,64,3,3,3]{0,4,3,2,1:T(4,128)(2,1)S(1)} %copy-done.4), kind=kOutput, calls=%fused_computation.11 | convolution fusion | flops 5696090112 | bytes 36194312 | tf_op jit(solution)/shard_map/conv_general_dilated | solution.py:14
  420.9 16.8 %copy.46 = f32[8,12,8,33,64]{4,0,3,2,1:T(8,128)} copy(f32[8,12,8,33,64]{4,2,3,1,0:T(8,128)} %fusion.7) | data formatting | bytes 12976128 | tf_op jit(solution)/shard_map/conv_general_dilated | solution.py:14
  437.8 9.9 %slice.22 = f32[8,12,1,256,64]{4,0,3,1,2:T(8,128)} slice(f32[8,12,1,264,64]{4,0,3,1,2:T(8,128)} %bitcast.46), slice={[0:8], [0:12], [0:1], [0:256], [0:64]} | slice | bytes 12582912 | tf_op jit(solution)/shard_map/conv_general_dilated | solution.py:14
  447.7 10.8 %copy.59 = f32[8,12,1,256,64]{3,0,1,4,2:T(8,128)} copy(f32[8,12,1,256,64]{4,0,3,1,2:T(8,128)} %slice.22) | data formatting | bytes 12582912
  458.5 0.0 copy-done.6
  458.5 6.0 fusion.19
  464.5 0.0 all-gather.2.cloned.1.call-update
  464.5 0.0 copy-start.3
  464.5 17.5 %all-gather.2.cloned.1.call-done = bf16[128,8,12,256]{3,1,2,0:T(8,128)(2,1)} async-done(((bf16[64,8,12,256]{3,1,2,0:T(8,128)(2,1)}), bf16[128,8,12,256]{3,1,2,0:T(8,128)(2,1)}) %all-gather.2.cloned.1.call-update) | async-done | bytes 6291472 | tf_op jit(solution)/shard_map/all_gather | solution.py:58
  482.0 4.6 slice.23
  486.6 0.2 copy.48
  486.8 1.3 collective-permute-start.2
  488.1 37.8 %collective-permute-done.2 = bf16[128,1,12,256]{3,0,2,1:T(8,128)(2,1)S(1)} collective-permute-done((bf16[128,1,12,256]{3,0,2,1:T(8,128)(2,1)S(1)}, bf16[128,1,12,256]{3,0,2,1:T(8,128)(2,1)S(1)}, u32[]{:S(2)}, u32[]{:S(2)}) %collective-permute-start.2) | collective-permute-done | bytes 786464 | tf_op jit(solution)/shard_map/ppermute | solution.py:10
  525.9 1.2 copy.49
  527.2 0.4 pad_maximum_fusion.1
  527.6 1.0 copy.50
  528.6 3.1 collective-permute-start.3
  531.7 1.2 copy.55
  532.9 1.9 reshape.11
  534.8 12.3 %collective-permute-done.3 = bf16[128,9,1,256]{3,0,2,1:T(8,128)(2,1)} collective-permute-done((bf16[128,9,1,256]{3,0,2,1:T(8,128)(2,1)}, bf16[128,9,1,256]{3,0,2,1:T(8,128)(2,1)}, u32[]{:S(2)}, u32[]{:S(2)}) %collective-permute-start.3) | collective-permute-done | bytes 589856 | tf_op jit(solution)/shard_map/ppermute | solution.py:10
  547.1 1.4 copy_select_fusion
  548.5 11.3 %maximum_bitcast_fusion.1 = bf16[128,9,13,1,256]{4,1,2,0,3:T(8,128)(2,1)} fusion(bf16[128,8,12,256]{3,1,2,0:T(8,128)(2,1)} %all-gather.2.cloned.1.call-done, bf16[128,1,12,256]{3,1,2,0:T(2,128)(2,1)S(1)} %copy.49, bf16[128,9,1,256]{3,1,2,0:T(8,128)(2,1)S(1)} %copy_select_fusion), kind=kLoop, calls=%fused_computation.10 | loop fusion | flops 23003136 | bytes 15335424 | tf_op jit(solution)/shard_map/broadcast_in_dim | solution.py:15
  559.8 19.1 %copy.60 = bf16[128,9,13,1,256]{0,4,2,1,3:T(8,128)(2,1)} copy(bf16[128,9,13,1,256]{4,1,2,0,3:T(8,128)(2,1)} %maximum_bitcast_fusion.1) | data formatting | bytes 15335424
  578.8 9.6 %pad.2.clone = bf16[128,9,13,1,272]{0,4,2,1,3:T(8,128)(2,1)} pad(bf16[128,9,13,1,256]{0,4,2,1,3:T(8,128)(2,1)} %copy.60, bf16[]{:T(256)} %constant.26.clone.1), padding=0_0x0_0x0_0x0_0x1_15 | pad | bytes 15814658 | tf_op jit(solution)/shard_map/broadcast_in_dim | solution.py:15
  588.4 13.3 %reshape.21 = bf16[128,9,13,1,8,34]{0,5,4,2,1,3:T(8,128)(2,1)} reshape(bf16[128,9,13,1,272]{0,4,2,1,3:T(8,128)(2,1)} %pad.2.clone) | data formatting | bytes 16293888 | tf_op jit(solution)/shard_map/conv_general_dilated | solution.py:14
  601.7 8.5 %copy.54 = bf16[128,9,13,1,8,34]{0,4,5,2,1,3:T(8,128)(2,1)} copy(bf16[128,9,13,1,8,34]{0,5,4,2,1,3:T(8,128)(2,1)} %reshape.21) | data formatting | bytes 16293888 | tf_op jit(solution)/shard_map/conv_general_dilated | solution.py:14
  610.2 1.2 slice.24
  611.4 8.5 %maximum_convert_fusion = bf16[4,6,8,17,128]{4,2,3,1,0:T(8,128)(2,1)S(1)} fusion(bf16[128,9,13,1,7,2]{0,4,5,2,1,3:T(8,128)(2,1)S(1)} %slice.24, bf16[128,9,13,1,8,34]{0,4,5,2,1,3:T(8,128)(2,1)} %copy.54, bf16[128,128,3,3,3]{0,4,3,2,1:T(4,128)(2,1)S(1)} %copy-done.2, f32[128]{0:T(128)S(1)} %copy-done.8, f32[128]{0:T(128)S(1)} %copy-done.9, ...), kind=kOutput, calls=%fused_computation.23 | convolution fusion | flops 2915745792 | bytes 10287752 | tf_op jit(solution)/shard_map/conv_general_dilated | solution.py:14
  619.9 0.3 copy.57
  620.2 0.3 slice_bitcast_fusion
  620.5 1.2 copy.58
  (21 shorter events, 0.0 us)
Async XLA Ops:
  6.5 475.4 %all-gather.2.cloned.1.call-start = ((), (), s32[]{:S(2)}) async-start(), calls=%async_computation | async-start | bytes 9437184 | tf_op jit(solution)/shard_map/all_gather | solution.py:58
  29.2 74.2 %copy-start = (bf16[1,64,16,24,512]{4,1,3,2,0:T(8,128)(2,1)}, bf16[1,64,16,24,512]{4,1,3,2,0:T(8,128)(2,1)S(1)}, u32[]{:S(2)}) copy-start(bf16[1,64,16,24,512]{4,1,3,2,0:T(8,128)(2,1)S(1)} %copy.67) | copy-start | bytes 75497472
  29.3 77.2 %copy-start.5 = (bf16[64,1728]{1,0:T(8,128)(2,1)S(1)}, bf16[64,1728]{1,0:T(8,128)(2,1)}, u32[]{:S(2)}) copy-start(bf16[64,1728]{1,0:T(8,128)(2,1)} %param.8) | copy-start | bytes 663556
  29.3 72.8 %collective-permute-start = (bf16[64,1,24,512]{3,0,2,1:T(8,128)(2,1)S(1)}, bf16[64,1,24,512]{3,0,2,1:T(8,128)(2,1)S(1)}, u32[]{:S(2)}, u32[]{:S(2)}) collective-permute-start(bf16[64,1,24,512]{3,0,2,1:T(8,128)(2,1)S(1)} %slice.20), channel_id=1, source_target_pairs={{0,16},{2,18},{4,20},{6,22},{8,24},{10,26},{12,28},{14,30},{1,17},... | collective-permute-start | bytes 4718600 | tf_op jit(solution)/shard_map/ppermute | solution.py:10
  103.3 29.5 %collective-permute-start.1 = (bf16[64,17,1,512]{3,0,2,1:T(8,128)(2,1)}, bf16[64,17,1,512]{3,0,2,1:T(8,128)(2,1)S(1)}, u32[]{:S(2)}, u32[]{:S(2)}) collective-permute-start(bf16[64,17,1,512]{3,0,2,1:T(8,128)(2,1)} %pad_maximum_fusion), channel_id=1, source_target_pairs={{0,2},{2,4},{4,6},{6,8},{8,10},{10,12},{12,14},{14,16},{16,18},{18... | collective-permute-start | bytes 3342344 | tf_op jit(solution)/shard_map/ppermute | solution.py:10
  256.4 87.9 %copy-start.4 = (bf16[64,64,3,3,3]{0,4,3,2,1:T(4,128)(2,1)S(1)}, bf16[64,64,3,3,3]{0,4,3,2,1:T(4,128)(2,1)}, u32[]{:S(2)}) copy-start(bf16[64,64,3,3,3]{0,4,3,2,1:T(4,128)(2,1)} %reshape.10) | copy-start | bytes 663556
  256.4 87.9 %copy-start.10 = (pred[8,33]{0,1:T(8,128)(4,1)S(1)}, pred[8,33]{0,1:T(8,128)(4,1)}, u32[]{:S(2)}) copy-start(pred[8,33]{0,1:T(8,128)(4,1)} %constant.38) | copy-start | bytes 796
  447.7 10.8 %copy-start.6 = (f32[64]{0:T(128)S(1)}, f32[64]{0:T(128)}, u32[]{:S(2)}) copy-start(f32[64]{0:T(128)} %param.10) | copy-start | bytes 772
  447.7 10.8 %copy-start.7 = (f32[64]{0:T(128)S(1)}, f32[64]{0:T(128)}, u32[]{:S(2)}) copy-start(f32[64]{0:T(128)} %param.9) | copy-start | bytes 772
  464.5 67.2 %copy-start.3 = (bf16[128,3456]{1,0:T(8,128)(2,1)S(1)}, bf16[128,3456]{1,0:T(8,128)(2,1)}, u32[]{:S(2)}) copy-start(bf16[128,3456]{1,0:T(8,128)(2,1)} %param.11) | copy-start | bytes 2654212
  482.0 45.2 %copy-start.1 = (bf16[128,8,12,256]{3,1,2,0:T(8,128)(2,1)S(1)}, bf16[128,8,12,256]{3,1,2,0:T(8,128)(2,1)}, u32[]{:S(2)}) copy-start(bf16[128,8,12,256]{3,1,2,0:T(8,128)(2,1)} %all-gather.2.cloned.1.call-done) | copy-start | bytes 18874372
  486.8 39.1 %collective-permute-start.2 = (bf16[128,1,12,256]{3,0,2,1:T(8,128)(2,1)S(1)}, bf16[128,1,12,256]{3,0,2,1:T(8,128)(2,1)S(1)}, u32[]{:S(2)}, u32[]{:S(2)}) collective-permute-start(bf16[128,1,12,256]{3,0,2,1:T(8,128)(2,1)S(1)} %copy.48), channel_id=1, source_target_pairs={{0,16},{2,18},{4,20},{6,22},{8,24},{10,26},{12,28},{14,30},{1,17},... | collective-permute-start | bytes 2359304 | tf_op jit(solution)/shard_map/ppermute | solution.py:10
  528.6 18.4 %collective-permute-start.3 = (bf16[128,9,1,256]{3,0,2,1:T(8,128)(2,1)}, bf16[128,9,1,256]{3,0,2,1:T(8,128)(2,1)}, u32[]{:S(2)}, u32[]{:S(2)}) collective-permute-start(bf16[128,9,1,256]{3,0,2,1:T(8,128)(2,1)} %copy.50), channel_id=1, source_target_pairs={{0,2},{2,4},{4,6},{6,8},{8,10},{10,12},{12,14},{14,16},{16,18},{18... | collective-permute-start | bytes 1769480 | tf_op jit(solution)/shard_map/ppermute | solution.py:10
  601.7 9.6 %copy-start.2 = (bf16[128,128,3,3,3]{0,4,3,2,1:T(4,128)(2,1)S(1)}, bf16[128,128,3,3,3]{0,4,3,2,1:T(4,128)(2,1)}, u32[]{:S(2)}) copy-start(bf16[128,128,3,3,3]{0,4,3,2,1:T(4,128)(2,1)} %reshape.11) | copy-start | bytes 2654212
  601.7 9.7 %copy-start.8 = (f32[128]{0:T(128)S(1)}, f32[128]{0:T(128)}, u32[]{:S(2)}) copy-start(f32[128]{0:T(128)} %param.13) | copy-start | bytes 1540
  601.7 9.7 %copy-start.9 = (f32[128]{0:T(128)S(1)}, f32[128]{0:T(128)}, u32[]{:S(2)}) copy-start(f32[128]{0:T(128)} %param.12) | copy-start | bytes 1540
  601.7 9.7 %copy-start.11 = (pred[8,17]{0,1:T(8,128)(4,1)S(1)}, pred[8,17]{0,1:T(8,128)(4,1)}, u32[]{:S(2)}) copy-start(pred[8,17]{0,1:T(8,128)(4,1)} %constant.37) | copy-start | bytes 412
Sparse Core Ops, SparseCore 0:
  464.6 17.3 all-gather.1
where the time goes:
time: 640 us; the launch traced here: 629 us
  local copies, waits for them, and re-layouts  318 us (50%)
  waiting for transfers between devices  164 us (26%)
  matrix products  85.2 us (13%)
  other arithmetic  38.9 us (6%)
  between operations  13.8 us (2%)
  starting transfers between devices  8.91 us (1%)
    conv_general_dilated x8, local copies, waits for them, and re-layouts, convolve(): lax.conv_general_dilated(slab[None], kernel, strides, pads, dimension_num...  221 us
    ppermute x4, waiting for transfers between devices, passed_along(): lax.ppermute(value, axis, [(source, source + steps) for source in range(i...  147 us
    conv_general_dilated x2, matrix products, convolve(): lax.conv_general_dilated(slab[None], kernel, strides, pads, dimension_num...  85.2 us
    unnamed x29, local copies, waits for them, and re-layouts  53.9 us
    broadcast_in_dim x2, local copies, waits for them, and re-layouts, convolve(): slab[None]  30.8 us
    broadcast_in_dim x2, other arithmetic, convolve(): slab[None]  29.8 us
    all_gather x1, waiting for transfers between devices, shards(): third = lax.all_gather(third_half, 'fl', axis=0, tiled=True)  17.5 us
  transfers between devices with their start and end apart: 5, of which 5 were waited for; matrix products, arithmetic and copies ran while one was open for 1% of the time, Pallas kernels for 0%

commit v1 on v0

v1 whole, which is shorter than its diff:
```python
import functools

import jax
import jax.numpy as jnp
import numpy as np
from jax import lax
from jax.experimental import pallas as pl
from jax.experimental.pallas import tpu as pltpu
from jax.sharding import PartitionSpec as P

F32 = jnp.float32
BF16 = jnp.bfloat16
LANES = 128
ROW_BLOCKS = 8
VMEM_LIMIT = 56 * 2**20


def even_odd(width):
    half = width // 2
    place = np.zeros((width, width), np.float32)
    place[np.arange(0, width, 2), np.arange(half)] = 1
    place[np.arange(1, width, 2), half + np.arange(half)] = 1
    return jnp.asarray(place, BF16)


def activate(total, gain, shift):
    return jnp.maximum(total * gain + shift, 0.0)


def shifted(odd):
    lane = lax.broadcasted_iota(jnp.int32, odd.shape, 1)
    return jnp.where(lane == 0, 0.0, pltpu.roll(odd, 1, 1))


def three_kernel(
    core_ref, x_ref, w_ref, place_ref, gain_ref, shift_ref,
    third_ref, plane_ref, row_ref, next_plane_ref, next_row_ref, next_corner_ref,
    split_ref, data_ref,
):
    step = pl.program_id(0)
    chans, rows, width = x_ref.shape[1], x_ref.shape[3], x_ref.shape[4]
    half = width // 2
    out_rows = rows // 2
    taps = 3 * chans
    group = 16

    @pl.when(step == 0)
    def _():
        data_ref[0] = jnp.zeros_like(data_ref[0])
        for slot in (1, 2):
            data_ref[slot, 0] = jnp.zeros_like(data_ref[slot, 0])
            data_ref[slot, rows + 1] = jnp.zeros_like(data_ref[slot, 0])
            data_ref[slot, rows + 2] = jnp.zeros_like(data_ref[slot, 0])

    @pl.when(step > 0)
    def _():
        data_ref[0] = data_ref[2]

    def separate(which, _):
        plane = which // (chans // group)
        first = (which % (chans // group)) * group
        x = x_ref[0, pl.ds(first, group), plane]
        x = x.astype(F32).reshape(group * rows, width).astype(BF16)
        quarter = half // 2
        for side in range(2):
            parts = jnp.dot(
                x[:, side * half : (side + 1) * half], place_ref[...], preferred_element_type=F32
            )
            for block in range(2 * quarter // LANES):
                odd, at = divmod(block, quarter // LANES)
                split_ref[odd, side * (quarter // LANES) + at] = parts[:, block * LANES : (block + 1) * LANES]
        for row in range(rows):
            even, odd = (
                jnp.concatenate(
                    [split_ref[odd, at, pl.ds(row, group, stride=rows), :] for at in range(half // LANES)], 1
                )
                for odd in range(2)
            )
            for tap, value in enumerate((shifted(odd), even, odd)):
                data_ref[plane + 1, row + 1, pl.ds(tap * chans + first, group), :] = value.astype(BF16)
        return 0

    lax.fori_loop(0, 2 * (chans // group), separate, 0)

    gain, shift = gain_ref[...], shift_ref[...]

    def sums(row):
        parts = [data_ref[slot, pl.ds(2 * row, 3)].reshape(3 * taps, half) for slot in range(3)]
        return jnp.dot(w_ref[...], jnp.concatenate(parts, 0), preferred_element_type=F32)

    def out_row(row, _):
        total = sums(row)
        third_ref[0, row] = activate(total, gain, shift).astype(BF16)

        @pl.when(step == 0)
        def _():
            plane_ref[row] = total

        @pl.when(row == 0)
        def _():
            row_ref[0] = total

        return 0

    lax.fori_loop(0, out_rows, out_row, 0)
    next_row_ref[0] = sums(out_rows).astype(BF16)

    @pl.when(step == pl.num_programs(0) - 1)
    def _():
        def beyond(row):
            return jnp.dot(
                w_ref[:, : 3 * taps],
                data_ref[2, pl.ds(2 * row, 3)].reshape(3 * taps, half),
                preferred_element_type=F32,
            ).astype(BF16)

        def plane_row(row, _):
            next_plane_ref[row] = beyond(row)
            return 0

        lax.fori_loop(0, out_rows, plane_row, 0)
        next_corner_ref[...] = beyond(out_rows)


def layer_three(volume, weights, gain, shift, core):
    _, chans, planes, rows, width = volume.shape
    outs = weights.shape[0]
    half = width // 2
    steps, out_rows = planes // 4, rows // 2
    full = lambda *shape: pl.BlockSpec(shape, lambda i, core: (0,) * len(shape))
    return pl.pallas_call(
        three_kernel,
        grid_spec=pltpu.PrefetchScalarGridSpec(
            num_scalar_prefetch=1,
            grid=(steps,),
            in_specs=[
                pl.BlockSpec((1, chans, 2, rows, width), lambda i, core: (0, 0, core[0] * steps + i, 0, 0)),
                full(*weights.shape),
                full(half, half),
                full(outs, 1),
                full(outs, 1),
            ],
            out_specs=[
                pl.BlockSpec((1, out_rows, outs, half), lambda i, core: (i, 0, 0, 0)),
                full(out_rows, outs, half),
                pl.BlockSpec((1, outs, half), lambda i, core: (i, 0, 0)),
                full(out_rows, outs, half),
                pl.BlockSpec((1, outs, half), lambda i, core: (i, 0, 0)),
                full(outs, half),
            ],
            scratch_shapes=[
                pltpu.VMEM((2, half // LANES, 16 * rows, LANES), F32),
                pltpu.VMEM((3, rows + 3, 3 * chans, half), BF16),
            ],
        ),
        out_shape=[
            jax.ShapeDtypeStruct((steps, out_rows, outs, half), BF16),
            jax.ShapeDtypeStruct((out_rows, outs, half), F32),
            jax.ShapeDtypeStruct((steps, outs, half), F32),
            jax.ShapeDtypeStruct((out_rows, outs, half), BF16),
            jax.ShapeDtypeStruct((steps, outs, half), BF16),
            jax.ShapeDtypeStruct((outs, half), BF16),
        ],
        compiler_params=pltpu.CompilerParams(vmem_limit_bytes=VMEM_LIMIT),
        name="layer_three",
    )(core, volume, weights, even_odd(half), gain, shift)


def four_kernel(
    third_ref, plane_ref, row_ref, halo_plane_ref, halo_row_ref, halo_corner_ref,
    w_ref, place_ref, gain_ref, shift_ref,
    sums_ref, next_plane_ref, next_row_ref, next_corner_ref,
    data_ref,
):
    planes, rows, chans, width = third_ref.shape
    half = width // 2
    out_rows = rows // 2
    count = planes // 2
    gain, shift = gain_ref[...], shift_ref[...]
    data_ref[:, 0] = jnp.zeros_like(data_ref[:, 0])
    for extra in (1, 2):
        data_ref[:, rows + extra] = jnp.zeros_like(data_ref[:, 0])
    data_ref[0, :, :, :half] = jnp.zeros_like(data_ref[0, :, :, :half])

    def place(plane, row, value):
        both = jnp.dot(value, place_ref[...], preferred_element_type=F32)
        even, odd = both[:, :half], both[:, half:]
        spots = [(1 + plane % 2, plane // 2)]
        if plane % 2 and plane // 2 + 1 < count:
            spots.append((0, plane // 2 + 1))
        for tap, part in enumerate((shifted(odd), even, odd)):
            for slot, lanes in spots:
                data_ref[slot, row + 1, tap * chans : (tap + 1) * chans, lanes * half : (lanes + 1) * half] = (
                    part.astype(BF16)
                )

    for plane in range(planes):
        if plane == 0:
            total = plane_ref[0] + halo_plane_ref[0].astype(F32) + halo_corner_ref[...].astype(F32)
        else:
            total = row_ref[plane]
        total = total + halo_row_ref[plane].astype(F32)
        place(plane, 0, activate(total, gain, shift).astype(BF16))

        def row_of(row, _, plane=plane):
            if plane == 0:
                total = plane_ref[row] + halo_plane_ref[row].astype(F32)
                value = activate(total, gain, shift).astype(BF16)
            else:
                value = third_ref[plane, row]
            place(plane, row, value)
            return 0

        lax.fori_loop(1, rows, row_of, 0)

    taps = 3 * chans

    def sums(row):
        parts = [data_ref[slot, pl.ds(2 * row, 3)].reshape(3 * taps, count * half) for slot in range(3)]
        return jnp.dot(w_ref[...], jnp.concatenate(parts, 0), preferred_element_type=F32)

    def beyond(row):
        part = data_ref[2, pl.ds(2 * row, 3), :, (count - 1) * half :].reshape(3 * taps, half)
        return jnp.dot(w_ref[:, : 3 * taps], part, preferred_element_type=F32).astype(BF16)

    def out_row(row, _):
        sums_ref[row] = sums(row)
        next_plane_ref[row] = beyond(row)
        return 0

    lax.fori_loop(0, out_rows, out_row, 0)
    next_row_ref[...] = sums(out_rows).astype(BF16)
    next_corner_ref[...] = beyond(out_rows)


def layer_four(third, plane, row, halos, weights, gain, shift):
    planes, rows, chans, width = third.shape
    outs = weights.shape[0]
    half = width // 2
    out_rows, count = rows // 2, planes // 2
    return pl.pallas_call(
        four_kernel,
        out_shape=[
            jax.ShapeDtypeStruct((out_rows, outs, count * half), F32),
            jax.ShapeDtypeStruct((out_rows, outs, half), BF16),
            jax.ShapeDtypeStruct((outs, count * half), BF16),
            jax.ShapeDtypeStruct((outs, half), BF16),
        ],
        scratch_shapes=[pltpu.VMEM((3, rows + 3, 3 * chans, count * half), BF16)],
        compiler_params=pltpu.CompilerParams(vmem_limit_bytes=VMEM_LIMIT),
        name="layer_four",
    )(third, plane, row, *halos, weights, even_odd(width), gain, shift)


def exchange(plane, row, corner):
    count = lax.axis_size("sp")
    axes = ("sp", "fl")
    blocks = range(count)
    inner = [b for b in blocks if b % ROW_BLOCKS != ROW_BLOCKS - 1]
    down = [(2 * b, 2 * b + 1) for b in blocks]
    down += [(2 * b + 1, 2 * (b + ROW_BLOCKS)) for b in blocks if b + ROW_BLOCKS < count]
    along = [(2 * b + core, 2 * (b + 1) + core) for b in inner for core in range(2)]
    both = [(2 * b, 2 * (b + 1) + 1) for b in inner]
    both += [(2 * b + 1, 2 * (b + 1 + ROW_BLOCKS)) for b in inner if b + ROW_BLOCKS < count]
    return (
        lax.ppermute(plane, axes, down),
        lax.ppermute(row, axes, along),
        lax.ppermute(corner, axes, both),
    )


def both_cores(value, core):
    other = lax.ppermute(value, "fl", [(0, 1), (1, 0)])
    return jnp.where(core == 0, jnp.concatenate([value, other], 0), jnp.concatenate([other, value], 0))


def tap_major(kernel, chans):
    outs = kernel.shape[0]
    return jnp.transpose(kernel.reshape(outs, chans, 27), (0, 2, 1)).reshape(outs, 27 * chans)


def shards(volume, kernel_three, gain_three, shift_three, kernel_four, gain_four, shift_four):
    core = lax.axis_index("fl")
    chans = volume.shape[1]
    mid = 2 * kernel_three.shape[0]
    scales_three = both_cores(jnp.stack([gain_three, shift_three], 1), core)
    scales_four = both_cores(jnp.stack([gain_four, shift_four], 1), core)
    weights_three = tap_major(both_cores(kernel_three, core), chans)
    weights_four = tap_major(both_cores(kernel_four, core), mid)
    gain, shift = scales_three[:, :1], scales_three[:, 1:]
    third, plane, row, *nexts = layer_three(volume, weights_three, gain, shift, core.reshape(1))
    halos = exchange(*nexts)
    total, *nexts = layer_four(third, plane, row, halos, weights_four, gain, shift)
    halo_plane, halo_row, halo_corner = exchange(*nexts)
    out_rows, outs, lanes = total.shape
    width = halo_plane.shape[2]
    total = total.reshape(out_rows, outs, lanes // width, width)
    total = total.at[:, :, 0].add(halo_plane.astype(F32))
    total = total.at[0].add(halo_row.reshape(outs, lanes // width, width).astype(F32))
    total = total.at[0, :, 0].add(halo_corner.astype(F32))
    fourth = activate(total, scales_four[:, :1, None], scales_four[:, 1:, None]).astype(BF16)
    fourth = jnp.transpose(fourth, (1, 2, 0, 3))
    half = outs // 2
    own = lax.dynamic_slice_in_dim(fourth, core * half, half, 0)
    theirs = lax.dynamic_slice_in_dim(fourth, (1 - core) * half, half, 0)
    other = lax.ppermute(theirs, "fl", [(0, 1), (1, 0)])
    return jnp.where(core == 0, jnp.concatenate([own, other], 1), jnp.concatenate([other, own], 1))[None]


def solution(mesh):
    return jax.shard_map(
        shards,
        mesh=mesh,
        in_specs=(
            P("sp", None, None, None, None),
            P("fl", None),
            P("fl"),
            P("fl"),
            P("fl", None),
            P("fl"),
            P("fl"),
        ),
        out_specs=P("sp", "fl", None, None, None),
        check_vma=False,
    )
```

time: 640 us -> 113 us (0.18); the launches traced: 629 us -> 112 us
  local copies, waits for them, and re-layouts: 318 us -> 16.4 us
  waiting for transfers between devices: 164 us -> 11.3 us
  matrix products: 85.2 us -> 0 us
  Pallas kernels: 0 us -> 58.5 us
  other arithmetic: 38.9 us -> 3.08 us
  starting transfers between devices: 8.91 us -> 22.6 us
  between operations: 13.8 us -> 0.31 us
    conv_general_dilated x8 -> x0, local copies, waits for them, and re-layouts: 221 us -> none  [convolve(): lax.conv_general_dilated(slab[None], kernel, strides, pads, dimension_num...]
    ppermute x4 -> x11, waiting for transfers between devices: 147 us -> 11.3 us  [the longest x2 4.65 us: exchange(): lax.ppermute(row, axes, along)]
    conv_general_dilated x2 -> x0, matrix products: 85.2 us -> none  [convolve(): lax.conv_general_dilated(slab[None], kernel, strides, pads, dimension_num...]
    pallas_call x0 -> x2, Pallas kernels: none -> 58.5 us  [the longest x1 37.1 us: layer_three(): pl.pallas_call(three_kernel, grid_spec=pltpu.PrefetchScalarGridSpec(num_s...]
    unnamed x29 -> x18, local copies, waits for them, and re-layouts: 53.9 us -> 2.95 us
    broadcast_in_dim x2 -> x0, local copies, waits for them, and re-layouts: 30.8 us -> none  [convolve(): slab[None]]
    broadcast_in_dim x2 -> x0, other arithmetic: 29.8 us -> none  [convolve(): slab[None]]
    all_gather x1 -> x0, waiting for transfers between devices: 17.5 us -> none  [shards(): third = lax.all_gather(third_half, 'fl', axis=0, tiled=True)]
  transfers between devices with their start and end apart: 5 -> 11, of which waited for: 5 -> 5; matrix products, arithmetic and copies ran while one was open for 1% -> 14% of each run, Pallas kernels for 0% -> 33%
where the time goes in v1:
time: 113 us; the launch traced here: 112 us
  Pallas kernels  58.5 us (52%)
  starting transfers between devices  22.6 us (20%)
  local copies, waits for them, and re-layouts  16.4 us (15%)
  waiting for transfers between devices  11.3 us (10%)
  other arithmetic  3.08 us (3%)
    pallas_call x1, Pallas kernels, layer_three(): pl.pallas_call(three_kernel, grid_spec=pltpu.PrefetchScalarGridSpec(num_s...  37.1 us
    pallas_call x1, Pallas kernels, layer_four(): pl.pallas_call(four_kernel, out_shape=[jax.ShapeDtypeStruct((out_rows, ou...  21.4 us
    ppermute x4, starting transfers between devices, both_cores(): other = lax.ppermute(value, 'fl', [(0, 1), (1, 0)])  7.72 us
    ppermute x2, starting transfers between devices, exchange(): lax.ppermute(row, axes, along)  7.12 us
    ppermute x2, waiting for transfers between devices, exchange(): lax.ppermute(row, axes, along)  4.65 us
    ppermute x2, waiting for transfers between devices, exchange(): lax.ppermute(corner, axes, both)  4.18 us
    reshape x2, local copies, waits for them, and re-layouts, tap_major(): jnp.transpose(kernel.reshape(outs, chans, 27), (0, 2, 1))  3.27 us
    unnamed x18, local copies, waits for them, and re-layouts  2.95 us
  transfers between devices with their start and end apart: 11, of which 5 were waited for; matrix products, arithmetic and copies ran while one was open for 14% of the time, Pallas kernels for 33%

profile of v1, /device:TPU:25, one launch (start us, length us, event | category | flops | bytes accessed | tf_op | source)
XLA Modules:
  0.0 112.1 jit_solution(1663229051982629961)
XLA Ops:
  0.0 0.7 pad_maximum_fusion
  0.7 0.7 collective-permute-start.1
  1.5 0.4 collective-permute-start.5
  1.9 1.2 %copy.37 = bf16[64,1728]{0,1:T(8,128)(2,1)S(1)} copy(bf16[64,1728]{1,0:T(8,128)(2,1)} %param.16) | data formatting | bytes 442368 | tf_op args[1]
  3.1 0.1 concatenate.66
  3.3 0.1 maximum_maximum_fusion
  3.4 0.1 copy.41
  3.5 0.1 copy.40
  3.6 0.7 fusion.4
  4.3 0.3 copy.38
  4.6 0.1 concatenate.67
  4.8 0.6 fusion.2
  5.4 0.2 copy.39
  5.6 1.0 copy.42.w_ref
  6.6 37.1 %layer_three.1 = (bf16[4,12,128,256]{3,2,1,0:T(8,128)(2,1)}, f32[12,128,256]{2,1,0:T(8,128)}, f32[4,128,256]{2,1,0:T(8,128)}, bf16[12,128,256]{2,1,0:T(8,128)(2,...) custom-call(s32[1]{0:T(128)} %bitcast.core_ref, bf16[1,64,16,24,512]{4,3,2,1,0:T(8,128)(2,1)} %x_ref.1, ...), custom_call_target="tpu_custom_call" | custom-call | tf_op jit(solution)/shard_map/layer_three/pallas_call | solution.py:131
  43.7 1.3 %collective-permute-start.2 = (bf16[12,128,256]{2,1,0:T(8,128)(2,1)}, bf16[12,128,256]{2,1,0:T(8,128)(2,1)}, u32[]{:S(2)}, u32[]{:S(2)}) collective-permute-start(bf16[12,128,256]{2,1,0:T(8,128)(2,1)} %get-tuple-element.54), channel_id=1, source_target_pairs={{0,1},{2,3},{4,5},{6,7},{8,9},{10,11},{12,13},{14,15},{16,17},{18,... | collective-permute-start | bytes 2359304 | tf_op jit(solution)/shard_map/ppermute | solution.py:266
  45.0 3.2 %collective-permute-start.3 = (bf16[4,128,256]{2,1,0:T(8,128)(2,1)}, bf16[4,128,256]{2,1,0:T(8,128)(2,1)S(1)}, u32[]{:S(2)}, u32[]{:S(2)}) collective-permute-start(bf16[4,128,256]{2,1,0:T(8,128)(2,1)} %get-tuple-element.55), channel_id=1, source_target_pairs={{0,2},{1,3},{2,4},{3,5},{4,6},{5,7},{6,8},{7,9},{8,10},{9,11},{10,... | collective-permute-start | bytes 786440 | tf_op jit(solution)/shard_map/ppermute | solution.py:267
  48.3 1.0 copy.43
  49.3 0.3 concatenate.72
  49.6 1.3 %collective-permute-start.4 = (bf16[128,256]{1,0:T(8,128)(2,1)S(1)}, bf16[128,256]{1,0:T(8,128)(2,1)S(1)}, u32[]{:S(2)}, u32[]{:S(2)}) collective-permute-start(bf16[128,256]{1,0:T(8,128)(2,1)S(1)} %copy-done.7), channel_id=1, source_target_pairs={{0,3},{2,5},{4,7},{6,9},{8,11},{10,13},{12,15},{16,19},{18,21},{20... | collective-permute-start | bytes 196616 | tf_op jit(solution)/shard_map/ppermute | solution.py:268
  50.9 1.9 %copy.44 = bf16[128,3456]{0,1:T(8,128)(2,1)S(1)} copy(bf16[128,3456]{1,0:T(8,128)(2,1)} %collective-permute-done.5) | data formatting | bytes 1769472 | tf_op jit(solution)/shard_map/ppermute | solution.py:273
  52.8 0.3 concatenate.73
  53.1 0.9 fusion
  54.0 1.0 copy.45
  55.0 2.3 %copy.46.w_ref = bf16[256,3456]{1,0:T(8,128)(2,1)} copy(bf16[256,3456]{0,1:T(8,128)(2,1)S(1)} %bitcast.36) | data formatting | bytes 3538944 | tf_op jit(solution)/shard_map/reshape | solution.py:279
  57.3 4.0 %collective-permute-done.4.halo_corner_ref = bf16[128,256]{1,0:T(8,128)(2,1)S(1)} collective-permute-done((bf16[128,256]{1,0:T(8,128)(2,1)S(1)}, bf16[128,256]{1,0:T(8,128)(2,1)S(1)}, u32[]{:S(2)}, u32[]{:S(2)}) %collective-permute-start.4) | collective-permute-done | bytes 65568 | tf_op jit(solution)/shard_map/ppermute | solution.py:268
  61.3 0.6 copy-done.2
  61.9 0.1 copy-done.1
  62.0 21.4 %layer_four.1 = (f32[6,256,256]{2,1,0:T(8,128)}, bf16[6,256,128]{2,1,0:T(8,128)(2,1)}, bf16[256,256]{1,0:T(8,128)(2,1)}, bf16[256,128]{1,0:T(8,128)(2,1)}) custom-call(bf16[4,12,128,256]{3,2,1,0:T(8,128)(2,1)} %get-tuple-element.51.third_ref, f32[12,128,256]{2,1,0:T(8,128)} %get-tuple-element.52.plane_ref, f32[4,128,256]{2,1,0:T(8,128)} %get-tuple-element.53.row_ref, ...), custom_call_target="tpu_custom_call" | custom-call | tf_op jit(solution)/shard_map/layer_four/pallas_call | solution.py:241
  83.4 1.3 %collective-permute-start.6 = (bf16[6,256,128]{2,1,0:T(8,128)(2,1)}, bf16[6,256,128]{2,1,0:T(8,128)(2,1)S(1)}, u32[]{:S(2)}, u32[]{:S(2)}) collective-permute-start(bf16[6,256,128]{2,1,0:T(8,128)(2,1)} %get-tuple-element.58), channel_id=1, source_target_pairs={{0,1},{2,3},{4,5},{6,7},{8,9},{10,11},{12,13},{14,15},{16,17},{18,... | collective-permute-start | bytes 1179656 | tf_op jit(solution)/shard_map/ppermute | solution.py:266
  84.7 6.5 %collective-permute-start.9 = (f32[128,2]{0,1:T(2,128)S(1)}, f32[128,2]{0,1:T(2,128)S(1)}, u32[]{:S(2)}, u32[]{:S(2)}) collective-permute-start(f32[128,2]{0,1:T(2,128)S(1)} %pad_maximum_fusion.2), channel_id=1, source_target_pairs={{0,1},{1,0},{2,3},{3,2},{4,5},{5,4},{6,7},{7,6},{8,9},{9,8},{10,11... | collective-permute-start | bytes 3080 | tf_op jit(solution)/shard_map/ppermute | solution.py:273
  91.3 1.1 collective-permute-done.9
  92.3 3.9 %collective-permute-start.7 = (bf16[256,256]{1,0:T(8,128)(2,1)}, bf16[256,256]{1,0:T(8,128)(2,1)}, u32[]{:S(2)}, u32[]{:S(2)}) collective-permute-start(bf16[256,256]{1,0:T(8,128)(2,1)} %get-tuple-element.59), channel_id=1, source_target_pairs={{0,2},{1,3},{2,4},{3,5},{4,6},{5,7},{6,8},{7,9},{8,10},{9,11},{10,... | collective-permute-start | bytes 393224 | tf_op jit(solution)/shard_map/ppermute | solution.py:267
  96.2 1.9 %copy.47 = f32[6,256,256]{1,2,0:T(8,128)S(1)} copy(f32[6,256,256]{2,1,0:T(8,128)} %get-tuple-element.57) | data formatting | bytes 3145728 | tf_op jit(solution)/shard_map/layer_four/pallas_call | solution.py:241
  98.1 0.5 copy.49
  98.6 1.3 %collective-permute-start.8 = (bf16[256,128]{1,0:T(8,128)(2,1)}, bf16[256,128]{1,0:T(8,128)(2,1)S(1)}, u32[]{:S(2)}, u32[]{:S(2)}) collective-permute-start(bf16[256,128]{1,0:T(8,128)(2,1)} %get-tuple-element.60), channel_id=1, source_target_pairs={{0,3},{2,5},{4,7},{6,9},{8,11},{10,13},{12,15},{16,19},{18,21},{20... | collective-permute-start | bytes 196616 | tf_op jit(solution)/shard_map/ppermute | solution.py:268
  99.9 4.6 %collective-permute-done.7 = bf16[256,256]{1,0:T(8,128)(2,1)} collective-permute-done((bf16[256,256]{1,0:T(8,128)(2,1)}, bf16[256,256]{1,0:T(8,128)(2,1)}, u32[]{:S(2)}, u32[]{:S(2)}) %collective-permute-start.7) | collective-permute-done | bytes 131104 | tf_op jit(solution)/shard_map/ppermute | solution.py:267
  104.5 1.0 copy.50
  105.5 0.1 copy.51
  105.7 0.2 fusion.1
  105.9 0.1 constant_dynamic-update-slice_fusion
  106.0 0.2 collective-permute-done.8
  106.2 0.3 maximum_convert_fusion
  106.5 0.1 dynamic-slice_bitcast_fusion.1
  106.6 2.6 %collective-permute-start.10 = (bf16[128,2,6,128]{3,0,1,2:T(8,128)(2,1)S(1)}, bf16[128,2,6,128]{3,0,1,2:T(8,128)(2,1)S(1)}, u32[]{:S(2)}, u32[]{:S(2)}) collective-permute-start(bf16[128,2,6,128]{3,0,1,2:T(8,128)(2,1)S(1)} %get-tuple-element.64), channel_id=1, source_target_pairs={{0,1},{1,0},{2,3},{3,2},{4,5},{5,4},{6,7},{7,6},{8,9},{9,8},{10,11... | collective-permute-start | bytes 1179656 | tf_op jit(solution)/shard_map/ppermute | solution.py:306
  109.2 1.3 %collective-permute-done.10 = bf16[128,2,6,128]{3,0,1,2:T(8,128)(2,1)S(1)} collective-permute-done((bf16[128,2,6,128]{3,0,1,2:T(8,128)(2,1)S(1)}, bf16[128,2,6,128]{3,0,1,2:T(8,128)(2,1)S(1)}, u32[]{:S(2)}, u32[]{:S(2)}) %collective-permute-start.10) | collective-permute-done | bytes 393248 | tf_op jit(solution)/shard_map/ppermute | solution.py:306
  110.6 0.1 maximum_select_fusion.1
  110.6 1.5 %copy.52 = bf16[1,128,4,6,128]{4,2,3,1,0:T(4,128)(2,1)} copy(bf16[1,128,4,6,128]{4,1,2,3,0:T(8,128)(2,1)S(1)} %maximum_select_fusion.1) | data formatting | bytes 1572864 | tf_op jit(solution)/shard_map/jit(_where)/select_n | solution.py:307
  (26 shorter events, 0.2 us)
Async XLA Ops:
  0.0 3.3 %copy-start.5 = (f32[64]{0:T(128)S(1)}, f32[64]{0:T(128)}, u32[]{:S(2)}) copy-start(f32[64]{0:T(128)} %param.18) | copy-start | bytes 772
  0.0 3.3 %copy-start.6 = (f32[64]{0:T(128)S(1)}, f32[64]{0:T(128)}, u32[]{:S(2)}) copy-start(f32[64]{0:T(128)} %param.17) | copy-start | bytes 772
  0.7 2.5 %collective-permute-start.1 = (f32[64,2]{0,1:T(2,128)S(1)}, f32[64,2]{0,1:T(2,128)S(1)}, u32[]{:S(2)}, u32[]{:S(2)}) collective-permute-start(f32[64,2]{0,1:T(2,128)S(1)} %pad_maximum_fusion), channel_id=1, source_target_pairs={{0,1},{1,0},{2,3},{3,2},{4,5},{5,4},{6,7},{7,6},{8,9},{9,8},{10,11... | collective-permute-start | bytes 1544 | tf_op jit(solution)/shard_map/ppermute | solution.py:273
  1.4 2.9 %collective-permute-start = (bf16[64,1728]{1,0:T(8,128)(2,1)}, bf16[64,1728]{1,0:T(8,128)(2,1)S(1)}, u32[]{:S(2)}, u32[]{:S(2)}) collective-permute-start(bf16[64,1728]{1,0:T(8,128)(2,1)} %param.16), channel_id=1, source_target_pairs={{0,1},{1,0},{2,3},{3,2},{4,5},{5,4},{6,7},{7,6},{8,9},{9,8},{10,11... | collective-permute-start | bytes 663560 | tf_op jit(solution)/shard_map/ppermute | solution.py:273
  1.5 49.4 %collective-permute-start.5 = (bf16[128,3456]{1,0:T(8,128)(2,1)}, bf16[128,3456]{1,0:T(8,128)(2,1)}, u32[]{:S(2)}, u32[]{:S(2)}) collective-permute-start(bf16[128,3456]{1,0:T(8,128)(2,1)} %param.19), channel_id=1, source_target_pairs={{0,1},{1,0},{2,3},{3,2},{4,5},{5,4},{6,7},{7,6},{8,9},{9,8},{10,11... | collective-permute-start | bytes 2654216 | tf_op jit(solution)/shard_map/ppermute | solution.py:273
  6.6 41.7 %copy-start = (bf16[128,3456]{1,0:T(8,128)(2,1)S(1)}, bf16[128,3456]{1,0:T(8,128)(2,1)}, u32[]{:S(2)}) copy-start(bf16[128,3456]{1,0:T(8,128)(2,1)} %param.19) | copy-start | bytes 2654212
  43.7 17.6 %collective-permute-start.2 = (bf16[12,128,256]{2,1,0:T(8,128)(2,1)}, bf16[12,128,256]{2,1,0:T(8,128)(2,1)}, u32[]{:S(2)}, u32[]{:S(2)}) collective-permute-start(bf16[12,128,256]{2,1,0:T(8,128)(2,1)} %get-tuple-element.54), channel_id=1, source_target_pairs={{0,1},{2,3},{4,5},{6,7},{8,9},{10,11},{12,13},{14,15},{16,17},{18,... | collective-permute-start | bytes 2359304 | tf_op jit(solution)/shard_map/ppermute | solution.py:266
  45.0 4.6 %copy-start.7 = (bf16[128,256]{1,0:T(8,128)(2,1)S(1)}, bf16[128,256]{1,0:T(8,128)(2,1)}, u32[]{:S(2)}) copy-start(bf16[128,256]{1,0:T(8,128)(2,1)} %get-tuple-element.56) | copy-start | bytes 196612
  45.0 16.3 %collective-permute-start.3 = (bf16[4,128,256]{2,1,0:T(8,128)(2,1)}, bf16[4,128,256]{2,1,0:T(8,128)(2,1)S(1)}, u32[]{:S(2)}, u32[]{:S(2)}) collective-permute-start(bf16[4,128,256]{2,1,0:T(8,128)(2,1)} %get-tuple-element.55), channel_id=1, source_target_pairs={{0,2},{1,3},{2,4},{3,5},{4,6},{5,7},{6,8},{7,9},{8,10},{9,11},{10,... | collective-permute-start | bytes 786440 | tf_op jit(solution)/shard_map/ppermute | solution.py:267
  49.6 11.7 %collective-permute-start.4 = (bf16[128,256]{1,0:T(8,128)(2,1)S(1)}, bf16[128,256]{1,0:T(8,128)(2,1)S(1)}, u32[]{:S(2)}, u32[]{:S(2)}) collective-permute-start(bf16[128,256]{1,0:T(8,128)(2,1)S(1)} %copy-done.7), channel_id=1, source_target_pairs={{0,3},{2,5},{4,7},{6,9},{8,11},{10,13},{12,15},{16,19},{18,21},{20... | collective-permute-start | bytes 196616 | tf_op jit(solution)/shard_map/ppermute | solution.py:268
  61.3 0.6 copy-start.2
  61.3 0.7 copy-start.1
  62.0 22.7 %copy-start.3 = (f32[128]{0:T(128)S(1)}, f32[128]{0:T(128)}, u32[]{:S(2)}) copy-start(f32[128]{0:T(128)} %param.21) | copy-start | bytes 1540
  62.0 22.7 %copy-start.4 = (f32[128]{0:T(128)S(1)}, f32[128]{0:T(128)}, u32[]{:S(2)}) copy-start(f32[128]{0:T(128)} %param.20) | copy-start | bytes 1540
  83.4 22.3 %collective-permute-start.6 = (bf16[6,256,128]{2,1,0:T(8,128)(2,1)}, bf16[6,256,128]{2,1,0:T(8,128)(2,1)S(1)}, u32[]{:S(2)}, u32[]{:S(2)}) collective-permute-start(bf16[6,256,128]{2,1,0:T(8,128)(2,1)} %get-tuple-element.58), channel_id=1, source_target_pairs={{0,1},{2,3},{4,5},{6,7},{8,9},{10,11},{12,13},{14,15},{16,17},{18,... | collective-permute-start | bytes 1179656 | tf_op jit(solution)/shard_map/ppermute | solution.py:266
  84.7 7.6 %collective-permute-start.9 = (f32[128,2]{0,1:T(2,128)S(1)}, f32[128,2]{0,1:T(2,128)S(1)}, u32[]{:S(2)}, u32[]{:S(2)}) collective-permute-start(f32[128,2]{0,1:T(2,128)S(1)} %pad_maximum_fusion.2), channel_id=1, source_target_pairs={{0,1},{1,0},{2,3},{3,2},{4,5},{5,4},{6,7},{7,6},{8,9},{9,8},{10,11... | collective-permute-start | bytes 3080 | tf_op jit(solution)/shard_map/ppermute | solution.py:273
  92.3 12.2 %collective-permute-start.7 = (bf16[256,256]{1,0:T(8,128)(2,1)}, bf16[256,256]{1,0:T(8,128)(2,1)}, u32[]{:S(2)}, u32[]{:S(2)}) collective-permute-start(bf16[256,256]{1,0:T(8,128)(2,1)} %get-tuple-element.59), channel_id=1, source_target_pairs={{0,2},{1,3},{2,4},{3,5},{4,6},{5,7},{6,8},{7,9},{8,10},{9,11},{10,... | collective-permute-start | bytes 393224 | tf_op jit(solution)/shard_map/ppermute | solution.py:267
  98.6 7.6 %collective-permute-start.8 = (bf16[256,128]{1,0:T(8,128)(2,1)}, bf16[256,128]{1,0:T(8,128)(2,1)S(1)}, u32[]{:S(2)}, u32[]{:S(2)}) collective-permute-start(bf16[256,128]{1,0:T(8,128)(2,1)} %get-tuple-element.60), channel_id=1, source_target_pairs={{0,3},{2,5},{4,7},{6,9},{8,11},{10,13},{12,15},{16,19},{18,21},{20... | collective-permute-start | bytes 196616 | tf_op jit(solution)/shard_map/ppermute | solution.py:268
  106.6 4.0 %collective-permute-start.10 = (bf16[128,2,6,128]{3,0,1,2:T(8,128)(2,1)S(1)}, bf16[128,2,6,128]{3,0,1,2:T(8,128)(2,1)S(1)}, u32[]{:S(2)}, u32[]{:S(2)}) collective-permute-start(bf16[128,2,6,128]{3,0,1,2:T(8,128)(2,1)S(1)} %get-tuple-element.64), channel_id=1, source_target_pairs={{0,1},{1,0},{2,3},{3,2},{4,5},{5,4},{6,7},{7,6},{8,9},{9,8},{10,11... | collective-permute-start | bytes 1179656 | tf_op jit(solution)/shard_map/ppermute | solution.py:306

commit v2 on v1

v2 whole, which is shorter than its diff:
```python
import functools

import jax
import jax.numpy as jnp
import numpy as np
from jax import lax
from jax.experimental import pallas as pl
from jax.experimental.pallas import tpu as pltpu
from jax.sharding import PartitionSpec as P

F32 = jnp.float32
BF16 = jnp.bfloat16
LANES = 128
ROW_BLOCKS = 8
SUB = 8
GROUP = 16
VMEM_LIMIT = 56 * 2**20


def even_odd(width):
    half = width // 2
    place = np.zeros((width, width), np.float32)
    place[np.arange(0, width, 2), np.arange(half)] = 1
    place[np.arange(1, width, 2), half + np.arange(half)] = 1
    return jnp.asarray(place, BF16)


def activate(total, gain, shift):
    return jnp.maximum(total * gain + shift, 0.0)


def shifted(odd):
    lane = lax.broadcasted_iota(jnp.int32, odd.shape, 1)
    return jnp.where(lane == 0, 0.0, pltpu.roll(odd, 1, 1))


def spread(sides, place):
    quarter = place.shape[0] // 2
    split = [jnp.dot(side, place, preferred_element_type=F32) for side in sides]
    even = jnp.concatenate([part[:, :quarter] for part in split], 1)
    odd = jnp.concatenate([part[:, quarter:] for part in split], 1)
    return shifted(odd), even, odd


def separate(x_ref, plane, place_ref, split_refs, store):
    chans, rows, width = x_ref.shape[1], x_ref.shape[3], x_ref.shape[4]
    half = width // 2
    quarter = half // 2
    for index, first in enumerate(range(0, chans, GROUP)):
        split_ref = split_refs[index % len(split_refs)]
        x = x_ref[0, pl.ds(first, GROUP), plane]
        x = x.astype(F32).reshape(GROUP * rows, width).astype(BF16)
        for side in range(2):
            parts = jnp.dot(
                x[:, side * half : (side + 1) * half], place_ref[...], preferred_element_type=F32
            )
            for block in range(half // LANES):
                odd, at = divmod(block, quarter // LANES)
                split_ref[odd, side * (quarter // LANES) + at] = parts[:, block * LANES : (block + 1) * LANES]
        for row in range(rows):
            even, odd = (
                jnp.concatenate(
                    [split_ref[odd, at, pl.ds(row, GROUP, stride=rows), :] for at in range(half // LANES)], 1
                )
                for odd in range(2)
            )
            for tap, value in enumerate((shifted(odd), even, odd)):
                store(tap, row, first, value.astype(BF16))


def three_edges_kernel(
    core_ref, last_ref, rim_ref, w_ref, place_ref,
    next_plane_ref, next_row_ref, next_corner_ref,
    *scratch,
):
    *split_refs, pick_ref, data_ref = scratch
    chans, rows, width = last_ref.shape[1], last_ref.shape[3], last_ref.shape[4]
    planes = rim_ref.shape[2]
    half = width // 2
    out_rows = rows // 2
    taps = 3 * chans
    rim = (rows - 1) % SUB

    picked = []
    for plane in range(planes):
        x = rim_ref[0, :, plane, :SUB].astype(F32).reshape(chans * SUB, width)
        for at in range(width // LANES):
            pick_ref[plane % 2, at] = x[:, at * LANES : (at + 1) * LANES]
        picked.append(
            jnp.concatenate(
                [pick_ref[plane % 2, at, pl.ds(rim, chans, stride=SUB), :] for at in range(width // LANES)], 1
            ).astype(BF16)
        )
    picked = jnp.concatenate(picked, 0)
    parts = spread((picked[:, :half], picked[:, half:]), place_ref[...])
    parts = [part.astype(BF16) for part in parts]

    def rim_data(plane):
        return jnp.concatenate([part[plane * chans : (plane + 1) * chans] for part in parts], 0)

    none = jnp.zeros((taps, half), BF16)
    for step in range(planes // 2):
        pieces = []
        for plane in range(2 * step - 1, 2 * step + 2):
            pieces += [none if plane < 0 else rim_data(plane), none, none]
        total = jnp.dot(w_ref[...], jnp.concatenate(pieces, 0), preferred_element_type=F32)
        next_row_ref[step] = total.astype(BF16)

    def beyond(data):
        return jnp.dot(w_ref[:, : 3 * taps], data, preferred_element_type=F32).astype(BF16)

    next_corner_ref[...] = beyond(jnp.concatenate([rim_data(planes - 1), none, none], 0))

    def store(tap, row, first, value):
        data_ref[row + 1, tap * chans + first : tap * chans + first + GROUP, :] = value

    data_ref[0] = jnp.zeros_like(data_ref[0])
    separate(last_ref, 0, place_ref, split_refs, store)
    for row in range(out_rows):
        next_plane_ref[row] = beyond(data_ref[2 * row : 2 * row + 3].reshape(3 * taps, half))


def three_edges(volume, weights, core):
    _, chans, planes, rows, width = volume.shape
    outs = weights.shape[0]
    half = width // 2
    own, out_rows = planes // 2, rows // 2
    full = lambda *shape: pl.BlockSpec(shape, lambda i, core: (0,) * len(shape))
    return pl.pallas_call(
        three_edges_kernel,
        grid_spec=pltpu.PrefetchScalarGridSpec(
            num_scalar_prefetch=1,
            grid=(1,),
            in_specs=[
                pl.BlockSpec((1, chans, 1, rows, width), lambda i, core: (0, 0, (core[0] + 1) * own - 1, 0, 0)),
                pl.BlockSpec((1, chans, own, 2 * SUB, width), lambda i, core: (0, 0, core[0], (rows - 1) // (2 * SUB), 0)),
                full(*weights.shape),
                full(half, half),
            ],
            out_specs=[
                full(out_rows, outs, half),
                full(own // 2, outs, half),
                full(outs, half),
            ],
            scratch_shapes=[pltpu.VMEM((2, half // LANES, GROUP * rows, LANES), F32)] * 4
            + [
                pltpu.VMEM((2, width // LANES, chans * SUB, LANES), F32),
                pltpu.VMEM((rows + 1, 3 * chans, half), BF16),
            ],
        ),
        out_shape=[
            jax.ShapeDtypeStruct((out_rows, outs, half), BF16),
            jax.ShapeDtypeStruct((own // 2, outs, half), BF16),
            jax.ShapeDtypeStruct((outs, half), BF16),
        ],
        compiler_params=pltpu.CompilerParams(vmem_limit_bytes=VMEM_LIMIT),
        cost_estimate=pl.CostEstimate(flops=2 * 10**9, bytes_accessed=8 * 10**6, transcendentals=0),
        name="three_edges",
    )(core, volume, volume, weights, even_odd(half))


def three_kernel(
    core_ref, x_ref, w_ref, place_ref, gain_ref, shift_ref,
    third_ref, plane_ref, row_ref,
    *scratch,
):
    *split_refs, data_ref, total_ref = scratch
    step = pl.program_id(0)
    chans, rows, width = x_ref.shape[1], x_ref.shape[3], x_ref.shape[4]
    half = width // 2
    out_rows = rows // 2
    taps = 3 * chans

    @pl.when(step == 0)
    def _():
        data_ref[0] = jnp.zeros_like(data_ref[0])
        for slot in (1, 2):
            data_ref[slot, 0] = jnp.zeros_like(data_ref[slot, 0])

    @pl.when(step > 0)
    def _():
        data_ref[0] = data_ref[2]

    for plane in range(2):

        def store(tap, row, first, value, slot=plane + 1):
            data_ref[slot, row + 1, tap * chans + first : tap * chans + first + GROUP, :] = value

        separate(x_ref, plane, place_ref, split_refs, store)

    gain, shift = gain_ref[...], shift_ref[...]
    for row in range(out_rows):
        parts = [data_ref[slot, 2 * row : 2 * row + 3].reshape(3 * taps, half) for slot in range(3)]
        total = jnp.dot(w_ref[...], jnp.concatenate(parts, 0), preferred_element_type=F32)
        third_ref[0, row] = activate(total, gain, shift).astype(BF16)
        total_ref[row] = total
    row_ref[0] = total_ref[0]

    @pl.when(step == 0)
    def _():
        plane_ref[...] = total_ref[...]


def layer_three(volume, weights, gain, shift, core):
    _, chans, planes, rows, width = volume.shape
    outs = weights.shape[0]
    half = width // 2
    steps, out_rows = planes // 4, rows // 2
    full = lambda *shape: pl.BlockSpec(shape, lambda i, core: (0,) * len(shape))
    return pl.pallas_call(
        three_kernel,
        grid_spec=pltpu.PrefetchScalarGridSpec(
            num_scalar_prefetch=1,
            grid=(steps,),
            in_specs=[
                pl.BlockSpec((1, chans, 2, rows, width), lambda i, core: (0, 0, core[0] * steps + i, 0, 0)),
                full(*weights.shape),
                full(half, half),
                full(outs, 1),
                full(outs, 1),
            ],
            out_specs=[
                pl.BlockSpec((1, out_rows, outs, half), lambda i, core: (i, 0, 0, 0)),
                full(out_rows, outs, half),
                pl.BlockSpec((1, outs, half), lambda i, core: (i, 0, 0)),
            ],
            scratch_shapes=[pltpu.VMEM((2, half // LANES, GROUP * rows, LANES), F32)] * 4
            + [
                pltpu.VMEM((3, rows + 1, 3 * chans, half), BF16),
                pltpu.VMEM((out_rows, outs, half), F32),
            ],
        ),
        out_shape=[
            jax.ShapeDtypeStruct((steps, out_rows, outs, half), BF16),
            jax.ShapeDtypeStruct((out_rows, outs, half), F32),
            jax.ShapeDtypeStruct((steps, outs, half), F32),
        ],
        compiler_params=pltpu.CompilerParams(vmem_limit_bytes=VMEM_LIMIT),
        cost_estimate=pl.CostEstimate(flops=10**10, bytes_accessed=2 * 10**7, transcendentals=0),
        name="layer_three",
    )(core, volume, weights, even_odd(half), gain, shift)


def third_value(refs, plane, row):
    third_ref, plane_ref, row_ref, halo_plane_ref, halo_row_ref, halo_corner_ref, gain_ref, shift_ref = refs
    if plane and row:
        return third_ref[plane, row]
    total = row_ref[plane] if plane else plane_ref[row] + halo_plane_ref[row].astype(F32)
    if not row:
        total = total + halo_row_ref[plane].astype(F32)
        if not plane:
            total = total + halo_corner_ref[...].astype(F32)
    return activate(total, gain_ref[...], shift_ref[...]).astype(BF16)


def four_edges_kernel(*refs):
    *thirds, w_ref, place_ref, next_plane_ref, next_row_ref, next_corner_ref = refs
    planes, rows, chans, width = thirds[0].shape
    half = width // 2
    out_rows, count = rows // 2, planes // 2
    taps = 3 * chans

    def data(spots):
        values = jnp.concatenate([third_value(thirds, *spot) for spot in spots], 0)
        parts = [part.astype(BF16) for part in spread((values,), place_ref[...])]
        return [
            jnp.concatenate([part[at * chans : (at + 1) * chans] for part in parts], 0) for at in range(len(spots))
        ]

    none = jnp.zeros((taps, half), BF16)
    rim = data([(plane, rows - 1) for plane in range(planes)])
    last = [none] + data([(planes - 1, row) for row in range(rows - 1)]) + [rim[planes - 1]]

    def beyond(pieces):
        return jnp.dot(w_ref[:, : 3 * taps], pieces, preferred_element_type=F32).astype(BF16)

    for row in range(0, out_rows, 2):
        pieces = [jnp.concatenate([last[2 * row + at], last[2 * row + 2 + at]], 1) for at in range(3)]
        both = beyond(jnp.concatenate(pieces, 0))
        next_plane_ref[row] = both[:, :half]
        next_plane_ref[row + 1] = both[:, half:]
    empty = jnp.zeros((taps, count * half), BF16)
    pieces = []
    for slot in range(3):
        pieces.append(
            jnp.concatenate([rim[2 * m + slot - 1] if 2 * m + slot else none for m in range(count)], 1)
        )
        pieces += [empty, empty]
    next_row_ref[...] = jnp.dot(
        w_ref[...], jnp.concatenate(pieces, 0), preferred_element_type=F32
    ).astype(BF16)
    next_corner_ref[...] = beyond(jnp.concatenate([rim[planes - 1], none, none], 0))


def four_edges(thirds, weights):
    planes, rows, chans, width = thirds[0].shape
    outs = weights.shape[0]
    half = width // 2
    return pl.pallas_call(
        four_edges_kernel,
        out_shape=[
            jax.ShapeDtypeStruct((rows // 2, outs, half), BF16),
            jax.ShapeDtypeStruct((outs, planes // 2 * half), BF16),
            jax.ShapeDtypeStruct((outs, half), BF16),
        ],
        compiler_params=pltpu.CompilerParams(vmem_limit_bytes=VMEM_LIMIT),
        cost_estimate=pl.CostEstimate(flops=2 * 10**9, bytes_accessed=8 * 10**6, transcendentals=0),
        name="four_edges",
    )(*thirds, weights, even_odd(width))


def four_kernel(*refs):
    *thirds, w_ref, place_ref, sums_ref, data_ref = refs
    planes, rows, chans, width = thirds[0].shape
    half = width // 2
    out_rows, count = rows // 2, planes // 2
    taps = 3 * chans
    data_ref[:, 0] = jnp.zeros_like(data_ref[:, 0])
    data_ref[0, :, :, :half] = jnp.zeros_like(data_ref[0, :, :, :half])
    batch = 4
    for plane in range(planes):
        spots = [(1 + plane % 2, plane // 2)]
        if plane % 2 and plane // 2 + 1 < count:
            spots.append((0, plane // 2 + 1))
        for first in range(0, rows, batch):
            values = jnp.concatenate([third_value(thirds, plane, row) for row in range(first, first + batch)], 0)
            for tap, part in enumerate(spread((values,), place_ref[...])):
                part = part.astype(BF16)
                for at in range(batch):
                    for slot, lanes in spots:
                        data_ref[
                            slot, first + at + 1, tap * chans : (tap + 1) * chans, lanes * half : (lanes + 1) * half
                        ] = part[at * chans : (at + 1) * chans]
    for row in range(out_rows):
        parts = [data_ref[slot, 2 * row : 2 * row + 3].reshape(3 * taps, count * half) for slot in range(3)]
        sums_ref[row] = jnp.dot(w_ref[...], jnp.concatenate(parts, 0), preferred_element_type=F32)


def layer_four(thirds, weights):
    planes, rows, chans, width = thirds[0].shape
    outs = weights.shape[0]
    half = width // 2
    out_rows, count = rows // 2, planes // 2
    return pl.pallas_call(
        four_kernel,
        out_shape=jax.ShapeDtypeStruct((out_rows, outs, count * half), F32),
        scratch_shapes=[pltpu.VMEM((3, rows + 1, 3 * chans, count * half), BF16)],
        compiler_params=pltpu.CompilerParams(vmem_limit_bytes=VMEM_LIMIT),
        cost_estimate=pl.CostEstimate(flops=8 * 10**9, bytes_accessed=10**7, transcendentals=0),
        name="layer_four",
    )(*thirds, weights, even_odd(width))


def exchange(plane, row, corner):
    count = lax.axis_size("sp")
    axes = ("sp", "fl")
    blocks = range(count)
    inner = [b for b in blocks if b % ROW_BLOCKS != ROW_BLOCKS - 1]
    down = [(2 * b, 2 * b + 1) for b in blocks]
    down += [(2 * b + 1, 2 * (b + ROW_BLOCKS)) for b in blocks if b + ROW_BLOCKS < count]
    along = [(2 * b + core, 2 * (b + 1) + core) for b in inner for core in range(2)]
    both = [(2 * b, 2 * (b + 1) + 1) for b in inner]
    both += [(2 * b + 1, 2 * (b + 1 + ROW_BLOCKS)) for b in inner if b + ROW_BLOCKS < count]
    return (
        lax.ppermute(plane, axes, down),
        lax.ppermute(row, axes, along),
        lax.ppermute(corner, axes, both),
    )


def both_cores(value, core):
    other = lax.ppermute(value, "fl", [(0, 1), (1, 0)])
    return jnp.where(core == 0, jnp.concatenate([value, other], 0), jnp.concatenate([other, value], 0))


def tap_major(kernel, chans):
    outs = kernel.shape[0]
    return jnp.transpose(kernel.reshape(outs, chans, 27), (0, 2, 1)).reshape(outs, 27 * chans)


def shards(volume, kernel_three, gain_three, shift_three, kernel_four, gain_four, shift_four):
    core = lax.axis_index("fl")
    chans = volume.shape[1]
    mid = 2 * kernel_three.shape[0]
    scales_three = both_cores(jnp.stack([gain_three, shift_three], 1), core)
    scales_four = both_cores(jnp.stack([gain_four, shift_four], 1), core)
    weights_three = tap_major(both_cores(kernel_three, core), chans)
    weights_four = tap_major(both_cores(kernel_four, core), mid)
    gain, shift = scales_three[:, :1], scales_three[:, 1:]
    index = core.reshape(1)
    halos = exchange(*three_edges(volume, weights_three, index))
    thirds = (*layer_three(volume, weights_three, gain, shift, index), *halos, gain, shift)
    halo_plane, halo_row, halo_corner = exchange(*four_edges(thirds, weights_four))
    total = layer_four(thirds, weights_four)
    out_rows, outs, lanes = total.shape
    width = halo_plane.shape[2]
    total = total.reshape(out_rows, outs, lanes // width, width)
    total = total.at[:, :, 0].add(halo_plane.astype(F32))
    total = total.at[0].add(halo_row.reshape(outs, lanes // width, width).astype(F32))
    total = total.at[0, :, 0].add(halo_corner.astype(F32))
    fourth = activate(total, scales_four[:, :1, None], scales_four[:, 1:, None]).astype(BF16)
    fourth = jnp.transpose(fourth, (1, 2, 0, 3))
    half = outs // 2
    own = lax.dynamic_slice_in_dim(fourth, core * half, half, 0)
    theirs = lax.dynamic_slice_in_dim(fourth, (1 - core) * half, half, 0)
    other = lax.ppermute(theirs, "fl", [(0, 1), (1, 0)])
    return jnp.where(core == 0, jnp.concatenate([own, other], 1), jnp.concatenate([other, own], 1))[None]


def solution(mesh):
    return jax.shard_map(
        shards,
        mesh=mesh,
        in_specs=(
            P("sp", None, None, None, None),
            P("fl", None),
            P("fl"),
            P("fl"),
            P("fl", None),
            P("fl"),
            P("fl"),
        ),
        out_specs=P("sp", "fl", None, None, None),
        check_vma=False,
    )
```

time: 113 us -> 87.5 us (0.77)
  Pallas kernels: 58.5 us -> 39.8 us
  starting transfers between devices: 22.6 us -> 16.5 us
  waiting for transfers between devices: 11.3 us -> 8.69 us
    pallas_call x1, Pallas kernels: 37.1 us -> 18.3 us  [layer_three(): pl.pallas_call(three_kernel, grid_spec=pltpu.PrefetchScalarGridSpec(num_s...]
    ppermute x4, starting transfers between devices: 7.72 us -> 1.26 us  [both_cores(): other = lax.ppermute(value, 'fl', [(0, 1), (1, 0)])]
    ppermute x2, waiting for transfers between devices: 4.65 us -> 0.01 us  [exchange(): lax.ppermute(row, axes, along)]
    ppermute x2, waiting for transfers between devices: 4.18 us -> 7.32 us  [exchange(): lax.ppermute(corner, axes, both)]
    unnamed x18 -> x14, local copies, waits for them, and re-layouts: 2.95 us -> 4 us
    pallas_call x1 -> x3, Pallas kernels: 21.4 us -> 21.5 us  [the longest x1 8.79 us: layer_four(): pl.pallas_call(four_kernel, out_shape=jax.ShapeDtypeStruct((out_rows, out...]
  transfers between devices with their start and end apart: 11 -> 11, of which waited for: 5 -> 2; matrix products, arithmetic and copies ran while one was open for 14% -> 20% of each run, Pallas kernels for 33% -> 39%
where the time goes in v2:
time: 87.5 us; the launch traced here: 86.4 us
  Pallas kernels  39.8 us (45%)
  local copies, waits for them, and re-layouts  17.4 us (20%)
  starting transfers between devices  16.5 us (19%)
  waiting for transfers between devices  8.69 us (10%)
  other arithmetic  3.68 us (4%)
    pallas_call x1, Pallas kernels, layer_three(): pl.pallas_call(three_kernel, grid_spec=pltpu.PrefetchScalarGridSpec(num_s...  18.3 us
    pallas_call x1, Pallas kernels, layer_four(): pl.pallas_call(four_kernel, out_shape=jax.ShapeDtypeStruct((out_rows, out...  8.79 us
    ppermute x2, waiting for transfers between devices, exchange(): lax.ppermute(corner, axes, both)  7.32 us
    pallas_call x1, Pallas kernels, three_edges(): pl.pallas_call(three_edges_kernel, grid_spec=pltpu.PrefetchScalarGridSpec...  6.66 us
    ppermute x2, starting transfers between devices, exchange(): lax.ppermute(row, axes, along)  6.23 us
    pallas_call x1, Pallas kernels, four_edges(): pl.pallas_call(four_edges_kernel, out_shape=[jax.ShapeDtypeStruct((rows /...  6.03 us
    unnamed x14, local copies, waits for them, and re-layouts  4 us
    ppermute x1, starting transfers between devices, shards(): other = lax.ppermute(theirs, 'fl', [(0, 1), (1, 0)])  3.44 us
  transfers between devices with their start and end apart: 11, of which 2 were waited for; matrix products, arithmetic and copies ran while one was open for 20% of the time, Pallas kernels for 39%

profile of v2, /device:TPU:25, one launch (start us, length us, event | category | flops | bytes accessed | tf_op | source)
XLA Modules:
  0.0 86.4 jit_solution(2856919874606322805)
XLA Ops:
  0.0 0.7 pad_maximum_fusion.2
  0.7 0.7 collective-permute-start.9
  1.4 0.7 pad_maximum_fusion
  2.0 0.5 collective-permute-start
  2.6 1.2 %copy.41 = bf16[64,1728]{0,1:T(8,128)(2,1)S(1)} copy(bf16[64,1728]{1,0:T(8,128)(2,1)} %param.18) | data formatting | bytes 442368 | tf_op args[1]
  3.8 1.9 %copy.48 = bf16[128,3456]{0,1:T(8,128)(2,1)S(1)} copy(bf16[128,3456]{1,0:T(8,128)(2,1)} %param.21) | data formatting | bytes 1769472 | tf_op args[4]
  5.8 0.1 concatenate.66
  5.9 0.3 concatenate.72
  6.2 0.2 copy-done.4
  6.4 0.1 maximum_maximum_fusion
  6.5 0.1 copy.45
  6.6 0.1 copy.44
  6.7 0.7 fusion.4
  7.5 0.3 copy.42
  7.8 0.1 concatenate.67
  7.9 0.6 fusion.2
  8.5 0.2 copy.43
  8.7 1.0 %copy.46.w_ref = bf16[128,1728]{1,0:T(8,128)(2,1)} copy(bf16[128,1728]{0,1:T(8,128)(2,1)S(1)} %bitcast.38) | data formatting | bytes 884736 | tf_op jit(solution)/shard_map/reshape | solution.py:378
  9.7 6.7 %three_edges.1 = (bf16[12,128,256]{2,1,0:T(8,128)(2,1)}, bf16[4,128,256]{2,1,0:T(8,128)(2,1)}, bf16[128,256]{1,0:T(8,128)(2,1)}) custom-call(s32[1]{0:T(128)} %bitcast.core_ref, bf16[1,64,16,24,512]{4,3,2,1,0:T(8,128)(2,1)} %rim_ref.1, bf16[1,64,16,24,512]{4,3,2,1,0:T(8,128)(2,1)} %rim_ref.1, bf16[128,1728]{1,0:T(8,128)(2,1)} %copy.46.w_ref, ...), custom_call_target="tpu_custom_call" | custom-call | flops 2000000000 | bytes 8000000 | tf_op jit(solution)/shard_map/three_edges/pallas_call | solution.py:129
  16.4 1.3 %collective-permute-start.4 = (bf16[128,256]{1,0:T(8,128)(2,1)}, bf16[128,256]{1,0:T(8,128)(2,1)S(1)}, u32[]{:S(2)}, u32[]{:S(2)}) collective-permute-start(bf16[128,256]{1,0:T(8,128)(2,1)} %get-tuple-element.55), channel_id=1, source_target_pairs={{0,3},{2,5},{4,7},{6,9},{8,11},{10,13},{12,15},{16,19},{18,21},{20... | collective-permute-start | bytes 196616 | tf_op jit(solution)/shard_map/ppermute | solution.py:367
  17.7 3.1 %collective-permute-start.3 = (bf16[4,128,256]{2,1,0:T(8,128)(2,1)}, bf16[4,128,256]{2,1,0:T(8,128)(2,1)S(1)}, u32[]{:S(2)}, u32[]{:S(2)}) collective-permute-start(bf16[4,128,256]{2,1,0:T(8,128)(2,1)} %get-tuple-element.54), channel_id=1, source_target_pairs={{0,2},{1,3},{2,4},{3,5},{4,6},{5,7},{6,8},{7,9},{8,10},{9,11},{10,... | collective-permute-start | bytes 786440 | tf_op jit(solution)/shard_map/ppermute | solution.py:366
  20.8 1.5 %collective-permute-start.2 = (bf16[12,128,256]{2,1,0:T(8,128)(2,1)}, bf16[12,128,256]{2,1,0:T(8,128)(2,1)}, u32[]{:S(2)}, u32[]{:S(2)}) collective-permute-start(bf16[12,128,256]{2,1,0:T(8,128)(2,1)} %get-tuple-element.53), channel_id=1, source_target_pairs={{0,1},{2,3},{4,5},{6,7},{8,9},{10,11},{12,13},{14,15},{16,17},{18,... | collective-permute-start | bytes 2359304 | tf_op jit(solution)/shard_map/ppermute | solution.py:365
  22.3 18.3 %layer_three.1 = (bf16[4,12,128,256]{3,2,1,0:T(8,128)(2,1)}, f32[12,128,256]{2,1,0:T(8,128)}, f32[4,128,256]{2,1,0:T(8,128)}) custom-call(s32[1]{0:T(128)} %bitcast.core_ref, bf16[1,64,16,24,512]{4,3,2,1,0:T(8,128)(2,1)} %rim_ref.1, bf16[128,1728]{1,0:T(8,128)(2,1)} %copy.46.w_ref, bf16[256,256]{1,0:T(8,128)(2,1)} %constant.96.clone.place_ref.refs_9_, ...), custom_call_target="tpu_custom_call" | custom-call | flops 10000000000 | bytes 20000000 | tf_op jit(solution)/shard_map/layer_three/pallas_call | solution.py:210
  40.6 1.9 %copy.49 = bf16[128,3456]{0,1:T(8,128)(2,1)S(1)} copy(bf16[128,3456]{1,0:T(8,128)(2,1)} %collective-permute-done.5) | data formatting | bytes 1769472 | tf_op jit(solution)/shard_map/ppermute | solution.py:372
  42.5 0.3 concatenate.73
  42.8 0.9 %fusion = bf16[256,27,128]{0,1,2:T(8,128)(2,1)S(1)} fusion(bf16[128,128,27]{0,2,1:T(8,128)(2,1)S(1)} %concatenate.73, bf16[128,128,27]{0,2,1:T(8,128)(2,1)S(1)} %concatenate.72, pred[]{:T(512)S(6)} %eq.2), kind=kLoop, calls=%fused_computation.1 | loop fusion | flops 7962624 | bytes 3538945 | tf_op jit(solution)/shard_map/transpose | solution.py:378
  43.7 1.0 %copy.50 = bf16[256,27,128]{0,2,1:T(8,128)(2,1)S(1)} copy(bf16[256,27,128]{0,1,2:T(8,128)(2,1)S(1)} %fusion) | data formatting | bytes 3538944 | tf_op jit(solution)/shard_map/transpose | solution.py:378
  44.7 2.3 %copy.51.refs_8_ = bf16[256,3456]{1,0:T(8,128)(2,1)} copy(bf16[256,3456]{0,1:T(8,128)(2,1)S(1)} %bitcast.36) | data formatting | bytes 3538944 | tf_op jit(solution)/shard_map/reshape | solution.py:378
  47.0 0.6 copy-done.1
  47.6 0.1 copy-done
  47.7 6.0 %four_edges.1 = (bf16[6,256,128]{2,1,0:T(8,128)(2,1)}, bf16[256,256]{1,0:T(8,128)(2,1)}, bf16[256,128]{1,0:T(8,128)(2,1)}) custom-call(bf16[4,12,128,256]{3,2,1,0:T(8,128)(2,1)} %get-tuple-element.50.refs_0_, f32[12,128,256]{2,1,0:T(8,128)} %get-tuple-element.51.refs_1_, f32[4,128,256]{2,1,0:T(8,128)} %get-tuple-element.52.refs_2_, ...), custom_call_target="tpu_custom_call" | custom-call | flops 2000000000 | bytes 8000000 | tf_op jit(solution)/shard_map/four_edges/pallas_call | solution.py:299
  53.7 3.1 %collective-permute-start.7 = (bf16[256,256]{1,0:T(8,128)(2,1)}, bf16[256,256]{1,0:T(8,128)(2,1)}, u32[]{:S(2)}, u32[]{:S(2)}) collective-permute-start(bf16[256,256]{1,0:T(8,128)(2,1)} %get-tuple-element.57), channel_id=1, source_target_pairs={{0,2},{1,3},{2,4},{3,5},{4,6},{5,7},{6,8},{7,9},{8,10},{9,11},{10,... | collective-permute-start | bytes 393224 | tf_op jit(solution)/shard_map/ppermute | solution.py:366
  56.8 1.5 %collective-permute-start.6 = (bf16[6,256,128]{2,1,0:T(8,128)(2,1)}, bf16[6,256,128]{2,1,0:T(8,128)(2,1)S(1)}, u32[]{:S(2)}, u32[]{:S(2)}) collective-permute-start(bf16[6,256,128]{2,1,0:T(8,128)(2,1)} %get-tuple-element.56), channel_id=1, source_target_pairs={{0,1},{2,3},{4,5},{6,7},{8,9},{10,11},{12,13},{14,15},{16,17},{18,... | collective-permute-start | bytes 1179656 | tf_op jit(solution)/shard_map/ppermute | solution.py:365
  58.4 8.8 %layer_four.1 = f32[6,256,256]{2,1,0:T(8,128)} custom-call(bf16[4,12,128,256]{3,2,1,0:T(8,128)(2,1)} %get-tuple-element.50.refs_0_, f32[12,128,256]{2,1,0:T(8,128)} %get-tuple-element.51.refs_1_, f32[4,128,256]{2,1,0:T(8,128)} %get-tuple-element.52.refs_2_, bf16[12,128,256]{2,1,0:T(8,128)(2,1)} %collective-permute-done.2.refs_3_, ...), custom_call_target="tpu_custom_call" | custom-call | flops 8000000000 | bytes 10000000 | tf_op jit(solution)/shard_map/layer_four/pallas_call | solution.py:344
  67.2 1.9 %copy.52 = f32[6,256,256]{1,2,0:T(8,128)S(1)} copy(f32[6,256,256]{2,1,0:T(8,128)} %layer_four.1) | data formatting | bytes 3145728 | tf_op jit(solution)/shard_map/layer_four/pallas_call | solution.py:344
  69.0 0.5 copy.55
  69.5 1.3 %collective-permute-start.8 = (bf16[256,128]{1,0:T(8,128)(2,1)}, bf16[256,128]{1,0:T(8,128)(2,1)S(1)}, u32[]{:S(2)}, u32[]{:S(2)}) collective-permute-start(bf16[256,128]{1,0:T(8,128)(2,1)} %get-tuple-element.58), channel_id=1, source_target_pairs={{0,3},{2,5},{4,7},{6,9},{8,11},{10,13},{12,15},{16,19},{18,21},{20... | collective-permute-start | bytes 196616 | tf_op jit(solution)/shard_map/ppermute | solution.py:367
  70.8 1.0 %copy.56 = f32[256,256]{0,1:T(8,128)S(1)} copy(bf16[256,256]{1,0:T(8,128)(2,1)} %collective-permute-done.7) | data formatting | bytes 393216 | tf_op jit(solution)/shard_map/convert_element_type | solution.py:399
  71.8 0.1 copy.57
  72.0 0.2 fusion.1
  72.1 0.1 constant_dynamic-update-slice_fusion
  72.2 7.3 %collective-permute-done.8 = bf16[256,128]{1,0:T(8,128)(2,1)S(1)} collective-permute-done((bf16[256,128]{1,0:T(8,128)(2,1)}, bf16[256,128]{1,0:T(8,128)(2,1)S(1)}, u32[]{:S(2)}, u32[]{:S(2)}) %collective-permute-start.8) | collective-permute-done | bytes 65568 | tf_op jit(solution)/shard_map/ppermute | solution.py:367
  79.6 0.3 maximum_convert_fusion
  79.9 0.1 dynamic-slice_bitcast_fusion.1
  80.0 3.4 %collective-permute-start.10 = (bf16[128,2,6,128]{3,0,1,2:T(8,128)(2,1)S(1)}, bf16[128,2,6,128]{3,0,1,2:T(8,128)(2,1)S(1)}, u32[]{:S(2)}, u32[]{:S(2)}) collective-permute-start(bf16[128,2,6,128]{3,0,1,2:T(8,128)(2,1)S(1)} %get-tuple-element.62), channel_id=1, source_target_pairs={{0,1},{1,0},{2,3},{3,2},{4,5},{5,4},{6,7},{7,6},{8,9},{9,8},{10,11... | collective-permute-start | bytes 1179656 | tf_op jit(solution)/shard_map/ppermute | solution.py:406
  83.4 1.3 %collective-permute-done.10 = bf16[128,2,6,128]{3,0,1,2:T(8,128)(2,1)S(1)} collective-permute-done((bf16[128,2,6,128]{3,0,1,2:T(8,128)(2,1)S(1)}, bf16[128,2,6,128]{3,0,1,2:T(8,128)(2,1)S(1)}, u32[]{:S(2)}, u32[]{:S(2)}) %collective-permute-start.10) | collective-permute-done | bytes 393248 | tf_op jit(solution)/shard_map/ppermute | solution.py:406
  84.8 0.1 maximum_select_fusion.1
  84.9 1.5 %copy.58 = bf16[1,128,4,6,128]{4,2,3,1,0:T(4,128)(2,1)} copy(bf16[1,128,4,6,128]{4,1,2,3,0:T(8,128)(2,1)S(1)} %maximum_select_fusion.1) | data formatting | bytes 1572864 | tf_op jit(solution)/shard_map/jit(_where)/select_n | solution.py:407
  (24 shorter events, 0.2 us)
Async XLA Ops:
  0.7 6.8 %collective-permute-start.9 = (f32[128,2]{0,1:T(2,128)S(1)}, f32[128,2]{0,1:T(2,128)S(1)}, u32[]{:S(2)}, u32[]{:S(2)}) collective-permute-start(f32[128,2]{0,1:T(2,128)S(1)} %pad_maximum_fusion.2), channel_id=1, source_target_pairs={{0,1},{1,0},{2,3},{3,2},{4,5},{5,4},{6,7},{7,6},{8,9},{9,8},{10,11... | collective-permute-start | bytes 3080 | tf_op jit(solution)/shard_map/ppermute | solution.py:372
  2.0 4.2 %collective-permute-start.1 = (f32[64,2]{0,1:T(2,128)S(1)}, f32[64,2]{0,1:T(2,128)S(1)}, u32[]{:S(2)}, u32[]{:S(2)}) collective-permute-start(f32[64,2]{0,1:T(2,128)S(1)} %pad_maximum_fusion), channel_id=1, source_target_pairs={{0,1},{1,0},{2,3},{3,2},{4,5},{5,4},{6,7},{7,6},{8,9},{9,8},{10,11... | collective-permute-start | bytes 1544 | tf_op jit(solution)/shard_map/ppermute | solution.py:372
  2.0 5.4 %collective-permute-start = (bf16[64,1728]{1,0:T(8,128)(2,1)}, bf16[64,1728]{1,0:T(8,128)(2,1)S(1)}, u32[]{:S(2)}, u32[]{:S(2)}) collective-permute-start(bf16[64,1728]{1,0:T(8,128)(2,1)} %param.18), channel_id=1, source_target_pairs={{0,1},{1,0},{2,3},{3,2},{4,5},{5,4},{6,7},{7,6},{8,9},{9,8},{10,11... | collective-permute-start | bytes 663560 | tf_op jit(solution)/shard_map/ppermute | solution.py:372
  2.5 38.0 %collective-permute-start.5 = (bf16[128,3456]{1,0:T(8,128)(2,1)}, bf16[128,3456]{1,0:T(8,128)(2,1)}, u32[]{:S(2)}, u32[]{:S(2)}) collective-permute-start(bf16[128,3456]{1,0:T(8,128)(2,1)} %param.21), channel_id=1, source_target_pairs={{0,1},{1,0},{2,3},{3,2},{4,5},{5,4},{6,7},{7,6},{8,9},{9,8},{10,11... | collective-permute-start | bytes 2654216 | tf_op jit(solution)/shard_map/ppermute | solution.py:372
  5.7 0.7 copy-start.4
  5.7 0.7 copy-start.5
  5.7 1.7 %copy-start.2 = (f32[128]{0:T(128)S(1)}, f32[128]{0:T(128)}, u32[]{:S(2)}) copy-start(f32[128]{0:T(128)} %param.23) | copy-start | bytes 1540
  5.8 1.7 %copy-start.3 = (f32[128]{0:T(128)S(1)}, f32[128]{0:T(128)}, u32[]{:S(2)}) copy-start(f32[128]{0:T(128)} %param.22) | copy-start | bytes 1540
  16.4 30.6 %collective-permute-start.4 = (bf16[128,256]{1,0:T(8,128)(2,1)}, bf16[128,256]{1,0:T(8,128)(2,1)S(1)}, u32[]{:S(2)}, u32[]{:S(2)}) collective-permute-start(bf16[128,256]{1,0:T(8,128)(2,1)} %get-tuple-element.55), channel_id=1, source_target_pairs={{0,3},{2,5},{4,7},{6,9},{8,11},{10,13},{12,15},{16,19},{18,21},{20... | collective-permute-start | bytes 196616 | tf_op jit(solution)/shard_map/ppermute | solution.py:367
  17.7 29.3 %collective-permute-start.3 = (bf16[4,128,256]{2,1,0:T(8,128)(2,1)}, bf16[4,128,256]{2,1,0:T(8,128)(2,1)S(1)}, u32[]{:S(2)}, u32[]{:S(2)}) collective-permute-start(bf16[4,128,256]{2,1,0:T(8,128)(2,1)} %get-tuple-element.54), channel_id=1, source_target_pairs={{0,2},{1,3},{2,4},{3,5},{4,6},{5,7},{6,8},{7,9},{8,10},{9,11},{10,... | collective-permute-start | bytes 786440 | tf_op jit(solution)/shard_map/ppermute | solution.py:366
  20.8 26.2 %collective-permute-start.2 = (bf16[12,128,256]{2,1,0:T(8,128)(2,1)}, bf16[12,128,256]{2,1,0:T(8,128)(2,1)}, u32[]{:S(2)}, u32[]{:S(2)}) collective-permute-start(bf16[12,128,256]{2,1,0:T(8,128)(2,1)} %get-tuple-element.53), channel_id=1, source_target_pairs={{0,1},{2,3},{4,5},{6,7},{8,9},{10,11},{12,13},{14,15},{16,17},{18,... | collective-permute-start | bytes 2359304 | tf_op jit(solution)/shard_map/ppermute | solution.py:365
  47.0 0.6 copy-start.1
  47.0 0.7 copy-start
  53.7 17.1 %collective-permute-start.7 = (bf16[256,256]{1,0:T(8,128)(2,1)}, bf16[256,256]{1,0:T(8,128)(2,1)}, u32[]{:S(2)}, u32[]{:S(2)}) collective-permute-start(bf16[256,256]{1,0:T(8,128)(2,1)} %get-tuple-element.57), channel_id=1, source_target_pairs={{0,2},{1,3},{2,4},{3,5},{4,6},{5,7},{6,8},{7,9},{8,10},{9,11},{10,... | collective-permute-start | bytes 393224 | tf_op jit(solution)/shard_map/ppermute | solution.py:366
  56.8 15.1 %collective-permute-start.6 = (bf16[6,256,128]{2,1,0:T(8,128)(2,1)}, bf16[6,256,128]{2,1,0:T(8,128)(2,1)S(1)}, u32[]{:S(2)}, u32[]{:S(2)}) collective-permute-start(bf16[6,256,128]{2,1,0:T(8,128)(2,1)} %get-tuple-element.56), channel_id=1, source_target_pairs={{0,1},{2,3},{4,5},{6,7},{8,9},{10,11},{12,13},{14,15},{16,17},{18,... | collective-permute-start | bytes 1179656 | tf_op jit(solution)/shard_map/ppermute | solution.py:365
  69.5 10.1 %collective-permute-start.8 = (bf16[256,128]{1,0:T(8,128)(2,1)}, bf16[256,128]{1,0:T(8,128)(2,1)S(1)}, u32[]{:S(2)}, u32[]{:S(2)}) collective-permute-start(bf16[256,128]{1,0:T(8,128)(2,1)} %get-tuple-element.58), channel_id=1, source_target_pairs={{0,3},{2,5},{4,7},{6,9},{8,11},{10,13},{12,15},{16,19},{18,21},{20... | collective-permute-start | bytes 196616 | tf_op jit(solution)/shard_map/ppermute | solution.py:367
  80.0 4.8 %collective-permute-start.10 = (bf16[128,2,6,128]{3,0,1,2:T(8,128)(2,1)S(1)}, bf16[128,2,6,128]{3,0,1,2:T(8,128)(2,1)S(1)}, u32[]{:S(2)}, u32[]{:S(2)}) collective-permute-start(bf16[128,2,6,128]{3,0,1,2:T(8,128)(2,1)S(1)} %get-tuple-element.62), channel_id=1, source_target_pairs={{0,1},{1,0},{2,3},{3,2},{4,5},{5,4},{6,7},{7,6},{8,9},{9,8},{10,11... | collective-permute-start | bytes 1179656 | tf_op jit(solution)/shard_map/ppermute | solution.py:406

commit v3 on v2

--- a/solution.py
+++ b/solution.py
@@ -13,6 +13,7 @@
 LANES = 128
 ROW_BLOCKS = 8
 SUB = 8
+TAPS = 27
 GROUP = 16
 VMEM_LIMIT = 56 * 2**20
 
@@ -66,14 +67,70 @@
             )
             for tap, value in enumerate((shifted(odd), even, odd)):
                 store(tap, row, first, value.astype(BF16))
+        yield
+
+
+def whole(own, other, core):
+    first = jnp.where(core == 0, own, other)
+    second = jnp.where(core == 0, other, own)
+    return jnp.concatenate([first, second], 0)
+
+
+def tap_major(kernel, turned_ref, w_ref, first):
+    columns = kernel.shape[1]
+    chans = columns // TAPS
+    for at in range(0, columns, LANES):
+        size = min(LANES, columns - at)
+        turned_ref[at : at + size, :] = kernel[:, at : at + size].T
+    for at in range(0, columns, LANES):
+        size = min(LANES, columns - at)
+        parts = [
+            turned_ref[pl.ds(tap, chans, stride=TAPS), :] for tap in range(at // chans, (at + size) // chans)
+        ]
+        w_ref[first : first + LANES, at : at + size] = jnp.concatenate(parts, 0).T.astype(BF16)
+
+
+def four_weights_kernel(core_ref, own_ref, other_ref, w_ref, *turned_refs):
+    core = core_ref[0]
+    for index, turned_ref in enumerate(turned_refs):
+        kernel = jnp.where(core == index, own_ref[...].astype(F32), other_ref[...].astype(F32))
+        tap_major(kernel, turned_ref, w_ref, index * LANES)
+
+
+def four_weights(own, other, core):
+    outs, columns = own.shape
+    return pl.pallas_call(
+        four_weights_kernel,
+        out_shape=jax.ShapeDtypeStruct((2 * outs, columns), BF16),
+        in_specs=[
+            pl.BlockSpec(memory_space=pltpu.SMEM),
+            pl.BlockSpec(memory_space=pltpu.VMEM),
+            pl.BlockSpec(memory_space=pltpu.VMEM),
+        ],
+        scratch_shapes=[pltpu.VMEM((columns, LANES), F32)] * 2,
+        compiler_params=pltpu.CompilerParams(vmem_limit_bytes=VMEM_LIMIT),
+        cost_estimate=pl.CostEstimate(flops=10**6, bytes_accessed=4 * 10**6, transcendentals=0),
+        name="four_weights",
+    )(core, own, other)
 
 
 def three_edges_kernel(
-    core_ref, last_ref, rim_ref, w_ref, place_ref,
-    next_plane_ref, next_row_ref, next_corner_ref,
+    core_ref, last_ref, rim_ref, own_ref, other_ref, own_scales_ref, other_scales_ref, place_ref,
+    next_plane_ref, next_row_ref, next_corner_ref, w_ref, gain_ref, shift_ref, scales_ref,
     *scratch,
 ):
-    *split_refs, pick_ref, data_ref = scratch
+    *split_refs, turned_ref, pick_ref, data_ref = scratch
+    core = core_ref[0]
+    tap_major(whole(own_ref[...].astype(F32), other_ref[...].astype(F32), core), turned_ref, w_ref, 0)
+    own_scales, other_scales = own_scales_ref[...], other_scales_ref[...]
+    lines = own_scales.shape[0]
+    scales = jnp.concatenate(
+        [own_scales, other_scales, jnp.zeros((LANES - 2 * lines, LANES), F32)], 0
+    ).T
+    scales_ref[...] = scales
+    share = own_ref.shape[0]
+    for ref, at in ((gain_ref, 0), (shift_ref, share)):
+        ref[...] = whole(scales[at : at + share, 0:1], scales[at : at + share, lines : lines + 1], core)
     chans, rows, width = last_ref.shape[1], last_ref.shape[3], last_ref.shape[4]
     planes = rim_ref.shape[2]
     half = width // 2
@@ -115,48 +172,54 @@
         data_ref[row + 1, tap * chans + first : tap * chans + first + GROUP, :] = value
 
     data_ref[0] = jnp.zeros_like(data_ref[0])
-    separate(last_ref, 0, place_ref, split_refs, store)
+    for _ in separate(last_ref, 0, place_ref, split_refs, store):
+        pass
     for row in range(out_rows):
         next_plane_ref[row] = beyond(data_ref[2 * row : 2 * row + 3].reshape(3 * taps, half))
 
 
-def three_edges(volume, weights, core):
+def three_edges(volume, own, other, own_scales, other_scales, core):
     _, chans, planes, rows, width = volume.shape
-    outs = weights.shape[0]
-    half = width // 2
-    own, out_rows = planes // 2, rows // 2
+    outs, columns = 2 * own.shape[0], own.shape[1]
+    half = width // 2
+    mine, out_rows = planes // 2, rows // 2
     full = lambda *shape: pl.BlockSpec(shape, lambda i, core: (0,) * len(shape))
+    shapes = [
+        ((out_rows, outs, half), BF16),
+        ((mine // 2, outs, half), BF16),
+        ((outs, half), BF16),
+        ((outs, columns), BF16),
+        ((outs, 1), F32),
+        ((outs, 1), F32),
+        ((LANES, LANES), F32),
+    ]
     return pl.pallas_call(
         three_edges_kernel,
         grid_spec=pltpu.PrefetchScalarGridSpec(
             num_scalar_prefetch=1,
             grid=(1,),
             in_specs=[
-                pl.BlockSpec((1, chans, 1, rows, width), lambda i, core: (0, 0, (core[0] + 1) * own - 1, 0, 0)),
-                pl.BlockSpec((1, chans, own, 2 * SUB, width), lambda i, core: (0, 0, core[0], (rows - 1) // (2 * SUB), 0)),
-                full(*weights.shape),
+                pl.BlockSpec((1, chans, 1, rows, width), lambda i, core: (0, 0, (core[0] + 1) * mine - 1, 0, 0)),
+                pl.BlockSpec((1, chans, mine, 2 * SUB, width), lambda i, core: (0, 0, core[0], (rows - 1) // (2 * SUB), 0)),
+                full(*own.shape),
+                full(*other.shape),
+                full(*own_scales.shape),
+                full(*other_scales.shape),
                 full(half, half),
             ],
-            out_specs=[
-                full(out_rows, outs, half),
-                full(own // 2, outs, half),
-                full(outs, half),
-            ],
+            out_specs=[full(*shape) for shape, _ in shapes],
             scratch_shapes=[pltpu.VMEM((2, half // LANES, GROUP * rows, LANES), F32)] * 4
             + [
+                pltpu.VMEM((columns, LANES), F32),
                 pltpu.VMEM((2, width // LANES, chans * SUB, LANES), F32),
                 pltpu.VMEM((rows + 1, 3 * chans, half), BF16),
             ],
         ),
-        out_shape=[
-            jax.ShapeDtypeStruct((out_rows, outs, half), BF16),
-            jax.ShapeDtypeStruct((own // 2, outs, half), BF16),
-            jax.ShapeDtypeStruct((outs, half), BF16),
-        ],
+        out_shape=[jax.ShapeDtypeStruct(*shape) for shape in shapes],
         compiler_params=pltpu.CompilerParams(vmem_limit_bytes=VMEM_LIMIT),
         cost_estimate=pl.CostEstimate(flops=2 * 10**9, bytes_accessed=8 * 10**6, transcendentals=0),
         name="three_edges",
-    )(core, volume, volume, weights, even_odd(half))
+    )(core, volume, volume, own, other, own_scales, other_scales, even_odd(half))
 
 
 def three_kernel(
@@ -164,39 +227,67 @@
     third_ref, plane_ref, row_ref,
     *scratch,
 ):
-    *split_refs, data_ref, total_ref = scratch
-    step = pl.program_id(0)
+    *split_refs, prior_ref, first_ref, second_ref, total_ref = scratch
+    step, steps = pl.program_id(0), pl.num_programs(0) - 1
     chans, rows, width = x_ref.shape[1], x_ref.shape[3], x_ref.shape[4]
     half = width // 2
     out_rows = rows // 2
     taps = 3 * chans
 
+    def splitting(pair_ref):
+        for plane in range(2):
+
+            def store(tap, row, first, value, plane=plane):
+                pair_ref[plane, row + 1, tap * chans + first : tap * chans + first + GROUP, :] = value
+
+            yield from separate(x_ref, plane, place_ref, split_refs, store)
+
+    def summing(pair_ref):
+        gain, shift = gain_ref[...], shift_ref[...]
+        for row in range(out_rows):
+            parts = [
+                ref[2 * row : 2 * row + 3].reshape(3 * taps, half)
+                for ref in (prior_ref, pair_ref.at[0], pair_ref.at[1])
+            ]
+            total = jnp.dot(w_ref[...], jnp.concatenate(parts, 0), preferred_element_type=F32)
+            third_ref[0, row] = activate(total, gain, shift).astype(BF16)
+            total_ref[row] = total
+            yield
+        row_ref[0] = total_ref[0]
+        prior_ref[...] = pair_ref[1]
+        yield
+
     @pl.when(step == 0)
     def _():
-        data_ref[0] = jnp.zeros_like(data_ref[0])
-        for slot in (1, 2):
-            data_ref[slot, 0] = jnp.zeros_like(data_ref[slot, 0])
-
-    @pl.when(step > 0)
-    def _():
-        data_ref[0] = data_ref[2]
-
-    for plane in range(2):
-
-        def store(tap, row, first, value, slot=plane + 1):
-            data_ref[slot, row + 1, tap * chans + first : tap * chans + first + GROUP, :] = value
-
-        separate(x_ref, plane, place_ref, split_refs, store)
-
-    gain, shift = gain_ref[...], shift_ref[...]
-    for row in range(out_rows):
-        parts = [data_ref[slot, 2 * row : 2 * row + 3].reshape(3 * taps, half) for slot in range(3)]
-        total = jnp.dot(w_ref[...], jnp.concatenate(parts, 0), preferred_element_type=F32)
-        third_ref[0, row] = activate(total, gain, shift).astype(BF16)
-        total_ref[row] = total
-    row_ref[0] = total_ref[0]
-
-    @pl.when(step == 0)
+        prior_ref[...] = jnp.zeros_like(prior_ref)
+        for ref in (first_ref, second_ref):
+            ref[:, 0] = jnp.zeros_like(ref[:, 0])
+        for _ in splitting(first_ref):
+            pass
+
+    def both(new_ref, old_ref):
+        new, old = splitting(new_ref), summing(old_ref)
+        for turn in range(2 * chans // GROUP):
+            next(new, None)
+            for _ in range(out_rows * (turn + 1) // (2 * chans // GROUP) - out_rows * turn // (2 * chans // GROUP)):
+                next(old, None)
+        for _ in new:
+            pass
+        for _ in old:
+            pass
+
+    for odd, (new_ref, old_ref) in enumerate(((first_ref, second_ref), (second_ref, first_ref))):
+
+        @pl.when((step > 0) & (step < steps) & (step % 2 == odd))
+        def _(new_ref=new_ref, old_ref=old_ref):
+            both(new_ref, old_ref)
+
+        @pl.when((step == steps) & (step % 2 == odd))
+        def _(old_ref=old_ref):
+            for _ in summing(old_ref):
+                pass
+
+    @pl.when(step == 1)
     def _():
         plane_ref[...] = total_ref[...]
 
@@ -211,22 +302,24 @@
         three_kernel,
         grid_spec=pltpu.PrefetchScalarGridSpec(
             num_scalar_prefetch=1,
-            grid=(steps,),
+            grid=(steps + 1,),
             in_specs=[
-                pl.BlockSpec((1, chans, 2, rows, width), lambda i, core: (0, 0, core[0] * steps + i, 0, 0)),
+                pl.BlockSpec((1, chans, 2, rows, width), lambda i, core: (0, 0, core[0] * steps + jnp.minimum(i, steps - 1), 0, 0)),
                 full(*weights.shape),
                 full(half, half),
                 full(outs, 1),
                 full(outs, 1),
             ],
             out_specs=[
-                pl.BlockSpec((1, out_rows, outs, half), lambda i, core: (i, 0, 0, 0)),
+                pl.BlockSpec((1, out_rows, outs, half), lambda i, core: (jnp.maximum(i - 1, 0), 0, 0, 0)),
                 full(out_rows, outs, half),
-                pl.BlockSpec((1, outs, half), lambda i, core: (i, 0, 0)),
+                pl.BlockSpec((1, outs, half), lambda i, core: (jnp.maximum(i - 1, 0), 0, 0)),
             ],
             scratch_shapes=[pltpu.VMEM((2, half // LANES, GROUP * rows, LANES), F32)] * 4
             + [
-                pltpu.VMEM((3, rows + 1, 3 * chans, half), BF16),
+                pltpu.VMEM((rows + 1, 3 * chans, half), BF16),
+                pltpu.VMEM((2, rows + 1, 3 * chans, half), BF16),
+                pltpu.VMEM((2, rows + 1, 3 * chans, half), BF16),
                 pltpu.VMEM((out_rows, outs, half), F32),
             ],
         ),
@@ -351,6 +444,64 @@
     )(*thirds, weights, even_odd(width))
 
 
+def finished(refs, row, first):
+    sums_ref, halo_plane_ref, halo_row_ref, halo_corner_ref, gain, shift = refs
+    chans = pl.ds(pl.multiple_of(first, LANES), LANES)
+    width = halo_plane_ref.shape[2]
+    total = sums_ref[row, chans]
+    edge = halo_plane_ref[row, chans].astype(F32)
+    if not row:
+        total = total + halo_row_ref[chans].astype(F32)
+        edge = edge + halo_corner_ref[chans].astype(F32)
+    total = jnp.concatenate([total[:, :width] + edge, total[:, width:]], 1)
+    return activate(total, gain, shift)
+
+
+def theirs_kernel(core_ref, sums_ref, halo_plane_ref, halo_row_ref, halo_corner_ref, scales_ref, theirs_ref):
+    refs = sums_ref, halo_plane_ref, halo_row_ref, halo_corner_ref, scales_ref[:, 4:5], scales_ref[:, 5:6]
+    for row in range(sums_ref.shape[0]):
+        theirs_ref[row] = finished(refs, row, (1 - core_ref[0]) * LANES).astype(BF16)
+
+
+def assemble_kernel(
+    core_ref, sums_ref, halo_plane_ref, halo_row_ref, halo_corner_ref, scales_ref, got_ref, out_ref, lines_ref
+):
+    core = core_ref[0]
+    refs = sums_ref, halo_plane_ref, halo_row_ref, halo_corner_ref, scales_ref[:, 1:2], scales_ref[:, 2:3]
+    rows, _, width = halo_plane_ref.shape
+    count = sums_ref.shape[2] // width
+    for row in range(rows):
+        own, got = finished(refs, row, core * LANES), got_ref[row].astype(F32)
+        for at, value in enumerate((jnp.where(core == 0, own, got), jnp.where(core == 0, got, own))):
+            for m in range(count):
+                place = row * 2 * count + at * count + m
+                lines_ref[pl.ds(place, LANES, stride=rows * 2 * count), :] = value[:, m * width : (m + 1) * width]
+    out_ref[...] = lines_ref[...].astype(BF16)
+
+
+def last_stage(core, sums, halos, scales):
+    rows, outs, lanes = sums.shape
+    in_specs = [pl.BlockSpec(memory_space=pltpu.SMEM)] + [pl.BlockSpec(memory_space=pltpu.VMEM)] * 5
+    params = pltpu.CompilerParams(vmem_limit_bytes=VMEM_LIMIT)
+    theirs = pl.pallas_call(
+        theirs_kernel,
+        out_shape=jax.ShapeDtypeStruct((rows, outs // 2, lanes), BF16),
+        in_specs=in_specs,
+        compiler_params=params,
+        name="theirs",
+    )(core, sums, *halos, scales)
+    got = lax.ppermute(theirs, "fl", [(0, 1), (1, 0)])
+    lines = (outs // 2 * rows * lanes * 2 // LANES, LANES)
+    return pl.pallas_call(
+        assemble_kernel,
+        out_shape=jax.ShapeDtypeStruct(lines, BF16),
+        in_specs=in_specs + [pl.BlockSpec(memory_space=pltpu.VMEM)],
+        scratch_shapes=[pltpu.VMEM(lines, F32)],
+        compiler_params=params,
+        name="assemble",
+    )(core, sums, *halos, scales, got)
+
+
 def exchange(plane, row, corner):
     count = lax.axis_size("sp")
     axes = ("sp", "fl")
@@ -368,43 +519,25 @@
     )
 
 
-def both_cores(value, core):
-    other = lax.ppermute(value, "fl", [(0, 1), (1, 0)])
-    return jnp.where(core == 0, jnp.concatenate([value, other], 0), jnp.concatenate([other, value], 0))
-
-
-def tap_major(kernel, chans):
-    outs = kernel.shape[0]
-    return jnp.transpose(kernel.reshape(outs, chans, 27), (0, 2, 1)).reshape(outs, 27 * chans)
+def swapped(value):
+    return lax.ppermute(value, "fl", [(0, 1), (1, 0)])
 
 
 def shards(volume, kernel_three, gain_three, shift_three, kernel_four, gain_four, shift_four):
-    core = lax.axis_index("fl")
-    chans = volume.shape[1]
-    mid = 2 * kernel_three.shape[0]
-    scales_three = both_cores(jnp.stack([gain_three, shift_three], 1), core)
-    scales_four = both_cores(jnp.stack([gain_four, shift_four], 1), core)
-    weights_three = tap_major(both_cores(kernel_three, core), chans)
-    weights_four = tap_major(both_cores(kernel_four, core), mid)
-    gain, shift = scales_three[:, :1], scales_three[:, 1:]
-    index = core.reshape(1)
-    halos = exchange(*three_edges(volume, weights_three, index))
-    thirds = (*layer_three(volume, weights_three, gain, shift, index), *halos, gain, shift)
-    halo_plane, halo_row, halo_corner = exchange(*four_edges(thirds, weights_four))
-    total = layer_four(thirds, weights_four)
-    out_rows, outs, lanes = total.shape
-    width = halo_plane.shape[2]
-    total = total.reshape(out_rows, outs, lanes // width, width)
-    total = total.at[:, :, 0].add(halo_plane.astype(F32))
-    total = total.at[0].add(halo_row.reshape(outs, lanes // width, width).astype(F32))
-    total = total.at[0, :, 0].add(halo_corner.astype(F32))
-    fourth = activate(total, scales_four[:, :1, None], scales_four[:, 1:, None]).astype(BF16)
-    fourth = jnp.transpose(fourth, (1, 2, 0, 3))
-    half = outs // 2
-    own = lax.dynamic_slice_in_dim(fourth, core * half, half, 0)
-    theirs = lax.dynamic_slice_in_dim(fourth, (1 - core) * half, half, 0)
-    other = lax.ppermute(theirs, "fl", [(0, 1), (1, 0)])
-    return jnp.where(core == 0, jnp.concatenate([own, other], 1), jnp.concatenate([other, own], 1))[None]
+    core = lax.axis_index("fl").reshape(1)
+    own_scales = jnp.concatenate([gain_three, shift_three, gain_four, shift_four]).reshape(-1, LANES)
+    *nexts, weights_three, gain, shift, scales = three_edges(
+        volume, kernel_three, swapped(kernel_three), own_scales, swapped(own_scales), core
+    )
+    halos = exchange(*nexts)
+    thirds = (*layer_three(volume, weights_three, gain, shift, core), *halos, gain, shift)
+    weights_four = four_weights(kernel_four, swapped(kernel_four), core)
+    halos = exchange(*four_edges(thirds, weights_four))
+    sums = layer_four(thirds, weights_four)
+    lines = last_stage(core, sums, halos, scales)
+    out_rows, outs, lanes = sums.shape
+    fourth = lines.reshape(outs // 2, out_rows, 2 * lanes // LANES, LANES)
+    return jnp.transpose(fourth, (0, 2, 1, 3))[None]
 
 
 def solution(mesh):

time: 87.5 us -> 77.7 us (0.89)
  local copies, waits for them, and re-layouts: 17.4 us -> 4.11 us
  Pallas kernels: 39.8 us -> 48.3 us
  waiting for transfers between devices: 8.69 us -> 2.28 us
  starting transfers between devices: 16.5 us -> 20.9 us
  other arithmetic: 3.68 us -> 0.78 us
    pallas_call x0 -> x3, Pallas kernels: none -> 9.33 us  [the longest x1 3.83 us: four_weights(): pl.pallas_call(four_weights_kernel, out_shape=jax.ShapeDtypeStruct((2 * o...]
    ppermute x2, waiting for transfers between devices: 7.32 us -> 0.06 us  [exchange(): lax.ppermute(corner, axes, both)]
    ppermute x5 -> x4, starting transfers between devices: 4.69 us -> 9.32 us  [the longest x1 8.14 us: last_stage(): got = lax.ppermute(theirs, 'fl', [(0, 1), (1, 0)])]
    reshape x3 -> x0, local copies, waits for them, and re-layouts: 3.73 us -> none  [the longest x2 3.27 us: tap_major(): jnp.transpose(kernel.reshape(outs, chans, 27), (0, 2, 1))]
    ppermute x2 -> x0, local copies, waits for them, and re-layouts: 2.15 us -> none  [both_cores(): other = lax.ppermute(value, 'fl', [(0, 1), (1, 0)])]
    pallas_call x1 -> x0, local copies, waits for them, and re-layouts: 1.87 us -> none  [layer_four(): pl.pallas_call(four_kernel, out_shape=jax.ShapeDtypeStruct((out_rows, out...]
    transpose x2 -> x0, other arithmetic: 1.53 us -> none  [tap_major(): jnp.transpose(kernel.reshape(outs, chans, 27), (0, 2, 1))]
    select_n x1 -> x0, local copies, waits for them, and re-layouts: 1.49 us -> none  [shards(): jnp.where(core == 0, jnp.concatenate([own, other], 1), jnp.concatenate([o...]
  transfers between devices with their start and end apart: 11 -> 10, of which waited for: 2 -> 3; matrix products, arithmetic and copies ran while one was open for 20% -> 1% of each run, Pallas kernels for 39% -> 48%
where the time goes in v3:
time: 77.7 us; the launch traced here: 76.5 us
  Pallas kernels  48.3 us (62%)
  starting transfers between devices  20.9 us (27%)
  local copies, waits for them, and re-layouts  4.11 us (5%)
  waiting for transfers between devices  2.28 us (3%)
  other arithmetic  0.78 us (1%)
    pallas_call x1, Pallas kernels, layer_three(): pl.pallas_call(three_kernel, grid_spec=pltpu.PrefetchScalarGridSpec(num_s...  17.2 us
    pallas_call x1, Pallas kernels, layer_four(): pl.pallas_call(four_kernel, out_shape=jax.ShapeDtypeStruct((out_rows, out...  8.84 us
    ppermute x1, starting transfers between devices, last_stage(): got = lax.ppermute(theirs, 'fl', [(0, 1), (1, 0)])  8.14 us
    pallas_call x1, Pallas kernels, three_edges(): pl.pallas_call(three_edges_kernel, grid_spec=pltpu.PrefetchScalarGridSpec...  6.85 us
    ppermute x2, starting transfers between devices, exchange(): lax.ppermute(row, axes, along)  6.25 us
    pallas_call x1, Pallas kernels, four_edges(): pl.pallas_call(four_edges_kernel, out_shape=[jax.ShapeDtypeStruct((rows /...  6.05 us
    unnamed x22, local copies, waits for them, and re-layouts  4.11 us
    pallas_call x1, Pallas kernels, four_weights(): pl.pallas_call(four_weights_kernel, out_shape=jax.ShapeDtypeStruct((2 * o...  3.83 us
  transfers between devices with their start and end apart: 10, of which 3 were waited for; matrix products, arithmetic and copies ran while one was open for 1% of the time, Pallas kernels for 48%

profile of v3, /device:TPU:25, one launch (start us, length us, event | category | flops | bytes accessed | tf_op | source)
XLA Modules:
  0.0 76.5 jit_solution(11950444325853148509)
XLA Ops:
  0.0 0.7 collective-permute-start
  0.7 0.8 %maximum_bitcast_fusion.own_scales_ref = f32[3,128]{1,0:T(4,128)S(1)} fusion(f32[128]{0:T(128)} %param.17, f32[128]{0:T(128)} %param.16, f32[64]{0:T(128)} %param.14, f32[64]{0:T(128)} %param.13), kind=kLoop, calls=%fused_computation | loop fusion | flops 1152 | bytes 3072 | tf_op jit(solution)/shard_map/reshape | solution.py:528
  1.5 0.0 copy-start.9
  1.5 0.0 collective-permute-start.1
  1.5 0.5 collective-permute-start.5
  2.0 0.6 collective-permute-done.1.other_scales_ref
  2.6 0.0 copy-start.10
  2.6 0.0 collective-permute-done.other_ref
  2.6 0.0 copy-start.7
  2.6 0.0 copy-done.9
  2.6 0.6 copy-done.10
  3.2 0.1 copy-done.7
  3.3 6.8 %three_edges.1 = (bf16[12,128,256]{2,1,0:T(8,128)(2,1)}, bf16[4,128,256]{2,1,0:T(8,128)(2,1)}, bf16[128,256]{1,0:T(8,128)(2,1)}, bf16[128,1728]{1,0:T(8,128)(2,1...) custom-call(s32[1]{0:T(128)} %bitcast.core_ref, bf16[1,64,16,24,512]{4,3,2,1,0:T(8,128)(2,1)} %x_ref.1, ...), custom_call_target="tpu_custom_call" | custom-call | flops 2000000000 | bytes 8000000 | tf_op jit(solution)/shard_map/three_edges/pallas_call | solution.py:196
  10.2 1.3 %collective-permute-start.4 = (bf16[128,256]{1,0:T(8,128)(2,1)}, bf16[128,256]{1,0:T(8,128)(2,1)S(1)}, u32[]{:S(2)}, u32[]{:S(2)}) collective-permute-start(bf16[128,256]{1,0:T(8,128)(2,1)} %get-tuple-element.26), channel_id=1, source_target_pairs={{0,3},{2,5},{4,7},{6,9},{8,11},{10,13},{12,15},{16,19},{18,21},{20... | collective-permute-start | bytes 196616 | tf_op jit(solution)/shard_map/ppermute | solution.py:518
  11.5 3.1 %collective-permute-start.3 = (bf16[4,128,256]{2,1,0:T(8,128)(2,1)}, bf16[4,128,256]{2,1,0:T(8,128)(2,1)S(1)}, u32[]{:S(2)}, u32[]{:S(2)}) collective-permute-start(bf16[4,128,256]{2,1,0:T(8,128)(2,1)} %get-tuple-element.25), channel_id=1, source_target_pairs={{0,2},{1,3},{2,4},{3,5},{4,6},{5,7},{6,8},{7,9},{8,10},{9,11},{10,... | collective-permute-start | bytes 786440 | tf_op jit(solution)/shard_map/ppermute | solution.py:517
  14.6 1.5 %collective-permute-start.2 = (bf16[12,128,256]{2,1,0:T(8,128)(2,1)}, bf16[12,128,256]{2,1,0:T(8,128)(2,1)S(1)}, u32[]{:S(2)}, u32[]{:S(2)}) collective-permute-start(bf16[12,128,256]{2,1,0:T(8,128)(2,1)} %get-tuple-element.24), channel_id=1, source_target_pairs={{0,1},{2,3},{4,5},{6,7},{8,9},{10,11},{12,13},{14,15},{16,17},{18,... | collective-permute-start | bytes 2359304 | tf_op jit(solution)/shard_map/ppermute | solution.py:516
  16.1 17.2 %layer_three.1 = (bf16[4,12,128,256]{3,2,1,0:T(8,128)(2,1)}, f32[12,128,256]{2,1,0:T(8,128)}, f32[4,128,256]{2,1,0:T(8,128)}) custom-call(s32[1]{0:T(128)} %bitcast.core_ref, bf16[1,64,16,24,512]{4,3,2,1,0:T(8,128)(2,1)} %x_ref.1, bf16[128,1728]{1,0:T(8,128)(2,1)} %get-tuple-element.18.w_ref, bf16[256,256]{1,0:T(8,128)(2,1)} %constant.6.clone.place_ref.refs_9_, ...), custom_call_target="tpu_custom_call" | custom-call | flops 10000000000 | bytes 20000000 | tf_op jit(solution)/shard_map/layer_three/pallas_call | solution.py:301
  33.3 0.0 collective-permute-done.5.other_ref
  33.3 0.0 copy-start.1
  33.3 0.9 %copy-done.1 = bf16[128,3456]{1,0:T(8,128)(2,1)} copy-done((bf16[128,3456]{1,0:T(8,128)(2,1)}, bf16[128,3456]{1,0:T(8,128)(2,1)S(1)}, u32[]{:S(2)}) %copy-start.1) | copy-done | bytes 884760
  34.2 3.8 %four_weights.1.refs_8_ = bf16[256,3456]{1,0:T(8,128)(2,1)} custom-call(s32[1]{0:T(128)} %bitcast.core_ref, bf16[128,3456]{1,0:T(8,128)(2,1)} %own_ref.3, bf16[128,3456]{1,0:T(8,128)(2,1)} %copy-done.1), custom_call_target="tpu_custom_call" | custom-call | flops 1000000 | bytes 4000000 | tf_op jit(solution)/shard_map/four_weights/pallas_call | solution.py:102
  38.0 0.0 collective-permute-done.4.refs_5_
  38.0 0.0 copy-start.8
  38.0 0.0 collective-permute-done.3.refs_4_
  38.0 0.0 copy-start.5
  38.0 0.0 collective-permute-done.2.refs_3_
  38.1 0.0 copy-start.2
  38.1 0.6 copy-done.8
  38.6 0.1 copy-done.5
  38.8 0.3 copy-done.2
  39.0 6.0 %four_edges.1 = (bf16[6,256,128]{2,1,0:T(8,128)(2,1)}, bf16[256,256]{1,0:T(8,128)(2,1)}, bf16[256,128]{1,0:T(8,128)(2,1)}) custom-call(bf16[4,12,128,256]{3,2,1,0:T(8,128)(2,1)} %get-tuple-element.21.refs_0_, f32[12,128,256]{2,1,0:T(8,128)} %get-tuple-element.22.refs_1_, f32[4,128,256]{2,1,0:T(8,128)} %get-tuple-element.23.refs_2_, ...), custom_call_target="tpu_custom_call" | custom-call | flops 2000000000 | bytes 8000000 | tf_op jit(solution)/shard_map/four_edges/pallas_call | solution.py:392
  45.1 1.3 %collective-permute-start.8 = (bf16[256,128]{1,0:T(8,128)(2,1)}, bf16[256,128]{1,0:T(8,128)(2,1)S(1)}, u32[]{:S(2)}, u32[]{:S(2)}) collective-permute-start(bf16[256,128]{1,0:T(8,128)(2,1)} %get-tuple-element.29), channel_id=1, source_target_pairs={{0,3},{2,5},{4,7},{6,9},{8,11},{10,13},{12,15},{16,19},{18,21},{20... | collective-permute-start | bytes 196616 | tf_op jit(solution)/shard_map/ppermute | solution.py:518
  46.4 3.1 %collective-permute-start.7 = (bf16[256,256]{1,0:T(8,128)(2,1)}, bf16[256,256]{1,0:T(8,128)(2,1)S(1)}, u32[]{:S(2)}, u32[]{:S(2)}) collective-permute-start(bf16[256,256]{1,0:T(8,128)(2,1)} %get-tuple-element.28), channel_id=1, source_target_pairs={{0,2},{1,3},{2,4},{3,5},{4,6},{5,7},{6,8},{7,9},{8,10},{9,11},{10,... | collective-permute-start | bytes 393224 | tf_op jit(solution)/shard_map/ppermute | solution.py:517
  49.5 1.3 %collective-permute-start.6 = (bf16[6,256,128]{2,1,0:T(8,128)(2,1)}, bf16[6,256,128]{2,1,0:T(8,128)(2,1)S(1)}, u32[]{:S(2)}, u32[]{:S(2)}) collective-permute-start(bf16[6,256,128]{2,1,0:T(8,128)(2,1)} %get-tuple-element.27), channel_id=1, source_target_pairs={{0,1},{2,3},{4,5},{6,7},{8,9},{10,11},{12,13},{14,15},{16,17},{18,... | collective-permute-start | bytes 1179656 | tf_op jit(solution)/shard_map/ppermute | solution.py:516
  50.8 8.8 %layer_four.1.sums_ref = f32[6,256,256]{2,1,0:T(8,128)} custom-call(bf16[4,12,128,256]{3,2,1,0:T(8,128)(2,1)} %get-tuple-element.21.refs_0_, f32[12,128,256]{2,1,0:T(8,128)} %get-tuple-element.22.refs_1_, f32[4,128,256]{2,1,0:T(8,128)} %get-tuple-element.23.refs_2_, bf16[12,128,256]{2,1,0:T(8,128)(2,1)} %copy-done.2, bf16[4,128,256]{2,1,0:T(8,128)(2,1)} %copy-done.5, ...), custom_call_target="tpu_custom_call" | custom-call | flops 8000000000 | bytes 10000000 | tf_op jit(solution)/shard_map/layer_four/pallas_call | solution.py:437
  59.6 0.1 collective-permute-done.8.halo_corner_ref
  59.7 0.0 copy-start.6
  59.7 0.0 collective-permute-done.7.halo_row_ref
  59.7 0.0 collective-permute-done.6.halo_plane_ref
  59.7 0.0 copy-start
  59.7 0.6 copy-done.6
  60.3 0.1 copy-done.3
  60.4 0.1 copy-done
  60.5 2.5 %theirs.1 = bf16[6,128,256]{2,1,0:T(8,128)(2,1)} custom-call(s32[1]{0:T(128)} %bitcast.core_ref, f32[6,256,256]{2,1,0:T(8,128)} %layer_four.1.sums_ref, bf16[6,256,128]{2,1,0:T(8,128)(2,1)} %copy-done, bf16[256,256]{1,0:T(8,128)(2,1)} %copy-done.3, bf16[256,128]{1,0:T(8,128)(2,1)} %copy-done.6, f32[128,128]{1,0:T(8,128)} %get-tuple-element.30.scales_ref), custom_call_target="tpu_custom_call" | custom-call | tf_op jit(solution)/shard_map/theirs/pallas_call | solution.py:486
  63.0 8.1 %collective-permute-start.9 = (bf16[6,128,256]{2,1,0:T(8,128)(2,1)}, bf16[6,128,256]{2,1,0:T(8,128)(2,1)S(1)}, u32[]{:S(2)}, u32[]{:S(2)}) collective-permute-start(bf16[6,128,256]{2,1,0:T(8,128)(2,1)} %theirs.1), channel_id=1, source_target_pairs={{0,1},{1,0},{2,3},{3,2},{4,5},{5,4},{6,7},{7,6},{8,9},{9,8},{10,11... | collective-permute-start | bytes 1179656 | tf_op jit(solution)/shard_map/ppermute | solution.py:493
  71.1 1.6 %collective-permute-done.9.got_ref = bf16[6,128,256]{2,1,0:T(8,128)(2,1)S(1)} collective-permute-done((bf16[6,128,256]{2,1,0:T(8,128)(2,1)}, bf16[6,128,256]{2,1,0:T(8,128)(2,1)S(1)}, u32[]{:S(2)}, u32[]{:S(2)}) %collective-permute-start.9) | collective-permute-done | bytes 393248 | tf_op jit(solution)/shard_map/ppermute | solution.py:493
  72.7 0.7 copy-done.4
  73.4 3.0 %assemble.1 = bf16[3072,128]{1,0:T(8,128)(2,1)} custom-call(s32[1]{0:T(128)} %bitcast.core_ref, f32[6,256,256]{2,1,0:T(8,128)} %layer_four.1.sums_ref, bf16[6,256,128]{2,1,0:T(8,128)(2,1)} %copy-done, bf16[256,256]{1,0:T(8,128)(2,1)} %copy-done.3, bf16[256,128]{1,0:T(8,128)(2,1)} %copy-done.6, f32[128,128]{1,0:T(8,128)} %get-tuple-element.30.scales_ref, ...), custom_call_target="tpu_custom_call" | custom-call | tf_op jit(solution)/shard_map/assemble/pallas_call | solution.py:495
  (2 shorter events, 0.0 us)
Async XLA Ops:
  0.0 2.6 %collective-permute-start = (bf16[64,1728]{1,0:T(8,128)(2,1)}, bf16[64,1728]{1,0:T(8,128)(2,1)S(1)}, u32[]{:S(2)}, u32[]{:S(2)}) collective-permute-start(bf16[64,1728]{1,0:T(8,128)(2,1)} %own_ref.2), channel_id=1, source_target_pairs={{0,1},{1,0},{2,3},{3,2},{4,5},{5,4},{6,7},{7,6},{8,9},{9,8},{10,11... | collective-permute-start | bytes 663560 | tf_op jit(solution)/shard_map/ppermute | solution.py:523
  1.5 1.2 %copy-start.9 = (f32[3,128]{1,0:T(4,128)}, f32[3,128]{1,0:T(4,128)S(1)}, u32[]{:S(2)}) copy-start(f32[3,128]{1,0:T(4,128)S(1)} %maximum_bitcast_fusion.own_scales_ref) | copy-start | bytes 4612
  1.5 1.2 %collective-permute-start.1 = (f32[3,128]{1,0:T(4,128)S(1)}, f32[3,128]{1,0:T(4,128)S(1)}, u32[]{:S(2)}, u32[]{:S(2)}) collective-permute-start(f32[3,128]{1,0:T(4,128)S(1)} %maximum_bitcast_fusion.own_scales_ref), channel_id=1, source_target_pairs={{0,1},{1,0},{2,3},{3,2},{4,5},{5,4},{6,7},{7,6},{8,9},{9,8},{10,11... | collective-permute-start | bytes 4616 | tf_op jit(solution)/shard_map/ppermute | solution.py:523
  1.5 31.8 %collective-permute-start.5 = (bf16[128,3456]{1,0:T(8,128)(2,1)}, bf16[128,3456]{1,0:T(8,128)(2,1)S(1)}, u32[]{:S(2)}, u32[]{:S(2)}) collective-permute-start(bf16[128,3456]{1,0:T(8,128)(2,1)} %own_ref.3), channel_id=1, source_target_pairs={{0,1},{1,0},{2,3},{3,2},{4,5},{5,4},{6,7},{7,6},{8,9},{9,8},{10,11... | collective-permute-start | bytes 2654216 | tf_op jit(solution)/shard_map/ppermute | solution.py:523
  2.6 0.6 copy-start.10
  2.6 0.7 copy-start.7
  10.2 27.9 %collective-permute-start.4 = (bf16[128,256]{1,0:T(8,128)(2,1)}, bf16[128,256]{1,0:T(8,128)(2,1)S(1)}, u32[]{:S(2)}, u32[]{:S(2)}) collective-permute-start(bf16[128,256]{1,0:T(8,128)(2,1)} %get-tuple-element.26), channel_id=1, source_target_pairs={{0,3},{2,5},{4,7},{6,9},{8,11},{10,13},{12,15},{16,19},{18,21},{20... | collective-permute-start | bytes 196616 | tf_op jit(solution)/shard_map/ppermute | solution.py:518
  11.5 26.6 %collective-permute-start.3 = (bf16[4,128,256]{2,1,0:T(8,128)(2,1)}, bf16[4,128,256]{2,1,0:T(8,128)(2,1)S(1)}, u32[]{:S(2)}, u32[]{:S(2)}) collective-permute-start(bf16[4,128,256]{2,1,0:T(8,128)(2,1)} %get-tuple-element.25), channel_id=1, source_target_pairs={{0,2},{1,3},{2,4},{3,5},{4,6},{5,7},{6,8},{7,9},{8,10},{9,11},{10,... | collective-permute-start | bytes 786440 | tf_op jit(solution)/shard_map/ppermute | solution.py:517
  14.6 23.5 %collective-permute-start.2 = (bf16[12,128,256]{2,1,0:T(8,128)(2,1)}, bf16[12,128,256]{2,1,0:T(8,128)(2,1)S(1)}, u32[]{:S(2)}, u32[]{:S(2)}) collective-permute-start(bf16[12,128,256]{2,1,0:T(8,128)(2,1)} %get-tuple-element.24), channel_id=1, source_target_pairs={{0,1},{2,3},{4,5},{6,7},{8,9},{10,11},{12,13},{14,15},{16,17},{18,... | collective-permute-start | bytes 2359304 | tf_op jit(solution)/shard_map/ppermute | solution.py:516
  33.3 0.9 %copy-start.1 = (bf16[128,3456]{1,0:T(8,128)(2,1)}, bf16[128,3456]{1,0:T(8,128)(2,1)S(1)}, u32[]{:S(2)}) copy-start(bf16[128,3456]{1,0:T(8,128)(2,1)S(1)} %collective-permute-done.5.other_ref) | copy-start | bytes 2654212
  38.0 0.6 copy-start.8
  38.0 0.7 copy-start.5
  38.1 1.0 %copy-start.2 = (bf16[12,128,256]{2,1,0:T(8,128)(2,1)}, bf16[12,128,256]{2,1,0:T(8,128)(2,1)S(1)}, u32[]{:S(2)}) copy-start(bf16[12,128,256]{2,1,0:T(8,128)(2,1)S(1)} %collective-permute-done.2.refs_3_) | copy-start | bytes 2359300
  45.1 14.6 %collective-permute-start.8 = (bf16[256,128]{1,0:T(8,128)(2,1)}, bf16[256,128]{1,0:T(8,128)(2,1)S(1)}, u32[]{:S(2)}, u32[]{:S(2)}) collective-permute-start(bf16[256,128]{1,0:T(8,128)(2,1)} %get-tuple-element.29), channel_id=1, source_target_pairs={{0,3},{2,5},{4,7},{6,9},{8,11},{10,13},{12,15},{16,19},{18,21},{20... | collective-permute-start | bytes 196616 | tf_op jit(solution)/shard_map/ppermute | solution.py:518
  46.4 13.3 %collective-permute-start.7 = (bf16[256,256]{1,0:T(8,128)(2,1)}, bf16[256,256]{1,0:T(8,128)(2,1)S(1)}, u32[]{:S(2)}, u32[]{:S(2)}) collective-permute-start(bf16[256,256]{1,0:T(8,128)(2,1)} %get-tuple-element.28), channel_id=1, source_target_pairs={{0,2},{1,3},{2,4},{3,5},{4,6},{5,7},{6,8},{7,9},{8,10},{9,11},{10,... | collective-permute-start | bytes 393224 | tf_op jit(solution)/shard_map/ppermute | solution.py:517
  49.5 10.2 %collective-permute-start.6 = (bf16[6,256,128]{2,1,0:T(8,128)(2,1)}, bf16[6,256,128]{2,1,0:T(8,128)(2,1)S(1)}, u32[]{:S(2)}, u32[]{:S(2)}) collective-permute-start(bf16[6,256,128]{2,1,0:T(8,128)(2,1)} %get-tuple-element.27), channel_id=1, source_target_pairs={{0,1},{2,3},{4,5},{6,7},{8,9},{10,11},{12,13},{14,15},{16,17},{18,... | collective-permute-start | bytes 1179656 | tf_op jit(solution)/shard_map/ppermute | solution.py:516
  59.7 0.6 copy-start.6
  59.7 0.7 copy-start.3
  59.7 0.8 %copy-start = (bf16[6,256,128]{2,1,0:T(8,128)(2,1)}, bf16[6,256,128]{2,1,0:T(8,128)(2,1)S(1)}, u32[]{:S(2)}) copy-start(bf16[6,256,128]{2,1,0:T(8,128)(2,1)S(1)} %collective-permute-done.6.halo_plane_ref) | copy-start | bytes 1179652
  63.0 9.7 %collective-permute-start.9 = (bf16[6,128,256]{2,1,0:T(8,128)(2,1)}, bf16[6,128,256]{2,1,0:T(8,128)(2,1)S(1)}, u32[]{:S(2)}, u32[]{:S(2)}) collective-permute-start(bf16[6,128,256]{2,1,0:T(8,128)(2,1)} %theirs.1), channel_id=1, source_target_pairs={{0,1},{1,0},{2,3},{3,2},{4,5},{5,4},{6,7},{7,6},{8,9},{9,8},{10,11... | collective-permute-start | bytes 1179656 | tf_op jit(solution)/shard_map/ppermute | solution.py:493
  72.7 0.7 copy-start.4

commit v4 on v3

v4 whole, which is shorter than its diff:
```python
import functools

import jax
import jax.numpy as jnp
import numpy as np
from jax import lax
from jax.experimental import pallas as pl
from jax.experimental.pallas import tpu as pltpu
from jax.sharding import PartitionSpec as P

F32 = jnp.float32
BF16 = jnp.bfloat16
LANES = 128
ROW_BLOCKS = 8
SUB = 8
TAPS = 27
RIM_TAPS = tuple(9 * a + e for a in range(3) for e in range(3))
GROUP = 16
VMEM_LIMIT = 56 * 2**20


def even_odd(width):
    half = width // 2
    place = np.zeros((width, width), np.float32)
    place[np.arange(0, width, 2), np.arange(half)] = 1
    place[np.arange(1, width, 2), half + np.arange(half)] = 1
    return jnp.asarray(place, BF16)


def activate(total, gain, shift):
    return jnp.maximum(total * gain + shift, 0.0)


def shifted(odd):
    lane = lax.broadcasted_iota(jnp.int32, odd.shape, 1)
    return jnp.where(lane == 0, 0.0, pltpu.roll(odd, 1, 1))


def spread(sides, place):
    quarter = place.shape[0] // 2
    split = [jnp.dot(side, place, preferred_element_type=F32) for side in sides]
    even = jnp.concatenate([part[:, :quarter] for part in split], 1)
    odd = jnp.concatenate([part[:, quarter:] for part in split], 1)
    return shifted(odd), even, odd


def separate(x_ref, plane, place_ref, split_refs, store):
    chans, rows, width = x_ref.shape[1], x_ref.shape[3], x_ref.shape[4]
    half = width // 2
    quarter = half // 2
    for index, first in enumerate(range(0, chans, GROUP)):
        split_ref = split_refs[index % len(split_refs)]
        x = x_ref[0, pl.ds(first, GROUP), plane]
        x = x.astype(F32).reshape(GROUP * rows, width).astype(BF16)
        for side in range(2):
            parts = jnp.dot(
                x[:, side * half : (side + 1) * half], place_ref[...], preferred_element_type=F32
            )
            for block in range(half // LANES):
                odd, at = divmod(block, quarter // LANES)
                split_ref[odd, side * (quarter // LANES) + at] = parts[:, block * LANES : (block + 1) * LANES]
        for row in range(rows):
            even, odd = (
                jnp.concatenate(
                    [split_ref[odd, at, pl.ds(row, GROUP, stride=rows), :] for at in range(half // LANES)], 1
                )
                for odd in range(2)
            )
            for tap, value in enumerate((shifted(odd), even, odd)):
                store(tap, row, first, value.astype(BF16))
        yield


def whole(own, other, core):
    first = jnp.where(core == 0, own, other)
    second = jnp.where(core == 0, other, own)
    return jnp.concatenate([first, second], 0)


def turn(kernel, turned_ref):
    columns = kernel.shape[1]
    for at in range(0, columns, LANES):
        size = min(LANES, columns - at)
        turned_ref[at : at + size, :] = kernel[:, at : at + size].T


def tap_major(turned_ref, taps, w_ref, first):
    chans = turned_ref.shape[0] // TAPS
    at = 0
    for index in range(0, len(taps), LANES // chans):
        parts = [turned_ref[pl.ds(tap, chans, stride=TAPS), :] for tap in taps[index : index + LANES // chans]]
        block = jnp.concatenate(parts, 0).T.astype(BF16)
        w_ref[first : first + LANES, at : at + block.shape[1]] = block
        at += block.shape[1]


def four_weights_kernel(core_ref, own_ref, other_ref, w_ref, *turned_refs):
    core = core_ref[0]
    for index, turned_ref in enumerate(turned_refs):
        turn(jnp.where(core == index, own_ref[...].astype(F32), other_ref[...].astype(F32)), turned_ref)
        tap_major(turned_ref, range(TAPS), w_ref, index * LANES)


def four_weights(own, other, core):
    outs, columns = own.shape
    return pl.pallas_call(
        four_weights_kernel,
        out_shape=jax.ShapeDtypeStruct((2 * outs, columns), BF16),
        in_specs=[
            pl.BlockSpec(memory_space=pltpu.SMEM),
            pl.BlockSpec(memory_space=pltpu.VMEM),
            pl.BlockSpec(memory_space=pltpu.VMEM),
        ],
        scratch_shapes=[pltpu.VMEM((columns, LANES), F32)] * 2,
        compiler_params=pltpu.CompilerParams(vmem_limit_bytes=VMEM_LIMIT),
        cost_estimate=pl.CostEstimate(flops=10**6, bytes_accessed=4 * 10**6, transcendentals=0),
        name="four_weights",
    )(core, own, other)


def three_edges_kernel(
    core_ref, last_ref, rim_ref, own_ref, other_ref, own_scales_ref, other_scales_ref, place_ref,
    message_ref, w_ref, gain_ref, shift_ref, scales_ref,
    *scratch,
):
    *split_refs, turned_ref, pick_ref, data_ref, rims_ref, rim_w_ref = scratch
    core, step, last = core_ref[0], pl.program_id(0), pl.num_programs(0) - 1
    chans, rows, width = last_ref.shape[1], last_ref.shape[3], last_ref.shape[4]
    block, planes = rim_ref.shape[2], rims_ref.shape[0]
    half = width // 2
    out_rows = rows // 2
    taps = 3 * chans
    rim = (rows - 1) % SUB

    @pl.when(step == 0)
    def _():
        turn(whole(own_ref[...].astype(F32), other_ref[...].astype(F32), core), turned_ref)
        tap_major(turned_ref, range(TAPS), w_ref, 0)
        tap_major(turned_ref, RIM_TAPS, rim_w_ref, 0)
        own_scales, other_scales = own_scales_ref[...], other_scales_ref[...]
        lines = own_scales.shape[0]
        scales = jnp.concatenate(
            [own_scales, other_scales, jnp.zeros((LANES - 2 * lines, LANES), F32)], 0
        ).T
        scales_ref[...] = scales
        share = own_ref.shape[0]
        for ref, at in ((gain_ref, 0), (shift_ref, share)):
            ref[...] = whole(scales[at : at + share, 0:1], scales[at : at + share, lines : lines + 1], core)

    def picked(spots):
        values, held = [], None
        for plane, row in spots:
            if plane != held:
                x = rim_ref[0, :, plane, :SUB].astype(F32).reshape(chans * SUB, width)
                for at in range(width // LANES):
                    pick_ref[plane % 2, at] = x[:, at * LANES : (at + 1) * LANES]
                held = plane
            values.append(
                jnp.concatenate(
                    [pick_ref[plane % 2, at, pl.ds(row, chans, stride=SUB), :] for at in range(width // LANES)], 1
                ).astype(BF16)
            )
        values = jnp.concatenate(values, 0)
        parts = [part.astype(BF16) for part in spread((values[:, :half], values[:, half:]), place_ref[...])]
        return [
            jnp.concatenate([part[at * chans : (at + 1) * chans] for part in parts], 0) for at in range(len(spots))
        ]

    @pl.when(core == 0)
    def _():
        for plane, data in enumerate(picked([(plane, rim) for plane in range(block)])):
            rims_ref[step * block + plane] = data

    @pl.when((core == 0) & (step == last))
    def _():
        none = jnp.zeros((taps, half), BF16)
        for index in range(planes // 2 + 1):
            pieces = [
                rims_ref[plane] if 0 <= plane < planes else none for plane in range(2 * index - 1, 2 * index + 2)
            ]
            total = jnp.dot(rim_w_ref[...], jnp.concatenate(pieces, 0), preferred_element_type=F32)
            message_ref[index] = total.astype(BF16)
        spots = [(plane, row) for plane in range(block - 3, block) for row in range(rim - 2, rim + 1)]
        total = jnp.dot(w_ref[...], jnp.concatenate(picked(spots), 0), preferred_element_type=F32)
        message_ref[planes // 2 + 1] = activate(total, gain_ref[...], shift_ref[...]).astype(BF16)
        for index in range(planes // 2 + 2, message_ref.shape[0]):
            message_ref[index] = jnp.zeros_like(message_ref[index])

    @pl.when((core == 1) & (step == 0))
    def _():
        def store(tap, row, first, value):
            data_ref[row + 1, tap * chans + first : tap * chans + first + GROUP, :] = value

        data_ref[0] = jnp.zeros_like(data_ref[0])
        for _ in separate(last_ref, 0, place_ref, split_refs, store):
            pass
        for row in range(out_rows):
            total = jnp.dot(
                w_ref[:, : 3 * taps],
                data_ref[2 * row : 2 * row + 3].reshape(3 * taps, half),
                preferred_element_type=F32,
            )
            message_ref[row] = total.astype(BF16)


def three_edges(volume, own, other, own_scales, other_scales, core):
    _, chans, planes, rows, width = volume.shape
    outs, columns = 2 * own.shape[0], own.shape[1]
    half = width // 2
    block, steps, out_rows = 4, planes // 4, rows // 2
    full = lambda *shape: pl.BlockSpec(shape, lambda i, core: (0,) * len(shape))
    shapes = [
        ((out_rows, outs, half), BF16),
        ((outs, columns), BF16),
        ((outs, 1), F32),
        ((outs, 1), F32),
        ((LANES, LANES), F32),
    ]
    return pl.pallas_call(
        three_edges_kernel,
        grid_spec=pltpu.PrefetchScalarGridSpec(
            num_scalar_prefetch=1,
            grid=(steps,),
            in_specs=[
                pl.BlockSpec((1, chans, 1, rows, width), lambda i, core: (0, 0, planes - 1, 0, 0)),
                pl.BlockSpec(
                    (1, chans, block, 2 * SUB, width),
                    lambda i, core: (0, 0, i + core[0] * (steps - 1 - i), (rows - 1) // (2 * SUB), 0),
                ),
                full(*own.shape),
                full(*other.shape),
                full(*own_scales.shape),
                full(*other_scales.shape),
                full(half, half),
            ],
            out_specs=[full(*shape) for shape, _ in shapes],
            scratch_shapes=[pltpu.VMEM((2, half // LANES, GROUP * rows, LANES), F32)] * 4
            + [
                pltpu.VMEM((columns, LANES), F32),
                pltpu.VMEM((2, width // LANES, chans * SUB, LANES), F32),
                pltpu.VMEM((rows + 1, 3 * chans, half), BF16),
                pltpu.VMEM((planes, 3 * chans, half), BF16),
                pltpu.VMEM((outs, columns // 3), BF16),
            ],
        ),
        out_shape=[jax.ShapeDtypeStruct(*shape) for shape in shapes],
        compiler_params=pltpu.CompilerParams(vmem_limit_bytes=VMEM_LIMIT),
        cost_estimate=pl.CostEstimate(flops=2 * 10**9, bytes_accessed=8 * 10**6, transcendentals=0),
        name="three_edges",
    )(core, volume, volume, own, other, own_scales, other_scales, even_odd(half))


def three_kernel(
    core_ref, x_ref, before_ref, w_ref, place_ref, gain_ref, shift_ref,
    third_ref, plane_ref, row_ref, last_row_ref, local_ref,
    *scratch,
):
    *split_refs, prior_ref, first_ref, second_ref, total_ref = scratch
    core, step, steps = core_ref[0], pl.program_id(0), pl.num_programs(0) - 1
    chans, rows, width = x_ref.shape[1], x_ref.shape[3], x_ref.shape[4]
    half = width // 2
    out_rows = rows // 2
    taps = 3 * chans

    def splitting(pair_ref):
        for plane in range(2):

            def store(tap, row, first, value, plane=plane):
                pair_ref[plane, row + 1, tap * chans + first : tap * chans + first + GROUP, :] = value

            yield from separate(x_ref, plane, place_ref, split_refs, store)

    def summing(pair_ref):
        gain, shift = gain_ref[...], shift_ref[...]
        for row in range(out_rows):
            parts = [
                ref[2 * row : 2 * row + 3].reshape(3 * taps, half)
                for ref in (prior_ref, pair_ref.at[0], pair_ref.at[1])
            ]
            total = jnp.dot(w_ref[...], jnp.concatenate(parts, 0), preferred_element_type=F32)
            third_ref[0, row] = activate(total, gain, shift).astype(BF16)
            total_ref[row] = total
            yield
        row_ref[0] = total_ref[0]
        prior_ref[...] = pair_ref[1]
        yield

    @pl.when(step == 0)
    def _():
        prior_ref[...] = jnp.zeros_like(prior_ref)

        @pl.when(core == 1)
        def _():
            def store(tap, row, first, value):
                prior_ref[row + 1, tap * chans + first : tap * chans + first + GROUP, :] = value

            for _ in separate(before_ref, 0, place_ref, split_refs, store):
                pass

        for ref in (first_ref, second_ref):
            ref[:, 0] = jnp.zeros_like(ref[:, 0])
        for _ in splitting(first_ref):
            pass

    def both(new_ref, old_ref):
        new, old = splitting(new_ref), summing(old_ref)
        for turn in range(2 * chans // GROUP):
            next(new, None)
            for _ in range(out_rows * (turn + 1) // (2 * chans // GROUP) - out_rows * turn // (2 * chans // GROUP)):
                next(old, None)
        for _ in new:
            pass
        for _ in old:
            pass

    for odd, (new_ref, old_ref) in enumerate(((first_ref, second_ref), (second_ref, first_ref))):

        @pl.when((step > 0) & (step < steps) & (step % 2 == odd))
        def _(new_ref=new_ref, old_ref=old_ref):
            both(new_ref, old_ref)

        @pl.when((step == steps) & (step % 2 == odd))
        def _(old_ref=old_ref):
            for _ in summing(old_ref):
                pass

    @pl.when(step == 1)
    def _():
        plane_ref[...] = total_ref[...]

    @pl.when((step > 0) & (core == 1))
    def _():
        local_ref[step - 1] = third_ref[0, out_rows - 1]

    @pl.when((step == steps) & (core == 0))
    def _():
        local_ref[...] = third_ref[0]
        last_row_ref[...] = total_ref[0]


def layer_three(volume, weights, gain, shift, core):
    _, chans, planes, rows, width = volume.shape
    outs = weights.shape[0]
    half = width // 2
    steps, out_rows = planes // 4, rows // 2
    full = lambda *shape: pl.BlockSpec(shape, lambda i, core: (0,) * len(shape))
    return pl.pallas_call(
        three_kernel,
        grid_spec=pltpu.PrefetchScalarGridSpec(
            num_scalar_prefetch=1,
            grid=(steps + 1,),
            in_specs=[
                pl.BlockSpec((1, chans, 2, rows, width), lambda i, core: (0, 0, core[0] * steps + jnp.minimum(i, steps - 1), 0, 0)),
                pl.BlockSpec(
                    (1, chans, 1, rows, width),
                    lambda i, core: (0, 0, jnp.maximum(core[0] * 2 * steps - 1, 0), 0, 0),
                ),
                full(*weights.shape),
                full(half, half),
                full(outs, 1),
                full(outs, 1),
            ],
            out_specs=[
                pl.BlockSpec((1, out_rows, outs, half), lambda i, core: (jnp.maximum(i - 1, 0), 0, 0, 0)),
                full(out_rows, outs, half),
                pl.BlockSpec((1, outs, half), lambda i, core: (jnp.maximum(i - 1, 0), 0, 0)),
                full(outs, half),
                full(out_rows, outs, half),
            ],
            scratch_shapes=[pltpu.VMEM((2, half // LANES, GROUP * rows, LANES), F32)] * 4
            + [
                pltpu.VMEM((rows + 1, 3 * chans, half), BF16),
                pltpu.VMEM((2, rows + 1, 3 * chans, half), BF16),
                pltpu.VMEM((2, rows + 1, 3 * chans, half), BF16),
                pltpu.VMEM((out_rows, outs, half), F32),
            ],
        ),
        out_shape=[
            jax.ShapeDtypeStruct((steps, out_rows, outs, half), BF16),
            jax.ShapeDtypeStruct((out_rows, outs, half), F32),
            jax.ShapeDtypeStruct((steps, outs, half), F32),
            jax.ShapeDtypeStruct((outs, half), F32),
            jax.ShapeDtypeStruct((out_rows, outs, half), BF16),
        ],
        compiler_params=pltpu.CompilerParams(vmem_limit_bytes=VMEM_LIMIT),
        cost_estimate=pl.CostEstimate(flops=10**10, bytes_accessed=2 * 10**7, transcendentals=0),
        name="layer_three",
    )(core, volume, volume, weights, even_odd(half), gain, shift)


def corner_total(core, refs):
    _, plane_ref, _, halo_ref, rows_ref, _, _ = refs
    planes = rows_ref.shape[0]
    first = jnp.where(core == 0, rows_ref[0].astype(F32), halo_ref[planes].astype(F32))
    return plane_ref[0] + jnp.where(core == 0, halo_ref[0].astype(F32), 0.0) + first


def third_value(core, refs, plane, row):
    third_ref, plane_ref, row_ref, halo_ref, rows_ref, gain_ref, shift_ref = refs
    planes = rows_ref.shape[0]
    if plane and row:
        return third_ref[plane, row]
    if plane:
        share = jnp.where(core == 0, rows_ref[plane].astype(F32), halo_ref[planes + plane].astype(F32))
        total = row_ref[plane] + share
    elif row:
        total = plane_ref[row] + jnp.where(core == 0, halo_ref[row].astype(F32), 0.0)
    else:
        total = corner_total(core, refs)
    value = activate(total, gain_ref[...], shift_ref[...])
    if not plane and not row:
        value = jnp.where(core == 0, 0.0, value)
    return value.astype(BF16)


def four_edges_kernel(core_ref, *refs):
    *thirds, local_ref, w_ref, place_ref, message_ref, mid_ref = refs
    core = core_ref[0]
    planes, rows, chans, width = thirds[0].shape
    half = width // 2
    out_rows = rows // 2
    taps = 3 * chans
    mid_ref[...] = w_ref[:, 4 * taps : 5 * taps]

    def data(values):
        parts = [part.astype(BF16) for part in spread((jnp.concatenate(values, 0),), place_ref[...])]
        return [
            jnp.concatenate([part[at * chans : (at + 1) * chans] for part in parts], 0) for at in range(len(values))
        ]

    @pl.when(core == 0)
    def _():
        none = jnp.zeros((taps, half), BF16)
        rim = [none] + data(
            [third_value(core, thirds, plane, rows - 1) for plane in range(planes)]
            + [local_ref[plane] for plane in range(planes)]
        )
        pieces = [jnp.concatenate([rim[2 * m + slot] for m in range(planes)], 1) for slot in range(3)]
        weights = jnp.concatenate([w_ref[:, 3 * slot * taps : (3 * slot + 1) * taps] for slot in range(3)], 1)
        total = jnp.dot(weights, jnp.concatenate(pieces, 0), preferred_element_type=F32).astype(BF16)
        for m in range(planes):
            message_ref[m] = total[:, m * half : (m + 1) * half]
        for index in range(planes, message_ref.shape[0]):
            message_ref[index] = jnp.zeros_like(message_ref[index])

    @pl.when(core == 1)
    def _():
        halo_ref = thirds[3]
        last = data(
            [halo_ref[2 * planes + 1]] + [third_value(core, thirds, planes - 1, row) for row in range(rows)]
        )
        for row in range(0, out_rows, 2):
            pieces = [jnp.concatenate([last[2 * row + at], last[2 * row + 2 + at]], 1) for at in range(3)]
            both = jnp.dot(w_ref[:, : 3 * taps], jnp.concatenate(pieces, 0), preferred_element_type=F32)
            both = both.astype(BF16)
            message_ref[row] = both[:, :half]
            message_ref[row + 1] = both[:, half:]
        corner = halo_ref[2 * planes]
        message_ref[out_rows, :chans] = corner[:, :half]
        message_ref[out_rows, chans:] = corner[:, half:]


def inputs(count):
    return [pl.BlockSpec(memory_space=pltpu.SMEM)] + [pl.BlockSpec(memory_space=pltpu.VMEM)] * count


def four_edges(core, thirds, local, weights):
    planes, rows, chans, width = thirds[0].shape
    outs = weights.shape[0]
    half = width // 2
    return pl.pallas_call(
        four_edges_kernel,
        out_shape=[
            jax.ShapeDtypeStruct((rows // 2 + 1, outs, half), BF16),
            jax.ShapeDtypeStruct((outs, 3 * chans), BF16),
        ],
        in_specs=inputs(len(thirds) + 3),
        compiler_params=pltpu.CompilerParams(vmem_limit_bytes=VMEM_LIMIT),
        cost_estimate=pl.CostEstimate(flops=2 * 10**9, bytes_accessed=8 * 10**6, transcendentals=0),
        name="four_edges",
    )(core, *thirds, local, weights, even_odd(width))


def four_kernel(core_ref, *refs):
    *thirds, local_ref, last_row_ref, w_ref, place_ref, sums_ref, data_ref = refs
    core = core_ref[0]
    planes, rows, chans, width = thirds[0].shape
    halo_ref, gain_ref, shift_ref = thirds[3], thirds[5], thirds[6]
    half = width // 2
    out_rows, count = rows // 2, planes // 2
    taps = 3 * chans
    batch = 4
    data_ref[:, 0] = jnp.zeros_like(data_ref[:, 0])

    def put(values, first, spots):
        for tap, part in enumerate(spread((jnp.concatenate(values, 0),), place_ref[...])):
            part = part.astype(BF16)
            for at in range(len(values)):
                for slot, lanes in spots:
                    data_ref[
                        slot, first + at + 1, tap * chans : (tap + 1) * chans, lanes * half : (lanes + 1) * half
                    ] = part[at * chans : (at + 1) * chans]

    @pl.when(core == 0)
    def _():
        data_ref[0, :, :, :half] = jnp.zeros_like(data_ref[0, :, :, :half])

    @pl.when(core == 1)
    def _():
        total = last_row_ref[...] + halo_ref[planes - 1].astype(F32)
        prior = [activate(total, gain_ref[...], shift_ref[...]).astype(BF16)]
        prior += [local_ref[row] for row in range(1, rows)]
        for first in range(0, rows, batch):
            put(prior[first : first + batch], first, [(0, 0)])

    for plane in range(planes):
        spots = [(1 + plane % 2, plane // 2)]
        if plane % 2 and plane // 2 + 1 < count:
            spots.append((0, plane // 2 + 1))
        for first in range(0, rows, batch):
            put([third_value(core, thirds, plane, row) for row in range(first, first + batch)], first, spots)
    for row in range(out_rows):
        parts = [data_ref[slot, 2 * row : 2 * row + 3].reshape(3 * taps, count * half) for slot in range(3)]
        sums_ref[row] = jnp.dot(w_ref[...], jnp.concatenate(parts, 0), preferred_element_type=F32)


def layer_four(core, thirds, local, last_row, weights):
    planes, rows, chans, width = thirds[0].shape
    outs = weights.shape[0]
    half = width // 2
    out_rows, count = rows // 2, planes // 2
    return pl.pallas_call(
        four_kernel,
        out_shape=jax.ShapeDtypeStruct((out_rows, outs, count * half), F32),
        in_specs=inputs(len(thirds) + 4),
        scratch_shapes=[pltpu.VMEM((3, rows + 1, 3 * chans, count * half), BF16)],
        compiler_params=pltpu.CompilerParams(vmem_limit_bytes=VMEM_LIMIT),
        cost_estimate=pl.CostEstimate(flops=8 * 10**9, bytes_accessed=10**7, transcendentals=0),
        name="layer_four",
    )(core, *thirds, local, last_row, weights, even_odd(width))


def theirs_kernel(
    core_ref, sums_ref, halo_ref, mid_ref, place_ref,
    third_ref, plane_ref, row_ref, three_halo_ref, rows_ref, gain_ref, shift_ref,
    theirs_ref, fix_ref,
):
    core = core_ref[0]
    thirds = third_ref, plane_ref, row_ref, three_halo_ref, rows_ref, gain_ref, shift_ref
    rows, width = halo_ref.shape[0] - 1, halo_ref.shape[2]

    @pl.when(core == 0)
    def _():
        corner = halo_ref[rows].astype(F32)
        total = corner_total(core, thirds) + jnp.concatenate([corner[:LANES], corner[LANES:]], 1)
        value = activate(total, gain_ref[...], shift_ref[...]).astype(BF16)
        data = jnp.concatenate([part.astype(BF16) for part in spread((value,), place_ref[...])], 0)
        fix = jnp.dot(mid_ref[...], data, preferred_element_type=F32)
        fix_ref[...] = fix[:LANES]
        for row in range(rows):
            total = sums_ref[row, LANES:]
            edge = halo_ref[row, LANES:].astype(F32)
            if not row:
                edge = edge + fix[LANES:]
            theirs_ref[row] = jnp.concatenate([total[:, :width] + edge, total[:, width:]], 1)
        theirs_ref[rows] = jnp.zeros_like(theirs_ref[rows])

    @pl.when(core == 1)
    def _():
        count = sums_ref.shape[2] // width
        fix_ref[...] = jnp.zeros_like(fix_ref)
        for row in range(rows):
            total = sums_ref[row, :LANES]
            if not row:
                total = total + jnp.concatenate([halo_ref[count + m, :LANES].astype(F32) for m in range(count)], 1)
            theirs_ref[row] = total
        theirs_ref[rows] = jnp.concatenate([halo_ref[m, :LANES].astype(F32) for m in range(count)], 1)


def assemble_kernel(core_ref, sums_ref, halo_ref, fix_ref, scales_ref, got_ref, out_ref, lines_ref):
    core = core_ref[0]
    gain, shift = scales_ref[:, 1:2], scales_ref[:, 2:3]
    rows, width = halo_ref.shape[0] - 1, halo_ref.shape[2]
    count = sums_ref.shape[2] // width

    def put(row, parts):
        for at, total in enumerate(parts):
            value = activate(total, gain, shift)
            for m in range(count):
                place = row * 2 * count + at * count + m
                lines_ref[pl.ds(place, LANES, stride=rows * 2 * count), :] = value[:, m * width : (m + 1) * width]

    @pl.when(core == 0)
    def _():
        for row in range(rows):
            total = sums_ref[row, :LANES]
            edge = halo_ref[row, :LANES].astype(F32)
            if not row:
                edge = edge + fix_ref[...]
            total = jnp.concatenate([total[:, :width] + edge, total[:, width:]], 1)
            if not row:
                total = total + got_ref[rows]
            put(row, (total, got_ref[row]))

    @pl.when(core == 1)
    def _():
        for row in range(rows):
            total, got = sums_ref[row, LANES:], got_ref[row]
            if not row:
                first = [halo_ref[m, LANES:].astype(F32) for m in range(2 * count)]
                total = total + jnp.concatenate(first[count:], 1)
                got = got + jnp.concatenate(first[:count], 1)
            put(row, (got, total))

    out_ref[...] = lines_ref[...].astype(BF16)


def last_stage(core, sums, halo, mid, thirds, scales):
    rows, outs, lanes = sums.shape
    params = pltpu.CompilerParams(vmem_limit_bytes=VMEM_LIMIT)
    theirs, fix = pl.pallas_call(
        theirs_kernel,
        out_shape=[
            jax.ShapeDtypeStruct((rows + 1, outs // 2, lanes), F32),
            jax.ShapeDtypeStruct((outs // 2, halo.shape[2]), F32),
        ],
        in_specs=inputs(4) + [pl.BlockSpec(memory_space=pl.ANY)] + inputs(6)[1:],
        compiler_params=params,
        name="theirs",
    )(core, sums, halo, mid, even_odd(lanes), *thirds)
    lines = (outs // 2 * rows * lanes * 2 // LANES, LANES)
    return pl.pallas_call(
        assemble_kernel,
        out_shape=jax.ShapeDtypeStruct(lines, BF16),
        in_specs=inputs(5),
        scratch_shapes=[pltpu.VMEM(lines, F32)],
        compiler_params=params,
        name="assemble",
    )(core, sums, halo, fix, scales, swapped(theirs))


def handed_on(message):
    count = lax.axis_size("sp")
    pairs = [(2 * b, 2 * (b + 1) + 1) for b in range(count) if b % ROW_BLOCKS != ROW_BLOCKS - 1]
    pairs += [(2 * b + 1, 2 * (b + ROW_BLOCKS)) for b in range(count - ROW_BLOCKS)]
    return lax.ppermute(message, ("sp", "fl"), pairs)


def swapped(value):
    return lax.ppermute(value, "fl", [(0, 1), (1, 0)])


def shards(volume, kernel_three, gain_three, shift_three, kernel_four, gain_four, shift_four):
    core = lax.axis_index("fl").reshape(1)
    own_scales = jnp.concatenate([gain_three, shift_three, gain_four, shift_four]).reshape(-1, LANES)
    message, weights_three, gain, shift, scales = three_edges(
        volume, kernel_three, swapped(kernel_three), own_scales, swapped(own_scales), core
    )
    halo = handed_on(message)
    *thirds, last_row, local = layer_three(volume, weights_three, gain, shift, core)
    rows = lax.ppermute(halo[: thirds[0].shape[0]], "fl", [(1, 0)])
    thirds = (*thirds, halo, rows, gain, shift)
    local, last_row = swapped(local), lax.ppermute(last_row, "fl", [(0, 1)])
    weights_four = four_weights(kernel_four, swapped(kernel_four), core)
    message, mid = four_edges(core, thirds, local, weights_four)
    halo = handed_on(message)
    sums = layer_four(core, thirds, local, last_row, weights_four)
    lines = last_stage(core, sums, halo, mid, thirds, scales)
    out_rows, outs, lanes = sums.shape
    fourth = lines.reshape(outs // 2, out_rows, 2 * lanes // LANES, LANES)
    return jnp.transpose(fourth, (0, 2, 1, 3))[None]


def solution(mesh):
    return jax.shard_map(
        shards,
        mesh=mesh,
        in_specs=(
            P("sp", None, None, None, None),
            P("fl", None),
            P("fl"),
            P("fl"),
            P("fl", None),
            P("fl"),
            P("fl"),
        ),
        out_specs=P("sp", "fl", None, None, None),
        check_vma=False,
    )
```

time: 77.7 us -> 78.4 us (level); the launches traced: 76.5 us -> 78.1 us
  starting transfers between devices: 20.9 us -> 12.7 us
  waiting for transfers between devices: 2.28 us -> 8.68 us
  Pallas kernels: 48.3 us -> 50.7 us
  local copies, waits for them, and re-layouts: 4.11 us -> 5.09 us
    ppermute x7 -> x4, starting transfers between devices: 19.7 us -> 8.18 us  [the longest x1 4.15 us: shards(): rows = lax.ppermute(halo[:thirds[0].shape[0]], 'fl', [(1, 0)])]
    ppermute x7 -> x4, waiting for transfers between devices: 1.63 us -> 5.35 us  [the longest x2 5.34 us: handed_on(): return lax.ppermute(message, ('sp', 'fl'), pairs)]
    ppermute x3 -> x5, starting transfers between devices: 1.19 us -> 4.49 us  [swapped(): return lax.ppermute(value, 'fl', [(0, 1), (1, 0)])]
    ppermute x3 -> x5, waiting for transfers between devices: 0.65 us -> 3.33 us  [swapped(): return lax.ppermute(value, 'fl', [(0, 1), (1, 0)])]
    pallas_call x1, Pallas kernels: 17.2 us -> 19.3 us  [layer_three(): pl.pallas_call(three_kernel, grid_spec=pltpu.PrefetchScalarGridSpec(num_s...]
    pallas_call x1, Pallas kernels: 2.5 us -> 3.62 us  [last_stage(): pl.pallas_call(theirs_kernel, out_shape=[jax.ShapeDtypeStruct((rows + 1,...]
    pallas_call x1, Pallas kernels: 6.85 us -> 5.75 us  [three_edges(): pl.pallas_call(three_edges_kernel, grid_spec=pltpu.PrefetchScalarGridSpec...]
    unnamed x22 -> x20, local copies, waits for them, and re-layouts: 4.11 us -> 5.07 us
  transfers between devices with their start and end apart: 10 -> 9, of which waited for: 3 -> 3; matrix products, arithmetic and copies ran while one was open for 1% -> 1% of each run, Pallas kernels for 48% -> 56%
where the time goes in v4:
time: 78.4 us; the launch traced here: 78.1 us
  Pallas kernels  50.7 us (65%)
  starting transfers between devices  12.7 us (16%)
  waiting for transfers between devices  8.68 us (11%)
  local copies, waits for them, and re-layouts  5.09 us (6%)
    pallas_call x1, Pallas kernels, layer_three(): pl.pallas_call(three_kernel, grid_spec=pltpu.PrefetchScalarGridSpec(num_s...  19.3 us
    pallas_call x1, Pallas kernels, layer_four(): pl.pallas_call(four_kernel, out_shape=jax.ShapeDtypeStruct((out_rows, out...  9.4 us
    pallas_call x1, Pallas kernels, three_edges(): pl.pallas_call(three_edges_kernel, grid_spec=pltpu.PrefetchScalarGridSpec...  5.75 us
    pallas_call x1, Pallas kernels, four_edges(): pl.pallas_call(four_edges_kernel, out_shape=[jax.ShapeDtypeStruct((rows /...  5.62 us
    ppermute x2, waiting for transfers between devices, handed_on(): return lax.ppermute(message, ('sp', 'fl'), pairs)  5.34 us
    unnamed x20, local copies, waits for them, and re-layouts  5.07 us
    ppermute x5, starting transfers between devices, swapped(): return lax.ppermute(value, 'fl', [(0, 1), (1, 0)])  4.49 us
    ppermute x1, starting transfers between devices, shards(): rows = lax.ppermute(halo[:thirds[0].shape[0]], 'fl', [(1, 0)])  4.15 us
  transfers between devices with their start and end apart: 9, of which 3 were waited for; matrix products, arithmetic and copies ran while one was open for 1% of the time, Pallas kernels for 56%

profile of v4, /device:TPU:25, one launch (start us, length us, event | category | flops | bytes accessed | tf_op | source)
XLA Modules:
  0.0 78.1 jit_solution(18125988563408115267)
XLA Ops:
  0.0 0.7 collective-permute-start
  0.7 0.8 maximum_bitcast_fusion.own_scales_ref
  1.5 0.0 copy-start.7
  1.5 0.0 collective-permute-start.1
  1.5 0.5 collective-permute-start.6
  2.0 0.6 collective-permute-done.1.other_scales_ref
  2.6 0.0 copy-start.8
  2.6 0.0 collective-permute-done.other_ref
  2.6 0.0 copy-start.6
  2.6 0.0 copy-done.7
  2.6 0.5 copy-done.8
  3.2 0.2 copy-done.6
  3.3 5.7 %three_edges.1 = (bf16[12,128,256]{2,1,0:T(8,128)(2,1)}, bf16[128,1728]{1,0:T(8,128)(2,1)}, f32[128,1]{1,0:T(8,128)}, f32[128,1]{1,0:T(8,128)}, f32[128,128]{1,0:T(8,128)}) custom-call(s32[1]{0:T(128)} %bitcast.core_ref, bf16[1,64,16,24,512]{4,3,2,1,0:T(8,128)(2,1)} %before_ref.1, bf16[1,64,16,24,512]{4,3,2,1,0:T(8,128)(2,1)} %before_ref.1, ...), custom_call_target="tpu_custom_call" | custom-call | flops 2000000000 | bytes 8000000 | tf_op jit(solution)/shard_map/three_edges/pallas_call | solution.py:219
  9.1 1.5 %collective-permute-start.2 = (bf16[12,128,256]{2,1,0:T(8,128)(2,1)}, bf16[12,128,256]{2,1,0:T(8,128)(2,1)S(1)}, u32[]{:S(2)}, u32[]{:S(2)}) collective-permute-start(bf16[12,128,256]{2,1,0:T(8,128)(2,1)} %get-tuple-element.25), channel_id=1, source_target_pairs={{0,3},{2,5},{4,7},{6,9},{8,11},{10,13},{12,15},{16,19},{18,21},{20... | collective-permute-start | bytes 2359304 | tf_op jit(solution)/shard_map/ppermute | solution.py:646
  10.5 19.3 %layer_three.1 = (bf16[4,12,128,256]{3,2,1,0:T(8,128)(2,1)}, f32[12,128,256]{2,1,0:T(8,128)}, f32[4,128,256]{2,1,0:T(8,128)}, f32[128,256]{1,0:T(8,128)}, bf16[12,128,256]{2,1,0:T(8,128)(2,1)}) custom-call(s32[1]{0:T(128)} %bitcast.core_ref, bf16[1,64,16,24,512]{4,3,2,1,0:T(8,128)(2,1)} %before_ref.1, bf16[1,64,16,24,512]{4,3,2,1,0:T(8,128)(2,1)} %before_ref.1, ...), custom_call_target="tpu_custom_call" | custom-call | flops 10000000000 | bytes 20000000 | tf_op jit(solution)/shard_map/layer_three/pallas_call | solution.py:347
  29.8 3.3 %collective-permute-start.4 = (bf16[12,128,256]{2,1,0:T(8,128)(2,1)}, bf16[12,128,256]{2,1,0:T(8,128)(2,1)S(1)}, u32[]{:S(2)}, u32[]{:S(2)}) collective-permute-start(bf16[12,128,256]{2,1,0:T(8,128)(2,1)} %get-tuple-element.26), channel_id=1, source_target_pairs={{0,1},{1,0},{2,3},{3,2},{4,5},{5,4},{6,7},{7,6},{8,9},{9,8},{10,11... | collective-permute-start | bytes 2359304 | tf_op jit(solution)/shard_map/ppermute | solution.py:650
  33.1 0.0 collective-permute-done.2.refs_3_.three_halo_ref
  33.1 0.0 copy-start
  33.1 4.1 %collective-permute-start.3 = (bf16[4,128,256]{2,1,0:T(8,128)(2,1)S(1)}, bf16[4,128,256]{2,1,0:T(8,128)(2,1)S(1)}, u32[]{:S(2)}, u32[]{:S(2)}) collective-permute-start(bf16[4,128,256]{2,1,0:T(8,128)(2,1)S(1)} %slice.4), channel_id=1, source_target_pairs={{1,0},{3,2},{5,4},{7,6},{9,8},{11,10},{13,12},{15,14},{17,16},{19,... | collective-permute-start | bytes 786440 | tf_op jit(solution)/shard_map/ppermute | solution.py:661
  37.3 1.3 %collective-permute-start.5 = (f32[128,256]{1,0:T(8,128)}, f32[128,256]{1,0:T(8,128)S(1)}, u32[]{:S(2)}, u32[]{:S(2)}) collective-permute-start(f32[128,256]{1,0:T(8,128)} %get-tuple-element.27), channel_id=1, source_target_pairs={{0,1},{2,3},{4,5},{6,7},{8,9},{10,11},{12,13},{14,15},{16,17},{18,... | collective-permute-start | bytes 393224 | tf_op jit(solution)/shard_map/ppermute | solution.py:663
  38.6 0.0 collective-permute-done.6.other_ref
  38.6 0.0 copy-start.4
  38.6 0.9 %copy-done.4 = bf16[128,3456]{1,0:T(8,128)(2,1)} copy-done((bf16[128,3456]{1,0:T(8,128)(2,1)}, bf16[128,3456]{1,0:T(8,128)(2,1)S(1)}, u32[]{:S(2)}) %copy-start.4) | copy-done | bytes 884760
  39.5 3.8 %four_weights.1.refs_9_.refs_8_ = bf16[256,3456]{1,0:T(8,128)(2,1)} custom-call(s32[1]{0:T(128)} %bitcast.core_ref, bf16[128,3456]{1,0:T(8,128)(2,1)} %own_ref.3, bf16[128,3456]{1,0:T(8,128)(2,1)} %copy-done.4), custom_call_target="tpu_custom_call" | custom-call | flops 1000000 | bytes 4000000 | tf_op jit(solution)/shard_map/four_weights/pallas_call | solution.py:106
  43.4 0.0 copy-done
  43.4 0.0 collective-permute-done.4.refs_7_
  43.4 0.0 copy-start.5
  43.4 0.0 collective-permute-done.3.refs_4_.rows_ref
  43.4 0.0 copy-start.2
  43.4 0.9 %copy-done.5 = bf16[12,128,256]{2,1,0:T(8,128)(2,1)} copy-done((bf16[12,128,256]{2,1,0:T(8,128)(2,1)}, bf16[12,128,256]{2,1,0:T(8,128)(2,1)S(1)}, u32[]{:S(2)}) %copy-start.5) | copy-done | bytes 786456
  44.3 0.1 copy-done.2
  44.4 5.6 %four_edges.1 = (bf16[7,256,128]{2,1,0:T(8,128)(2,1)}, bf16[256,384]{1,0:T(8,128)(2,1)}) custom-call(s32[1]{0:T(128)} %bitcast.core_ref, bf16[4,12,128,256]{3,2,1,0:T(8,128)(2,1)} %get-tuple-element.22.refs_0_.third_ref, f32[12,128,256]{2,1,0:T(8,128)} %get-tuple-element.23.refs_1_.plane_ref, f32[4,128,256]{2,1,0:T(8,128)} %get-tuple-element.24.refs_2_.row_ref, ...), custom_call_target="tpu_custom_call" | custom-call | flops 2000000000 | bytes 8000000 | tf_op jit(solution)/shard_map/four_edges/pallas_call | solution.py:471
  50.0 1.3 %collective-permute-start.7 = (bf16[7,256,128]{2,1,0:T(8,128)(2,1)}, bf16[7,256,128]{2,1,0:T(8,128)(2,1)S(1)}, u32[]{:S(2)}, u32[]{:S(2)}) collective-permute-start(bf16[7,256,128]{2,1,0:T(8,128)(2,1)} %get-tuple-element.28), channel_id=1, source_target_pairs={{0,3},{2,5},{4,7},{6,9},{8,11},{10,13},{12,15},{16,19},{18,21},{20... | collective-permute-start | bytes 1376264 | tf_op jit(solution)/shard_map/ppermute | solution.py:646
  51.3 0.0 collective-permute-done.5.refs_8_
  51.3 0.0 copy-start.9
  51.4 0.7 copy-done.9
  52.0 9.4 %layer_four.1.sums_ref = f32[6,256,256]{2,1,0:T(8,128)} custom-call(s32[1]{0:T(128)} %bitcast.core_ref, bf16[4,12,128,256]{3,2,1,0:T(8,128)(2,1)} %get-tuple-element.22.refs_0_.third_ref, f32[12,128,256]{2,1,0:T(8,128)} %get-tuple-element.23.refs_1_.plane_ref, f32[4,128,256]{2,1,0:T(8,128)} %get-tuple-element.24.refs_2_.row_ref, ...), custom_call_target="tpu_custom_call" | custom-call | flops 8000000000 | bytes 10000000 | tf_op jit(solution)/shard_map/layer_four/pallas_call | solution.py:532
  61.4 5.3 %collective-permute-done.7.halo_ref = bf16[7,256,128]{2,1,0:T(8,128)(2,1)S(1)} collective-permute-done((bf16[7,256,128]{2,1,0:T(8,128)(2,1)}, bf16[7,256,128]{2,1,0:T(8,128)(2,1)S(1)}, u32[]{:S(2)}, u32[]{:S(2)}) %collective-permute-start.7) | collective-permute-done | bytes 458784 | tf_op jit(solution)/shard_map/ppermute | solution.py:646
  66.8 0.0 copy-start.1
  66.8 0.8 %copy-done.1 = bf16[7,256,128]{2,1,0:T(8,128)(2,1)} copy-done((bf16[7,256,128]{2,1,0:T(8,128)(2,1)}, bf16[7,256,128]{2,1,0:T(8,128)(2,1)S(1)}, u32[]{:S(2)}) %copy-start.1) | copy-done | bytes 458776
  67.6 3.6 %theirs.1 = (f32[7,128,256]{2,1,0:T(8,128)}, f32[128,128]{1,0:T(8,128)}) custom-call(s32[1]{0:T(128)} %bitcast.core_ref, f32[6,256,256]{2,1,0:T(8,128)} %layer_four.1.sums_ref, bf16[7,256,128]{2,1,0:T(8,128)(2,1)} %copy-done.1, bf16[256,384]{1,0:T(8,128)(2,1)} %get-tuple-element.29.mid_ref, bf16[256,256]{1,0:T(8,128)(2,1)} %constant.6.clone.place_ref.refs_10_.refs_9_, ...), custom_call_target="tpu_custom_call" | custom-call | tf_op jit(solution)/shard_map/theirs/pallas_call | solution.py:621
  71.2 0.0 collective-permute-start.8
  71.2 2.7 %collective-permute-done.8.got_ref = f32[7,128,256]{2,1,0:T(8,128)S(1)} collective-permute-done((f32[7,128,256]{2,1,0:T(8,128)}, f32[7,128,256]{2,1,0:T(8,128)S(1)}, u32[]{:S(2)}, u32[]{:S(2)}) %collective-permute-start.8) | collective-permute-done | bytes 917536 | tf_op jit(solution)/shard_map/ppermute | solution.py:650
  73.9 0.0 copy-start.3
  73.9 0.9 %copy-done.3 = f32[7,128,256]{2,1,0:T(8,128)} copy-done((f32[7,128,256]{2,1,0:T(8,128)}, f32[7,128,256]{2,1,0:T(8,128)S(1)}, u32[]{:S(2)}) %copy-start.3) | copy-done | bytes 917528
  74.8 3.2 %assemble.1 = bf16[3072,128]{1,0:T(8,128)(2,1)} custom-call(s32[1]{0:T(128)} %bitcast.core_ref, f32[6,256,256]{2,1,0:T(8,128)} %layer_four.1.sums_ref, bf16[7,256,128]{2,1,0:T(8,128)(2,1)} %copy-done.1, f32[128,128]{1,0:T(8,128)} %get-tuple-element.30.fix_ref, f32[128,128]{1,0:T(8,128)} %get-tuple-element.31.scales_ref, f32[7,128,256]{2,1,0:T(8,128)} %copy-done.3), custom_call_target="tpu_custom_call" | custom-call | tf_op jit(solution)/shard_map/assemble/pallas_call | solution.py:632
  (1 shorter events, 0.0 us)
Async XLA Ops:
  0.0 2.6 %collective-permute-start = (bf16[64,1728]{1,0:T(8,128)(2,1)}, bf16[64,1728]{1,0:T(8,128)(2,1)S(1)}, u32[]{:S(2)}, u32[]{:S(2)}) collective-permute-start(bf16[64,1728]{1,0:T(8,128)(2,1)} %own_ref.2), channel_id=1, source_target_pairs={{0,1},{1,0},{2,3},{3,2},{4,5},{5,4},{6,7},{7,6},{8,9},{9,8},{10,11... | collective-permute-start | bytes 663560 | tf_op jit(solution)/shard_map/ppermute | solution.py:650
  1.5 1.2 %copy-start.7 = (f32[3,128]{1,0:T(4,128)}, f32[3,128]{1,0:T(4,128)S(1)}, u32[]{:S(2)}) copy-start(f32[3,128]{1,0:T(4,128)S(1)} %maximum_bitcast_fusion.own_scales_ref) | copy-start | bytes 4612
  1.5 1.2 %collective-permute-start.1 = (f32[3,128]{1,0:T(4,128)S(1)}, f32[3,128]{1,0:T(4,128)S(1)}, u32[]{:S(2)}, u32[]{:S(2)}) collective-permute-start(f32[3,128]{1,0:T(4,128)S(1)} %maximum_bitcast_fusion.own_scales_ref), channel_id=1, source_target_pairs={{0,1},{1,0},{2,3},{3,2},{4,5},{5,4},{6,7},{7,6},{8,9},{9,8},{10,11... | collective-permute-start | bytes 4616 | tf_op jit(solution)/shard_map/ppermute | solution.py:650
  1.5 37.1 %collective-permute-start.6 = (bf16[128,3456]{1,0:T(8,128)(2,1)}, bf16[128,3456]{1,0:T(8,128)(2,1)S(1)}, u32[]{:S(2)}, u32[]{:S(2)}) collective-permute-start(bf16[128,3456]{1,0:T(8,128)(2,1)} %own_ref.3), channel_id=1, source_target_pairs={{0,1},{1,0},{2,3},{3,2},{4,5},{5,4},{6,7},{7,6},{8,9},{9,8},{10,11... | collective-permute-start | bytes 2654216 | tf_op jit(solution)/shard_map/ppermute | solution.py:650
  2.6 0.5 copy-start.8
  2.6 0.7 copy-start.6
  9.1 24.1 %collective-permute-start.2 = (bf16[12,128,256]{2,1,0:T(8,128)(2,1)}, bf16[12,128,256]{2,1,0:T(8,128)(2,1)S(1)}, u32[]{:S(2)}, u32[]{:S(2)}) collective-permute-start(bf16[12,128,256]{2,1,0:T(8,128)(2,1)} %get-tuple-element.25), channel_id=1, source_target_pairs={{0,3},{2,5},{4,7},{6,9},{8,11},{10,13},{12,15},{16,19},{18,21},{20... | collective-permute-start | bytes 2359304 | tf_op jit(solution)/shard_map/ppermute | solution.py:646
  29.8 13.6 %collective-permute-start.4 = (bf16[12,128,256]{2,1,0:T(8,128)(2,1)}, bf16[12,128,256]{2,1,0:T(8,128)(2,1)S(1)}, u32[]{:S(2)}, u32[]{:S(2)}) collective-permute-start(bf16[12,128,256]{2,1,0:T(8,128)(2,1)} %get-tuple-element.26), channel_id=1, source_target_pairs={{0,1},{1,0},{2,3},{3,2},{4,5},{5,4},{6,7},{7,6},{8,9},{9,8},{10,11... | collective-permute-start | bytes 2359304 | tf_op jit(solution)/shard_map/ppermute | solution.py:650
  33.1 10.3 %copy-start = (bf16[12,128,256]{2,1,0:T(8,128)(2,1)}, bf16[12,128,256]{2,1,0:T(8,128)(2,1)S(1)}, u32[]{:S(2)}) copy-start(bf16[12,128,256]{2,1,0:T(8,128)(2,1)S(1)} %collective-permute-done.2.refs_3_.three_halo_ref) | copy-start | bytes 2359300
  33.1 10.2 %collective-permute-start.3 = (bf16[4,128,256]{2,1,0:T(8,128)(2,1)S(1)}, bf16[4,128,256]{2,1,0:T(8,128)(2,1)S(1)}, u32[]{:S(2)}, u32[]{:S(2)}) collective-permute-start(bf16[4,128,256]{2,1,0:T(8,128)(2,1)S(1)} %slice.4), channel_id=1, source_target_pairs={{1,0},{3,2},{5,4},{7,6},{9,8},{11,10},{13,12},{15,14},{17,16},{19,... | collective-permute-start | bytes 786440 | tf_op jit(solution)/shard_map/ppermute | solution.py:661
  37.3 14.0 %collective-permute-start.5 = (f32[128,256]{1,0:T(8,128)}, f32[128,256]{1,0:T(8,128)S(1)}, u32[]{:S(2)}, u32[]{:S(2)}) collective-permute-start(f32[128,256]{1,0:T(8,128)} %get-tuple-element.27), channel_id=1, source_target_pairs={{0,1},{2,3},{4,5},{6,7},{8,9},{10,11},{12,13},{14,15},{16,17},{18,... | collective-permute-start | bytes 393224 | tf_op jit(solution)/shard_map/ppermute | solution.py:663
  38.6 0.9 %copy-start.4 = (bf16[128,3456]{1,0:T(8,128)(2,1)}, bf16[128,3456]{1,0:T(8,128)(2,1)S(1)}, u32[]{:S(2)}) copy-start(bf16[128,3456]{1,0:T(8,128)(2,1)S(1)} %collective-permute-done.6.other_ref) | copy-start | bytes 2654212
  43.4 0.9 %copy-start.5 = (bf16[12,128,256]{2,1,0:T(8,128)(2,1)}, bf16[12,128,256]{2,1,0:T(8,128)(2,1)S(1)}, u32[]{:S(2)}) copy-start(bf16[12,128,256]{2,1,0:T(8,128)(2,1)S(1)} %collective-permute-done.4.refs_7_) | copy-start | bytes 2359300
  43.4 1.0 %copy-start.2 = (bf16[4,128,256]{2,1,0:T(8,128)(2,1)}, bf16[4,128,256]{2,1,0:T(8,128)(2,1)S(1)}, u32[]{:S(2)}) copy-start(bf16[4,128,256]{2,1,0:T(8,128)(2,1)S(1)} %collective-permute-done.3.refs_4_.rows_ref) | copy-start | bytes 786436
  50.0 16.7 %collective-permute-start.7 = (bf16[7,256,128]{2,1,0:T(8,128)(2,1)}, bf16[7,256,128]{2,1,0:T(8,128)(2,1)S(1)}, u32[]{:S(2)}, u32[]{:S(2)}) collective-permute-start(bf16[7,256,128]{2,1,0:T(8,128)(2,1)} %get-tuple-element.28), channel_id=1, source_target_pairs={{0,3},{2,5},{4,7},{6,9},{8,11},{10,13},{12,15},{16,19},{18,21},{20... | collective-permute-start | bytes 1376264 | tf_op jit(solution)/shard_map/ppermute | solution.py:646
  51.3 0.7 copy-start.9
  66.8 0.8 %copy-start.1 = (bf16[7,256,128]{2,1,0:T(8,128)(2,1)}, bf16[7,256,128]{2,1,0:T(8,128)(2,1)S(1)}, u32[]{:S(2)}) copy-start(bf16[7,256,128]{2,1,0:T(8,128)(2,1)S(1)} %collective-permute-done.7.halo_ref) | copy-start | bytes 1376260
  71.2 2.7 %collective-permute-start.8 = (f32[7,128,256]{2,1,0:T(8,128)}, f32[7,128,256]{2,1,0:T(8,128)S(1)}, u32[]{:S(2)}, u32[]{:S(2)}) collective-permute-start(f32[7,128,256]{2,1,0:T(8,128)} %get-tuple-element.32), channel_id=1, source_target_pairs={{0,1},{1,0},{2,3},{3,2},{4,5},{5,4},{6,7},{7,6},{8,9},{9,8},{10,11... | collective-permute-start | bytes 2752520 | tf_op jit(solution)/shard_map/ppermute | solution.py:650
  73.9 0.9 %copy-start.3 = (f32[7,128,256]{2,1,0:T(8,128)}, f32[7,128,256]{2,1,0:T(8,128)S(1)}, u32[]{:S(2)}) copy-start(f32[7,128,256]{2,1,0:T(8,128)S(1)} %collective-permute-done.8.got_ref) | copy-start | bytes 2752516

commit v5 on v4

--- a/solution.py
+++ b/solution.py
@@ -16,7 +16,7 @@
 TAPS = 27
 RIM_TAPS = tuple(9 * a + e for a in range(3) for e in range(3))
 GROUP = 16
-VMEM_LIMIT = 56 * 2**20
+MIB = 2**20
 
 
 def even_odd(width):
@@ -112,7 +112,7 @@
             pl.BlockSpec(memory_space=pltpu.VMEM),
         ],
         scratch_shapes=[pltpu.VMEM((columns, LANES), F32)] * 2,
-        compiler_params=pltpu.CompilerParams(vmem_limit_bytes=VMEM_LIMIT),
+        compiler_params=pltpu.CompilerParams(vmem_limit_bytes=16 * MIB),
         cost_estimate=pl.CostEstimate(flops=10**6, bytes_accessed=4 * 10**6, transcendentals=0),
         name="four_weights",
     )(core, own, other)
@@ -125,7 +125,7 @@
 ):
     *split_refs, turned_ref, pick_ref, data_ref, rims_ref, rim_w_ref = scratch
     core, step, last = core_ref[0], pl.program_id(0), pl.num_programs(0) - 1
-    chans, rows, width = last_ref.shape[1], last_ref.shape[3], last_ref.shape[4]
+    chans, rows, width = rim_ref.shape[1], last_ref.shape[3], last_ref.shape[4]
     block, planes = rim_ref.shape[2], rims_ref.shape[0]
     half = width // 2
     out_rows = rows // 2
@@ -186,14 +186,20 @@
         for index in range(planes // 2 + 2, message_ref.shape[0]):
             message_ref[index] = jnp.zeros_like(message_ref[index])
 
-    @pl.when((core == 1) & (step == 0))
-    def _():
+    @pl.when(core == 1)
+    def _():
+        part = last_ref.shape[1]
+
         def store(tap, row, first, value):
-            data_ref[row + 1, tap * chans + first : tap * chans + first + GROUP, :] = value
-
-        data_ref[0] = jnp.zeros_like(data_ref[0])
+            at = pl.multiple_of(tap * chans + step * part + first, GROUP)
+            data_ref[row + 1, pl.ds(at, GROUP), :] = value
+
         for _ in separate(last_ref, 0, place_ref, split_refs, store):
             pass
+
+    @pl.when((core == 1) & (step == last))
+    def _():
+        data_ref[0] = jnp.zeros_like(data_ref[0])
         for row in range(out_rows):
             total = jnp.dot(
                 w_ref[:, : 3 * taps],
@@ -222,7 +228,7 @@
             num_scalar_prefetch=1,
             grid=(steps,),
             in_specs=[
-                pl.BlockSpec((1, chans, 1, rows, width), lambda i, core: (0, 0, planes - 1, 0, 0)),
+                pl.BlockSpec((1, chans // steps, 1, rows, width), lambda i, core: (0, i * core[0], planes - 1, 0, 0)),
                 pl.BlockSpec(
                     (1, chans, block, 2 * SUB, width),
                     lambda i, core: (0, 0, i + core[0] * (steps - 1 - i), (rows - 1) // (2 * SUB), 0),
@@ -244,7 +250,7 @@
             ],
         ),
         out_shape=[jax.ShapeDtypeStruct(*shape) for shape in shapes],
-        compiler_params=pltpu.CompilerParams(vmem_limit_bytes=VMEM_LIMIT),
+        compiler_params=pltpu.CompilerParams(vmem_limit_bytes=36 * MIB),
         cost_estimate=pl.CostEstimate(flops=2 * 10**9, bytes_accessed=8 * 10**6, transcendentals=0),
         name="three_edges",
     )(core, volume, volume, own, other, own_scales, other_scales, even_odd(half))
@@ -252,7 +258,7 @@
 
 def three_kernel(
     core_ref, x_ref, before_ref, w_ref, place_ref, gain_ref, shift_ref,
-    third_ref, plane_ref, row_ref, last_row_ref, local_ref,
+    third_ref, plane_ref, row_ref, local_ref,
     *scratch,
 ):
     *split_refs, prior_ref, first_ref, second_ref, total_ref = scratch
@@ -335,7 +341,7 @@
     @pl.when((step == steps) & (core == 0))
     def _():
         local_ref[...] = third_ref[0]
-        last_row_ref[...] = total_ref[0]
+        local_ref[0] = total_ref[0].astype(BF16)
 
 
 def layer_three(volume, weights, gain, shift, core):
@@ -364,7 +370,6 @@
                 pl.BlockSpec((1, out_rows, outs, half), lambda i, core: (jnp.maximum(i - 1, 0), 0, 0, 0)),
                 full(out_rows, outs, half),
                 pl.BlockSpec((1, outs, half), lambda i, core: (jnp.maximum(i - 1, 0), 0, 0)),
-                full(outs, half),
                 full(out_rows, outs, half),
             ],
             scratch_shapes=[pltpu.VMEM((2, half // LANES, GROUP * rows, LANES), F32)] * 4
@@ -379,10 +384,9 @@
             jax.ShapeDtypeStruct((steps, out_rows, outs, half), BF16),
             jax.ShapeDtypeStruct((out_rows, outs, half), F32),
             jax.ShapeDtypeStruct((steps, outs, half), F32),
-            jax.ShapeDtypeStruct((outs, half), F32),
             jax.ShapeDtypeStruct((out_rows, outs, half), BF16),
         ],
-        compiler_params=pltpu.CompilerParams(vmem_limit_bytes=VMEM_LIMIT),
+        compiler_params=pltpu.CompilerParams(vmem_limit_bytes=46 * MIB),
         cost_estimate=pl.CostEstimate(flops=10**10, bytes_accessed=2 * 10**7, transcendentals=0),
         name="layer_three",
     )(core, volume, volume, weights, even_odd(half), gain, shift)
@@ -475,14 +479,14 @@
             jax.ShapeDtypeStruct((outs, 3 * chans), BF16),
         ],
         in_specs=inputs(len(thirds) + 3),
-        compiler_params=pltpu.CompilerParams(vmem_limit_bytes=VMEM_LIMIT),
+        compiler_params=pltpu.CompilerParams(vmem_limit_bytes=24 * MIB),
         cost_estimate=pl.CostEstimate(flops=2 * 10**9, bytes_accessed=8 * 10**6, transcendentals=0),
         name="four_edges",
     )(core, *thirds, local, weights, even_odd(width))
 
 
 def four_kernel(core_ref, *refs):
-    *thirds, local_ref, last_row_ref, w_ref, place_ref, sums_ref, data_ref = refs
+    *thirds, local_ref, w_ref, place_ref, sums_ref, corner_ref, data_ref = refs
     core = core_ref[0]
     planes, rows, chans, width = thirds[0].shape
     halo_ref, gain_ref, shift_ref = thirds[3], thirds[5], thirds[6]
@@ -491,6 +495,7 @@
     taps = 3 * chans
     batch = 4
     data_ref[:, 0] = jnp.zeros_like(data_ref[:, 0])
+    corner_ref[...] = corner_total(core, thirds)
 
     def put(values, first, spots):
         for tap, part in enumerate(spread((jnp.concatenate(values, 0),), place_ref[...])):
@@ -507,7 +512,7 @@
 
     @pl.when(core == 1)
     def _():
-        total = last_row_ref[...] + halo_ref[planes - 1].astype(F32)
+        total = local_ref[0].astype(F32) + halo_ref[planes - 1].astype(F32)
         prior = [activate(total, gain_ref[...], shift_ref[...]).astype(BF16)]
         prior += [local_ref[row] for row in range(1, rows)]
         for first in range(0, rows, batch):
@@ -524,35 +529,35 @@
         sums_ref[row] = jnp.dot(w_ref[...], jnp.concatenate(parts, 0), preferred_element_type=F32)
 
 
-def layer_four(core, thirds, local, last_row, weights):
+def layer_four(core, thirds, local, weights):
     planes, rows, chans, width = thirds[0].shape
     outs = weights.shape[0]
     half = width // 2
     out_rows, count = rows // 2, planes // 2
     return pl.pallas_call(
         four_kernel,
-        out_shape=jax.ShapeDtypeStruct((out_rows, outs, count * half), F32),
-        in_specs=inputs(len(thirds) + 4),
+        out_shape=[
+            jax.ShapeDtypeStruct((out_rows, outs, count * half), F32),
+            jax.ShapeDtypeStruct((chans, width), F32),
+        ],
+        in_specs=inputs(len(thirds) + 3),
         scratch_shapes=[pltpu.VMEM((3, rows + 1, 3 * chans, count * half), BF16)],
-        compiler_params=pltpu.CompilerParams(vmem_limit_bytes=VMEM_LIMIT),
+        compiler_params=pltpu.CompilerParams(vmem_limit_bytes=32 * MIB),
         cost_estimate=pl.CostEstimate(flops=8 * 10**9, bytes_accessed=10**7, transcendentals=0),
         name="layer_four",
-    )(core, *thirds, local, last_row, weights, even_odd(width))
+    )(core, *thirds, local, weights, even_odd(width))
 
 
 def theirs_kernel(
-    core_ref, sums_ref, halo_ref, mid_ref, place_ref,
-    third_ref, plane_ref, row_ref, three_halo_ref, rows_ref, gain_ref, shift_ref,
-    theirs_ref, fix_ref,
+    core_ref, sums_ref, corner_ref, halo_ref, mid_ref, place_ref, gain_ref, shift_ref, theirs_ref, fix_ref
 ):
     core = core_ref[0]
-    thirds = third_ref, plane_ref, row_ref, three_halo_ref, rows_ref, gain_ref, shift_ref
     rows, width = halo_ref.shape[0] - 1, halo_ref.shape[2]
 
     @pl.when(core == 0)
     def _():
         corner = halo_ref[rows].astype(F32)
-        total = corner_total(core, thirds) + jnp.concatenate([corner[:LANES], corner[LANES:]], 1)
+        total = corner_ref[...] + jnp.concatenate([corner[:LANES], corner[LANES:]], 1)
         value = activate(total, gain_ref[...], shift_ref[...]).astype(BF16)
         data = jnp.concatenate([part.astype(BF16) for part in spread((value,), place_ref[...])], 0)
         fix = jnp.dot(mid_ref[...], data, preferred_element_type=F32)
@@ -615,19 +620,19 @@
     out_ref[...] = lines_ref[...].astype(BF16)
 
 
-def last_stage(core, sums, halo, mid, thirds, scales):
+def last_stage(core, sums, corner, halo, mid, gain, shift, scales):
     rows, outs, lanes = sums.shape
-    params = pltpu.CompilerParams(vmem_limit_bytes=VMEM_LIMIT)
+    params = pltpu.CompilerParams(vmem_limit_bytes=16 * MIB)
     theirs, fix = pl.pallas_call(
         theirs_kernel,
         out_shape=[
             jax.ShapeDtypeStruct((rows + 1, outs // 2, lanes), F32),
             jax.ShapeDtypeStruct((outs // 2, halo.shape[2]), F32),
         ],
-        in_specs=inputs(4) + [pl.BlockSpec(memory_space=pl.ANY)] + inputs(6)[1:],
+        in_specs=inputs(7),
         compiler_params=params,
         name="theirs",
-    )(core, sums, halo, mid, even_odd(lanes), *thirds)
+    )(core, sums, corner, halo, mid, even_odd(lanes), gain, shift)
     lines = (outs // 2 * rows * lanes * 2 // LANES, LANES)
     return pl.pallas_call(
         assemble_kernel,
@@ -657,15 +662,15 @@
         volume, kernel_three, swapped(kernel_three), own_scales, swapped(own_scales), core
     )
     halo = handed_on(message)
-    *thirds, last_row, local = layer_three(volume, weights_three, gain, shift, core)
+    *thirds, local = layer_three(volume, weights_three, gain, shift, core)
     rows = lax.ppermute(halo[: thirds[0].shape[0]], "fl", [(1, 0)])
     thirds = (*thirds, halo, rows, gain, shift)
-    local, last_row = swapped(local), lax.ppermute(last_row, "fl", [(0, 1)])
+    local = swapped(local)
     weights_four = four_weights(kernel_four, swapped(kernel_four), core)
     message, mid = four_edges(core, thirds, local, weights_four)
     halo = handed_on(message)
-    sums = layer_four(core, thirds, local, last_row, weights_four)
-    lines = last_stage(core, sums, halo, mid, thirds, scales)
+    sums, corner = layer_four(core, thirds, local, weights_four)
+    lines = last_stage(core, sums, corner, halo, mid, gain, shift, scales)
     out_rows, outs, lanes = sums.shape
     fourth = lines.reshape(outs // 2, out_rows, 2 * lanes // LANES, LANES)
     return jnp.transpose(fourth, (0, 2, 1, 3))[None]

time: 78.4 us -> 60 us (0.77)
  Pallas kernels: 50.7 us -> 32.2 us
  waiting for transfers between devices: 8.68 us -> 13.7 us
  local copies, waits for them, and re-layouts: 5.09 us -> 1.87 us
  starting transfers between devices: 12.7 us -> 11 us
    ppermute x2, waiting for transfers between devices: 5.34 us -> 10.6 us  [handed_on(): return lax.ppermute(message, ('sp', 'fl'), pairs)]
    pallas_call x1, Pallas kernels: 9.4 us -> 4.83 us  [layer_four(): pl.pallas_call(four_kernel, out_shape=[jax.ShapeDtypeStruct((out_rows, ou...]
    pallas_call x1, Pallas kernels: 5.62 us -> 1.19 us  [four_edges(): pl.pallas_call(four_edges_kernel, out_shape=[jax.ShapeDtypeStruct((rows /...]
    pallas_call x1, Pallas kernels: 3.62 us -> 0.07 us  [last_stage(): pl.pallas_call(theirs_kernel, out_shape=[jax.ShapeDtypeStruct((rows + 1,...]
    unnamed x20 -> x8, local copies, waits for them, and re-layouts: 5.07 us -> 1.85 us
    pallas_call x1, Pallas kernels: 3.84 us -> 1.22 us  [four_weights(): pl.pallas_call(four_weights_kernel, out_shape=jax.ShapeDtypeStruct((2 * o...]
    pallas_call x1, Pallas kernels: 3.23 us -> 1.39 us  [last_stage(): pl.pallas_call(assemble_kernel, out_shape=jax.ShapeDtypeStruct(lines, BF1...]
    pallas_call x1, Pallas kernels: 19.3 us -> 17.9 us  [layer_three(): pl.pallas_call(three_kernel, grid_spec=pltpu.PrefetchScalarGridSpec(num_s...]
  transfers between devices with their start and end apart: 9 -> 8, of which waited for: 3 -> 4; matrix products, arithmetic and copies ran while one was open for 1% -> 1% of each run, Pallas kernels for 56% -> 49%
where the time goes in v5:
time: 60 us; the launch traced here: 59.7 us
  Pallas kernels  32.2 us (54%)
  waiting for transfers between devices  13.7 us (23%)
  starting transfers between devices  11 us (18%)
  local copies, waits for them, and re-layouts  1.87 us (3%)
  other arithmetic  0.78 us (1%)
    pallas_call x1, Pallas kernels, layer_three(): pl.pallas_call(three_kernel, grid_spec=pltpu.PrefetchScalarGridSpec(num_s...  17.9 us
    ppermute x2, waiting for transfers between devices, handed_on(): return lax.ppermute(message, ('sp', 'fl'), pairs)  10.6 us
    pallas_call x1, Pallas kernels, three_edges(): pl.pallas_call(three_edges_kernel, grid_spec=pltpu.PrefetchScalarGridSpec...  5.61 us
    ppermute x1, starting transfers between devices, shards(): rows = lax.ppermute(halo[:thirds[0].shape[0]], 'fl', [(1, 0)])  5.08 us
    pallas_call x1, Pallas kernels, layer_four(): pl.pallas_call(four_kernel, out_shape=[jax.ShapeDtypeStruct((out_rows, ou...  4.83 us
    ppermute x5, starting transfers between devices, swapped(): return lax.ppermute(value, 'fl', [(0, 1), (1, 0)])  3.18 us
    ppermute x5, waiting for transfers between devices, swapped(): return lax.ppermute(value, 'fl', [(0, 1), (1, 0)])  3.11 us
    ppermute x2, starting transfers between devices, handed_on(): return lax.ppermute(message, ('sp', 'fl'), pairs)  2.76 us
  transfers between devices with their start and end apart: 8, of which 4 were waited for; matrix products, arithmetic and copies ran while one was open for 1% of the time, Pallas kernels for 49%

profile of v5, /device:TPU:25, one launch (start us, length us, event | category | flops | bytes accessed | tf_op | source)
XLA Modules:
  0.0 59.7 jit_solution(16336812371610605666)
XLA Ops:
  0.0 0.7 %collective-permute-start = (bf16[64,1728]{1,0:T(8,128)(2,1)}, bf16[64,1728]{1,0:T(8,128)(2,1)S(1)}, u32[]{:S(2)}, u32[]{:S(2)}) collective-permute-start(bf16[64,1728]{1,0:T(8,128)(2,1)} %own_ref.2), channel_id=1, source_target_pairs={{0,1},{1,0},{2,3},{3,2},{4,5},{5,4},{6,7},{7,6},{8,9},{9,8},{10,11... | collective-permute-start | bytes 663560 | tf_op jit(solution)/shard_map/ppermute | solution.py:655
  0.7 0.8 %maximum_bitcast_fusion.own_scales_ref = f32[3,128]{1,0:T(4,128)S(1)} fusion(f32[128]{0:T(128)} %param.18, f32[128]{0:T(128)} %param.17, f32[64]{0:T(128)} %param.15, f32[64]{0:T(128)} %param.14), kind=kLoop, calls=%fused_computation | loop fusion | flops 1152 | bytes 3072 | tf_op jit(solution)/shard_map/reshape | solution.py:660
  1.5 0.0 collective-permute-start.1
  1.5 0.5 collective-permute-start.5
  2.0 0.6 %collective-permute-done.1.other_scales_ref = f32[3,128]{1,0:T(4,128)S(1)} collective-permute-done((f32[3,128]{1,0:T(4,128)S(1)}, f32[3,128]{1,0:T(4,128)S(1)}, u32[]{:S(2)}, u32[]{:S(2)}) %collective-permute-start.1) | collective-permute-done | bytes 1568 | tf_op jit(solution)/shard_map/ppermute | solution.py:655
  2.6 0.0 collective-permute-done.other_ref
  2.6 0.0 copy-start
  2.6 0.9 %copy-done = bf16[256,256]{1,0:T(8,128)(2,1)S(1)} copy-done((bf16[256,256]{1,0:T(8,128)(2,1)S(1)}, bf16[256,256]{1,0:T(8,128)(2,1)}, u32[]{:S(2)}) %copy-start) | copy-done | bytes 131096
  3.5 0.0 copy-start.3
  3.5 0.9 %copy-done.3 = bf16[64,1728]{1,0:T(8,128)(2,1)S(1)} copy-done((bf16[64,1728]{1,0:T(8,128)(2,1)S(1)}, bf16[64,1728]{1,0:T(8,128)(2,1)}, u32[]{:S(2)}) %copy-start.3) | copy-done | bytes 221208
  4.5 0.0 copy-start.1
  4.5 5.6 %three_edges.1 = (bf16[12,128,256]{2,1,0:T(8,128)(2,1)S(1)}, bf16[128,1728]{1,0:T(8,128)(2,1)S(1)}, f32[128,1]{1,0:T(8,128)S(1)}, f32[128,1]{1,0:T(8,128)S(1)}, f32[128,128]{1,0:T(8,128)S(1)}) custom-call(s32[1]{0:T(128)} %bitcast.core_ref, bf16[1,64,16,24,512]{4,3,2,1,0:T(8,128)(2,1)} %before_ref.1, bf16[1,64,16,24,512]{4,3,2,1,0:T(8,128)(2,1)} %before_ref.1, ...), custom_call_target="tpu_custom_call" | custom-call | flops 2000000000 | bytes 8000000 | tf_op jit(solution)/shard_map/three_edges/pallas_call | solution.py:225
  10.1 1.5 %collective-permute-start.2 = (bf16[12,128,256]{2,1,0:T(8,128)(2,1)S(1)}, bf16[12,128,256]{2,1,0:T(8,128)(2,1)S(1)}, u32[]{:S(2)}, u32[]{:S(2)}) collective-permute-start(bf16[12,128,256]{2,1,0:T(8,128)(2,1)S(1)} %get-tuple-element.26), channel_id=1, source_target_pairs={{0,3},{2,5},{4,7},{6,9},{8,11},{10,13},{12,15},{16,19},{18,21},{20... | collective-permute-start | bytes 2359304 | tf_op jit(solution)/shard_map/ppermute | solution.py:651
  11.6 0.0 copy-done.1
  11.6 0.0 copy-start.2
  11.6 17.9 %layer_three.1 = (bf16[4,12,128,256]{3,2,1,0:T(8,128)(2,1)S(1)}, f32[12,128,256]{2,1,0:T(8,128)S(1)}, f32[4,128,256]{2,1,0:T(8,128)S(1)}, bf16[12,128,256]{2,1,0:T(8,128)(2,1)S(1)}) custom-call(s32[1]{0:T(128)} %bitcast.core_ref, bf16[1,64,16,24,512]{4,3,2,1,0:T(8,128)(2,1)} %before_ref.1, bf16[1,64,16,24,512]{4,3,2,1,0:T(8,128)(2,1)} %before_ref.1, ...), custom_call_target="tpu_custom_call" | custom-call | flops 10000000000 | bytes 20000000 | tf_op jit(solution)/shard_map/layer_three/pallas_call | solution.py:353
  29.5 1.9 %collective-permute-start.4 = (bf16[12,128,256]{2,1,0:T(8,128)(2,1)S(1)}, bf16[12,128,256]{2,1,0:T(8,128)(2,1)S(1)}, u32[]{:S(2)}, u32[]{:S(2)}) collective-permute-start(bf16[12,128,256]{2,1,0:T(8,128)(2,1)S(1)} %get-tuple-element.27), channel_id=1, source_target_pairs={{0,1},{1,0},{2,3},{3,2},{4,5},{5,4},{6,7},{7,6},{8,9},{9,8},{10,11... | collective-permute-start | bytes 2359304 | tf_op jit(solution)/shard_map/ppermute | solution.py:655
  31.4 0.2 collective-permute-done.2.refs_3_
  31.7 5.1 %collective-permute-start.3 = (bf16[4,128,256]{2,1,0:T(8,128)(2,1)S(1)}, bf16[4,128,256]{2,1,0:T(8,128)(2,1)S(1)}, u32[]{:S(2)}, u32[]{:S(2)}) collective-permute-start(bf16[4,128,256]{2,1,0:T(8,128)(2,1)S(1)} %slice.4), channel_id=1, source_target_pairs={{1,0},{3,2},{5,4},{7,6},{9,8},{11,10},{13,12},{15,14},{17,16},{19,... | collective-permute-start | bytes 786440 | tf_op jit(solution)/shard_map/ppermute | solution.py:666
  36.7 0.0 collective-permute-done.5.other_ref
  36.8 0.0 copy-done.2
  36.8 1.2 %four_weights.1.refs_8_ = bf16[256,3456]{1,0:T(8,128)(2,1)S(1)} custom-call(s32[1]{0:T(128)} %bitcast.core_ref, bf16[128,3456]{1,0:T(8,128)(2,1)S(1)} %copy-done.2, bf16[128,3456]{1,0:T(8,128)(2,1)S(1)} %collective-permute-done.5.other_ref), custom_call_target="tpu_custom_call" | custom-call | flops 1000000 | bytes 4000000 | tf_op jit(solution)/shard_map/four_weights/pallas_call | solution.py:106
  38.0 0.0 collective-permute-done.4.refs_7_
  38.0 0.0 collective-permute-done.3.refs_4_
  38.0 1.2 %four_edges.1 = (bf16[7,256,128]{2,1,0:T(8,128)(2,1)S(1)}, bf16[256,384]{1,0:T(8,128)(2,1)S(1)}) custom-call(s32[1]{0:T(128)} %bitcast.core_ref, bf16[4,12,128,256]{3,2,1,0:T(8,128)(2,1)S(1)} %get-tuple-element.23.refs_0_, f32[12,128,256]{2,1,0:T(8,128)S(1)} %get-tuple-element.24.refs_1_, f32[4,128,256]{2,1,0:T(8,128)S(1)} %get-tuple-element.25.refs_2_, ...), custom_call_target="tpu_custom_call" | custom-call | flops 2000000000 | bytes 8000000 | tf_op jit(solution)/shard_map/four_edges/pallas_call | solution.py:475
  39.2 1.3 %collective-permute-start.6 = (bf16[7,256,128]{2,1,0:T(8,128)(2,1)S(1)}, bf16[7,256,128]{2,1,0:T(8,128)(2,1)S(1)}, u32[]{:S(2)}, u32[]{:S(2)}) collective-permute-start(bf16[7,256,128]{2,1,0:T(8,128)(2,1)S(1)} %get-tuple-element.29), channel_id=1, source_target_pairs={{0,3},{2,5},{4,7},{6,9},{8,11},{10,13},{12,15},{16,19},{18,21},{20... | collective-permute-start | bytes 1376264 | tf_op jit(solution)/shard_map/ppermute | solution.py:651
  40.5 4.8 %layer_four.1 = (f32[6,256,256]{2,1,0:T(8,128)S(1)}, f32[128,256]{1,0:T(8,128)S(1)}) custom-call(s32[1]{0:T(128)} %bitcast.core_ref, bf16[4,12,128,256]{3,2,1,0:T(8,128)(2,1)S(1)} %get-tuple-element.23.refs_0_, f32[12,128,256]{2,1,0:T(8,128)S(1)} %get-tuple-element.24.refs_1_, f32[4,128,256]{2,1,0:T(8,128)S(1)} %get-tuple-element.25.refs_2_, ...), custom_call_target="tpu_custom_call" | custom-call | flops 8000000000 | bytes 10000000 | tf_op jit(solution)/shard_map/layer_four/pallas_call | solution.py:537
  45.3 10.4 %collective-permute-done.6.halo_ref = bf16[7,256,128]{2,1,0:T(8,128)(2,1)S(1)} collective-permute-done((bf16[7,256,128]{2,1,0:T(8,128)(2,1)S(1)}, bf16[7,256,128]{2,1,0:T(8,128)(2,1)S(1)}, u32[]{:S(2)}, u32[]{:S(2)}) %collective-permute-start.6) | collective-permute-done | bytes 458784 | tf_op jit(solution)/shard_map/ppermute | solution.py:651
  55.7 0.1 theirs.1
  55.8 0.1 collective-permute-start.7
  55.9 2.5 %collective-permute-done.7.got_ref = f32[7,128,256]{2,1,0:T(8,128)S(1)} collective-permute-done((f32[7,128,256]{2,1,0:T(8,128)S(1)}, f32[7,128,256]{2,1,0:T(8,128)S(1)}, u32[]{:S(2)}, u32[]{:S(2)}) %collective-permute-start.7) | collective-permute-done | bytes 917536 | tf_op jit(solution)/shard_map/ppermute | solution.py:655
  58.3 1.4 %assemble.1 = bf16[3072,128]{1,0:T(8,128)(2,1)} custom-call(s32[1]{0:T(128)} %bitcast.core_ref, f32[6,256,256]{2,1,0:T(8,128)S(1)} %get-tuple-element.28.sums_ref, bf16[7,256,128]{2,1,0:T(8,128)(2,1)S(1)} %collective-permute-done.6.halo_ref, f32[128,128]{1,0:T(8,128)S(1)} %get-tuple-element.32.fix_ref, f32[128,128]{1,0:T(8,128)S(1)} %get-tuple-element.33.scales_ref, ...), custom_call_target="tpu_custom_call" | custom-call | tf_op jit(solution)/shard_map/assemble/pallas_call | solution.py:637
  (1 shorter events, 0.0 us)
Async XLA Ops:
  0.0 2.6 %collective-permute-start = (bf16[64,1728]{1,0:T(8,128)(2,1)}, bf16[64,1728]{1,0:T(8,128)(2,1)S(1)}, u32[]{:S(2)}, u32[]{:S(2)}) collective-permute-start(bf16[64,1728]{1,0:T(8,128)(2,1)} %own_ref.2), channel_id=1, source_target_pairs={{0,1},{1,0},{2,3},{3,2},{4,5},{5,4},{6,7},{7,6},{8,9},{9,8},{10,11... | collective-permute-start | bytes 663560 | tf_op jit(solution)/shard_map/ppermute | solution.py:655
  1.5 1.2 %collective-permute-start.1 = (f32[3,128]{1,0:T(4,128)S(1)}, f32[3,128]{1,0:T(4,128)S(1)}, u32[]{:S(2)}, u32[]{:S(2)}) collective-permute-start(f32[3,128]{1,0:T(4,128)S(1)} %maximum_bitcast_fusion.own_scales_ref), channel_id=1, source_target_pairs={{0,1},{1,0},{2,3},{3,2},{4,5},{5,4},{6,7},{7,6},{8,9},{9,8},{10,11... | collective-permute-start | bytes 4616 | tf_op jit(solution)/shard_map/ppermute | solution.py:655
  1.5 35.3 %collective-permute-start.5 = (bf16[128,3456]{1,0:T(8,128)(2,1)}, bf16[128,3456]{1,0:T(8,128)(2,1)S(1)}, u32[]{:S(2)}, u32[]{:S(2)}) collective-permute-start(bf16[128,3456]{1,0:T(8,128)(2,1)} %own_ref.3), channel_id=1, source_target_pairs={{0,1},{1,0},{2,3},{3,2},{4,5},{5,4},{6,7},{7,6},{8,9},{9,8},{10,11... | collective-permute-start | bytes 2654216 | tf_op jit(solution)/shard_map/ppermute | solution.py:655
  2.6 0.9 %copy-start = (bf16[256,256]{1,0:T(8,128)(2,1)S(1)}, bf16[256,256]{1,0:T(8,128)(2,1)}, u32[]{:S(2)}) copy-start(bf16[256,256]{1,0:T(8,128)(2,1)} %constant.6.clone.place_ref.refs_9_) | copy-start | bytes 393220
  3.5 0.9 %copy-start.3 = (bf16[64,1728]{1,0:T(8,128)(2,1)S(1)}, bf16[64,1728]{1,0:T(8,128)(2,1)}, u32[]{:S(2)}) copy-start(bf16[64,1728]{1,0:T(8,128)(2,1)} %own_ref.2) | copy-start | bytes 663556
  4.5 7.1 %copy-start.1 = (bf16[256,256]{1,0:T(8,128)(2,1)S(1)}, bf16[256,256]{1,0:T(8,128)(2,1)}, u32[]{:S(2)}) copy-start(bf16[256,256]{1,0:T(8,128)(2,1)} %constant.6.clone.place_ref.refs_9_) | copy-start | bytes 393220
  10.1 21.5 %collective-permute-start.2 = (bf16[12,128,256]{2,1,0:T(8,128)(2,1)S(1)}, bf16[12,128,256]{2,1,0:T(8,128)(2,1)S(1)}, u32[]{:S(2)}, u32[]{:S(2)}) collective-permute-start(bf16[12,128,256]{2,1,0:T(8,128)(2,1)S(1)} %get-tuple-element.26), channel_id=1, source_target_pairs={{0,3},{2,5},{4,7},{6,9},{8,11},{10,13},{12,15},{16,19},{18,21},{20... | collective-permute-start | bytes 2359304 | tf_op jit(solution)/shard_map/ppermute | solution.py:651
  11.6 25.2 %copy-start.2 = (bf16[128,3456]{1,0:T(8,128)(2,1)S(1)}, bf16[128,3456]{1,0:T(8,128)(2,1)}, u32[]{:S(2)}) copy-start(bf16[128,3456]{1,0:T(8,128)(2,1)} %own_ref.3) | copy-start | bytes 2654212
  29.5 8.5 %collective-permute-start.4 = (bf16[12,128,256]{2,1,0:T(8,128)(2,1)S(1)}, bf16[12,128,256]{2,1,0:T(8,128)(2,1)S(1)}, u32[]{:S(2)}, u32[]{:S(2)}) collective-permute-start(bf16[12,128,256]{2,1,0:T(8,128)(2,1)S(1)} %get-tuple-element.27), channel_id=1, source_target_pairs={{0,1},{1,0},{2,3},{3,2},{4,5},{5,4},{6,7},{7,6},{8,9},{9,8},{10,11... | collective-permute-start | bytes 2359304 | tf_op jit(solution)/shard_map/ppermute | solution.py:655
  31.7 6.4 %collective-permute-start.3 = (bf16[4,128,256]{2,1,0:T(8,128)(2,1)S(1)}, bf16[4,128,256]{2,1,0:T(8,128)(2,1)S(1)}, u32[]{:S(2)}, u32[]{:S(2)}) collective-permute-start(bf16[4,128,256]{2,1,0:T(8,128)(2,1)S(1)} %slice.4), channel_id=1, source_target_pairs={{1,0},{3,2},{5,4},{7,6},{9,8},{11,10},{13,12},{15,14},{17,16},{19,... | collective-permute-start | bytes 786440 | tf_op jit(solution)/shard_map/ppermute | solution.py:666
  39.2 16.5 %collective-permute-start.6 = (bf16[7,256,128]{2,1,0:T(8,128)(2,1)S(1)}, bf16[7,256,128]{2,1,0:T(8,128)(2,1)S(1)}, u32[]{:S(2)}, u32[]{:S(2)}) collective-permute-start(bf16[7,256,128]{2,1,0:T(8,128)(2,1)S(1)} %get-tuple-element.29), channel_id=1, source_target_pairs={{0,3},{2,5},{4,7},{6,9},{8,11},{10,13},{12,15},{16,19},{18,21},{20... | collective-permute-start | bytes 1376264 | tf_op jit(solution)/shard_map/ppermute | solution.py:651
  55.8 2.5 %collective-permute-start.7 = (f32[7,128,256]{2,1,0:T(8,128)S(1)}, f32[7,128,256]{2,1,0:T(8,128)S(1)}, u32[]{:S(2)}, u32[]{:S(2)}) collective-permute-start(f32[7,128,256]{2,1,0:T(8,128)S(1)} %get-tuple-element.34), channel_id=1, source_target_pairs={{0,1},{1,0},{2,3},{3,2},{4,5},{5,4},{6,7},{7,6},{8,9},{9,8},{10,11... | collective-permute-start | bytes 2752520 | tf_op jit(solution)/shard_map/ppermute | solution.py:655

commit v6 on v5

--- a/solution.py
+++ b/solution.py
@@ -71,6 +71,10 @@
         yield
 
 
+def inputs(count):
+    return [pl.BlockSpec(memory_space=pltpu.SMEM)] + [pl.BlockSpec(memory_space=pltpu.VMEM)] * count
+
+
 def whole(own, other, core):
     first = jnp.where(core == 0, own, other)
     second = jnp.where(core == 0, other, own)
@@ -118,34 +122,14 @@
     )(core, own, other)
 
 
-def three_edges_kernel(
-    core_ref, last_ref, rim_ref, own_ref, other_ref, own_scales_ref, other_scales_ref, place_ref,
-    message_ref, w_ref, gain_ref, shift_ref, scales_ref,
-    *scratch,
-):
-    *split_refs, turned_ref, pick_ref, data_ref, rims_ref, rim_w_ref = scratch
+def three_picks_kernel(core_ref, last_ref, before_ref, rim_ref, place_ref, picked_ref, prior_ref, *scratch):
+    *split_refs, pick_ref = scratch
     core, step, last = core_ref[0], pl.program_id(0), pl.num_programs(0) - 1
-    chans, rows, width = rim_ref.shape[1], last_ref.shape[3], last_ref.shape[4]
-    block, planes = rim_ref.shape[2], rims_ref.shape[0]
-    half = width // 2
-    out_rows = rows // 2
-    taps = 3 * chans
+    chans, block, width = rim_ref.shape[1], rim_ref.shape[2], rim_ref.shape[4]
+    rows, part = last_ref.shape[3], last_ref.shape[1]
+    planes = block * 4
+    half = width // 2
     rim = (rows - 1) % SUB
-
-    @pl.when(step == 0)
-    def _():
-        turn(whole(own_ref[...].astype(F32), other_ref[...].astype(F32), core), turned_ref)
-        tap_major(turned_ref, range(TAPS), w_ref, 0)
-        tap_major(turned_ref, RIM_TAPS, rim_w_ref, 0)
-        own_scales, other_scales = own_scales_ref[...], other_scales_ref[...]
-        lines = own_scales.shape[0]
-        scales = jnp.concatenate(
-            [own_scales, other_scales, jnp.zeros((LANES - 2 * lines, LANES), F32)], 0
-        ).T
-        scales_ref[...] = scales
-        share = own_ref.shape[0]
-        for ref, at in ((gain_ref, 0), (shift_ref, share)):
-            ref[...] = whole(scales[at : at + share, 0:1], scales[at : at + share, lines : lines + 1], core)
 
     def picked(spots):
         values, held = [], None
@@ -169,52 +153,114 @@
     @pl.when(core == 0)
     def _():
         for plane, data in enumerate(picked([(plane, rim) for plane in range(block)])):
-            rims_ref[step * block + plane] = data
+            picked_ref[step * block + plane] = data
 
     @pl.when((core == 0) & (step == last))
     def _():
+        spots = [(plane, row) for plane in range(block - 3, block) for row in range(rim - 2, rim + 1)]
+        for index, data in enumerate(picked(spots)):
+            picked_ref[planes + index] = data
+        prior_ref[...] = jnp.zeros_like(prior_ref)
+
+    @pl.when(core == 1)
+    def _():
+        for source_ref, to_ref in ((last_ref, picked_ref), (before_ref, prior_ref)):
+
+            def store(tap, row, first, value):
+                at = pl.multiple_of(tap * chans + step * part + first, GROUP)
+                to_ref[row + 1, pl.ds(at, GROUP), :] = value
+
+            for _ in separate(source_ref, 0, place_ref, split_refs, store):
+                pass
+
+    @pl.when((core == 1) & (step == last))
+    def _():
+        for ref in (picked_ref, prior_ref):
+            ref[0] = jnp.zeros_like(ref[0])
+
+
+def three_picks(volume, core):
+    _, chans, planes, rows, width = volume.shape
+    half = width // 2
+    block, steps = planes // 4, 4
+    shape = (rows + 1, 3 * chans, half)
+    full = lambda *shape: pl.BlockSpec(shape, lambda i, core: (0,) * len(shape))
+    return pl.pallas_call(
+        three_picks_kernel,
+        grid_spec=pltpu.PrefetchScalarGridSpec(
+            num_scalar_prefetch=1,
+            grid=(steps,),
+            in_specs=[
+                pl.BlockSpec((1, chans // steps, 1, rows, width), lambda i, core: (0, i * core[0], planes - 1, 0, 0)),
+                pl.BlockSpec(
+                    (1, chans // steps, 1, rows, width), lambda i, core: (0, i * core[0], planes // 2 - 1, 0, 0)
+                ),
+                pl.BlockSpec(
+                    (1, chans, block, 2 * SUB, width),
+                    lambda i, core: (0, 0, i + core[0] * (steps - 1 - i), (rows - 1) // (2 * SUB), 0),
+                ),
+                full(half, half),
+            ],
+            out_specs=[full(*shape), full(*shape)],
+            scratch_shapes=[pltpu.VMEM((2, half // LANES, GROUP * rows, LANES), F32)] * 2
+            + [pltpu.VMEM((2, width // LANES, chans * SUB, LANES), F32)],
+        ),
+        out_shape=[jax.ShapeDtypeStruct(shape, BF16)] * 2,
+        compiler_params=pltpu.CompilerParams(vmem_limit_bytes=36 * MIB),
+        cost_estimate=pl.CostEstimate(flops=10**9, bytes_accessed=10**7, transcendentals=0),
+        name="three_picks",
+    )(core, volume, volume, volume, even_odd(half))
+
+
+def three_edges_kernel(
+    core_ref, picked_ref, own_ref, other_ref, own_scales_ref, other_scales_ref,
+    message_ref, w_ref, gain_ref, shift_ref, scales_ref,
+    turned_ref, rim_w_ref,
+):
+    core = core_ref[0]
+    count, taps, half = picked_ref.shape
+    out_rows = message_ref.shape[0]
+    planes = count - 9
+    turn(whole(own_ref[...].astype(F32), other_ref[...].astype(F32), core), turned_ref)
+    tap_major(turned_ref, range(TAPS), w_ref, 0)
+    own_scales, other_scales = own_scales_ref[...], other_scales_ref[...]
+    lines = own_scales.shape[0]
+    scales = jnp.concatenate([own_scales, other_scales, jnp.zeros((LANES - 2 * lines, LANES), F32)], 0).T
+    scales_ref[...] = scales
+    share = own_ref.shape[0]
+    for ref, at in ((gain_ref, 0), (shift_ref, share)):
+        ref[...] = whole(scales[at : at + share, 0:1], scales[at : at + share, lines : lines + 1], core)
+
+    @pl.when(core == 0)
+    def _():
+        tap_major(turned_ref, RIM_TAPS, rim_w_ref, 0)
         none = jnp.zeros((taps, half), BF16)
         for index in range(planes // 2 + 1):
             pieces = [
-                rims_ref[plane] if 0 <= plane < planes else none for plane in range(2 * index - 1, 2 * index + 2)
+                picked_ref[plane] if 0 <= plane < planes else none for plane in range(2 * index - 1, 2 * index + 2)
             ]
             total = jnp.dot(rim_w_ref[...], jnp.concatenate(pieces, 0), preferred_element_type=F32)
             message_ref[index] = total.astype(BF16)
-        spots = [(plane, row) for plane in range(block - 3, block) for row in range(rim - 2, rim + 1)]
-        total = jnp.dot(w_ref[...], jnp.concatenate(picked(spots), 0), preferred_element_type=F32)
+        data = picked_ref[planes:].reshape(9 * taps, half)
+        total = jnp.dot(w_ref[...], data, preferred_element_type=F32)
         message_ref[planes // 2 + 1] = activate(total, gain_ref[...], shift_ref[...]).astype(BF16)
-        for index in range(planes // 2 + 2, message_ref.shape[0]):
+        for index in range(planes // 2 + 2, out_rows):
             message_ref[index] = jnp.zeros_like(message_ref[index])
 
     @pl.when(core == 1)
     def _():
-        part = last_ref.shape[1]
-
-        def store(tap, row, first, value):
-            at = pl.multiple_of(tap * chans + step * part + first, GROUP)
-            data_ref[row + 1, pl.ds(at, GROUP), :] = value
-
-        for _ in separate(last_ref, 0, place_ref, split_refs, store):
-            pass
-
-    @pl.when((core == 1) & (step == last))
-    def _():
-        data_ref[0] = jnp.zeros_like(data_ref[0])
         for row in range(out_rows):
             total = jnp.dot(
                 w_ref[:, : 3 * taps],
-                data_ref[2 * row : 2 * row + 3].reshape(3 * taps, half),
+                picked_ref[2 * row : 2 * row + 3].reshape(3 * taps, half),
                 preferred_element_type=F32,
             )
             message_ref[row] = total.astype(BF16)
 
 
-def three_edges(volume, own, other, own_scales, other_scales, core):
-    _, chans, planes, rows, width = volume.shape
+def three_edges(picked, own, other, own_scales, other_scales, core):
     outs, columns = 2 * own.shape[0], own.shape[1]
-    half = width // 2
-    block, steps, out_rows = 4, planes // 4, rows // 2
-    full = lambda *shape: pl.BlockSpec(shape, lambda i, core: (0,) * len(shape))
+    out_rows, half = picked.shape[0] // 2, picked.shape[2]
     shapes = [
         ((out_rows, outs, half), BF16),
         ((outs, columns), BF16),
@@ -224,36 +270,13 @@
     ]
     return pl.pallas_call(
         three_edges_kernel,
-        grid_spec=pltpu.PrefetchScalarGridSpec(
-            num_scalar_prefetch=1,
-            grid=(steps,),
-            in_specs=[
-                pl.BlockSpec((1, chans // steps, 1, rows, width), lambda i, core: (0, i * core[0], planes - 1, 0, 0)),
-                pl.BlockSpec(
-                    (1, chans, block, 2 * SUB, width),
-                    lambda i, core: (0, 0, i + core[0] * (steps - 1 - i), (rows - 1) // (2 * SUB), 0),
-                ),
-                full(*own.shape),
-                full(*other.shape),
-                full(*own_scales.shape),
-                full(*other_scales.shape),
-                full(half, half),
-            ],
-            out_specs=[full(*shape) for shape, _ in shapes],
-            scratch_shapes=[pltpu.VMEM((2, half // LANES, GROUP * rows, LANES), F32)] * 4
-            + [
-                pltpu.VMEM((columns, LANES), F32),
-                pltpu.VMEM((2, width // LANES, chans * SUB, LANES), F32),
-                pltpu.VMEM((rows + 1, 3 * chans, half), BF16),
-                pltpu.VMEM((planes, 3 * chans, half), BF16),
-                pltpu.VMEM((outs, columns // 3), BF16),
-            ],
-        ),
+        in_specs=inputs(5),
         out_shape=[jax.ShapeDtypeStruct(*shape) for shape in shapes],
-        compiler_params=pltpu.CompilerParams(vmem_limit_bytes=36 * MIB),
-        cost_estimate=pl.CostEstimate(flops=2 * 10**9, bytes_accessed=8 * 10**6, transcendentals=0),
+        scratch_shapes=[pltpu.VMEM((columns, LANES), F32), pltpu.VMEM((outs, columns // 3), BF16)],
+        compiler_params=pltpu.CompilerParams(vmem_limit_bytes=16 * MIB),
+        cost_estimate=pl.CostEstimate(flops=10**9, bytes_accessed=10**6, transcendentals=0),
         name="three_edges",
-    )(core, volume, volume, own, other, own_scales, other_scales, even_odd(half))
+    )(core, picked, own, other, own_scales, other_scales)
 
 
 def three_kernel(
@@ -293,16 +316,7 @@
 
     @pl.when(step == 0)
     def _():
-        prior_ref[...] = jnp.zeros_like(prior_ref)
-
-        @pl.when(core == 1)
-        def _():
-            def store(tap, row, first, value):
-                prior_ref[row + 1, tap * chans + first : tap * chans + first + GROUP, :] = value
-
-            for _ in separate(before_ref, 0, place_ref, split_refs, store):
-                pass
-
+        prior_ref[...] = before_ref[...]
         for ref in (first_ref, second_ref):
             ref[:, 0] = jnp.zeros_like(ref[:, 0])
         for _ in splitting(first_ref):
@@ -344,7 +358,7 @@
         local_ref[0] = total_ref[0].astype(BF16)
 
 
-def layer_three(volume, weights, gain, shift, core):
+def layer_three(volume, prior, weights, gain, shift, core):
     _, chans, planes, rows, width = volume.shape
     outs = weights.shape[0]
     half = width // 2
@@ -357,10 +371,7 @@
             grid=(steps + 1,),
             in_specs=[
                 pl.BlockSpec((1, chans, 2, rows, width), lambda i, core: (0, 0, core[0] * steps + jnp.minimum(i, steps - 1), 0, 0)),
-                pl.BlockSpec(
-                    (1, chans, 1, rows, width),
-                    lambda i, core: (0, 0, jnp.maximum(core[0] * 2 * steps - 1, 0), 0, 0),
-                ),
+                pl.BlockSpec(prior.shape, lambda i, core: (0, 0, 0), pipeline_mode=pl.Buffered(1)),
                 full(*weights.shape),
                 full(half, half),
                 full(outs, 1),
@@ -387,9 +398,9 @@
             jax.ShapeDtypeStruct((out_rows, outs, half), BF16),
         ],
         compiler_params=pltpu.CompilerParams(vmem_limit_bytes=46 * MIB),
-        cost_estimate=pl.CostEstimate(flops=10**10, bytes_accessed=2 * 10**7, transcendentals=0),
+        cost_estimate=pl.CostEstimate(flops=2 * 10**9, bytes_accessed=2 * 10**6, transcendentals=0),
         name="layer_three",
-    )(core, volume, volume, weights, even_odd(half), gain, shift)
+    )(core, volume, prior, weights, even_odd(half), gain, shift)
 
 
 def corner_total(core, refs):
@@ -464,10 +475,6 @@
         message_ref[out_rows, chans:] = corner[:, half:]
 
 
-def inputs(count):
-    return [pl.BlockSpec(memory_space=pltpu.SMEM)] + [pl.BlockSpec(memory_space=pltpu.VMEM)] * count
-
-
 def four_edges(core, thirds, local, weights):
     planes, rows, chans, width = thirds[0].shape
     outs = weights.shape[0]
@@ -480,13 +487,13 @@
         ],
         in_specs=inputs(len(thirds) + 3),
         compiler_params=pltpu.CompilerParams(vmem_limit_bytes=24 * MIB),
-        cost_estimate=pl.CostEstimate(flops=2 * 10**9, bytes_accessed=8 * 10**6, transcendentals=0),
+        cost_estimate=pl.CostEstimate(flops=10**9, bytes_accessed=10**6, transcendentals=0),
         name="four_edges",
     )(core, *thirds, local, weights, even_odd(width))
 
 
 def four_kernel(core_ref, *refs):
-    *thirds, local_ref, w_ref, place_ref, sums_ref, corner_ref, data_ref = refs
+    *thirds, local_ref, w_ref, place_ref, own_ref, theirs_ref, corner_ref, data_ref = refs
     core = core_ref[0]
     planes, rows, chans, width = thirds[0].shape
     halo_ref, gain_ref, shift_ref = thirds[3], thirds[5], thirds[6]
@@ -526,7 +533,9 @@
             put([third_value(core, thirds, plane, row) for row in range(first, first + batch)], first, spots)
     for row in range(out_rows):
         parts = [data_ref[slot, 2 * row : 2 * row + 3].reshape(3 * taps, count * half) for slot in range(3)]
-        sums_ref[row] = jnp.dot(w_ref[...], jnp.concatenate(parts, 0), preferred_element_type=F32)
+        total = jnp.dot(w_ref[...], jnp.concatenate(parts, 0), preferred_element_type=F32)
+        own_ref[row] = jnp.where(core == 0, total[:LANES], total[LANES:])
+        theirs_ref[row] = jnp.where(core == 0, total[LANES:], total[:LANES])
 
 
 def layer_four(core, thirds, local, weights):
@@ -537,22 +546,21 @@
     return pl.pallas_call(
         four_kernel,
         out_shape=[
-            jax.ShapeDtypeStruct((out_rows, outs, count * half), F32),
+            jax.ShapeDtypeStruct((out_rows, outs // 2, count * half), F32),
+            jax.ShapeDtypeStruct((out_rows, outs // 2, count * half), F32),
             jax.ShapeDtypeStruct((chans, width), F32),
         ],
         in_specs=inputs(len(thirds) + 3),
         scratch_shapes=[pltpu.VMEM((3, rows + 1, 3 * chans, count * half), BF16)],
         compiler_params=pltpu.CompilerParams(vmem_limit_bytes=32 * MIB),
-        cost_estimate=pl.CostEstimate(flops=8 * 10**9, bytes_accessed=10**7, transcendentals=0),
+        cost_estimate=pl.CostEstimate(flops=2 * 10**9, bytes_accessed=10**6, transcendentals=0),
         name="layer_four",
     )(core, *thirds, local, weights, even_odd(width))
 
 
-def theirs_kernel(
-    core_ref, sums_ref, corner_ref, halo_ref, mid_ref, place_ref, gain_ref, shift_ref, theirs_ref, fix_ref
-):
+def shares_kernel(core_ref, corner_ref, halo_ref, mid_ref, place_ref, gain_ref, shift_ref, shares_ref, fix_ref):
     core = core_ref[0]
-    rows, width = halo_ref.shape[0] - 1, halo_ref.shape[2]
+    rows = halo_ref.shape[0] - 1
 
     @pl.when(core == 0)
     def _():
@@ -562,31 +570,22 @@
         data = jnp.concatenate([part.astype(BF16) for part in spread((value,), place_ref[...])], 0)
         fix = jnp.dot(mid_ref[...], data, preferred_element_type=F32)
         fix_ref[...] = fix[:LANES]
-        for row in range(rows):
-            total = sums_ref[row, LANES:]
-            edge = halo_ref[row, LANES:].astype(F32)
-            if not row:
-                edge = edge + fix[LANES:]
-            theirs_ref[row] = jnp.concatenate([total[:, :width] + edge, total[:, width:]], 1)
-        theirs_ref[rows] = jnp.zeros_like(theirs_ref[rows])
+        shares_ref[...] = halo_ref[:rows, LANES:].astype(F32)
+        shares_ref[0] += fix[LANES:]
 
     @pl.when(core == 1)
     def _():
-        count = sums_ref.shape[2] // width
         fix_ref[...] = jnp.zeros_like(fix_ref)
-        for row in range(rows):
-            total = sums_ref[row, :LANES]
-            if not row:
-                total = total + jnp.concatenate([halo_ref[count + m, :LANES].astype(F32) for m in range(count)], 1)
-            theirs_ref[row] = total
-        theirs_ref[rows] = jnp.concatenate([halo_ref[m, :LANES].astype(F32) for m in range(count)], 1)
-
-
-def assemble_kernel(core_ref, sums_ref, halo_ref, fix_ref, scales_ref, got_ref, out_ref, lines_ref):
+        shares_ref[...] = halo_ref[:rows, :LANES].astype(F32)
+
+
+def assemble_kernel(
+    core_ref, own_ref, got_ref, halo_ref, fix_ref, scales_ref, shares_ref, out_ref, lines_ref
+):
     core = core_ref[0]
     gain, shift = scales_ref[:, 1:2], scales_ref[:, 2:3]
     rows, width = halo_ref.shape[0] - 1, halo_ref.shape[2]
-    count = sums_ref.shape[2] // width
+    count = own_ref.shape[2] // width
 
     def put(row, parts):
         for at, total in enumerate(parts):
@@ -595,22 +594,26 @@
                 place = row * 2 * count + at * count + m
                 lines_ref[pl.ds(place, LANES, stride=rows * 2 * count), :] = value[:, m * width : (m + 1) * width]
 
+    def with_edge(total, edge):
+        return jnp.concatenate([total[:, :width] + edge, total[:, width:]], 1)
+
     @pl.when(core == 0)
     def _():
         for row in range(rows):
-            total = sums_ref[row, :LANES]
             edge = halo_ref[row, :LANES].astype(F32)
             if not row:
                 edge = edge + fix_ref[...]
-            total = jnp.concatenate([total[:, :width] + edge, total[:, width:]], 1)
+            total, got = with_edge(own_ref[row], edge), got_ref[row]
             if not row:
-                total = total + got_ref[rows]
-            put(row, (total, got_ref[row]))
+                first = [shares_ref[m] for m in range(2 * count)]
+                total = total + jnp.concatenate(first[:count], 1)
+                got = got + jnp.concatenate(first[count:], 1)
+            put(row, (total, got))
 
     @pl.when(core == 1)
     def _():
         for row in range(rows):
-            total, got = sums_ref[row, LANES:], got_ref[row]
+            total, got = own_ref[row], with_edge(got_ref[row], shares_ref[row])
             if not row:
                 first = [halo_ref[m, LANES:].astype(F32) for m in range(2 * count)]
                 total = total + jnp.concatenate(first[count:], 1)
@@ -620,28 +623,29 @@
     out_ref[...] = lines_ref[...].astype(BF16)
 
 
-def last_stage(core, sums, corner, halo, mid, gain, shift, scales):
-    rows, outs, lanes = sums.shape
-    params = pltpu.CompilerParams(vmem_limit_bytes=16 * MIB)
-    theirs, fix = pl.pallas_call(
-        theirs_kernel,
+def last_stage(core, own, theirs, corner, halo, mid, gain, shift, scales):
+    rows, outs, lanes = own.shape
+    got = swapped(theirs)
+    shares, fix = pl.pallas_call(
+        shares_kernel,
         out_shape=[
-            jax.ShapeDtypeStruct((rows + 1, outs // 2, lanes), F32),
-            jax.ShapeDtypeStruct((outs // 2, halo.shape[2]), F32),
+            jax.ShapeDtypeStruct((rows, outs, halo.shape[2]), F32),
+            jax.ShapeDtypeStruct((outs, halo.shape[2]), F32),
         ],
-        in_specs=inputs(7),
-        compiler_params=params,
-        name="theirs",
-    )(core, sums, corner, halo, mid, even_odd(lanes), gain, shift)
-    lines = (outs // 2 * rows * lanes * 2 // LANES, LANES)
+        in_specs=inputs(6),
+        compiler_params=pltpu.CompilerParams(vmem_limit_bytes=16 * MIB),
+        cost_estimate=pl.CostEstimate(flops=10**8, bytes_accessed=10**6, transcendentals=0),
+        name="shares",
+    )(core, corner, halo, mid, even_odd(lanes), gain, shift)
+    lines = (outs * rows * lanes * 2 // LANES, LANES)
     return pl.pallas_call(
         assemble_kernel,
         out_shape=jax.ShapeDtypeStruct(lines, BF16),
-        in_specs=inputs(5),
+        in_specs=inputs(6),
         scratch_shapes=[pltpu.VMEM(lines, F32)],
-        compiler_params=params,
+        compiler_params=pltpu.CompilerParams(vmem_limit_bytes=16 * MIB),
         name="assemble",
-    )(core, sums, halo, fix, scales, swapped(theirs))
+    )(core, own, got, halo, fix, scales, swapped(shares))
 
 
 def handed_on(message):
@@ -658,21 +662,22 @@
 def shards(volume, kernel_three, gain_three, shift_three, kernel_four, gain_four, shift_four):
     core = lax.axis_index("fl").reshape(1)
     own_scales = jnp.concatenate([gain_three, shift_three, gain_four, shift_four]).reshape(-1, LANES)
+    picked, prior = three_picks(volume, core)
     message, weights_three, gain, shift, scales = three_edges(
-        volume, kernel_three, swapped(kernel_three), own_scales, swapped(own_scales), core
+        picked, kernel_three, swapped(kernel_three), own_scales, swapped(own_scales), core
     )
     halo = handed_on(message)
-    *thirds, local = layer_three(volume, weights_three, gain, shift, core)
+    *thirds, local = layer_three(volume, prior, weights_three, gain, shift, core)
     rows = lax.ppermute(halo[: thirds[0].shape[0]], "fl", [(1, 0)])
     thirds = (*thirds, halo, rows, gain, shift)
     local = swapped(local)
     weights_four = four_weights(kernel_four, swapped(kernel_four), core)
     message, mid = four_edges(core, thirds, local, weights_four)
     halo = handed_on(message)
-    sums, corner = layer_four(core, thirds, local, weights_four)
-    lines = last_stage(core, sums, corner, halo, mid, gain, shift, scales)
-    out_rows, outs, lanes = sums.shape
-    fourth = lines.reshape(outs // 2, out_rows, 2 * lanes // LANES, LANES)
+    own, theirs, corner = layer_four(core, thirds, local, weights_four)
+    lines = last_stage(core, own, theirs, corner, halo, mid, gain, shift, scales)
+    out_rows, outs, lanes = own.shape
+    fourth = lines.reshape(outs, out_rows, 2 * lanes // LANES, LANES)
     return jnp.transpose(fourth, (0, 2, 1, 3))[None]
 
 

time: 60 us -> 57.9 us (0.965)
  waiting for transfers between devices: 13.7 us -> 10.6 us
  starting transfers between devices: 11 us -> 13.1 us
  local copies, waits for them, and re-layouts: 1.87 us -> 0.94 us
    ppermute x5 -> x6, starting transfers between devices: 3.18 us -> 5.36 us  [swapped(): return lax.ppermute(value, 'fl', [(0, 1), (1, 0)])]
    ppermute x2, waiting for transfers between devices: 10.6 us -> 8.84 us  [handed_on(): return lax.ppermute(message, ('sp', 'fl'), pairs)]
    ppermute x5 -> x6, waiting for transfers between devices: 3.11 us -> 1.71 us  [swapped(): return lax.ppermute(value, 'fl', [(0, 1), (1, 0)])]
    unnamed x8 -> x10, local copies, waits for them, and re-layouts: 1.85 us -> 0.92 us
    pallas_call x1, Pallas kernels: 17.9 us -> 17 us  [layer_three(): pl.pallas_call(three_kernel, grid_spec=pltpu.PrefetchScalarGridSpec(num_s...]
    pallas_call x2 -> x3, Pallas kernels: 5.68 us -> 6.53 us  [the longest x1 5.16 us: three_picks(): pl.pallas_call(three_picks_kernel, grid_spec=pltpu.PrefetchScalarGridSpec...]
  transfers between devices with their start and end apart: 8 -> 9, of which waited for: 4 -> 3; matrix products, arithmetic and copies ran while one was open for 1% -> 1% of each run, Pallas kernels for 49% -> 49%
where the time goes in v6:
time: 57.9 us; the launch traced here: 57.6 us
  Pallas kernels  32.1 us (55%)
  starting transfers between devices  13.1 us (23%)
  waiting for transfers between devices  10.6 us (18%)
  local copies, waits for them, and re-layouts  0.94 us (2%)
  other arithmetic  0.78 us (1%)
    pallas_call x1, Pallas kernels, layer_three(): pl.pallas_call(three_kernel, grid_spec=pltpu.PrefetchScalarGridSpec(num_s...  17 us
    ppermute x2, waiting for transfers between devices, handed_on(): return lax.ppermute(message, ('sp', 'fl'), pairs)  8.84 us
    ppermute x6, starting transfers between devices, swapped(): return lax.ppermute(value, 'fl', [(0, 1), (1, 0)])  5.36 us
    pallas_call x1, Pallas kernels, three_picks(): pl.pallas_call(three_picks_kernel, grid_spec=pltpu.PrefetchScalarGridSpec...  5.16 us
    ppermute x1, starting transfers between devices, shards(): rows = lax.ppermute(halo[:thirds[0].shape[0]], 'fl', [(1, 0)])  4.97 us
    pallas_call x1, Pallas kernels, layer_four(): pl.pallas_call(four_kernel, out_shape=[jax.ShapeDtypeStruct((out_rows, ou...  4.84 us
    ppermute x2, starting transfers between devices, handed_on(): return lax.ppermute(message, ('sp', 'fl'), pairs)  2.76 us
    ppermute x6, waiting for transfers between devices, swapped(): return lax.ppermute(value, 'fl', [(0, 1), (1, 0)])  1.71 us
  transfers between devices with their start and end apart: 9, of which 3 were waited for; matrix products, arithmetic and copies ran while one was open for 1% of the time, Pallas kernels for 49%

profile of v6, /device:TPU:25, one launch (start us, length us, event | category | flops | bytes accessed | tf_op | source)
XLA Modules:
  0.0 57.6 jit_solution(10918607551049602115)
XLA Ops:
  0.0 0.7 %collective-permute-start = (bf16[64,1728]{1,0:T(8,128)(2,1)}, bf16[64,1728]{1,0:T(8,128)(2,1)S(1)}, u32[]{:S(2)}, u32[]{:S(2)}) collective-permute-start(bf16[64,1728]{1,0:T(8,128)(2,1)} %own_ref.2), channel_id=1, source_target_pairs={{0,1},{1,0},{2,3},{3,2},{4,5},{5,4},{6,7},{7,6},{8,9},{9,8},{10,11... | collective-permute-start | bytes 663560 | tf_op jit(solution)/shard_map/ppermute | solution.py:659
  0.7 0.8 %maximum_bitcast_fusion.own_scales_ref = f32[3,128]{1,0:T(4,128)S(1)} fusion(f32[128]{0:T(128)} %param.18, f32[128]{0:T(128)} %param.17, f32[64]{0:T(128)} %param.15, f32[64]{0:T(128)} %param.14), kind=kLoop, calls=%fused_computation | loop fusion | flops 1152 | bytes 3072 | tf_op jit(solution)/shard_map/reshape | solution.py:664
  1.5 0.0 collective-permute-start.1
  1.5 0.0 copy-start.1
  1.5 0.9 %copy-done.1 = bf16[256,256]{1,0:T(8,128)(2,1)S(1)} copy-done((bf16[256,256]{1,0:T(8,128)(2,1)S(1)}, bf16[256,256]{1,0:T(8,128)(2,1)}, u32[]{:S(2)}) %copy-start.1) | copy-done | bytes 131096
  2.4 0.0 copy-start.4
  2.4 5.2 %three_picks.1 = (bf16[25,192,256]{2,1,0:T(8,128)(2,1)S(1)}, bf16[25,192,256]{2,1,0:T(8,128)(2,1)S(1)}) custom-call(s32[1]{0:T(128)} %bitcast.core_ref, bf16[1,64,16,24,512]{4,3,2,1,0:T(8,128)(2,1)} %x_ref.1, bf16[1,64,16,24,512]{4,3,2,1,0:T(8,128)(2,1)} %x_ref.1, bf16[1,64,16,24,512]{4,3,2,1,0:T(8,128)(2,1)} %x_ref.1, bf16[256,256]{1,0:T(8,128)(2,1)S(1)} %copy-done.1), custom_call_target="tpu_custom_call" | custom-call | flops 1000000000 | bytes 10000000 | tf_op jit(solution)/shard_map/three_picks/pallas_call | solution.py:188
  7.6 0.0 copy-start.3
  7.6 0.0 copy-start.2
  7.6 0.0 collective-permute-done.1.other_scales_ref
  7.6 0.0 collective-permute-done.other_ref
  7.6 0.0 copy-done.4
  7.6 1.3 %three_edges.1 = (bf16[12,128,256]{2,1,0:T(8,128)(2,1)S(1)}, bf16[128,1728]{1,0:T(8,128)(2,1)S(1)}, f32[128,1]{1,0:T(8,128)S(1)}, f32[128,1]{1,0:T(8,128)S(1)}, f32[128,128]{1,0:T(8,128)S(1)}) custom-call(s32[1]{0:T(128)} %bitcast.core_ref, bf16[25,192,256]{2,1,0:T(8,128)(2,1)S(1)} %get-tuple-element.24.picked_ref, bf16[64,1728]{1,0:T(8,128)(2,1)S(1)} %copy-done.4, ...), custom_call_target="tpu_custom_call" | custom-call | flops 1000000000 | bytes 1000000 | tf_op jit(solution)/shard_map/three_edges/pallas_call | solution.py:271
  9.0 1.5 %collective-permute-start.2 = (bf16[12,128,256]{2,1,0:T(8,128)(2,1)S(1)}, bf16[12,128,256]{2,1,0:T(8,128)(2,1)S(1)}, u32[]{:S(2)}, u32[]{:S(2)}) collective-permute-start(bf16[12,128,256]{2,1,0:T(8,128)(2,1)S(1)} %get-tuple-element.31), channel_id=1, source_target_pairs={{0,3},{2,5},{4,7},{6,9},{8,11},{10,13},{12,15},{16,19},{18,21},{20... | collective-permute-start | bytes 2359304 | tf_op jit(solution)/shard_map/ppermute | solution.py:655
  10.4 0.0 copy-done.3
  10.4 2.5 %collective-permute-start.5 = (bf16[128,3456]{1,0:T(8,128)(2,1)S(1)}, bf16[128,3456]{1,0:T(8,128)(2,1)S(1)}, u32[]{:S(2)}, u32[]{:S(2)}) collective-permute-start(bf16[128,3456]{1,0:T(8,128)(2,1)S(1)} %copy-done.3), channel_id=1, source_target_pairs={{0,1},{1,0},{2,3},{3,2},{4,5},{5,4},{6,7},{7,6},{8,9},{9,8},{10,11... | collective-permute-start | bytes 2654216 | tf_op jit(solution)/shard_map/ppermute | solution.py:659
  13.0 0.0 copy-done.2
  13.0 17.0 %layer_three.1 = (bf16[4,12,128,256]{3,2,1,0:T(8,128)(2,1)}, f32[12,128,256]{2,1,0:T(8,128)S(1)}, f32[4,128,256]{2,1,0:T(8,128)S(1)}, bf16[12,128,256]{2,1,0:T(8,128)(2,1)S(1)}) custom-call(s32[1]{0:T(128)} %bitcast.core_ref, bf16[1,64,16,24,512]{4,3,2,1,0:T(8,128)(2,1)} %x_ref.1, bf16[25,192,256]{2,1,0:T(8,128)(2,1)S(1)} %get-tuple-element.23.before_ref, ...), custom_call_target="tpu_custom_call" | custom-call | flops 2000000000 | bytes 2000000 | tf_op jit(solution)/shard_map/layer_three/pallas_call | solution.py:367
  29.9 0.0 copy-start
  29.9 0.1 collective-permute-start.4
  30.0 0.5 collective-permute-done.2.refs_3_
  30.5 5.0 %collective-permute-start.3 = (bf16[4,128,256]{2,1,0:T(8,128)(2,1)S(1)}, bf16[4,128,256]{2,1,0:T(8,128)(2,1)S(1)}, u32[]{:S(2)}, u32[]{:S(2)}) collective-permute-start(bf16[4,128,256]{2,1,0:T(8,128)(2,1)S(1)} %slice.4), channel_id=1, source_target_pairs={{1,0},{3,2},{5,4},{7,6},{9,8},{11,10},{13,12},{15,14},{17,16},{19,... | collective-permute-start | bytes 786440 | tf_op jit(solution)/shard_map/ppermute | solution.py:671
  35.5 0.0 collective-permute-done.5.other_ref
  35.5 1.2 %four_weights.1.refs_8_ = bf16[256,3456]{1,0:T(8,128)(2,1)S(1)} custom-call(s32[1]{0:T(128)} %bitcast.core_ref, bf16[128,3456]{1,0:T(8,128)(2,1)S(1)} %copy-done.3, bf16[128,3456]{1,0:T(8,128)(2,1)S(1)} %collective-permute-done.5.other_ref), custom_call_target="tpu_custom_call" | custom-call | flops 1000000 | bytes 4000000 | tf_op jit(solution)/shard_map/four_weights/pallas_call | solution.py:110
  36.7 0.0 collective-permute-done.4.refs_7_
  36.7 0.0 collective-permute-done.3.refs_4_
  36.7 0.0 copy-done
  36.7 1.2 %four_edges.1 = (bf16[7,256,128]{2,1,0:T(8,128)(2,1)S(1)}, bf16[256,384]{1,0:T(8,128)(2,1)S(1)}) custom-call(s32[1]{0:T(128)} %bitcast.core_ref, bf16[4,12,128,256]{3,2,1,0:T(8,128)(2,1)S(1)} %copy-done, f32[12,128,256]{2,1,0:T(8,128)S(1)} %get-tuple-element.29.refs_1_, f32[4,128,256]{2,1,0:T(8,128)S(1)} %get-tuple-element.30.refs_2_, ...), custom_call_target="tpu_custom_call" | custom-call | flops 1000000000 | bytes 1000000 | tf_op jit(solution)/shard_map/four_edges/pallas_call | solution.py:482
  37.9 1.3 %collective-permute-start.7 = (bf16[7,256,128]{2,1,0:T(8,128)(2,1)S(1)}, bf16[7,256,128]{2,1,0:T(8,128)(2,1)S(1)}, u32[]{:S(2)}, u32[]{:S(2)}) collective-permute-start(bf16[7,256,128]{2,1,0:T(8,128)(2,1)S(1)} %get-tuple-element.35), channel_id=1, source_target_pairs={{0,3},{2,5},{4,7},{6,9},{8,11},{10,13},{12,15},{16,19},{18,21},{20... | collective-permute-start | bytes 1376264 | tf_op jit(solution)/shard_map/ppermute | solution.py:655
  39.2 4.8 %layer_four.1 = (f32[6,128,256]{2,1,0:T(8,128)S(1)}, f32[6,128,256]{2,1,0:T(8,128)S(1)}, f32[128,256]{1,0:T(8,128)S(1)}) custom-call(s32[1]{0:T(128)} %bitcast.core_ref, bf16[4,12,128,256]{3,2,1,0:T(8,128)(2,1)S(1)} %copy-done, f32[12,128,256]{2,1,0:T(8,128)S(1)} %get-tuple-element.29.refs_1_, f32[4,128,256]{2,1,0:T(8,128)S(1)} %get-tuple-element.30.refs_2_, ...), custom_call_target="tpu_custom_call" | custom-call | flops 2000000000 | bytes 1000000 | tf_op jit(solution)/shard_map/layer_four/pallas_call | solution.py:546
  44.1 2.0 %collective-permute-start.6 = (f32[6,128,256]{2,1,0:T(8,128)S(1)}, f32[6,128,256]{2,1,0:T(8,128)S(1)}, u32[]{:S(2)}, u32[]{:S(2)}) collective-permute-start(f32[6,128,256]{2,1,0:T(8,128)S(1)} %get-tuple-element.34), channel_id=1, source_target_pairs={{0,1},{1,0},{2,3},{3,2},{4,5},{5,4},{6,7},{7,6},{8,9},{9,8},{10,11... | collective-permute-start | bytes 2359304 | tf_op jit(solution)/shard_map/ppermute | solution.py:659
  46.0 8.4 %collective-permute-done.7.halo_ref = bf16[7,256,128]{2,1,0:T(8,128)(2,1)S(1)} collective-permute-done((bf16[7,256,128]{2,1,0:T(8,128)(2,1)S(1)}, bf16[7,256,128]{2,1,0:T(8,128)(2,1)S(1)}, u32[]{:S(2)}, u32[]{:S(2)}) %collective-permute-start.7) | collective-permute-done | bytes 458784 | tf_op jit(solution)/shard_map/ppermute | solution.py:655
  54.5 0.1 collective-permute-start.8
  54.5 0.0 collective-permute-done.6.got_ref
  54.5 1.7 %collective-permute-done.8.shares_ref = f32[6,128,128]{2,1,0:T(8,128)S(1)} collective-permute-done((f32[6,128,128]{2,1,0:T(8,128)S(1)}, f32[6,128,128]{2,1,0:T(8,128)S(1)}, u32[]{:S(2)}, u32[]{:S(2)}) %collective-permute-start.8) | collective-permute-done | bytes 393248 | tf_op jit(solution)/shard_map/ppermute | solution.py:659
  56.2 1.4 %assemble.1 = bf16[3072,128]{1,0:T(8,128)(2,1)} custom-call(s32[1]{0:T(128)} %bitcast.core_ref, f32[6,128,256]{2,1,0:T(8,128)S(1)} %get-tuple-element.33.own_ref, f32[6,128,256]{2,1,0:T(8,128)S(1)} %collective-permute-done.6.got_ref, bf16[7,256,128]{2,1,0:T(8,128)(2,1)S(1)} %collective-permute-done.7.halo_ref, f32[128,128]{1,0:T(8,128)S(1)} %get-tuple-element.38.fix_ref, ...), custom_call_target="tpu_custom_call" | custom-call | tf_op jit(solution)/shard_map/assemble/pallas_call | solution.py:641
  (2 shorter events, 0.0 us)
Async XLA Ops:
  0.0 7.6 %collective-permute-start = (bf16[64,1728]{1,0:T(8,128)(2,1)}, bf16[64,1728]{1,0:T(8,128)(2,1)S(1)}, u32[]{:S(2)}, u32[]{:S(2)}) collective-permute-start(bf16[64,1728]{1,0:T(8,128)(2,1)} %own_ref.2), channel_id=1, source_target_pairs={{0,1},{1,0},{2,3},{3,2},{4,5},{5,4},{6,7},{7,6},{8,9},{9,8},{10,11... | collective-permute-start | bytes 663560 | tf_op jit(solution)/shard_map/ppermute | solution.py:659
  1.5 6.1 %collective-permute-start.1 = (f32[3,128]{1,0:T(4,128)S(1)}, f32[3,128]{1,0:T(4,128)S(1)}, u32[]{:S(2)}, u32[]{:S(2)}) collective-permute-start(f32[3,128]{1,0:T(4,128)S(1)} %maximum_bitcast_fusion.own_scales_ref), channel_id=1, source_target_pairs={{0,1},{1,0},{2,3},{3,2},{4,5},{5,4},{6,7},{7,6},{8,9},{9,8},{10,11... | collective-permute-start | bytes 4616 | tf_op jit(solution)/shard_map/ppermute | solution.py:659
  1.5 0.9 %copy-start.1 = (bf16[256,256]{1,0:T(8,128)(2,1)S(1)}, bf16[256,256]{1,0:T(8,128)(2,1)}, u32[]{:S(2)}) copy-start(bf16[256,256]{1,0:T(8,128)(2,1)} %constant.6.clone.place_ref.refs_9_) | copy-start | bytes 393220
  2.4 5.2 %copy-start.4 = (bf16[64,1728]{1,0:T(8,128)(2,1)S(1)}, bf16[64,1728]{1,0:T(8,128)(2,1)}, u32[]{:S(2)}) copy-start(bf16[64,1728]{1,0:T(8,128)(2,1)} %own_ref.2) | copy-start | bytes 663556
  7.6 2.9 %copy-start.3 = (bf16[128,3456]{1,0:T(8,128)(2,1)S(1)}, bf16[128,3456]{1,0:T(8,128)(2,1)}, u32[]{:S(2)}) copy-start(bf16[128,3456]{1,0:T(8,128)(2,1)} %own_ref.3) | copy-start | bytes 2654212
  7.6 5.4 %copy-start.2 = (bf16[256,256]{1,0:T(8,128)(2,1)S(1)}, bf16[256,256]{1,0:T(8,128)(2,1)}, u32[]{:S(2)}) copy-start(bf16[256,256]{1,0:T(8,128)(2,1)} %constant.6.clone.place_ref.refs_9_) | copy-start | bytes 393220
  9.0 21.5 %collective-permute-start.2 = (bf16[12,128,256]{2,1,0:T(8,128)(2,1)S(1)}, bf16[12,128,256]{2,1,0:T(8,128)(2,1)S(1)}, u32[]{:S(2)}, u32[]{:S(2)}) collective-permute-start(bf16[12,128,256]{2,1,0:T(8,128)(2,1)S(1)} %get-tuple-element.31), channel_id=1, source_target_pairs={{0,3},{2,5},{4,7},{6,9},{8,11},{10,13},{12,15},{16,19},{18,21},{20... | collective-permute-start | bytes 2359304 | tf_op jit(solution)/shard_map/ppermute | solution.py:655
  10.4 25.0 %collective-permute-start.5 = (bf16[128,3456]{1,0:T(8,128)(2,1)S(1)}, bf16[128,3456]{1,0:T(8,128)(2,1)S(1)}, u32[]{:S(2)}, u32[]{:S(2)}) collective-permute-start(bf16[128,3456]{1,0:T(8,128)(2,1)S(1)} %copy-done.3), channel_id=1, source_target_pairs={{0,1},{1,0},{2,3},{3,2},{4,5},{5,4},{6,7},{7,6},{8,9},{9,8},{10,11... | collective-permute-start | bytes 2654216 | tf_op jit(solution)/shard_map/ppermute | solution.py:659
  29.9 6.8 %copy-start = (bf16[4,12,128,256]{3,2,1,0:T(8,128)(2,1)S(1)}, bf16[4,12,128,256]{3,2,1,0:T(8,128)(2,1)}, u32[]{:S(2)}) copy-start(bf16[4,12,128,256]{3,2,1,0:T(8,128)(2,1)} %get-tuple-element.28.refs_0_) | copy-start | bytes 9437188
  29.9 6.7 %collective-permute-start.4 = (bf16[12,128,256]{2,1,0:T(8,128)(2,1)S(1)}, bf16[12,128,256]{2,1,0:T(8,128)(2,1)S(1)}, u32[]{:S(2)}, u32[]{:S(2)}) collective-permute-start(bf16[12,128,256]{2,1,0:T(8,128)(2,1)S(1)} %get-tuple-element.32), channel_id=1, source_target_pairs={{0,1},{1,0},{2,3},{3,2},{4,5},{5,4},{6,7},{7,6},{8,9},{9,8},{10,11... | collective-permute-start | bytes 2359304 | tf_op jit(solution)/shard_map/ppermute | solution.py:659
  30.5 6.2 %collective-permute-start.3 = (bf16[4,128,256]{2,1,0:T(8,128)(2,1)S(1)}, bf16[4,128,256]{2,1,0:T(8,128)(2,1)S(1)}, u32[]{:S(2)}, u32[]{:S(2)}) collective-permute-start(bf16[4,128,256]{2,1,0:T(8,128)(2,1)S(1)} %slice.4), channel_id=1, source_target_pairs={{1,0},{3,2},{5,4},{7,6},{9,8},{11,10},{13,12},{15,14},{17,16},{19,... | collective-permute-start | bytes 786440 | tf_op jit(solution)/shard_map/ppermute | solution.py:671
  37.9 16.5 %collective-permute-start.7 = (bf16[7,256,128]{2,1,0:T(8,128)(2,1)S(1)}, bf16[7,256,128]{2,1,0:T(8,128)(2,1)S(1)}, u32[]{:S(2)}, u32[]{:S(2)}) collective-permute-start(bf16[7,256,128]{2,1,0:T(8,128)(2,1)S(1)} %get-tuple-element.35), channel_id=1, source_target_pairs={{0,3},{2,5},{4,7},{6,9},{8,11},{10,13},{12,15},{16,19},{18,21},{20... | collective-permute-start | bytes 1376264 | tf_op jit(solution)/shard_map/ppermute | solution.py:655
  44.1 10.5 %collective-permute-start.6 = (f32[6,128,256]{2,1,0:T(8,128)S(1)}, f32[6,128,256]{2,1,0:T(8,128)S(1)}, u32[]{:S(2)}, u32[]{:S(2)}) collective-permute-start(f32[6,128,256]{2,1,0:T(8,128)S(1)} %get-tuple-element.34), channel_id=1, source_target_pairs={{0,1},{1,0},{2,3},{3,2},{4,5},{5,4},{6,7},{7,6},{8,9},{9,8},{10,11... | collective-permute-start | bytes 2359304 | tf_op jit(solution)/shard_map/ppermute | solution.py:659
  54.5 1.8 %collective-permute-start.8 = (f32[6,128,128]{2,1,0:T(8,128)S(1)}, f32[6,128,128]{2,1,0:T(8,128)S(1)}, u32[]{:S(2)}, u32[]{:S(2)}) collective-permute-start(f32[6,128,128]{2,1,0:T(8,128)S(1)} %get-tuple-element.40), channel_id=1, source_target_pairs={{0,1},{1,0},{2,3},{3,2},{4,5},{5,4},{6,7},{7,6},{8,9},{9,8},{10,11... | collective-permute-start | bytes 1179656 | tf_op jit(solution)/shard_map/ppermute | solution.py:659

commit v7 on v6

--- a/solution.py
+++ b/solution.py
@@ -117,7 +117,7 @@
         ],
         scratch_shapes=[pltpu.VMEM((columns, LANES), F32)] * 2,
         compiler_params=pltpu.CompilerParams(vmem_limit_bytes=16 * MIB),
-        cost_estimate=pl.CostEstimate(flops=10**6, bytes_accessed=4 * 10**6, transcendentals=0),
+        cost_estimate=pl.CostEstimate(flops=10**3, bytes_accessed=10**3, transcendentals=0),
         name="four_weights",
     )(core, own, other)
 
@@ -398,30 +398,32 @@
             jax.ShapeDtypeStruct((out_rows, outs, half), BF16),
         ],
         compiler_params=pltpu.CompilerParams(vmem_limit_bytes=46 * MIB),
-        cost_estimate=pl.CostEstimate(flops=2 * 10**9, bytes_accessed=2 * 10**6, transcendentals=0),
+        cost_estimate=pl.CostEstimate(flops=10**10, bytes_accessed=2 * 10**7, transcendentals=0),
         name="layer_three",
     )(core, volume, prior, weights, even_odd(half), gain, shift)
 
 
-def corner_total(core, refs):
-    _, plane_ref, _, halo_ref, rows_ref, _, _ = refs
-    planes = rows_ref.shape[0]
+def corner_total(core, refs, rows_ref):
+    third_ref, plane_ref, _, halo_ref, _, _ = refs
+    planes = third_ref.shape[0]
     first = jnp.where(core == 0, rows_ref[0].astype(F32), halo_ref[planes].astype(F32))
     return plane_ref[0] + jnp.where(core == 0, halo_ref[0].astype(F32), 0.0) + first
 
 
-def third_value(core, refs, plane, row):
-    third_ref, plane_ref, row_ref, halo_ref, rows_ref, gain_ref, shift_ref = refs
-    planes = rows_ref.shape[0]
+def third_value(core, refs, plane, row, rows_ref=None):
+    third_ref, plane_ref, row_ref, halo_ref, gain_ref, shift_ref = refs
+    planes = third_ref.shape[0]
     if plane and row:
         return third_ref[plane, row]
     if plane:
-        share = jnp.where(core == 0, rows_ref[plane].astype(F32), halo_ref[planes + plane].astype(F32))
+        share = halo_ref[planes + plane].astype(F32)
+        if rows_ref is not None:
+            share = jnp.where(core == 0, rows_ref[plane].astype(F32), share)
         total = row_ref[plane] + share
     elif row:
         total = plane_ref[row] + jnp.where(core == 0, halo_ref[row].astype(F32), 0.0)
     else:
-        total = corner_total(core, refs)
+        total = corner_total(core, refs, rows_ref)
     value = activate(total, gain_ref[...], shift_ref[...])
     if not plane and not row:
         value = jnp.where(core == 0, 0.0, value)
@@ -429,9 +431,10 @@
 
 
 def four_edges_kernel(core_ref, *refs):
-    *thirds, local_ref, w_ref, place_ref, message_ref, mid_ref = refs
+    *thirds, local_ref, w_ref, place_ref, message_ref, mid_ref, rows_ref = refs
     core = core_ref[0]
     planes, rows, chans, width = thirds[0].shape
+    rows_ref[...] = thirds[3][:planes]
     half = width // 2
     out_rows = rows // 2
     taps = 3 * chans
@@ -484,6 +487,7 @@
         out_shape=[
             jax.ShapeDtypeStruct((rows // 2 + 1, outs, half), BF16),
             jax.ShapeDtypeStruct((outs, 3 * chans), BF16),
+            jax.ShapeDtypeStruct((planes, chans, width), BF16),
         ],
         in_specs=inputs(len(thirds) + 3),
         compiler_params=pltpu.CompilerParams(vmem_limit_bytes=24 * MIB),
@@ -493,16 +497,16 @@
 
 
 def four_kernel(core_ref, *refs):
-    *thirds, local_ref, w_ref, place_ref, own_ref, theirs_ref, corner_ref, data_ref = refs
+    *thirds, rows_ref, local_ref, w_ref, place_ref, own_ref, theirs_ref, corner_ref, data_ref = refs
     core = core_ref[0]
     planes, rows, chans, width = thirds[0].shape
-    halo_ref, gain_ref, shift_ref = thirds[3], thirds[5], thirds[6]
+    halo_ref, gain_ref, shift_ref = thirds[3:]
     half = width // 2
     out_rows, count = rows // 2, planes // 2
     taps = 3 * chans
     batch = 4
     data_ref[:, 0] = jnp.zeros_like(data_ref[:, 0])
-    corner_ref[...] = corner_total(core, thirds)
+    corner_ref[...] = corner_total(core, thirds, rows_ref)
 
     def put(values, first, spots):
         for tap, part in enumerate(spread((jnp.concatenate(values, 0),), place_ref[...])):
@@ -530,7 +534,7 @@
         if plane % 2 and plane // 2 + 1 < count:
             spots.append((0, plane // 2 + 1))
         for first in range(0, rows, batch):
-            put([third_value(core, thirds, plane, row) for row in range(first, first + batch)], first, spots)
+            put([third_value(core, thirds, plane, row, rows_ref) for row in range(first, first + batch)], first, spots)
     for row in range(out_rows):
         parts = [data_ref[slot, 2 * row : 2 * row + 3].reshape(3 * taps, count * half) for slot in range(3)]
         total = jnp.dot(w_ref[...], jnp.concatenate(parts, 0), preferred_element_type=F32)
@@ -538,7 +542,7 @@
         theirs_ref[row] = jnp.where(core == 0, total[LANES:], total[:LANES])
 
 
-def layer_four(core, thirds, local, weights):
+def layer_four(core, thirds, rows_before, local, weights):
     planes, rows, chans, width = thirds[0].shape
     outs = weights.shape[0]
     half = width // 2
@@ -550,12 +554,12 @@
             jax.ShapeDtypeStruct((out_rows, outs // 2, count * half), F32),
             jax.ShapeDtypeStruct((chans, width), F32),
         ],
-        in_specs=inputs(len(thirds) + 3),
+        in_specs=inputs(len(thirds) + 4),
         scratch_shapes=[pltpu.VMEM((3, rows + 1, 3 * chans, count * half), BF16)],
         compiler_params=pltpu.CompilerParams(vmem_limit_bytes=32 * MIB),
-        cost_estimate=pl.CostEstimate(flops=2 * 10**9, bytes_accessed=10**6, transcendentals=0),
+        cost_estimate=pl.CostEstimate(flops=4 * 10**9, bytes_accessed=4 * 10**6, transcendentals=0),
         name="layer_four",
-    )(core, *thirds, local, weights, even_odd(width))
+    )(core, *thirds, rows_before, local, weights, even_odd(width))
 
 
 def shares_kernel(core_ref, corner_ref, halo_ref, mid_ref, place_ref, gain_ref, shift_ref, shares_ref, fix_ref):
@@ -663,18 +667,20 @@
     core = lax.axis_index("fl").reshape(1)
     own_scales = jnp.concatenate([gain_three, shift_three, gain_four, shift_four]).reshape(-1, LANES)
     picked, prior = three_picks(volume, core)
+    others = lax.optimization_barrier((swapped(kernel_three), swapped(own_scales), swapped(kernel_four)))
     message, weights_three, gain, shift, scales = three_edges(
-        picked, kernel_three, swapped(kernel_three), own_scales, swapped(own_scales), core
+        picked, kernel_three, others[0], own_scales, others[1], core
     )
     halo = handed_on(message)
     *thirds, local = layer_three(volume, prior, weights_three, gain, shift, core)
-    rows = lax.ppermute(halo[: thirds[0].shape[0]], "fl", [(1, 0)])
-    thirds = (*thirds, halo, rows, gain, shift)
+    halo, local = lax.optimization_barrier((halo, local))
+    thirds = (*thirds, halo, gain, shift)
     local = swapped(local)
-    weights_four = four_weights(kernel_four, swapped(kernel_four), core)
-    message, mid = four_edges(core, thirds, local, weights_four)
+    weights_four = four_weights(kernel_four, others[2], core)
+    message, mid, rows = four_edges(core, thirds, local, weights_four)
     halo = handed_on(message)
-    own, theirs, corner = layer_four(core, thirds, local, weights_four)
+    rows = lax.ppermute(rows, "fl", [(1, 0)])
+    own, theirs, corner = layer_four(core, thirds, rows, local, weights_four)
     lines = last_stage(core, own, theirs, corner, halo, mid, gain, shift, scales)
     out_rows, outs, lanes = own.shape
     fourth = lines.reshape(outs, out_rows, 2 * lanes // LANES, LANES)

time: 57.9 us -> 58.3 us (level)
  waiting for transfers between devices: 10.6 us -> 13.8 us
  starting transfers between devices: 13.1 us -> 10.2 us
    ppermute x1, starting transfers between devices: 4.97 us -> 2.03 us  [shards(): rows = lax.ppermute(rows, 'fl', [(1, 0)])]
    ppermute x2, waiting for transfers between devices: 8.84 us -> 11.4 us  [handed_on(): return lax.ppermute(message, ('sp', 'fl'), pairs)]
    ppermute x6, waiting for transfers between devices: 1.71 us -> 2.4 us  [swapped(): return lax.ppermute(value, 'fl', [(0, 1), (1, 0)])]
  transfers between devices with their start and end apart: 9 -> 9, of which waited for: 3 -> 4; matrix products, arithmetic and copies ran while one was open for 1% -> 1% of each run, Pallas kernels for 49% -> 49%
where the time goes in v7:
time: 58.3 us; the launch traced here: 58.1 us
  Pallas kernels  32.2 us (55%)
  waiting for transfers between devices  13.8 us (24%)
  starting transfers between devices  10.2 us (17%)
  local copies, waits for them, and re-layouts  0.92 us (2%)
  other arithmetic  0.78 us (1%)
    pallas_call x1, Pallas kernels, layer_three(): pl.pallas_call(three_kernel, grid_spec=pltpu.PrefetchScalarGridSpec(num_s...  17.1 us
    ppermute x2, waiting for transfers between devices, handed_on(): return lax.ppermute(message, ('sp', 'fl'), pairs)  11.4 us
    ppermute x6, starting transfers between devices, swapped(): return lax.ppermute(value, 'fl', [(0, 1), (1, 0)])  5.39 us
    pallas_call x1, Pallas kernels, three_picks(): pl.pallas_call(three_picks_kernel, grid_spec=pltpu.PrefetchScalarGridSpec...  5.16 us
    pallas_call x1, Pallas kernels, layer_four(): pl.pallas_call(four_kernel, out_shape=[jax.ShapeDtypeStruct((out_rows, ou...  4.84 us
    ppermute x2, starting transfers between devices, handed_on(): return lax.ppermute(message, ('sp', 'fl'), pairs)  2.76 us
    ppermute x6, waiting for transfers between devices, swapped(): return lax.ppermute(value, 'fl', [(0, 1), (1, 0)])  2.4 us
    ppermute x1, starting transfers between devices, shards(): rows = lax.ppermute(rows, 'fl', [(1, 0)])  2.03 us
  transfers between devices with their start and end apart: 9, of which 4 were waited for; matrix products, arithmetic and copies ran while one was open for 1% of the time, Pallas kernels for 49%

profile of v7, /device:TPU:25, one launch (start us, length us, event | category | flops | bytes accessed | tf_op | source)
XLA Modules:
  0.0 58.1 jit_solution(12432749936908534069)
XLA Ops:
  0.0 0.7 %collective-permute-start.2 = (bf16[128,3456]{1,0:T(8,128)(2,1)}, bf16[128,3456]{1,0:T(8,128)(2,1)S(1)}, u32[]{:S(2)}, u32[]{:S(2)}) collective-permute-start(bf16[128,3456]{1,0:T(8,128)(2,1)} %own_ref.3), channel_id=1, source_target_pairs={{0,1},{1,0},{2,3},{3,2},{4,5},{5,4},{6,7},{7,6},{8,9},{9,8},{10,11... | collective-permute-start | bytes 2654216 | tf_op jit(solution)/shard_map/ppermute | solution.py:663
  0.7 0.0 collective-permute-start
  0.7 0.8 %maximum_bitcast_fusion.own_scales_ref = f32[3,128]{1,0:T(4,128)S(1)} fusion(f32[128]{0:T(128)} %param.18, f32[128]{0:T(128)} %param.17, f32[64]{0:T(128)} %param.15, f32[64]{0:T(128)} %param.14), kind=kLoop, calls=%fused_computation | loop fusion | flops 1152 | bytes 3072 | tf_op jit(solution)/shard_map/reshape | solution.py:668
  1.5 0.5 collective-permute-start.1
  2.0 0.0 copy-start.1
  2.0 0.9 %copy-done.1 = bf16[256,256]{1,0:T(8,128)(2,1)S(1)} copy-done((bf16[256,256]{1,0:T(8,128)(2,1)S(1)}, bf16[256,256]{1,0:T(8,128)(2,1)}, u32[]{:S(2)}) %copy-start.1) | copy-done | bytes 131096
  2.9 0.0 copy-start.4
  2.9 5.2 %three_picks.1 = (bf16[25,192,256]{2,1,0:T(8,128)(2,1)S(1)}, bf16[25,192,256]{2,1,0:T(8,128)(2,1)S(1)}) custom-call(s32[1]{0:T(128)} %bitcast.core_ref, bf16[1,64,16,24,512]{4,3,2,1,0:T(8,128)(2,1)} %x_ref.1, bf16[1,64,16,24,512]{4,3,2,1,0:T(8,128)(2,1)} %x_ref.1, bf16[1,64,16,24,512]{4,3,2,1,0:T(8,128)(2,1)} %x_ref.1, bf16[256,256]{1,0:T(8,128)(2,1)S(1)} %copy-done.1), custom_call_target="tpu_custom_call" | custom-call | flops 1000000000 | bytes 10000000 | tf_op jit(solution)/shard_map/three_picks/pallas_call | solution.py:188
  8.0 0.0 copy-start.2
  8.1 0.0 collective-permute-done.1.other_scales_ref
  8.1 0.0 collective-permute-done.other_ref
  8.1 0.0 collective-permute-done.2.other_ref
  8.1 0.0 copy-done.4
  8.1 1.3 %three_edges.1 = (bf16[12,128,256]{2,1,0:T(8,128)(2,1)S(1)}, bf16[128,1728]{1,0:T(8,128)(2,1)S(1)}, f32[128,1]{1,0:T(8,128)S(1)}, f32[128,1]{1,0:T(8,128)S(1)}, f32[128,128]{1,0:T(8,128)S(1)}) custom-call(s32[1]{0:T(128)} %bitcast.core_ref, bf16[25,192,256]{2,1,0:T(8,128)(2,1)S(1)} %get-tuple-element.30.picked_ref, bf16[64,1728]{1,0:T(8,128)(2,1)S(1)} %copy-done.4, ...), custom_call_target="tpu_custom_call" | custom-call | flops 1000000000 | bytes 1000000 | tf_op jit(solution)/shard_map/three_edges/pallas_call | solution.py:271
  9.4 1.5 %collective-permute-start.3 = (bf16[12,128,256]{2,1,0:T(8,128)(2,1)S(1)}, bf16[12,128,256]{2,1,0:T(8,128)(2,1)S(1)}, u32[]{:S(2)}, u32[]{:S(2)}) collective-permute-start(bf16[12,128,256]{2,1,0:T(8,128)(2,1)S(1)} %get-tuple-element.39), channel_id=1, source_target_pairs={{0,3},{2,5},{4,7},{6,9},{8,11},{10,13},{12,15},{16,19},{18,21},{20... | collective-permute-start | bytes 2359304 | tf_op jit(solution)/shard_map/ppermute | solution.py:659
  10.9 0.0 copy-done.2
  10.9 0.0 copy-start.3
  10.9 17.1 %layer_three.1 = (bf16[4,12,128,256]{3,2,1,0:T(8,128)(2,1)}, f32[12,128,256]{2,1,0:T(8,128)S(1)}, f32[4,128,256]{2,1,0:T(8,128)S(1)}, bf16[12,128,256]{2,1,0:T(8,128)(2,1)S(1)}) custom-call(s32[1]{0:T(128)} %bitcast.core_ref, bf16[1,64,16,24,512]{4,3,2,1,0:T(8,128)(2,1)} %x_ref.1, bf16[25,192,256]{2,1,0:T(8,128)(2,1)S(1)} %get-tuple-element.29.before_ref, ...), custom_call_target="tpu_custom_call" | custom-call | flops 10000000000 | bytes 20000000 | tf_op jit(solution)/shard_map/layer_three/pallas_call | solution.py:367
  28.0 0.0 copy-start
  28.0 3.2 %collective-permute-done.3.refs_3_ = bf16[12,128,256]{2,1,0:T(8,128)(2,1)S(1)} collective-permute-done((bf16[12,128,256]{2,1,0:T(8,128)(2,1)S(1)}, bf16[12,128,256]{2,1,0:T(8,128)(2,1)S(1)}, u32[]{:S(2)}, u32[]{:S(2)}) %collective-permute-start.3) | collective-permute-done | bytes 786464 | tf_op jit(solution)/shard_map/ppermute | solution.py:659
  31.2 2.2 %collective-permute-start.4 = (bf16[12,128,256]{2,1,0:T(8,128)(2,1)S(1)}, bf16[12,128,256]{2,1,0:T(8,128)(2,1)S(1)}, u32[]{:S(2)}, u32[]{:S(2)}) collective-permute-start(bf16[12,128,256]{2,1,0:T(8,128)(2,1)S(1)} %get-tuple-element.42), channel_id=1, source_target_pairs={{0,1},{1,0},{2,3},{3,2},{4,5},{5,4},{6,7},{7,6},{8,9},{9,8},{10,11... | collective-permute-start | bytes 2359304 | tf_op jit(solution)/shard_map/ppermute | solution.py:663
  33.3 0.0 copy-done.3
  33.3 1.2 %four_weights.1.refs_7_.refs_8_ = bf16[256,3456]{1,0:T(8,128)(2,1)S(1)} custom-call(s32[1]{0:T(128)} %bitcast.core_ref, bf16[128,3456]{1,0:T(8,128)(2,1)S(1)} %copy-done.3, bf16[128,3456]{1,0:T(8,128)(2,1)S(1)} %collective-permute-done.2.other_ref), custom_call_target="tpu_custom_call" | custom-call | flops 1000 | bytes 1000 | tf_op jit(solution)/shard_map/four_weights/pallas_call | solution.py:110
  34.6 0.7 %collective-permute-done.4.refs_6_.refs_7_ = bf16[12,128,256]{2,1,0:T(8,128)(2,1)S(1)} collective-permute-done((bf16[12,128,256]{2,1,0:T(8,128)(2,1)S(1)}, bf16[12,128,256]{2,1,0:T(8,128)(2,1)S(1)}, u32[]{:S(2)}, u32[]{:S(2)}) %collective-permute-start.4) | collective-permute-done | bytes 786464 | tf_op jit(solution)/shard_map/ppermute | solution.py:663
  35.3 0.0 copy-done
  35.3 1.2 %four_edges.1 = (bf16[7,256,128]{2,1,0:T(8,128)(2,1)S(1)}, bf16[256,384]{1,0:T(8,128)(2,1)S(1)}, bf16[4,128,256]{2,1,0:T(8,128)(2,1)S(1)}) custom-call(s32[1]{0:T(128)} %bitcast.core_ref, bf16[4,12,128,256]{3,2,1,0:T(8,128)(2,1)S(1)} %copy-done, f32[12,128,256]{2,1,0:T(8,128)S(1)} %get-tuple-element.37.refs_1_, ...), custom_call_target="tpu_custom_call" | custom-call | flops 1000000000 | bytes 1000000 | tf_op jit(solution)/shard_map/four_edges/pallas_call | solution.py:485
  36.5 2.0 %collective-permute-start.5 = (bf16[4,128,256]{2,1,0:T(8,128)(2,1)S(1)}, bf16[4,128,256]{2,1,0:T(8,128)(2,1)S(1)}, u32[]{:S(2)}, u32[]{:S(2)}) collective-permute-start(bf16[4,128,256]{2,1,0:T(8,128)(2,1)S(1)} %get-tuple-element.44), channel_id=1, source_target_pairs={{1,0},{3,2},{5,4},{7,6},{9,8},{11,10},{13,12},{15,14},{17,16},{19,... | collective-permute-start | bytes 786440 | tf_op jit(solution)/shard_map/ppermute | solution.py:682
  38.5 1.3 %collective-permute-start.7 = (bf16[7,256,128]{2,1,0:T(8,128)(2,1)S(1)}, bf16[7,256,128]{2,1,0:T(8,128)(2,1)S(1)}, u32[]{:S(2)}, u32[]{:S(2)}) collective-permute-start(bf16[7,256,128]{2,1,0:T(8,128)(2,1)S(1)} %get-tuple-element.47), channel_id=1, source_target_pairs={{0,3},{2,5},{4,7},{6,9},{8,11},{10,13},{12,15},{16,19},{18,21},{20... | collective-permute-start | bytes 1376264 | tf_op jit(solution)/shard_map/ppermute | solution.py:659
  39.8 0.0 collective-permute-done.5.refs_6_
  39.8 4.8 %layer_four.1 = (f32[6,128,256]{2,1,0:T(8,128)S(1)}, f32[6,128,256]{2,1,0:T(8,128)S(1)}, f32[128,256]{1,0:T(8,128)S(1)}) custom-call(s32[1]{0:T(128)} %bitcast.core_ref, bf16[4,12,128,256]{3,2,1,0:T(8,128)(2,1)S(1)} %copy-done, f32[12,128,256]{2,1,0:T(8,128)S(1)} %get-tuple-element.37.refs_1_, f32[4,128,256]{2,1,0:T(8,128)S(1)} %get-tuple-element.38.refs_2_, ...), custom_call_target="tpu_custom_call" | custom-call | flops 4000000000 | bytes 4000000 | tf_op jit(solution)/shard_map/layer_four/pallas_call | solution.py:550
  44.7 2.0 %collective-permute-start.6 = (f32[6,128,256]{2,1,0:T(8,128)S(1)}, f32[6,128,256]{2,1,0:T(8,128)S(1)}, u32[]{:S(2)}, u32[]{:S(2)}) collective-permute-start(f32[6,128,256]{2,1,0:T(8,128)S(1)} %get-tuple-element.46), channel_id=1, source_target_pairs={{0,1},{1,0},{2,3},{3,2},{4,5},{5,4},{6,7},{7,6},{8,9},{9,8},{10,11... | collective-permute-start | bytes 2359304 | tf_op jit(solution)/shard_map/ppermute | solution.py:663
  46.6 8.2 %collective-permute-done.7.halo_ref = bf16[7,256,128]{2,1,0:T(8,128)(2,1)S(1)} collective-permute-done((bf16[7,256,128]{2,1,0:T(8,128)(2,1)S(1)}, bf16[7,256,128]{2,1,0:T(8,128)(2,1)S(1)}, u32[]{:S(2)}, u32[]{:S(2)}) %collective-permute-start.7) | collective-permute-done | bytes 458784 | tf_op jit(solution)/shard_map/ppermute | solution.py:659
  54.9 0.1 collective-permute-start.8
  55.0 1.7 %collective-permute-done.8.shares_ref = f32[6,128,128]{2,1,0:T(8,128)S(1)} collective-permute-done((f32[6,128,128]{2,1,0:T(8,128)S(1)}, f32[6,128,128]{2,1,0:T(8,128)S(1)}, u32[]{:S(2)}, u32[]{:S(2)}) %collective-permute-start.8) | collective-permute-done | bytes 393248 | tf_op jit(solution)/shard_map/ppermute | solution.py:663
  56.7 0.0 collective-permute-done.6.got_ref
  56.7 1.4 %assemble.1 = bf16[3072,128]{1,0:T(8,128)(2,1)} custom-call(s32[1]{0:T(128)} %bitcast.core_ref, f32[6,128,256]{2,1,0:T(8,128)S(1)} %get-tuple-element.45.own_ref, f32[6,128,256]{2,1,0:T(8,128)S(1)} %collective-permute-done.6.got_ref, bf16[7,256,128]{2,1,0:T(8,128)(2,1)S(1)} %collective-permute-done.7.halo_ref, f32[128,128]{1,0:T(8,128)S(1)} %get-tuple-element.50.fix_ref, ...), custom_call_target="tpu_custom_call" | custom-call | tf_op jit(solution)/shard_map/assemble/pallas_call | solution.py:645
  (1 shorter events, 0.0 us)
Async XLA Ops:
  0.0 8.1 %collective-permute-start.2 = (bf16[128,3456]{1,0:T(8,128)(2,1)}, bf16[128,3456]{1,0:T(8,128)(2,1)S(1)}, u32[]{:S(2)}, u32[]{:S(2)}) collective-permute-start(bf16[128,3456]{1,0:T(8,128)(2,1)} %own_ref.3), channel_id=1, source_target_pairs={{0,1},{1,0},{2,3},{3,2},{4,5},{5,4},{6,7},{7,6},{8,9},{9,8},{10,11... | collective-permute-start | bytes 2654216 | tf_op jit(solution)/shard_map/ppermute | solution.py:663
  0.7 7.4 %collective-permute-start = (bf16[64,1728]{1,0:T(8,128)(2,1)}, bf16[64,1728]{1,0:T(8,128)(2,1)S(1)}, u32[]{:S(2)}, u32[]{:S(2)}) collective-permute-start(bf16[64,1728]{1,0:T(8,128)(2,1)} %own_ref.2), channel_id=1, source_target_pairs={{0,1},{1,0},{2,3},{3,2},{4,5},{5,4},{6,7},{7,6},{8,9},{9,8},{10,11... | collective-permute-start | bytes 663560 | tf_op jit(solution)/shard_map/ppermute | solution.py:663
  1.5 6.6 %collective-permute-start.1 = (f32[3,128]{1,0:T(4,128)S(1)}, f32[3,128]{1,0:T(4,128)S(1)}, u32[]{:S(2)}, u32[]{:S(2)}) collective-permute-start(f32[3,128]{1,0:T(4,128)S(1)} %maximum_bitcast_fusion.own_scales_ref), channel_id=1, source_target_pairs={{0,1},{1,0},{2,3},{3,2},{4,5},{5,4},{6,7},{7,6},{8,9},{9,8},{10,11... | collective-permute-start | bytes 4616 | tf_op jit(solution)/shard_map/ppermute | solution.py:663
  2.0 0.9 %copy-start.1 = (bf16[256,256]{1,0:T(8,128)(2,1)S(1)}, bf16[256,256]{1,0:T(8,128)(2,1)}, u32[]{:S(2)}) copy-start(bf16[256,256]{1,0:T(8,128)(2,1)} %constant.6.clone.place_ref.refs_8_.refs_9_) | copy-start | bytes 393220
  2.9 5.2 %copy-start.4 = (bf16[64,1728]{1,0:T(8,128)(2,1)S(1)}, bf16[64,1728]{1,0:T(8,128)(2,1)}, u32[]{:S(2)}) copy-start(bf16[64,1728]{1,0:T(8,128)(2,1)} %own_ref.2) | copy-start | bytes 663556
  8.0 2.9 %copy-start.2 = (bf16[256,256]{1,0:T(8,128)(2,1)S(1)}, bf16[256,256]{1,0:T(8,128)(2,1)}, u32[]{:S(2)}) copy-start(bf16[256,256]{1,0:T(8,128)(2,1)} %constant.6.clone.place_ref.refs_8_.refs_9_) | copy-start | bytes 393220
  9.4 21.8 %collective-permute-start.3 = (bf16[12,128,256]{2,1,0:T(8,128)(2,1)S(1)}, bf16[12,128,256]{2,1,0:T(8,128)(2,1)S(1)}, u32[]{:S(2)}, u32[]{:S(2)}) collective-permute-start(bf16[12,128,256]{2,1,0:T(8,128)(2,1)S(1)} %get-tuple-element.39), channel_id=1, source_target_pairs={{0,3},{2,5},{4,7},{6,9},{8,11},{10,13},{12,15},{16,19},{18,21},{20... | collective-permute-start | bytes 2359304 | tf_op jit(solution)/shard_map/ppermute | solution.py:659
  10.9 22.4 %copy-start.3 = (bf16[128,3456]{1,0:T(8,128)(2,1)S(1)}, bf16[128,3456]{1,0:T(8,128)(2,1)}, u32[]{:S(2)}) copy-start(bf16[128,3456]{1,0:T(8,128)(2,1)} %own_ref.3) | copy-start | bytes 2654212
  28.0 7.3 %copy-start = (bf16[4,12,128,256]{3,2,1,0:T(8,128)(2,1)S(1)}, bf16[4,12,128,256]{3,2,1,0:T(8,128)(2,1)}, u32[]{:S(2)}) copy-start(bf16[4,12,128,256]{3,2,1,0:T(8,128)(2,1)} %get-tuple-element.36.refs_0_) | copy-start | bytes 9437188
  31.2 4.1 %collective-permute-start.4 = (bf16[12,128,256]{2,1,0:T(8,128)(2,1)S(1)}, bf16[12,128,256]{2,1,0:T(8,128)(2,1)S(1)}, u32[]{:S(2)}, u32[]{:S(2)}) collective-permute-start(bf16[12,128,256]{2,1,0:T(8,128)(2,1)S(1)} %get-tuple-element.42), channel_id=1, source_target_pairs={{0,1},{1,0},{2,3},{3,2},{4,5},{5,4},{6,7},{7,6},{8,9},{9,8},{10,11... | collective-permute-start | bytes 2359304 | tf_op jit(solution)/shard_map/ppermute | solution.py:663
  36.5 3.3 %collective-permute-start.5 = (bf16[4,128,256]{2,1,0:T(8,128)(2,1)S(1)}, bf16[4,128,256]{2,1,0:T(8,128)(2,1)S(1)}, u32[]{:S(2)}, u32[]{:S(2)}) collective-permute-start(bf16[4,128,256]{2,1,0:T(8,128)(2,1)S(1)} %get-tuple-element.44), channel_id=1, source_target_pairs={{1,0},{3,2},{5,4},{7,6},{9,8},{11,10},{13,12},{15,14},{17,16},{19,... | collective-permute-start | bytes 786440 | tf_op jit(solution)/shard_map/ppermute | solution.py:682
  38.5 16.4 %collective-permute-start.7 = (bf16[7,256,128]{2,1,0:T(8,128)(2,1)S(1)}, bf16[7,256,128]{2,1,0:T(8,128)(2,1)S(1)}, u32[]{:S(2)}, u32[]{:S(2)}) collective-permute-start(bf16[7,256,128]{2,1,0:T(8,128)(2,1)S(1)} %get-tuple-element.47), channel_id=1, source_target_pairs={{0,3},{2,5},{4,7},{6,9},{8,11},{10,13},{12,15},{16,19},{18,21},{20... | collective-permute-start | bytes 1376264 | tf_op jit(solution)/shard_map/ppermute | solution.py:659
  44.7 12.1 %collective-permute-start.6 = (f32[6,128,256]{2,1,0:T(8,128)S(1)}, f32[6,128,256]{2,1,0:T(8,128)S(1)}, u32[]{:S(2)}, u32[]{:S(2)}) collective-permute-start(f32[6,128,256]{2,1,0:T(8,128)S(1)} %get-tuple-element.46), channel_id=1, source_target_pairs={{0,1},{1,0},{2,3},{3,2},{4,5},{5,4},{6,7},{7,6},{8,9},{9,8},{10,11... | collective-permute-start | bytes 2359304 | tf_op jit(solution)/shard_map/ppermute | solution.py:663
  54.9 1.8 %collective-permute-start.8 = (f32[6,128,128]{2,1,0:T(8,128)S(1)}, f32[6,128,128]{2,1,0:T(8,128)S(1)}, u32[]{:S(2)}, u32[]{:S(2)}) collective-permute-start(f32[6,128,128]{2,1,0:T(8,128)S(1)} %get-tuple-element.52), channel_id=1, source_target_pairs={{0,1},{1,0},{2,3},{3,2},{4,5},{5,4},{6,7},{7,6},{8,9},{9,8},{10,11... | collective-permute-start | bytes 1179656 | tf_op jit(solution)/shard_map/ppermute | solution.py:663

commit v8 on v7

--- a/solution.py
+++ b/solution.py
@@ -431,10 +431,9 @@
 
 
 def four_edges_kernel(core_ref, *refs):
-    *thirds, local_ref, w_ref, place_ref, message_ref, mid_ref, rows_ref = refs
+    *thirds, local_ref, w_ref, place_ref, message_ref, mid_ref = refs
     core = core_ref[0]
     planes, rows, chans, width = thirds[0].shape
-    rows_ref[...] = thirds[3][:planes]
     half = width // 2
     out_rows = rows // 2
     taps = 3 * chans
@@ -487,7 +486,6 @@
         out_shape=[
             jax.ShapeDtypeStruct((rows // 2 + 1, outs, half), BF16),
             jax.ShapeDtypeStruct((outs, 3 * chans), BF16),
-            jax.ShapeDtypeStruct((planes, chans, width), BF16),
         ],
         in_specs=inputs(len(thirds) + 3),
         compiler_params=pltpu.CompilerParams(vmem_limit_bytes=24 * MIB),
@@ -497,10 +495,11 @@
 
 
 def four_kernel(core_ref, *refs):
-    *thirds, rows_ref, local_ref, w_ref, place_ref, own_ref, theirs_ref, corner_ref, data_ref = refs
+    *thirds, local_ref, w_ref, place_ref, own_ref, theirs_ref, corner_ref, data_ref = refs
     core = core_ref[0]
     planes, rows, chans, width = thirds[0].shape
     halo_ref, gain_ref, shift_ref = thirds[3:]
+    rows_ref = local_ref.at[planes : 2 * planes]
     half = width // 2
     out_rows, count = rows // 2, planes // 2
     taps = 3 * chans
@@ -542,7 +541,7 @@
         theirs_ref[row] = jnp.where(core == 0, total[LANES:], total[:LANES])
 
 
-def layer_four(core, thirds, rows_before, local, weights):
+def layer_four(core, thirds, local, weights):
     planes, rows, chans, width = thirds[0].shape
     outs = weights.shape[0]
     half = width // 2
@@ -554,12 +553,12 @@
             jax.ShapeDtypeStruct((out_rows, outs // 2, count * half), F32),
             jax.ShapeDtypeStruct((chans, width), F32),
         ],
-        in_specs=inputs(len(thirds) + 4),
+        in_specs=inputs(len(thirds) + 3),
         scratch_shapes=[pltpu.VMEM((3, rows + 1, 3 * chans, count * half), BF16)],
         compiler_params=pltpu.CompilerParams(vmem_limit_bytes=32 * MIB),
         cost_estimate=pl.CostEstimate(flops=4 * 10**9, bytes_accessed=4 * 10**6, transcendentals=0),
         name="layer_four",
-    )(core, *thirds, rows_before, local, weights, even_odd(width))
+    )(core, *thirds, local, weights, even_odd(width))
 
 
 def shares_kernel(core_ref, corner_ref, halo_ref, mid_ref, place_ref, gain_ref, shift_ref, shares_ref, fix_ref):
@@ -671,16 +670,17 @@
     message, weights_three, gain, shift, scales = three_edges(
         picked, kernel_three, others[0], own_scales, others[1], core
     )
+    weights_three, kernel_four = lax.optimization_barrier((weights_three, kernel_four))
     halo = handed_on(message)
     *thirds, local = layer_three(volume, prior, weights_three, gain, shift, core)
-    halo, local = lax.optimization_barrier((halo, local))
+    planes = thirds[0].shape[0]
+    passed = jnp.where(core[0] == 1, halo[:planes], local[planes : 2 * planes])
+    local = swapped(lax.dynamic_update_slice(local, passed, (planes, 0, 0)))
     thirds = (*thirds, halo, gain, shift)
-    local = swapped(local)
     weights_four = four_weights(kernel_four, others[2], core)
-    message, mid, rows = four_edges(core, thirds, local, weights_four)
+    message, mid = four_edges(core, thirds, local, weights_four)
     halo = handed_on(message)
-    rows = lax.ppermute(rows, "fl", [(1, 0)])
-    own, theirs, corner = layer_four(core, thirds, rows, local, weights_four)
+    own, theirs, corner = layer_four(core, thirds, local, weights_four)
     lines = last_stage(core, own, theirs, corner, halo, mid, gain, shift, scales)
     out_rows, outs, lanes = own.shape
     fourth = lines.reshape(outs, out_rows, 2 * lanes // LANES, LANES)

time: 58.3 us -> 61.7 us (1.058)
  local copies, waits for them, and re-layouts: 0.92 us -> 5.04 us
  starting transfers between devices: 10.2 us -> 8.21 us
  Pallas kernels: 32.2 us -> 33 us
    unnamed x10 -> x14, local copies, waits for them, and re-layouts: 0.92 us -> 5.04 us
    ppermute x1 -> x0, starting transfers between devices: 2.03 us -> none  [shards(): rows = lax.ppermute(rows, 'fl', [(1, 0)])]
    pallas_call x1, Pallas kernels: 1.33 us -> 2.27 us  [three_edges(): pl.pallas_call(three_edges_kernel, in_specs=inputs(5), out_shape=[jax.Sha...]
  transfers between devices with their start and end apart: 9 -> 8, of which waited for: 4 -> 4; matrix products, arithmetic and copies ran while one was open for 1% -> 1% of each run, Pallas kernels for 49% -> 46%
where the time goes in v8:
time: 61.7 us; the launch traced here: 61.4 us
  Pallas kernels  33 us (53%)
  waiting for transfers between devices  14.1 us (23%)
  starting transfers between devices  8.21 us (13%)
  local copies, waits for them, and re-layouts  5.04 us (8%)
  other arithmetic  0.88 us (1%)
    pallas_call x1, Pallas kernels, layer_three(): pl.pallas_call(three_kernel, grid_spec=pltpu.PrefetchScalarGridSpec(num_s...  17 us
    ppermute x2, waiting for transfers between devices, handed_on(): return lax.ppermute(message, ('sp', 'fl'), pairs)  11.7 us
    ppermute x6, starting transfers between devices, swapped(): return lax.ppermute(value, 'fl', [(0, 1), (1, 0)])  5.45 us
    pallas_call x1, Pallas kernels, three_picks(): pl.pallas_call(three_picks_kernel, grid_spec=pltpu.PrefetchScalarGridSpec...  5.13 us
    unnamed x14, local copies, waits for them, and re-layouts  5.04 us
    pallas_call x1, Pallas kernels, layer_four(): pl.pallas_call(four_kernel, out_shape=[jax.ShapeDtypeStruct((out_rows, ou...  4.85 us
    ppermute x2, starting transfers between devices, handed_on(): return lax.ppermute(message, ('sp', 'fl'), pairs)  2.76 us
    ppermute x6, waiting for transfers between devices, swapped(): return lax.ppermute(value, 'fl', [(0, 1), (1, 0)])  2.39 us
  transfers between devices with their start and end apart: 8, of which 4 were waited for; matrix products, arithmetic and copies ran while one was open for 1% of the time, Pallas kernels for 46%

profile of v8, /device:TPU:25, one launch (start us, length us, event | category | flops | bytes accessed | tf_op | source)
XLA Modules:
  0.0 61.4 jit_solution(2998281633017750687)
XLA Ops:
  0.0 0.7 %collective-permute-start.2 = (bf16[128,3456]{1,0:T(8,128)(2,1)}, bf16[128,3456]{1,0:T(8,128)(2,1)S(1)}, u32[]{:S(2)}, u32[]{:S(2)}) collective-permute-start(bf16[128,3456]{1,0:T(8,128)(2,1)} %own_ref.2), channel_id=1, source_target_pairs={{0,1},{1,0},{2,3},{3,2},{4,5},{5,4},{6,7},{7,6},{8,9},{9,8},{10,11... | collective-permute-start | bytes 2654216 | tf_op jit(solution)/shard_map/ppermute | solution.py:662
  0.7 0.0 collective-permute-start
  0.7 0.8 %maximum_bitcast_fusion.own_scales_ref = f32[3,128]{1,0:T(4,128)S(1)} fusion(f32[128]{0:T(128)} %param.18, f32[128]{0:T(128)} %param.17, f32[64]{0:T(128)} %param.15, f32[64]{0:T(128)} %param.14), kind=kLoop, calls=%fused_computation.2 | loop fusion | flops 1152 | bytes 3072 | tf_op jit(solution)/shard_map/reshape | solution.py:667
  1.5 0.5 collective-permute-start.1
  2.0 0.0 copy-start.1
  2.0 0.9 %copy-done.1 = bf16[256,256]{1,0:T(8,128)(2,1)S(1)} copy-done((bf16[256,256]{1,0:T(8,128)(2,1)S(1)}, bf16[256,256]{1,0:T(8,128)(2,1)}, u32[]{:S(2)}) %copy-start.1) | copy-done | bytes 131096
  2.9 5.1 %three_picks.1 = (bf16[25,192,256]{2,1,0:T(8,128)(2,1)S(1)}, bf16[25,192,256]{2,1,0:T(8,128)(2,1)S(1)}) custom-call(s32[1]{0:T(128)} %bitcast.core_ref, bf16[1,64,16,24,512]{4,3,2,1,0:T(8,128)(2,1)} %x_ref.1, bf16[1,64,16,24,512]{4,3,2,1,0:T(8,128)(2,1)} %x_ref.1, bf16[1,64,16,24,512]{4,3,2,1,0:T(8,128)(2,1)} %x_ref.1, bf16[256,256]{1,0:T(8,128)(2,1)S(1)} %copy-done.1), custom_call_target="tpu_custom_call" | custom-call | flops 1000000000 | bytes 10000000 | tf_op jit(solution)/shard_map/three_picks/pallas_call | solution.py:188
  8.0 0.0 copy-start.4
  8.0 1.5 %copy-done.4 = bf16[25,192,256]{2,1,0:T(8,128)(2,1)} copy-done((bf16[25,192,256]{2,1,0:T(8,128)(2,1)}, bf16[25,192,256]{2,1,0:T(8,128)(2,1)S(1)}, u32[]{:S(2)}) %copy-start.4) | copy-done | bytes 2457624
  9.5 0.0 copy-start.2
  9.5 0.0 collective-permute-done.1.other_scales_ref
  9.5 0.0 collective-permute-done.other_ref
  9.5 0.0 collective-permute-done.2.other_ref
  9.5 0.0 copy-start.5
  9.5 1.7 %copy-done.5 = bf16[25,192,256]{2,1,0:T(8,128)(2,1)S(1)} copy-done((bf16[25,192,256]{2,1,0:T(8,128)(2,1)S(1)}, bf16[25,192,256]{2,1,0:T(8,128)(2,1)}, u32[]{:S(2)}) %copy-start.5) | copy-done | bytes 2457624
  11.2 0.0 copy-start.6
  11.2 0.9 %copy-done.6 = bf16[64,1728]{1,0:T(8,128)(2,1)S(1)} copy-done((bf16[64,1728]{1,0:T(8,128)(2,1)S(1)}, bf16[64,1728]{1,0:T(8,128)(2,1)}, u32[]{:S(2)}) %copy-start.6) | copy-done | bytes 221208
  12.2 2.3 %three_edges.1 = (bf16[12,128,256]{2,1,0:T(8,128)(2,1)S(1)}, bf16[128,1728]{1,0:T(8,128)(2,1)S(1)}, f32[128,1]{1,0:T(8,128)S(1)}, f32[128,1]{1,0:T(8,128)S(1)}, f32[128,128]{1,0:T(8,128)S(1)}) custom-call(s32[1]{0:T(128)} %bitcast.core_ref, bf16[25,192,256]{2,1,0:T(8,128)(2,1)S(1)} %copy-done.5, bf16[64,1728]{1,0:T(8,128)(2,1)S(1)} %copy-done.6, ...), custom_call_target="tpu_custom_call" | custom-call | flops 1000000000 | bytes 1000000 | tf_op jit(solution)/shard_map/three_edges/pallas_call | solution.py:271
  14.5 1.5 %collective-permute-start.3 = (bf16[12,128,256]{2,1,0:T(8,128)(2,1)S(1)}, bf16[12,128,256]{2,1,0:T(8,128)(2,1)S(1)}, u32[]{:S(2)}, u32[]{:S(2)}) collective-permute-start(bf16[12,128,256]{2,1,0:T(8,128)(2,1)S(1)} %get-tuple-element.39), channel_id=1, source_target_pairs={{0,3},{2,5},{4,7},{6,9},{8,11},{10,13},{12,15},{16,19},{18,21},{20... | collective-permute-start | bytes 2359304 | tf_op jit(solution)/shard_map/ppermute | solution.py:658
  15.9 0.0 copy-done.2
  15.9 0.0 copy-start.3
  16.0 17.0 %layer_three.1 = (bf16[4,12,128,256]{3,2,1,0:T(8,128)(2,1)}, f32[12,128,256]{2,1,0:T(8,128)S(1)}, f32[4,128,256]{2,1,0:T(8,128)S(1)}, bf16[12,128,256]{2,1,0:T(8,128)(2,1)S(1)}) custom-call(s32[1]{0:T(128)} %bitcast.core_ref, bf16[1,64,16,24,512]{4,3,2,1,0:T(8,128)(2,1)} %x_ref.1, bf16[25,192,256]{2,1,0:T(8,128)(2,1)S(1)} %get-tuple-element.28.before_ref, ...), custom_call_target="tpu_custom_call" | custom-call | flops 10000000000 | bytes 20000000 | tf_op jit(solution)/shard_map/layer_three/pallas_call | solution.py:367
  32.9 0.0 copy-start
  32.9 3.3 %collective-permute-done.3.refs_3_ = bf16[12,128,256]{2,1,0:T(8,128)(2,1)S(1)} collective-permute-done((bf16[12,128,256]{2,1,0:T(8,128)(2,1)S(1)}, bf16[12,128,256]{2,1,0:T(8,128)(2,1)S(1)}, u32[]{:S(2)}, u32[]{:S(2)}) %collective-permute-start.3) | collective-permute-done | bytes 786464 | tf_op jit(solution)/shard_map/ppermute | solution.py:658
  36.2 0.1 fusion
  36.3 2.2 %collective-permute-start.4 = (bf16[12,128,256]{2,1,0:T(8,128)(2,1)S(1)}, bf16[12,128,256]{2,1,0:T(8,128)(2,1)S(1)}, u32[]{:S(2)}, u32[]{:S(2)}) collective-permute-start(bf16[12,128,256]{2,1,0:T(8,128)(2,1)S(1)} %fusion), channel_id=1, source_target_pairs={{0,1},{1,0},{2,3},{3,2},{4,5},{5,4},{6,7},{7,6},{8,9},{9,8},{10,11... | collective-permute-start | bytes 2359304 | tf_op jit(solution)/shard_map/ppermute | solution.py:662
  38.5 0.0 copy-done.3
  38.5 1.2 %four_weights.1.refs_7_ = bf16[256,3456]{1,0:T(8,128)(2,1)S(1)} custom-call(s32[1]{0:T(128)} %bitcast.core_ref, bf16[128,3456]{1,0:T(8,128)(2,1)S(1)} %copy-done.3, bf16[128,3456]{1,0:T(8,128)(2,1)S(1)} %collective-permute-done.2.other_ref), custom_call_target="tpu_custom_call" | custom-call | flops 1000 | bytes 1000 | tf_op jit(solution)/shard_map/four_weights/pallas_call | solution.py:110
  39.8 0.7 %collective-permute-done.4.refs_6_ = bf16[12,128,256]{2,1,0:T(8,128)(2,1)S(1)} collective-permute-done((bf16[12,128,256]{2,1,0:T(8,128)(2,1)S(1)}, bf16[12,128,256]{2,1,0:T(8,128)(2,1)S(1)}, u32[]{:S(2)}, u32[]{:S(2)}) %collective-permute-start.4) | collective-permute-done | bytes 786464 | tf_op jit(solution)/shard_map/ppermute | solution.py:662
  40.4 0.0 copy-done
  40.4 1.2 %four_edges.1 = (bf16[7,256,128]{2,1,0:T(8,128)(2,1)S(1)}, bf16[256,384]{1,0:T(8,128)(2,1)S(1)}) custom-call(s32[1]{0:T(128)} %bitcast.core_ref, bf16[4,12,128,256]{3,2,1,0:T(8,128)(2,1)S(1)} %copy-done, f32[12,128,256]{2,1,0:T(8,128)S(1)} %get-tuple-element.37.refs_1_, f32[4,128,256]{2,1,0:T(8,128)S(1)} %get-tuple-element.38.refs_2_, ...), custom_call_target="tpu_custom_call" | custom-call | flops 1000000000 | bytes 1000000 | tf_op jit(solution)/shard_map/four_edges/pallas_call | solution.py:484
  41.6 1.3 %collective-permute-start.6 = (bf16[7,256,128]{2,1,0:T(8,128)(2,1)S(1)}, bf16[7,256,128]{2,1,0:T(8,128)(2,1)S(1)}, u32[]{:S(2)}, u32[]{:S(2)}) collective-permute-start(bf16[7,256,128]{2,1,0:T(8,128)(2,1)S(1)} %get-tuple-element.45), channel_id=1, source_target_pairs={{0,3},{2,5},{4,7},{6,9},{8,11},{10,13},{12,15},{16,19},{18,21},{20... | collective-permute-start | bytes 1376264 | tf_op jit(solution)/shard_map/ppermute | solution.py:658
  42.9 4.8 %layer_four.1 = (f32[6,128,256]{2,1,0:T(8,128)S(1)}, f32[6,128,256]{2,1,0:T(8,128)S(1)}, f32[128,256]{1,0:T(8,128)S(1)}) custom-call(s32[1]{0:T(128)} %bitcast.core_ref, bf16[4,12,128,256]{3,2,1,0:T(8,128)(2,1)S(1)} %copy-done, f32[12,128,256]{2,1,0:T(8,128)S(1)} %get-tuple-element.37.refs_1_, f32[4,128,256]{2,1,0:T(8,128)S(1)} %get-tuple-element.38.refs_2_, ...), custom_call_target="tpu_custom_call" | custom-call | flops 4000000000 | bytes 4000000 | tf_op jit(solution)/shard_map/layer_four/pallas_call | solution.py:549
  47.8 2.0 %collective-permute-start.5 = (f32[6,128,256]{2,1,0:T(8,128)S(1)}, f32[6,128,256]{2,1,0:T(8,128)S(1)}, u32[]{:S(2)}, u32[]{:S(2)}) collective-permute-start(f32[6,128,256]{2,1,0:T(8,128)S(1)} %get-tuple-element.44), channel_id=1, source_target_pairs={{0,1},{1,0},{2,3},{3,2},{4,5},{5,4},{6,7},{7,6},{8,9},{9,8},{10,11... | collective-permute-start | bytes 2359304 | tf_op jit(solution)/shard_map/ppermute | solution.py:662
  49.8 8.4 %collective-permute-done.6.halo_ref = bf16[7,256,128]{2,1,0:T(8,128)(2,1)S(1)} collective-permute-done((bf16[7,256,128]{2,1,0:T(8,128)(2,1)S(1)}, bf16[7,256,128]{2,1,0:T(8,128)(2,1)S(1)}, u32[]{:S(2)}, u32[]{:S(2)}) %collective-permute-start.6) | collective-permute-done | bytes 458784 | tf_op jit(solution)/shard_map/ppermute | solution.py:658
  58.2 0.1 collective-permute-start.7
  58.3 0.0 collective-permute-done.5.got_ref
  58.3 1.7 %collective-permute-done.7.shares_ref = f32[6,128,128]{2,1,0:T(8,128)S(1)} collective-permute-done((f32[6,128,128]{2,1,0:T(8,128)S(1)}, f32[6,128,128]{2,1,0:T(8,128)S(1)}, u32[]{:S(2)}, u32[]{:S(2)}) %collective-permute-start.7) | collective-permute-done | bytes 393248 | tf_op jit(solution)/shard_map/ppermute | solution.py:662
  60.0 1.4 %assemble.1 = bf16[3072,128]{1,0:T(8,128)(2,1)} custom-call(s32[1]{0:T(128)} %bitcast.core_ref, f32[6,128,256]{2,1,0:T(8,128)S(1)} %get-tuple-element.43.own_ref, f32[6,128,256]{2,1,0:T(8,128)S(1)} %collective-permute-done.5.got_ref, bf16[7,256,128]{2,1,0:T(8,128)(2,1)S(1)} %collective-permute-done.6.halo_ref, f32[128,128]{1,0:T(8,128)S(1)} %get-tuple-element.48.fix_ref, ...), custom_call_target="tpu_custom_call" | custom-call | tf_op jit(solution)/shard_map/assemble/pallas_call | solution.py:644
  (1 shorter events, 0.0 us)
Async XLA Ops:
  0.0 9.5 %collective-permute-start.2 = (bf16[128,3456]{1,0:T(8,128)(2,1)}, bf16[128,3456]{1,0:T(8,128)(2,1)S(1)}, u32[]{:S(2)}, u32[]{:S(2)}) collective-permute-start(bf16[128,3456]{1,0:T(8,128)(2,1)} %own_ref.2), channel_id=1, source_target_pairs={{0,1},{1,0},{2,3},{3,2},{4,5},{5,4},{6,7},{7,6},{8,9},{9,8},{10,11... | collective-permute-start | bytes 2654216 | tf_op jit(solution)/shard_map/ppermute | solution.py:662
  0.7 8.8 %collective-permute-start = (bf16[64,1728]{1,0:T(8,128)(2,1)}, bf16[64,1728]{1,0:T(8,128)(2,1)}, u32[]{:S(2)}, u32[]{:S(2)}) collective-permute-start(bf16[64,1728]{1,0:T(8,128)(2,1)} %own_ref.1), channel_id=1, source_target_pairs={{0,1},{1,0},{2,3},{3,2},{4,5},{5,4},{6,7},{7,6},{8,9},{9,8},{10,11... | collective-permute-start | bytes 663560 | tf_op jit(solution)/shard_map/ppermute | solution.py:662
  1.5 8.0 %collective-permute-start.1 = (f32[3,128]{1,0:T(4,128)S(1)}, f32[3,128]{1,0:T(4,128)S(1)}, u32[]{:S(2)}, u32[]{:S(2)}) collective-permute-start(f32[3,128]{1,0:T(4,128)S(1)} %maximum_bitcast_fusion.own_scales_ref), channel_id=1, source_target_pairs={{0,1},{1,0},{2,3},{3,2},{4,5},{5,4},{6,7},{7,6},{8,9},{9,8},{10,11... | collective-permute-start | bytes 4616 | tf_op jit(solution)/shard_map/ppermute | solution.py:662
  2.0 0.9 %copy-start.1 = (bf16[256,256]{1,0:T(8,128)(2,1)S(1)}, bf16[256,256]{1,0:T(8,128)(2,1)}, u32[]{:S(2)}) copy-start(bf16[256,256]{1,0:T(8,128)(2,1)} %constant.12.clone.place_ref.refs_8_) | copy-start | bytes 393220
  8.0 1.5 %copy-start.4 = (bf16[25,192,256]{2,1,0:T(8,128)(2,1)}, bf16[25,192,256]{2,1,0:T(8,128)(2,1)S(1)}, u32[]{:S(2)}) copy-start(bf16[25,192,256]{2,1,0:T(8,128)(2,1)S(1)} %get-tuple-element.29.picked_ref) | copy-start | bytes 7372804
  9.5 6.4 %copy-start.2 = (bf16[256,256]{1,0:T(8,128)(2,1)S(1)}, bf16[256,256]{1,0:T(8,128)(2,1)}, u32[]{:S(2)}) copy-start(bf16[256,256]{1,0:T(8,128)(2,1)} %constant.12.clone.place_ref.refs_8_) | copy-start | bytes 393220
  9.5 1.7 %copy-start.5 = (bf16[25,192,256]{2,1,0:T(8,128)(2,1)S(1)}, bf16[25,192,256]{2,1,0:T(8,128)(2,1)}, u32[]{:S(2)}) copy-start(bf16[25,192,256]{2,1,0:T(8,128)(2,1)} %copy-done.4) | copy-start | bytes 7372804
  11.2 0.9 %copy-start.6 = (bf16[64,1728]{1,0:T(8,128)(2,1)S(1)}, bf16[64,1728]{1,0:T(8,128)(2,1)}, u32[]{:S(2)}) copy-start(bf16[64,1728]{1,0:T(8,128)(2,1)} %own_ref.1) | copy-start | bytes 663556
  14.5 21.8 %collective-permute-start.3 = (bf16[12,128,256]{2,1,0:T(8,128)(2,1)S(1)}, bf16[12,128,256]{2,1,0:T(8,128)(2,1)S(1)}, u32[]{:S(2)}, u32[]{:S(2)}) collective-permute-start(bf16[12,128,256]{2,1,0:T(8,128)(2,1)S(1)} %get-tuple-element.39), channel_id=1, source_target_pairs={{0,3},{2,5},{4,7},{6,9},{8,11},{10,13},{12,15},{16,19},{18,21},{20... | collective-permute-start | bytes 2359304 | tf_op jit(solution)/shard_map/ppermute | solution.py:658
  15.9 22.6 %copy-start.3 = (bf16[128,3456]{1,0:T(8,128)(2,1)S(1)}, bf16[128,3456]{1,0:T(8,128)(2,1)}, u32[]{:S(2)}) copy-start(bf16[128,3456]{1,0:T(8,128)(2,1)} %own_ref.2) | copy-start | bytes 2654212
  32.9 7.5 %copy-start = (bf16[4,12,128,256]{3,2,1,0:T(8,128)(2,1)S(1)}, bf16[4,12,128,256]{3,2,1,0:T(8,128)(2,1)}, u32[]{:S(2)}) copy-start(bf16[4,12,128,256]{3,2,1,0:T(8,128)(2,1)} %get-tuple-element.36.refs_0_) | copy-start | bytes 9437188
  36.3 4.1 %collective-permute-start.4 = (bf16[12,128,256]{2,1,0:T(8,128)(2,1)S(1)}, bf16[12,128,256]{2,1,0:T(8,128)(2,1)S(1)}, u32[]{:S(2)}, u32[]{:S(2)}) collective-permute-start(bf16[12,128,256]{2,1,0:T(8,128)(2,1)S(1)} %fusion), channel_id=1, source_target_pairs={{0,1},{1,0},{2,3},{3,2},{4,5},{5,4},{6,7},{7,6},{8,9},{9,8},{10,11... | collective-permute-start | bytes 2359304 | tf_op jit(solution)/shard_map/ppermute | solution.py:662
  41.6 16.5 %collective-permute-start.6 = (bf16[7,256,128]{2,1,0:T(8,128)(2,1)S(1)}, bf16[7,256,128]{2,1,0:T(8,128)(2,1)S(1)}, u32[]{:S(2)}, u32[]{:S(2)}) collective-permute-start(bf16[7,256,128]{2,1,0:T(8,128)(2,1)S(1)} %get-tuple-element.45), channel_id=1, source_target_pairs={{0,3},{2,5},{4,7},{6,9},{8,11},{10,13},{12,15},{16,19},{18,21},{20... | collective-permute-start | bytes 1376264 | tf_op jit(solution)/shard_map/ppermute | solution.py:658
  47.8 10.5 %collective-permute-start.5 = (f32[6,128,256]{2,1,0:T(8,128)S(1)}, f32[6,128,256]{2,1,0:T(8,128)S(1)}, u32[]{:S(2)}, u32[]{:S(2)}) collective-permute-start(f32[6,128,256]{2,1,0:T(8,128)S(1)} %get-tuple-element.44), channel_id=1, source_target_pairs={{0,1},{1,0},{2,3},{3,2},{4,5},{5,4},{6,7},{7,6},{8,9},{9,8},{10,11... | collective-permute-start | bytes 2359304 | tf_op jit(solution)/shard_map/ppermute | solution.py:662
  58.2 1.8 %collective-permute-start.7 = (f32[6,128,128]{2,1,0:T(8,128)S(1)}, f32[6,128,128]{2,1,0:T(8,128)S(1)}, u32[]{:S(2)}, u32[]{:S(2)}) collective-permute-start(f32[6,128,128]{2,1,0:T(8,128)S(1)} %get-tuple-element.50), channel_id=1, source_target_pairs={{0,1},{1,0},{2,3},{3,2},{4,5},{5,4},{6,7},{7,6},{8,9},{9,8},{10,11... | collective-permute-start | bytes 1179656 | tf_op jit(solution)/shard_map/ppermute | solution.py:662

commit v9 on v8

--- a/solution.py
+++ b/solution.py
@@ -122,14 +122,22 @@
     )(core, own, other)
 
 
-def three_picks_kernel(core_ref, last_ref, before_ref, rim_ref, place_ref, picked_ref, prior_ref, *scratch):
-    *split_refs, pick_ref = scratch
+def three_picks_kernel(core_ref, last_ref, before_ref, rim_ref, picked_ref, prior_ref, *scratch):
+    *split_refs, pick_ref, place_ref = scratch
     core, step, last = core_ref[0], pl.program_id(0), pl.num_programs(0) - 1
     chans, block, width = rim_ref.shape[1], rim_ref.shape[2], rim_ref.shape[4]
     rows, part = last_ref.shape[3], last_ref.shape[1]
     planes = block * 4
     half = width // 2
     rim = (rows - 1) % SUB
+
+    @pl.when(step == 0)
+    def _():
+        source = lax.broadcasted_iota(jnp.int32, place_ref.shape, 0)
+        target = lax.broadcasted_iota(jnp.int32, place_ref.shape, 1)
+        quarter = half // 2
+        wanted = jnp.where(target < quarter, 2 * target, 2 * (target - quarter) + 1)
+        place_ref[...] = jnp.where(source == wanted, 1.0, 0.0).astype(BF16)
 
     def picked(spots):
         values, held = [], None
@@ -199,17 +207,16 @@
                     (1, chans, block, 2 * SUB, width),
                     lambda i, core: (0, 0, i + core[0] * (steps - 1 - i), (rows - 1) // (2 * SUB), 0),
                 ),
-                full(half, half),
             ],
             out_specs=[full(*shape), full(*shape)],
             scratch_shapes=[pltpu.VMEM((2, half // LANES, GROUP * rows, LANES), F32)] * 2
-            + [pltpu.VMEM((2, width // LANES, chans * SUB, LANES), F32)],
+            + [pltpu.VMEM((2, width // LANES, chans * SUB, LANES), F32), pltpu.VMEM((half, half), BF16)],
         ),
         out_shape=[jax.ShapeDtypeStruct(shape, BF16)] * 2,
-        compiler_params=pltpu.CompilerParams(vmem_limit_bytes=36 * MIB),
+        compiler_params=pltpu.CompilerParams(vmem_limit_bytes=28 * MIB),
         cost_estimate=pl.CostEstimate(flops=10**9, bytes_accessed=10**7, transcendentals=0),
         name="three_picks",
-    )(core, volume, volume, volume, even_odd(half))
+    )(core, volume, volume, volume)
 
 
 def three_edges_kernel(
@@ -284,78 +291,59 @@
     third_ref, plane_ref, row_ref, local_ref,
     *scratch,
 ):
-    *split_refs, prior_ref, first_ref, second_ref, total_ref = scratch
-    core, step, steps = core_ref[0], pl.program_id(0), pl.num_programs(0) - 1
+    *split_refs, even_ref, odd_ref = scratch
+    core, step, last = core_ref[0], pl.program_id(0), pl.num_programs(0) - 1
     chans, rows, width = x_ref.shape[1], x_ref.shape[3], x_ref.shape[4]
     half = width // 2
     out_rows = rows // 2
     taps = 3 * chans
-
-    def splitting(pair_ref):
-        for plane in range(2):
-
-            def store(tap, row, first, value, plane=plane):
-                pair_ref[plane, row + 1, tap * chans + first : tap * chans + first + GROUP, :] = value
-
-            yield from separate(x_ref, plane, place_ref, split_refs, store)
-
-    def summing(pair_ref):
+    prior, new = (step + 1) % 2, step % 2
+
+    @pl.when(step == 0)
+    def _():
+        odd_ref[1] = before_ref[...]
+        even_ref[0] = jnp.zeros_like(even_ref[0])
+        odd_ref[0, 0] = jnp.zeros_like(even_ref[0])
+
+    def store_even(tap, row, first, value):
+        even_ref[row + 1, tap * chans + first : tap * chans + first + GROUP, :] = value
+
+    def store_odd(tap, row, first, value):
+        odd_ref[new, row + 1, tap * chans + first : tap * chans + first + GROUP, :] = value
+
+    for plane, store in enumerate((store_even, store_odd)):
+        for _ in separate(x_ref, plane, place_ref, split_refs, store):
+            pass
+
+    def summing(keep):
         gain, shift = gain_ref[...], shift_ref[...]
         for row in range(out_rows):
-            parts = [
-                ref[2 * row : 2 * row + 3].reshape(3 * taps, half)
-                for ref in (prior_ref, pair_ref.at[0], pair_ref.at[1])
-            ]
-            total = jnp.dot(w_ref[...], jnp.concatenate(parts, 0), preferred_element_type=F32)
+            span = slice(2 * row, 2 * row + 3)
+            parts = [odd_ref[prior, span], even_ref[span], odd_ref[new, span]]
+            data = jnp.concatenate([part.reshape(3 * taps, half) for part in parts], 0)
+            total = jnp.dot(w_ref[...], data, preferred_element_type=F32)
             third_ref[0, row] = activate(total, gain, shift).astype(BF16)
-            total_ref[row] = total
-            yield
-        row_ref[0] = total_ref[0]
-        prior_ref[...] = pair_ref[1]
-        yield
+            if keep:
+                plane_ref[row] = total
+            if not row:
+                row_ref[0] = total
 
     @pl.when(step == 0)
     def _():
-        prior_ref[...] = before_ref[...]
-        for ref in (first_ref, second_ref):
-            ref[:, 0] = jnp.zeros_like(ref[:, 0])
-        for _ in splitting(first_ref):
-            pass
-
-    def both(new_ref, old_ref):
-        new, old = splitting(new_ref), summing(old_ref)
-        for turn in range(2 * chans // GROUP):
-            next(new, None)
-            for _ in range(out_rows * (turn + 1) // (2 * chans // GROUP) - out_rows * turn // (2 * chans // GROUP)):
-                next(old, None)
-        for _ in new:
-            pass
-        for _ in old:
-            pass
-
-    for odd, (new_ref, old_ref) in enumerate(((first_ref, second_ref), (second_ref, first_ref))):
-
-        @pl.when((step > 0) & (step < steps) & (step % 2 == odd))
-        def _(new_ref=new_ref, old_ref=old_ref):
-            both(new_ref, old_ref)
-
-        @pl.when((step == steps) & (step % 2 == odd))
-        def _(old_ref=old_ref):
-            for _ in summing(old_ref):
-                pass
-
-    @pl.when(step == 1)
-    def _():
-        plane_ref[...] = total_ref[...]
-
-    @pl.when((step > 0) & (core == 1))
-    def _():
-        local_ref[step - 1] = third_ref[0, out_rows - 1]
-
-    @pl.when((step == steps) & (core == 0))
+        summing(True)
+
+    @pl.when(step > 0)
+    def _():
+        summing(False)
+
+    @pl.when(core == 1)
+    def _():
+        local_ref[step] = third_ref[0, out_rows - 1]
+
+    @pl.when((step == last) & (core == 0))
     def _():
         local_ref[...] = third_ref[0]
-        local_ref[0] = total_ref[0].astype(BF16)
+        local_ref[0] = row_ref[0].astype(BF16)
 
 
 def layer_three(volume, prior, weights, gain, shift, core):
@@ -368,9 +356,9 @@
         three_kernel,
         grid_spec=pltpu.PrefetchScalarGridSpec(
             num_scalar_prefetch=1,
-            grid=(steps + 1,),
+            grid=(steps,),
             in_specs=[
-                pl.BlockSpec((1, chans, 2, rows, width), lambda i, core: (0, 0, core[0] * steps + jnp.minimum(i, steps - 1), 0, 0)),
+                pl.BlockSpec((1, chans, 2, rows, width), lambda i, core: (0, 0, core[0] * steps + i, 0, 0)),
                 pl.BlockSpec(prior.shape, lambda i, core: (0, 0, 0), pipeline_mode=pl.Buffered(1)),
                 full(*weights.shape),
                 full(half, half),
@@ -378,17 +366,15 @@
                 full(outs, 1),
             ],
             out_specs=[
-                pl.BlockSpec((1, out_rows, outs, half), lambda i, core: (jnp.maximum(i - 1, 0), 0, 0, 0)),
+                pl.BlockSpec((1, out_rows, outs, half), lambda i, core: (i, 0, 0, 0)),
                 full(out_rows, outs, half),
-                pl.BlockSpec((1, outs, half), lambda i, core: (jnp.maximum(i - 1, 0), 0, 0)),
+                pl.BlockSpec((1, outs, half), lambda i, core: (i, 0, 0)),
                 full(out_rows, outs, half),
             ],
             scratch_shapes=[pltpu.VMEM((2, half // LANES, GROUP * rows, LANES), F32)] * 4
             + [
                 pltpu.VMEM((rows + 1, 3 * chans, half), BF16),
                 pltpu.VMEM((2, rows + 1, 3 * chans, half), BF16),
-                pltpu.VMEM((2, rows + 1, 3 * chans, half), BF16),
-                pltpu.VMEM((out_rows, outs, half), F32),
             ],
         ),
         out_shape=[
@@ -397,7 +383,7 @@
             jax.ShapeDtypeStruct((steps, outs, half), F32),
             jax.ShapeDtypeStruct((out_rows, outs, half), BF16),
         ],
-        compiler_params=pltpu.CompilerParams(vmem_limit_bytes=46 * MIB),
+        compiler_params=pltpu.CompilerParams(vmem_limit_bytes=34 * MIB),
         cost_estimate=pl.CostEstimate(flops=10**10, bytes_accessed=2 * 10**7, transcendentals=0),
         name="layer_three",
     )(core, volume, prior, weights, even_odd(half), gain, shift)

time: 61.7 us -> 61 us (0.989)
  waiting for transfers between devices: 14.1 us -> 15.2 us
  local copies, waits for them, and re-layouts: 5.04 us -> 4.13 us
  Pallas kernels: 33 us -> 32.2 us
    ppermute x2, waiting for transfers between devices: 11.7 us -> 12.8 us  [handed_on(): return lax.ppermute(message, ('sp', 'fl'), pairs)]
    pallas_call x1, Pallas kernels: 17 us -> 16 us  [layer_three(): pl.pallas_call(three_kernel, grid_spec=pltpu.PrefetchScalarGridSpec(num_s...]
    unnamed x14 -> x10, local copies, waits for them, and re-layouts: 5.04 us -> 4.13 us
  transfers between devices with their start and end apart: 8 -> 8, of which waited for: 4 -> 4; matrix products, arithmetic and copies ran while one was open for 1% -> 1% of each run, Pallas kernels for 46% -> 45%
where the time goes in v9:
time: 61 us; the launch traced here: 60.7 us
  Pallas kernels  32.2 us (53%)
  waiting for transfers between devices  15.2 us (25%)
  starting transfers between devices  8.1 us (13%)
  local copies, waits for them, and re-layouts  4.13 us (7%)
  other arithmetic  0.88 us (1%)
    pallas_call x1, Pallas kernels, layer_three(): pl.pallas_call(three_kernel, grid_spec=pltpu.PrefetchScalarGridSpec(num_s...  16 us
    ppermute x2, waiting for transfers between devices, handed_on(): return lax.ppermute(message, ('sp', 'fl'), pairs)  12.8 us
    ppermute x6, starting transfers between devices, swapped(): return lax.ppermute(value, 'fl', [(0, 1), (1, 0)])  5.52 us
    pallas_call x1, Pallas kernels, three_picks(): pl.pallas_call(three_picks_kernel, grid_spec=pltpu.PrefetchScalarGridSpec...  5.16 us
    pallas_call x1, Pallas kernels, layer_four(): pl.pallas_call(four_kernel, out_shape=[jax.ShapeDtypeStruct((out_rows, ou...  4.85 us
    unnamed x10, local copies, waits for them, and re-layouts  4.13 us
    ppermute x2, starting transfers between devices, handed_on(): return lax.ppermute(message, ('sp', 'fl'), pairs)  2.58 us
    ppermute x6, waiting for transfers between devices, swapped(): return lax.ppermute(value, 'fl', [(0, 1), (1, 0)])  2.39 us
  transfers between devices with their start and end apart: 8, of which 4 were waited for; matrix products, arithmetic and copies ran while one was open for 1% of the time, Pallas kernels for 45%

profile of v9, /device:TPU:25, one launch (start us, length us, event | category | flops | bytes accessed | tf_op | source)
XLA Modules:
  0.0 60.7 jit_solution(266152676369411950)
XLA Ops:
  0.0 0.7 %collective-permute-start.2 = (bf16[128,3456]{1,0:T(8,128)(2,1)}, bf16[128,3456]{1,0:T(8,128)(2,1)S(1)}, u32[]{:S(2)}, u32[]{:S(2)}) collective-permute-start(bf16[128,3456]{1,0:T(8,128)(2,1)} %own_ref.2), channel_id=1, source_target_pairs={{0,1},{1,0},{2,3},{3,2},{4,5},{5,4},{6,7},{7,6},{8,9},{9,8},{10,11... | collective-permute-start | bytes 2654216 | tf_op jit(solution)/shard_map/ppermute | solution.py:648
  0.7 0.0 collective-permute-start
  0.7 0.8 %maximum_bitcast_fusion.own_scales_ref = f32[3,128]{1,0:T(4,128)S(1)} fusion(f32[128]{0:T(128)} %param.17, f32[128]{0:T(128)} %param.16, f32[64]{0:T(128)} %param.14, f32[64]{0:T(128)} %param.13), kind=kLoop, calls=%fused_computation.2 | loop fusion | flops 1152 | bytes 3072 | tf_op jit(solution)/shard_map/reshape | solution.py:653
  1.5 0.5 collective-permute-start.1
  2.0 5.2 %three_picks.1 = (bf16[25,192,256]{2,1,0:T(8,128)(2,1)S(1)}, bf16[25,192,256]{2,1,0:T(8,128)(2,1)S(1)}) custom-call(s32[1]{0:T(128)} %bitcast.core_ref, bf16[1,64,16,24,512]{4,3,2,1,0:T(8,128)(2,1)} %x_ref.1, bf16[1,64,16,24,512]{4,3,2,1,0:T(8,128)(2,1)} %x_ref.1, bf16[1,64,16,24,512]{4,3,2,1,0:T(8,128)(2,1)} %x_ref.1), custom_call_target="tpu_custom_call" | custom-call | flops 1000000000 | bytes 10000000 | tf_op jit(solution)/shard_map/three_picks/pallas_call | solution.py:196
  7.1 0.0 copy-start.2
  7.1 1.5 %copy-done.2 = bf16[25,192,256]{2,1,0:T(8,128)(2,1)} copy-done((bf16[25,192,256]{2,1,0:T(8,128)(2,1)}, bf16[25,192,256]{2,1,0:T(8,128)(2,1)S(1)}, u32[]{:S(2)}) %copy-start.2) | copy-done | bytes 2457624
  8.6 0.0 copy-start.1
  8.6 0.0 collective-permute-done.1.other_scales_ref
  8.6 0.0 collective-permute-done.other_ref
  8.6 0.0 collective-permute-done.2.other_ref
  8.6 0.0 copy-start.3
  8.6 1.7 %copy-done.3 = bf16[25,192,256]{2,1,0:T(8,128)(2,1)S(1)} copy-done((bf16[25,192,256]{2,1,0:T(8,128)(2,1)S(1)}, bf16[25,192,256]{2,1,0:T(8,128)(2,1)}, u32[]{:S(2)}) %copy-start.3) | copy-done | bytes 2457624
  10.4 0.0 copy-start.4
  10.4 0.9 %copy-done.4 = bf16[64,1728]{1,0:T(8,128)(2,1)S(1)} copy-done((bf16[64,1728]{1,0:T(8,128)(2,1)S(1)}, bf16[64,1728]{1,0:T(8,128)(2,1)}, u32[]{:S(2)}) %copy-start.4) | copy-done | bytes 221208
  11.3 2.3 %three_edges.1 = (bf16[12,128,256]{2,1,0:T(8,128)(2,1)S(1)}, bf16[128,1728]{1,0:T(8,128)(2,1)S(1)}, f32[128,1]{1,0:T(8,128)S(1)}, f32[128,1]{1,0:T(8,128)S(1)}, f32[128,128]{1,0:T(8,128)S(1)}) custom-call(s32[1]{0:T(128)} %bitcast.core_ref, bf16[25,192,256]{2,1,0:T(8,128)(2,1)S(1)} %copy-done.3, bf16[64,1728]{1,0:T(8,128)(2,1)S(1)} %copy-done.4, ...), custom_call_target="tpu_custom_call" | custom-call | flops 1000000000 | bytes 1000000 | tf_op jit(solution)/shard_map/three_edges/pallas_call | solution.py:278
  13.6 1.3 %collective-permute-start.3 = (bf16[12,128,256]{2,1,0:T(8,128)(2,1)S(1)}, bf16[12,128,256]{2,1,0:T(8,128)(2,1)S(1)}, u32[]{:S(2)}, u32[]{:S(2)}) collective-permute-start(bf16[12,128,256]{2,1,0:T(8,128)(2,1)S(1)} %get-tuple-element.39), channel_id=1, source_target_pairs={{0,3},{2,5},{4,7},{6,9},{8,11},{10,13},{12,15},{16,19},{18,21},{20... | collective-permute-start | bytes 2359304 | tf_op jit(solution)/shard_map/ppermute | solution.py:644
  14.9 0.0 copy-done.1
  14.9 0.0 copy-start
  14.9 16.0 %layer_three.1 = (bf16[4,12,128,256]{3,2,1,0:T(8,128)(2,1)S(1)}, f32[12,128,256]{2,1,0:T(8,128)S(1)}, f32[4,128,256]{2,1,0:T(8,128)S(1)}, bf16[12,128,256]{2,1,0:T(8,128)(2,1)S(1)}) custom-call(s32[1]{0:T(128)} %bitcast.core_ref, bf16[1,64,16,24,512]{4,3,2,1,0:T(8,128)(2,1)} %x_ref.1, bf16[25,192,256]{2,1,0:T(8,128)(2,1)S(1)} %get-tuple-element.28.before_ref, ...), custom_call_target="tpu_custom_call" | custom-call | flops 10000000000 | bytes 20000000 | tf_op jit(solution)/shard_map/layer_three/pallas_call | solution.py:355
  30.9 4.4 %collective-permute-done.3.refs_3_ = bf16[12,128,256]{2,1,0:T(8,128)(2,1)S(1)} collective-permute-done((bf16[12,128,256]{2,1,0:T(8,128)(2,1)S(1)}, bf16[12,128,256]{2,1,0:T(8,128)(2,1)S(1)}, u32[]{:S(2)}, u32[]{:S(2)}) %collective-permute-start.3) | collective-permute-done | bytes 786464 | tf_op jit(solution)/shard_map/ppermute | solution.py:644
  35.3 0.1 fusion
  35.4 2.3 %collective-permute-start.4 = (bf16[12,128,256]{2,1,0:T(8,128)(2,1)S(1)}, bf16[12,128,256]{2,1,0:T(8,128)(2,1)S(1)}, u32[]{:S(2)}, u32[]{:S(2)}) collective-permute-start(bf16[12,128,256]{2,1,0:T(8,128)(2,1)S(1)} %fusion), channel_id=1, source_target_pairs={{0,1},{1,0},{2,3},{3,2},{4,5},{5,4},{6,7},{7,6},{8,9},{9,8},{10,11... | collective-permute-start | bytes 2359304 | tf_op jit(solution)/shard_map/ppermute | solution.py:648
  37.7 0.0 copy-done
  37.7 1.2 %four_weights.1.refs_7_ = bf16[256,3456]{1,0:T(8,128)(2,1)S(1)} custom-call(s32[1]{0:T(128)} %bitcast.core_ref, bf16[128,3456]{1,0:T(8,128)(2,1)S(1)} %copy-done, bf16[128,3456]{1,0:T(8,128)(2,1)S(1)} %collective-permute-done.2.other_ref), custom_call_target="tpu_custom_call" | custom-call | flops 1000 | bytes 1000 | tf_op jit(solution)/shard_map/four_weights/pallas_call | solution.py:110
  38.9 0.7 %collective-permute-done.4.refs_6_ = bf16[12,128,256]{2,1,0:T(8,128)(2,1)S(1)} collective-permute-done((bf16[12,128,256]{2,1,0:T(8,128)(2,1)S(1)}, bf16[12,128,256]{2,1,0:T(8,128)(2,1)S(1)}, u32[]{:S(2)}, u32[]{:S(2)}) %collective-permute-start.4) | collective-permute-done | bytes 786464 | tf_op jit(solution)/shard_map/ppermute | solution.py:648
  39.6 1.4 %four_edges.1 = (bf16[7,256,128]{2,1,0:T(8,128)(2,1)S(1)}, bf16[256,384]{1,0:T(8,128)(2,1)S(1)}) custom-call(s32[1]{0:T(128)} %bitcast.core_ref, bf16[4,12,128,256]{3,2,1,0:T(8,128)(2,1)S(1)} %get-tuple-element.36.refs_0_, f32[12,128,256]{2,1,0:T(8,128)S(1)} %get-tuple-element.37.refs_1_, f32[4,128,256]{2,1,0:T(8,128)S(1)} %get-tuple-element.38.refs_2_, ...), custom_call_target="tpu_custom_call" | custom-call | flops 1000000000 | bytes 1000000 | tf_op jit(solution)/shard_map/four_edges/pallas_call | solution.py:470
  41.0 1.3 %collective-permute-start.6 = (bf16[7,256,128]{2,1,0:T(8,128)(2,1)S(1)}, bf16[7,256,128]{2,1,0:T(8,128)(2,1)S(1)}, u32[]{:S(2)}, u32[]{:S(2)}) collective-permute-start(bf16[7,256,128]{2,1,0:T(8,128)(2,1)S(1)} %get-tuple-element.45), channel_id=1, source_target_pairs={{0,3},{2,5},{4,7},{6,9},{8,11},{10,13},{12,15},{16,19},{18,21},{20... | collective-permute-start | bytes 1376264 | tf_op jit(solution)/shard_map/ppermute | solution.py:644
  42.3 4.8 %layer_four.1 = (f32[6,128,256]{2,1,0:T(8,128)S(1)}, f32[6,128,256]{2,1,0:T(8,128)S(1)}, f32[128,256]{1,0:T(8,128)S(1)}) custom-call(s32[1]{0:T(128)} %bitcast.core_ref, bf16[4,12,128,256]{3,2,1,0:T(8,128)(2,1)S(1)} %get-tuple-element.36.refs_0_, f32[12,128,256]{2,1,0:T(8,128)S(1)} %get-tuple-element.37.refs_1_, ...), custom_call_target="tpu_custom_call" | custom-call | flops 4000000000 | bytes 4000000 | tf_op jit(solution)/shard_map/layer_four/pallas_call | solution.py:535
  47.1 2.0 %collective-permute-start.5 = (f32[6,128,256]{2,1,0:T(8,128)S(1)}, f32[6,128,256]{2,1,0:T(8,128)S(1)}, u32[]{:S(2)}, u32[]{:S(2)}) collective-permute-start(f32[6,128,256]{2,1,0:T(8,128)S(1)} %get-tuple-element.44), channel_id=1, source_target_pairs={{0,1},{1,0},{2,3},{3,2},{4,5},{5,4},{6,7},{7,6},{8,9},{9,8},{10,11... | collective-permute-start | bytes 2359304 | tf_op jit(solution)/shard_map/ppermute | solution.py:648
  49.1 8.4 %collective-permute-done.6.halo_ref = bf16[7,256,128]{2,1,0:T(8,128)(2,1)S(1)} collective-permute-done((bf16[7,256,128]{2,1,0:T(8,128)(2,1)S(1)}, bf16[7,256,128]{2,1,0:T(8,128)(2,1)S(1)}, u32[]{:S(2)}, u32[]{:S(2)}) %collective-permute-start.6) | collective-permute-done | bytes 458784 | tf_op jit(solution)/shard_map/ppermute | solution.py:644
  57.5 0.1 collective-permute-start.7
  57.6 0.0 collective-permute-done.5.got_ref
  57.6 1.7 %collective-permute-done.7.shares_ref = f32[6,128,128]{2,1,0:T(8,128)S(1)} collective-permute-done((f32[6,128,128]{2,1,0:T(8,128)S(1)}, f32[6,128,128]{2,1,0:T(8,128)S(1)}, u32[]{:S(2)}, u32[]{:S(2)}) %collective-permute-start.7) | collective-permute-done | bytes 393248 | tf_op jit(solution)/shard_map/ppermute | solution.py:648
  59.3 1.4 %assemble.1 = bf16[3072,128]{1,0:T(8,128)(2,1)} custom-call(s32[1]{0:T(128)} %bitcast.core_ref, f32[6,128,256]{2,1,0:T(8,128)S(1)} %get-tuple-element.43.own_ref, f32[6,128,256]{2,1,0:T(8,128)S(1)} %collective-permute-done.5.got_ref, bf16[7,256,128]{2,1,0:T(8,128)(2,1)S(1)} %collective-permute-done.6.halo_ref, f32[128,128]{1,0:T(8,128)S(1)} %get-tuple-element.48.fix_ref, ...), custom_call_target="tpu_custom_call" | custom-call | tf_op jit(solution)/shard_map/assemble/pallas_call | solution.py:630
  (1 shorter events, 0.0 us)
Async XLA Ops:
  0.0 8.6 %collective-permute-start.2 = (bf16[128,3456]{1,0:T(8,128)(2,1)}, bf16[128,3456]{1,0:T(8,128)(2,1)S(1)}, u32[]{:S(2)}, u32[]{:S(2)}) collective-permute-start(bf16[128,3456]{1,0:T(8,128)(2,1)} %own_ref.2), channel_id=1, source_target_pairs={{0,1},{1,0},{2,3},{3,2},{4,5},{5,4},{6,7},{7,6},{8,9},{9,8},{10,11... | collective-permute-start | bytes 2654216 | tf_op jit(solution)/shard_map/ppermute | solution.py:648
  0.7 7.9 %collective-permute-start = (bf16[64,1728]{1,0:T(8,128)(2,1)}, bf16[64,1728]{1,0:T(8,128)(2,1)}, u32[]{:S(2)}, u32[]{:S(2)}) collective-permute-start(bf16[64,1728]{1,0:T(8,128)(2,1)} %own_ref.1), channel_id=1, source_target_pairs={{0,1},{1,0},{2,3},{3,2},{4,5},{5,4},{6,7},{7,6},{8,9},{9,8},{10,11... | collective-permute-start | bytes 663560 | tf_op jit(solution)/shard_map/ppermute | solution.py:648
  1.5 7.1 %collective-permute-start.1 = (f32[3,128]{1,0:T(4,128)S(1)}, f32[3,128]{1,0:T(4,128)S(1)}, u32[]{:S(2)}, u32[]{:S(2)}) collective-permute-start(f32[3,128]{1,0:T(4,128)S(1)} %maximum_bitcast_fusion.own_scales_ref), channel_id=1, source_target_pairs={{0,1},{1,0},{2,3},{3,2},{4,5},{5,4},{6,7},{7,6},{8,9},{9,8},{10,11... | collective-permute-start | bytes 4616 | tf_op jit(solution)/shard_map/ppermute | solution.py:648
  7.1 1.5 %copy-start.2 = (bf16[25,192,256]{2,1,0:T(8,128)(2,1)}, bf16[25,192,256]{2,1,0:T(8,128)(2,1)S(1)}, u32[]{:S(2)}) copy-start(bf16[25,192,256]{2,1,0:T(8,128)(2,1)S(1)} %get-tuple-element.29.picked_ref) | copy-start | bytes 7372804
  8.6 6.3 %copy-start.1 = (bf16[256,256]{1,0:T(8,128)(2,1)S(1)}, bf16[256,256]{1,0:T(8,128)(2,1)}, u32[]{:S(2)}) copy-start(bf16[256,256]{1,0:T(8,128)(2,1)} %constant.12.clone.place_ref.refs_8_) | copy-start | bytes 393220
  8.6 1.7 %copy-start.3 = (bf16[25,192,256]{2,1,0:T(8,128)(2,1)S(1)}, bf16[25,192,256]{2,1,0:T(8,128)(2,1)}, u32[]{:S(2)}) copy-start(bf16[25,192,256]{2,1,0:T(8,128)(2,1)} %copy-done.2) | copy-start | bytes 7372804
  10.4 0.9 %copy-start.4 = (bf16[64,1728]{1,0:T(8,128)(2,1)S(1)}, bf16[64,1728]{1,0:T(8,128)(2,1)}, u32[]{:S(2)}) copy-start(bf16[64,1728]{1,0:T(8,128)(2,1)} %own_ref.1) | copy-start | bytes 663556
  13.6 21.7 %collective-permute-start.3 = (bf16[12,128,256]{2,1,0:T(8,128)(2,1)S(1)}, bf16[12,128,256]{2,1,0:T(8,128)(2,1)S(1)}, u32[]{:S(2)}, u32[]{:S(2)}) collective-permute-start(bf16[12,128,256]{2,1,0:T(8,128)(2,1)S(1)} %get-tuple-element.39), channel_id=1, source_target_pairs={{0,3},{2,5},{4,7},{6,9},{8,11},{10,13},{12,15},{16,19},{18,21},{20... | collective-permute-start | bytes 2359304 | tf_op jit(solution)/shard_map/ppermute | solution.py:644
  14.9 22.8 %copy-start = (bf16[128,3456]{1,0:T(8,128)(2,1)S(1)}, bf16[128,3456]{1,0:T(8,128)(2,1)}, u32[]{:S(2)}) copy-start(bf16[128,3456]{1,0:T(8,128)(2,1)} %own_ref.2) | copy-start | bytes 2654212
  35.4 4.2 %collective-permute-start.4 = (bf16[12,128,256]{2,1,0:T(8,128)(2,1)S(1)}, bf16[12,128,256]{2,1,0:T(8,128)(2,1)S(1)}, u32[]{:S(2)}, u32[]{:S(2)}) collective-permute-start(bf16[12,128,256]{2,1,0:T(8,128)(2,1)S(1)} %fusion), channel_id=1, source_target_pairs={{0,1},{1,0},{2,3},{3,2},{4,5},{5,4},{6,7},{7,6},{8,9},{9,8},{10,11... | collective-permute-start | bytes 2359304 | tf_op jit(solution)/shard_map/ppermute | solution.py:648
  41.0 16.5 %collective-permute-start.6 = (bf16[7,256,128]{2,1,0:T(8,128)(2,1)S(1)}, bf16[7,256,128]{2,1,0:T(8,128)(2,1)S(1)}, u32[]{:S(2)}, u32[]{:S(2)}) collective-permute-start(bf16[7,256,128]{2,1,0:T(8,128)(2,1)S(1)} %get-tuple-element.45), channel_id=1, source_target_pairs={{0,3},{2,5},{4,7},{6,9},{8,11},{10,13},{12,15},{16,19},{18,21},{20... | collective-permute-start | bytes 1376264 | tf_op jit(solution)/shard_map/ppermute | solution.py:644
  47.1 10.5 %collective-permute-start.5 = (f32[6,128,256]{2,1,0:T(8,128)S(1)}, f32[6,128,256]{2,1,0:T(8,128)S(1)}, u32[]{:S(2)}, u32[]{:S(2)}) collective-permute-start(f32[6,128,256]{2,1,0:T(8,128)S(1)} %get-tuple-element.44), channel_id=1, source_target_pairs={{0,1},{1,0},{2,3},{3,2},{4,5},{5,4},{6,7},{7,6},{8,9},{9,8},{10,11... | collective-permute-start | bytes 2359304 | tf_op jit(solution)/shard_map/ppermute | solution.py:648
  57.5 1.8 %collective-permute-start.7 = (f32[6,128,128]{2,1,0:T(8,128)S(1)}, f32[6,128,128]{2,1,0:T(8,128)S(1)}, u32[]{:S(2)}, u32[]{:S(2)}) collective-permute-start(f32[6,128,128]{2,1,0:T(8,128)S(1)} %get-tuple-element.50), channel_id=1, source_target_pairs={{0,1},{1,0},{2,3},{3,2},{4,5},{5,4},{6,7},{7,6},{8,9},{9,8},{10,11... | collective-permute-start | bytes 1179656 | tf_op jit(solution)/shard_map/ppermute | solution.py:648

commit v10 on v9

--- a/solution.py
+++ b/solution.py
@@ -417,9 +417,10 @@
 
 
 def four_edges_kernel(core_ref, *refs):
-    *thirds, local_ref, w_ref, place_ref, message_ref, mid_ref = refs
+    *thirds, local_ref, w_ref, place_ref, message_ref, mid_ref, rows_ref = refs
     core = core_ref[0]
     planes, rows, chans, width = thirds[0].shape
+    rows_ref[...] = thirds[3][:planes]
     half = width // 2
     out_rows = rows // 2
     taps = 3 * chans
@@ -472,6 +473,7 @@
         out_shape=[
             jax.ShapeDtypeStruct((rows // 2 + 1, outs, half), BF16),
             jax.ShapeDtypeStruct((outs, 3 * chans), BF16),
+            jax.ShapeDtypeStruct((planes, chans, width), BF16),
         ],
         in_specs=inputs(len(thirds) + 3),
         compiler_params=pltpu.CompilerParams(vmem_limit_bytes=24 * MIB),
@@ -481,11 +483,10 @@
 
 
 def four_kernel(core_ref, *refs):
-    *thirds, local_ref, w_ref, place_ref, own_ref, theirs_ref, corner_ref, data_ref = refs
+    *thirds, rows_ref, local_ref, w_ref, place_ref, own_ref, theirs_ref, corner_ref, data_ref = refs
     core = core_ref[0]
     planes, rows, chans, width = thirds[0].shape
     halo_ref, gain_ref, shift_ref = thirds[3:]
-    rows_ref = local_ref.at[planes : 2 * planes]
     half = width // 2
     out_rows, count = rows // 2, planes // 2
     taps = 3 * chans
@@ -527,7 +528,7 @@
         theirs_ref[row] = jnp.where(core == 0, total[LANES:], total[:LANES])
 
 
-def layer_four(core, thirds, local, weights):
+def layer_four(core, thirds, rows_before, local, weights):
     planes, rows, chans, width = thirds[0].shape
     outs = weights.shape[0]
     half = width // 2
@@ -539,12 +540,12 @@
             jax.ShapeDtypeStruct((out_rows, outs // 2, count * half), F32),
             jax.ShapeDtypeStruct((chans, width), F32),
         ],
-        in_specs=inputs(len(thirds) + 3),
+        in_specs=inputs(len(thirds) + 4),
         scratch_shapes=[pltpu.VMEM((3, rows + 1, 3 * chans, count * half), BF16)],
         compiler_params=pltpu.CompilerParams(vmem_limit_bytes=32 * MIB),
         cost_estimate=pl.CostEstimate(flops=4 * 10**9, bytes_accessed=4 * 10**6, transcendentals=0),
         name="layer_four",
-    )(core, *thirds, local, weights, even_odd(width))
+    )(core, *thirds, rows_before, local, weights, even_odd(width))
 
 
 def shares_kernel(core_ref, corner_ref, halo_ref, mid_ref, place_ref, gain_ref, shift_ref, shares_ref, fix_ref):
@@ -656,17 +657,16 @@
     message, weights_three, gain, shift, scales = three_edges(
         picked, kernel_three, others[0], own_scales, others[1], core
     )
-    weights_three, kernel_four = lax.optimization_barrier((weights_three, kernel_four))
     halo = handed_on(message)
     *thirds, local = layer_three(volume, prior, weights_three, gain, shift, core)
-    planes = thirds[0].shape[0]
-    passed = jnp.where(core[0] == 1, halo[:planes], local[planes : 2 * planes])
-    local = swapped(lax.dynamic_update_slice(local, passed, (planes, 0, 0)))
+    halo, local = lax.optimization_barrier((halo, local))
     thirds = (*thirds, halo, gain, shift)
+    local = swapped(local)
     weights_four = four_weights(kernel_four, others[2], core)
-    message, mid = four_edges(core, thirds, local, weights_four)
+    message, mid, rows = four_edges(core, thirds, local, weights_four)
     halo = handed_on(message)
-    own, theirs, corner = layer_four(core, thirds, local, weights_four)
+    rows = lax.ppermute(rows, "fl", [(1, 0)])
+    own, theirs, corner = layer_four(core, thirds, rows, local, weights_four)
     lines = last_stage(core, own, theirs, corner, halo, mid, gain, shift, scales)
     out_rows, outs, lanes = own.shape
     fourth = lines.reshape(outs, out_rows, 2 * lanes // LANES, LANES)

time: 61 us -> 57.7 us (0.946)
  local copies, waits for them, and re-layouts: 4.13 us -> 0.02 us
  starting transfers between devices: 8.1 us -> 10.3 us
  Pallas kernels: 32.2 us -> 31.2 us
    unnamed x10 -> x6, local copies, waits for them, and re-layouts: 4.13 us -> 0.02 us
    ppermute x0 -> x1, starting transfers between devices: none -> 2.21 us  [shards(): rows = lax.ppermute(rows, 'fl', [(1, 0)])]
    pallas_call x1, Pallas kernels: 2.27 us -> 1.33 us  [three_edges(): pl.pallas_call(three_edges_kernel, in_specs=inputs(5), out_shape=[jax.Sha...]
  transfers between devices with their start and end apart: 8 -> 9, of which waited for: 4 -> 4; matrix products, arithmetic and copies ran while one was open for 1% -> 1% of each run, Pallas kernels for 45% -> 48%
where the time goes in v10:
time: 57.7 us; the launch traced here: 57.5 us
  Pallas kernels  31.2 us (54%)
  waiting for transfers between devices  15 us (26%)
  starting transfers between devices  10.3 us (18%)
  other arithmetic  0.78 us (1%)
    pallas_call x1, Pallas kernels, layer_three(): pl.pallas_call(three_kernel, grid_spec=pltpu.PrefetchScalarGridSpec(num_s...  16 us
    ppermute x2, waiting for transfers between devices, handed_on(): return lax.ppermute(message, ('sp', 'fl'), pairs)  12.6 us
    ppermute x6, starting transfers between devices, swapped(): return lax.ppermute(value, 'fl', [(0, 1), (1, 0)])  5.49 us
    pallas_call x1, Pallas kernels, three_picks(): pl.pallas_call(three_picks_kernel, grid_spec=pltpu.PrefetchScalarGridSpec...  5.19 us
    pallas_call x1, Pallas kernels, layer_four(): pl.pallas_call(four_kernel, out_shape=[jax.ShapeDtypeStruct((out_rows, ou...  4.84 us
    ppermute x2, starting transfers between devices, handed_on(): return lax.ppermute(message, ('sp', 'fl'), pairs)  2.58 us
    ppermute x6, waiting for transfers between devices, swapped(): return lax.ppermute(value, 'fl', [(0, 1), (1, 0)])  2.4 us
    ppermute x1, starting transfers between devices, shards(): rows = lax.ppermute(rows, 'fl', [(1, 0)])  2.21 us
  transfers between devices with their start and end apart: 9, of which 4 were waited for; matrix products, arithmetic and copies ran while one was open for 1% of the time, Pallas kernels for 48%

profile of v10, /device:TPU:25, one launch (start us, length us, event | category | flops | bytes accessed | tf_op | source)
XLA Modules:
  0.0 57.5 jit_solution(18332523205484220453)
XLA Ops:
  0.0 0.7 %collective-permute-start.2 = (bf16[128,3456]{1,0:T(8,128)(2,1)}, bf16[128,3456]{1,0:T(8,128)(2,1)S(1)}, u32[]{:S(2)}, u32[]{:S(2)}) collective-permute-start(bf16[128,3456]{1,0:T(8,128)(2,1)} %own_ref.3), channel_id=1, source_target_pairs={{0,1},{1,0},{2,3},{3,2},{4,5},{5,4},{6,7},{7,6},{8,9},{9,8},{10,11... | collective-permute-start | bytes 2654216 | tf_op jit(solution)/shard_map/ppermute | solution.py:649
  0.7 0.0 collective-permute-start
  0.7 0.8 %maximum_bitcast_fusion.own_scales_ref = f32[3,128]{1,0:T(4,128)S(1)} fusion(f32[128]{0:T(128)} %param.17, f32[128]{0:T(128)} %param.16, f32[64]{0:T(128)} %param.14, f32[64]{0:T(128)} %param.13), kind=kLoop, calls=%fused_computation | loop fusion | flops 1152 | bytes 3072 | tf_op jit(solution)/shard_map/reshape | solution.py:654
  1.5 0.5 collective-permute-start.1
  2.0 0.0 copy-start.2
  2.0 5.2 %three_picks.1 = (bf16[25,192,256]{2,1,0:T(8,128)(2,1)S(1)}, bf16[25,192,256]{2,1,0:T(8,128)(2,1)S(1)}) custom-call(s32[1]{0:T(128)} %bitcast.core_ref, bf16[1,64,16,24,512]{4,3,2,1,0:T(8,128)(2,1)} %x_ref.1, bf16[1,64,16,24,512]{4,3,2,1,0:T(8,128)(2,1)} %x_ref.1, bf16[1,64,16,24,512]{4,3,2,1,0:T(8,128)(2,1)} %x_ref.1), custom_call_target="tpu_custom_call" | custom-call | flops 1000000000 | bytes 10000000 | tf_op jit(solution)/shard_map/three_picks/pallas_call | solution.py:196
  7.2 0.0 copy-start.1
  7.2 0.0 collective-permute-done.1.other_scales_ref
  7.2 0.0 collective-permute-done.other_ref
  7.2 0.0 collective-permute-done.2.other_ref
  7.2 0.0 copy-done.2
  7.2 1.3 %three_edges.1 = (bf16[12,128,256]{2,1,0:T(8,128)(2,1)S(1)}, bf16[128,1728]{1,0:T(8,128)(2,1)S(1)}, f32[128,1]{1,0:T(8,128)S(1)}, f32[128,1]{1,0:T(8,128)S(1)}, f32[128,128]{1,0:T(8,128)S(1)}) custom-call(s32[1]{0:T(128)} %bitcast.core_ref, bf16[25,192,256]{2,1,0:T(8,128)(2,1)S(1)} %get-tuple-element.30.picked_ref, bf16[64,1728]{1,0:T(8,128)(2,1)S(1)} %copy-done.2, ...), custom_call_target="tpu_custom_call" | custom-call | flops 1000000000 | bytes 1000000 | tf_op jit(solution)/shard_map/three_edges/pallas_call | solution.py:278
  8.6 1.3 %collective-permute-start.3 = (bf16[12,128,256]{2,1,0:T(8,128)(2,1)S(1)}, bf16[12,128,256]{2,1,0:T(8,128)(2,1)S(1)}, u32[]{:S(2)}, u32[]{:S(2)}) collective-permute-start(bf16[12,128,256]{2,1,0:T(8,128)(2,1)S(1)} %get-tuple-element.39), channel_id=1, source_target_pairs={{0,3},{2,5},{4,7},{6,9},{8,11},{10,13},{12,15},{16,19},{18,21},{20... | collective-permute-start | bytes 2359304 | tf_op jit(solution)/shard_map/ppermute | solution.py:645
  9.9 0.0 copy-done.1
  9.9 0.0 copy-start
  9.9 16.0 %layer_three.1 = (bf16[4,12,128,256]{3,2,1,0:T(8,128)(2,1)S(1)}, f32[12,128,256]{2,1,0:T(8,128)S(1)}, f32[4,128,256]{2,1,0:T(8,128)S(1)}, bf16[12,128,256]{2,1,0:T(8,128)(2,1)S(1)}) custom-call(s32[1]{0:T(128)} %bitcast.core_ref, bf16[1,64,16,24,512]{4,3,2,1,0:T(8,128)(2,1)} %x_ref.1, bf16[25,192,256]{2,1,0:T(8,128)(2,1)S(1)} %get-tuple-element.29.before_ref, ...), custom_call_target="tpu_custom_call" | custom-call | flops 10000000000 | bytes 20000000 | tf_op jit(solution)/shard_map/layer_three/pallas_call | solution.py:355
  25.9 4.3 %collective-permute-done.3.refs_3_ = bf16[12,128,256]{2,1,0:T(8,128)(2,1)S(1)} collective-permute-done((bf16[12,128,256]{2,1,0:T(8,128)(2,1)S(1)}, bf16[12,128,256]{2,1,0:T(8,128)(2,1)S(1)}, u32[]{:S(2)}, u32[]{:S(2)}) %collective-permute-start.3) | collective-permute-done | bytes 786464 | tf_op jit(solution)/shard_map/ppermute | solution.py:645
  30.3 2.3 %collective-permute-start.4 = (bf16[12,128,256]{2,1,0:T(8,128)(2,1)S(1)}, bf16[12,128,256]{2,1,0:T(8,128)(2,1)S(1)}, u32[]{:S(2)}, u32[]{:S(2)}) collective-permute-start(bf16[12,128,256]{2,1,0:T(8,128)(2,1)S(1)} %get-tuple-element.42), channel_id=1, source_target_pairs={{0,1},{1,0},{2,3},{3,2},{4,5},{5,4},{6,7},{7,6},{8,9},{9,8},{10,11... | collective-permute-start | bytes 2359304 | tf_op jit(solution)/shard_map/ppermute | solution.py:649
  32.5 0.0 copy-done
  32.5 1.2 %four_weights.1.refs_7_.refs_8_ = bf16[256,3456]{1,0:T(8,128)(2,1)S(1)} custom-call(s32[1]{0:T(128)} %bitcast.core_ref, bf16[128,3456]{1,0:T(8,128)(2,1)S(1)} %copy-done, bf16[128,3456]{1,0:T(8,128)(2,1)S(1)} %collective-permute-done.2.other_ref), custom_call_target="tpu_custom_call" | custom-call | flops 1000 | bytes 1000 | tf_op jit(solution)/shard_map/four_weights/pallas_call | solution.py:110
  33.8 0.7 %collective-permute-done.4.refs_6_.refs_7_ = bf16[12,128,256]{2,1,0:T(8,128)(2,1)S(1)} collective-permute-done((bf16[12,128,256]{2,1,0:T(8,128)(2,1)S(1)}, bf16[12,128,256]{2,1,0:T(8,128)(2,1)S(1)}, u32[]{:S(2)}, u32[]{:S(2)}) %collective-permute-start.4) | collective-permute-done | bytes 786464 | tf_op jit(solution)/shard_map/ppermute | solution.py:649
  34.4 1.2 %four_edges.1 = (bf16[7,256,128]{2,1,0:T(8,128)(2,1)S(1)}, bf16[256,384]{1,0:T(8,128)(2,1)S(1)}, bf16[4,128,256]{2,1,0:T(8,128)(2,1)S(1)}) custom-call(s32[1]{0:T(128)} %bitcast.core_ref, bf16[4,12,128,256]{3,2,1,0:T(8,128)(2,1)S(1)} %get-tuple-element.36.refs_0_, f32[12,128,256]{2,1,0:T(8,128)S(1)} %get-tuple-element.37.refs_1_, ...), custom_call_target="tpu_custom_call" | custom-call | flops 1000000000 | bytes 1000000 | tf_op jit(solution)/shard_map/four_edges/pallas_call | solution.py:471
  35.6 2.2 %collective-permute-start.5 = (bf16[4,128,256]{2,1,0:T(8,128)(2,1)S(1)}, bf16[4,128,256]{2,1,0:T(8,128)(2,1)S(1)}, u32[]{:S(2)}, u32[]{:S(2)}) collective-permute-start(bf16[4,128,256]{2,1,0:T(8,128)(2,1)S(1)} %get-tuple-element.44), channel_id=1, source_target_pairs={{1,0},{3,2},{5,4},{7,6},{9,8},{11,10},{13,12},{15,14},{17,16},{19,... | collective-permute-start | bytes 786440 | tf_op jit(solution)/shard_map/ppermute | solution.py:668
  37.9 1.3 %collective-permute-start.7 = (bf16[7,256,128]{2,1,0:T(8,128)(2,1)S(1)}, bf16[7,256,128]{2,1,0:T(8,128)(2,1)S(1)}, u32[]{:S(2)}, u32[]{:S(2)}) collective-permute-start(bf16[7,256,128]{2,1,0:T(8,128)(2,1)S(1)} %get-tuple-element.47), channel_id=1, source_target_pairs={{0,3},{2,5},{4,7},{6,9},{8,11},{10,13},{12,15},{16,19},{18,21},{20... | collective-permute-start | bytes 1376264 | tf_op jit(solution)/shard_map/ppermute | solution.py:645
  39.2 0.0 collective-permute-done.5.refs_6_
  39.2 4.8 %layer_four.1 = (f32[6,128,256]{2,1,0:T(8,128)S(1)}, f32[6,128,256]{2,1,0:T(8,128)S(1)}, f32[128,256]{1,0:T(8,128)S(1)}) custom-call(s32[1]{0:T(128)} %bitcast.core_ref, bf16[4,12,128,256]{3,2,1,0:T(8,128)(2,1)S(1)} %get-tuple-element.36.refs_0_, f32[12,128,256]{2,1,0:T(8,128)S(1)} %get-tuple-element.37.refs_1_, ...), custom_call_target="tpu_custom_call" | custom-call | flops 4000000000 | bytes 4000000 | tf_op jit(solution)/shard_map/layer_four/pallas_call | solution.py:536
  44.0 2.0 %collective-permute-start.6 = (f32[6,128,256]{2,1,0:T(8,128)S(1)}, f32[6,128,256]{2,1,0:T(8,128)S(1)}, u32[]{:S(2)}, u32[]{:S(2)}) collective-permute-start(f32[6,128,256]{2,1,0:T(8,128)S(1)} %get-tuple-element.46), channel_id=1, source_target_pairs={{0,1},{1,0},{2,3},{3,2},{4,5},{5,4},{6,7},{7,6},{8,9},{9,8},{10,11... | collective-permute-start | bytes 2359304 | tf_op jit(solution)/shard_map/ppermute | solution.py:649
  46.0 8.3 %collective-permute-done.7.halo_ref = bf16[7,256,128]{2,1,0:T(8,128)(2,1)S(1)} collective-permute-done((bf16[7,256,128]{2,1,0:T(8,128)(2,1)S(1)}, bf16[7,256,128]{2,1,0:T(8,128)(2,1)S(1)}, u32[]{:S(2)}, u32[]{:S(2)}) %collective-permute-start.7) | collective-permute-done | bytes 458784 | tf_op jit(solution)/shard_map/ppermute | solution.py:645
  54.3 0.1 collective-permute-start.8
  54.4 1.7 %collective-permute-done.8.shares_ref = f32[6,128,128]{2,1,0:T(8,128)S(1)} collective-permute-done((f32[6,128,128]{2,1,0:T(8,128)S(1)}, f32[6,128,128]{2,1,0:T(8,128)S(1)}, u32[]{:S(2)}, u32[]{:S(2)}) %collective-permute-start.8) | collective-permute-done | bytes 393248 | tf_op jit(solution)/shard_map/ppermute | solution.py:649
  56.1 0.0 collective-permute-done.6.got_ref
  56.1 1.4 %assemble.1 = bf16[3072,128]{1,0:T(8,128)(2,1)} custom-call(s32[1]{0:T(128)} %bitcast.core_ref, f32[6,128,256]{2,1,0:T(8,128)S(1)} %get-tuple-element.45.own_ref, f32[6,128,256]{2,1,0:T(8,128)S(1)} %collective-permute-done.6.got_ref, bf16[7,256,128]{2,1,0:T(8,128)(2,1)S(1)} %collective-permute-done.7.halo_ref, f32[128,128]{1,0:T(8,128)S(1)} %get-tuple-element.50.fix_ref, ...), custom_call_target="tpu_custom_call" | custom-call | tf_op jit(solution)/shard_map/assemble/pallas_call | solution.py:631
  (1 shorter events, 0.0 us)
Async XLA Ops:
  0.0 7.2 %collective-permute-start.2 = (bf16[128,3456]{1,0:T(8,128)(2,1)}, bf16[128,3456]{1,0:T(8,128)(2,1)S(1)}, u32[]{:S(2)}, u32[]{:S(2)}) collective-permute-start(bf16[128,3456]{1,0:T(8,128)(2,1)} %own_ref.3), channel_id=1, source_target_pairs={{0,1},{1,0},{2,3},{3,2},{4,5},{5,4},{6,7},{7,6},{8,9},{9,8},{10,11... | collective-permute-start | bytes 2654216 | tf_op jit(solution)/shard_map/ppermute | solution.py:649
  0.7 6.5 %collective-permute-start = (bf16[64,1728]{1,0:T(8,128)(2,1)}, bf16[64,1728]{1,0:T(8,128)(2,1)S(1)}, u32[]{:S(2)}, u32[]{:S(2)}) collective-permute-start(bf16[64,1728]{1,0:T(8,128)(2,1)} %own_ref.2), channel_id=1, source_target_pairs={{0,1},{1,0},{2,3},{3,2},{4,5},{5,4},{6,7},{7,6},{8,9},{9,8},{10,11... | collective-permute-start | bytes 663560 | tf_op jit(solution)/shard_map/ppermute | solution.py:649
  1.5 5.7 %collective-permute-start.1 = (f32[3,128]{1,0:T(4,128)S(1)}, f32[3,128]{1,0:T(4,128)S(1)}, u32[]{:S(2)}, u32[]{:S(2)}) collective-permute-start(f32[3,128]{1,0:T(4,128)S(1)} %maximum_bitcast_fusion.own_scales_ref), channel_id=1, source_target_pairs={{0,1},{1,0},{2,3},{3,2},{4,5},{5,4},{6,7},{7,6},{8,9},{9,8},{10,11... | collective-permute-start | bytes 4616 | tf_op jit(solution)/shard_map/ppermute | solution.py:649
  2.0 5.2 %copy-start.2 = (bf16[64,1728]{1,0:T(8,128)(2,1)S(1)}, bf16[64,1728]{1,0:T(8,128)(2,1)}, u32[]{:S(2)}) copy-start(bf16[64,1728]{1,0:T(8,128)(2,1)} %own_ref.2) | copy-start | bytes 663556
  7.2 2.7 %copy-start.1 = (bf16[256,256]{1,0:T(8,128)(2,1)S(1)}, bf16[256,256]{1,0:T(8,128)(2,1)}, u32[]{:S(2)}) copy-start(bf16[256,256]{1,0:T(8,128)(2,1)} %constant.6.clone.place_ref.refs_8_.refs_9_) | copy-start | bytes 393220
  8.6 21.7 %collective-permute-start.3 = (bf16[12,128,256]{2,1,0:T(8,128)(2,1)S(1)}, bf16[12,128,256]{2,1,0:T(8,128)(2,1)S(1)}, u32[]{:S(2)}, u32[]{:S(2)}) collective-permute-start(bf16[12,128,256]{2,1,0:T(8,128)(2,1)S(1)} %get-tuple-element.39), channel_id=1, source_target_pairs={{0,3},{2,5},{4,7},{6,9},{8,11},{10,13},{12,15},{16,19},{18,21},{20... | collective-permute-start | bytes 2359304 | tf_op jit(solution)/shard_map/ppermute | solution.py:645
  9.9 22.6 %copy-start = (bf16[128,3456]{1,0:T(8,128)(2,1)S(1)}, bf16[128,3456]{1,0:T(8,128)(2,1)}, u32[]{:S(2)}) copy-start(bf16[128,3456]{1,0:T(8,128)(2,1)} %own_ref.3) | copy-start | bytes 2654212
  30.3 4.2 %collective-permute-start.4 = (bf16[12,128,256]{2,1,0:T(8,128)(2,1)S(1)}, bf16[12,128,256]{2,1,0:T(8,128)(2,1)S(1)}, u32[]{:S(2)}, u32[]{:S(2)}) collective-permute-start(bf16[12,128,256]{2,1,0:T(8,128)(2,1)S(1)} %get-tuple-element.42), channel_id=1, source_target_pairs={{0,1},{1,0},{2,3},{3,2},{4,5},{5,4},{6,7},{7,6},{8,9},{9,8},{10,11... | collective-permute-start | bytes 2359304 | tf_op jit(solution)/shard_map/ppermute | solution.py:649
  35.6 3.5 %collective-permute-start.5 = (bf16[4,128,256]{2,1,0:T(8,128)(2,1)S(1)}, bf16[4,128,256]{2,1,0:T(8,128)(2,1)S(1)}, u32[]{:S(2)}, u32[]{:S(2)}) collective-permute-start(bf16[4,128,256]{2,1,0:T(8,128)(2,1)S(1)} %get-tuple-element.44), channel_id=1, source_target_pairs={{1,0},{3,2},{5,4},{7,6},{9,8},{11,10},{13,12},{15,14},{17,16},{19,... | collective-permute-start | bytes 786440 | tf_op jit(solution)/shard_map/ppermute | solution.py:668
  37.9 16.4 %collective-permute-start.7 = (bf16[7,256,128]{2,1,0:T(8,128)(2,1)S(1)}, bf16[7,256,128]{2,1,0:T(8,128)(2,1)S(1)}, u32[]{:S(2)}, u32[]{:S(2)}) collective-permute-start(bf16[7,256,128]{2,1,0:T(8,128)(2,1)S(1)} %get-tuple-element.47), channel_id=1, source_target_pairs={{0,3},{2,5},{4,7},{6,9},{8,11},{10,13},{12,15},{16,19},{18,21},{20... | collective-permute-start | bytes 1376264 | tf_op jit(solution)/shard_map/ppermute | solution.py:645
  44.0 12.1 %collective-permute-start.6 = (f32[6,128,256]{2,1,0:T(8,128)S(1)}, f32[6,128,256]{2,1,0:T(8,128)S(1)}, u32[]{:S(2)}, u32[]{:S(2)}) collective-permute-start(f32[6,128,256]{2,1,0:T(8,128)S(1)} %get-tuple-element.46), channel_id=1, source_target_pairs={{0,1},{1,0},{2,3},{3,2},{4,5},{5,4},{6,7},{7,6},{8,9},{9,8},{10,11... | collective-permute-start | bytes 2359304 | tf_op jit(solution)/shard_map/ppermute | solution.py:649
  54.3 1.8 %collective-permute-start.8 = (f32[6,128,128]{2,1,0:T(8,128)S(1)}, f32[6,128,128]{2,1,0:T(8,128)S(1)}, u32[]{:S(2)}, u32[]{:S(2)}) collective-permute-start(f32[6,128,128]{2,1,0:T(8,128)S(1)} %get-tuple-element.52), channel_id=1, source_target_pairs={{0,1},{1,0},{2,3},{3,2},{4,5},{5,4},{6,7},{7,6},{8,9},{9,8},{10,11... | collective-permute-start | bytes 1179656 | tf_op jit(solution)/shard_map/ppermute | solution.py:649

commit v11 on v10

--- a/solution.py
+++ b/solution.py
@@ -659,10 +659,10 @@
     )
     halo = handed_on(message)
     *thirds, local = layer_three(volume, prior, weights_three, gain, shift, core)
-    halo, local = lax.optimization_barrier((halo, local))
+    halo, other_four = lax.optimization_barrier((halo, others[2]))
     thirds = (*thirds, halo, gain, shift)
     local = swapped(local)
-    weights_four = four_weights(kernel_four, others[2], core)
+    weights_four = four_weights(kernel_four, other_four, core)
     message, mid, rows = four_edges(core, thirds, local, weights_four)
     halo = handed_on(message)
     rows = lax.ppermute(rows, "fl", [(1, 0)])

time: 57.7 us -> 56.6 us (0.981)
  waiting for transfers between devices: 15 us -> 12 us
  starting transfers between devices: 10.3 us -> 12.3 us
    ppermute x2, waiting for transfers between devices: 12.6 us -> 10.2 us  [handed_on(): return lax.ppermute(message, ('sp', 'fl'), pairs)]
    ppermute x1, starting transfers between devices: 2.21 us -> 4.09 us  [shards(): rows = lax.ppermute(rows, 'fl', [(1, 0)])]
    ppermute x6, waiting for transfers between devices: 2.4 us -> 1.72 us  [swapped(): return lax.ppermute(value, 'fl', [(0, 1), (1, 0)])]
  transfers between devices with their start and end apart: 9 -> 9, of which waited for: 4 -> 3; matrix products, arithmetic and copies ran while one was open for 1% -> 1% of each run, Pallas kernels for 48% -> 48%
where the time goes in v11:
time: 56.6 us; the launch traced here: 56.4 us
  Pallas kernels  31.3 us (55%)
  starting transfers between devices  12.3 us (22%)
  waiting for transfers between devices  12 us (21%)
  other arithmetic  0.78 us (1%)
    pallas_call x1, Pallas kernels, layer_three(): pl.pallas_call(three_kernel, grid_spec=pltpu.PrefetchScalarGridSpec(num_s...  16 us
    ppermute x2, waiting for transfers between devices, handed_on(): return lax.ppermute(message, ('sp', 'fl'), pairs)  10.2 us
    ppermute x6, starting transfers between devices, swapped(): return lax.ppermute(value, 'fl', [(0, 1), (1, 0)])  5.57 us
    pallas_call x1, Pallas kernels, three_picks(): pl.pallas_call(three_picks_kernel, grid_spec=pltpu.PrefetchScalarGridSpec...  5.19 us
    pallas_call x1, Pallas kernels, layer_four(): pl.pallas_call(four_kernel, out_shape=[jax.ShapeDtypeStruct((out_rows, ou...  4.84 us
    ppermute x1, starting transfers between devices, shards(): rows = lax.ppermute(rows, 'fl', [(1, 0)])  4.09 us
    ppermute x2, starting transfers between devices, handed_on(): return lax.ppermute(message, ('sp', 'fl'), pairs)  2.58 us
    ppermute x6, waiting for transfers between devices, swapped(): return lax.ppermute(value, 'fl', [(0, 1), (1, 0)])  1.72 us
  transfers between devices with their start and end apart: 9, of which 3 were waited for; matrix products, arithmetic and copies ran while one was open for 1% of the time, Pallas kernels for 48%

profile of v11, /device:TPU:25, one launch (start us, length us, event | category | flops | bytes accessed | tf_op | source)
XLA Modules:
  0.0 56.4 jit_solution(1556090710253671900)
XLA Ops:
  0.0 0.7 %collective-permute-start.2 = (bf16[128,3456]{1,0:T(8,128)(2,1)}, bf16[128,3456]{1,0:T(8,128)(2,1)S(1)}, u32[]{:S(2)}, u32[]{:S(2)}) collective-permute-start(bf16[128,3456]{1,0:T(8,128)(2,1)} %own_ref.3), channel_id=1, source_target_pairs={{0,1},{1,0},{2,3},{3,2},{4,5},{5,4},{6,7},{7,6},{8,9},{9,8},{10,11... | collective-permute-start | bytes 2654216 | tf_op jit(solution)/shard_map/ppermute | solution.py:649
  0.7 0.0 collective-permute-start
  0.7 0.8 %maximum_bitcast_fusion.own_scales_ref = f32[3,128]{1,0:T(4,128)S(1)} fusion(f32[128]{0:T(128)} %param.17, f32[128]{0:T(128)} %param.16, f32[64]{0:T(128)} %param.14, f32[64]{0:T(128)} %param.13), kind=kLoop, calls=%fused_computation | loop fusion | flops 1152 | bytes 3072 | tf_op jit(solution)/shard_map/reshape | solution.py:654
  1.5 0.5 collective-permute-start.1
  2.0 0.0 copy-start.2
  2.0 5.2 %three_picks.1 = (bf16[25,192,256]{2,1,0:T(8,128)(2,1)S(1)}, bf16[25,192,256]{2,1,0:T(8,128)(2,1)S(1)}) custom-call(s32[1]{0:T(128)} %bitcast.core_ref, bf16[1,64,16,24,512]{4,3,2,1,0:T(8,128)(2,1)} %x_ref.1, bf16[1,64,16,24,512]{4,3,2,1,0:T(8,128)(2,1)} %x_ref.1, bf16[1,64,16,24,512]{4,3,2,1,0:T(8,128)(2,1)} %x_ref.1), custom_call_target="tpu_custom_call" | custom-call | flops 1000000000 | bytes 10000000 | tf_op jit(solution)/shard_map/three_picks/pallas_call | solution.py:196
  7.2 0.0 copy-start.1
  7.2 0.0 collective-permute-done.1.other_scales_ref
  7.2 0.0 collective-permute-done.other_ref
  7.2 0.0 collective-permute-done.2.other_ref
  7.2 0.0 copy-done.2
  7.2 1.3 %three_edges.1 = (bf16[12,128,256]{2,1,0:T(8,128)(2,1)S(1)}, bf16[128,1728]{1,0:T(8,128)(2,1)S(1)}, f32[128,1]{1,0:T(8,128)S(1)}, f32[128,1]{1,0:T(8,128)S(1)}, f32[128,128]{1,0:T(8,128)S(1)}) custom-call(s32[1]{0:T(128)} %bitcast.core_ref, bf16[25,192,256]{2,1,0:T(8,128)(2,1)S(1)} %get-tuple-element.30.picked_ref, bf16[64,1728]{1,0:T(8,128)(2,1)S(1)} %copy-done.2, ...), custom_call_target="tpu_custom_call" | custom-call | flops 1000000000 | bytes 1000000 | tf_op jit(solution)/shard_map/three_edges/pallas_call | solution.py:278
  8.6 1.3 %collective-permute-start.3 = (bf16[12,128,256]{2,1,0:T(8,128)(2,1)S(1)}, bf16[12,128,256]{2,1,0:T(8,128)(2,1)S(1)}, u32[]{:S(2)}, u32[]{:S(2)}) collective-permute-start(bf16[12,128,256]{2,1,0:T(8,128)(2,1)S(1)} %get-tuple-element.39), channel_id=1, source_target_pairs={{0,3},{2,5},{4,7},{6,9},{8,11},{10,13},{12,15},{16,19},{18,21},{20... | collective-permute-start | bytes 2359304 | tf_op jit(solution)/shard_map/ppermute | solution.py:645
  9.9 0.0 copy-done.1
  9.9 0.0 copy-start
  9.9 16.0 %layer_three.1 = (bf16[4,12,128,256]{3,2,1,0:T(8,128)(2,1)S(1)}, f32[12,128,256]{2,1,0:T(8,128)S(1)}, f32[4,128,256]{2,1,0:T(8,128)S(1)}, bf16[12,128,256]{2,1,0:T(8,128)(2,1)S(1)}) custom-call(s32[1]{0:T(128)} %bitcast.core_ref, bf16[1,64,16,24,512]{4,3,2,1,0:T(8,128)(2,1)} %x_ref.1, bf16[25,192,256]{2,1,0:T(8,128)(2,1)S(1)} %get-tuple-element.29.before_ref, ...), custom_call_target="tpu_custom_call" | custom-call | flops 10000000000 | bytes 20000000 | tf_op jit(solution)/shard_map/layer_three/pallas_call | solution.py:355
  25.9 2.3 %collective-permute-start.4 = (bf16[12,128,256]{2,1,0:T(8,128)(2,1)S(1)}, bf16[12,128,256]{2,1,0:T(8,128)(2,1)S(1)}, u32[]{:S(2)}, u32[]{:S(2)}) collective-permute-start(bf16[12,128,256]{2,1,0:T(8,128)(2,1)S(1)} %get-tuple-element.42), channel_id=1, source_target_pairs={{0,1},{1,0},{2,3},{3,2},{4,5},{5,4},{6,7},{7,6},{8,9},{9,8},{10,11... | collective-permute-start | bytes 2359304 | tf_op jit(solution)/shard_map/ppermute | solution.py:649
  28.3 2.0 %collective-permute-done.3.refs_3_ = bf16[12,128,256]{2,1,0:T(8,128)(2,1)S(1)} collective-permute-done((bf16[12,128,256]{2,1,0:T(8,128)(2,1)S(1)}, bf16[12,128,256]{2,1,0:T(8,128)(2,1)S(1)}, u32[]{:S(2)}, u32[]{:S(2)}) %collective-permute-start.3) | collective-permute-done | bytes 786464 | tf_op jit(solution)/shard_map/ppermute | solution.py:645
  30.3 0.0 copy-done
  30.3 1.2 %four_weights.1.refs_7_.refs_8_ = bf16[256,3456]{1,0:T(8,128)(2,1)S(1)} custom-call(s32[1]{0:T(128)} %bitcast.core_ref, bf16[128,3456]{1,0:T(8,128)(2,1)S(1)} %copy-done, bf16[128,3456]{1,0:T(8,128)(2,1)S(1)} %collective-permute-done.2.other_ref), custom_call_target="tpu_custom_call" | custom-call | flops 1000 | bytes 1000 | tf_op jit(solution)/shard_map/four_weights/pallas_call | solution.py:110
  31.5 0.0 collective-permute-done.4.refs_6_.refs_7_
  31.5 1.2 %four_edges.1 = (bf16[7,256,128]{2,1,0:T(8,128)(2,1)S(1)}, bf16[256,384]{1,0:T(8,128)(2,1)S(1)}, bf16[4,128,256]{2,1,0:T(8,128)(2,1)S(1)}) custom-call(s32[1]{0:T(128)} %bitcast.core_ref, bf16[4,12,128,256]{3,2,1,0:T(8,128)(2,1)S(1)} %get-tuple-element.36.refs_0_, f32[12,128,256]{2,1,0:T(8,128)S(1)} %get-tuple-element.37.refs_1_, ...), custom_call_target="tpu_custom_call" | custom-call | flops 1000000000 | bytes 1000000 | tf_op jit(solution)/shard_map/four_edges/pallas_call | solution.py:471
  32.7 4.1 %collective-permute-start.5 = (bf16[4,128,256]{2,1,0:T(8,128)(2,1)S(1)}, bf16[4,128,256]{2,1,0:T(8,128)(2,1)S(1)}, u32[]{:S(2)}, u32[]{:S(2)}) collective-permute-start(bf16[4,128,256]{2,1,0:T(8,128)(2,1)S(1)} %get-tuple-element.44), channel_id=1, source_target_pairs={{1,0},{3,2},{5,4},{7,6},{9,8},{11,10},{13,12},{15,14},{17,16},{19,... | collective-permute-start | bytes 786440 | tf_op jit(solution)/shard_map/ppermute | solution.py:668
  36.8 1.3 %collective-permute-start.7 = (bf16[7,256,128]{2,1,0:T(8,128)(2,1)S(1)}, bf16[7,256,128]{2,1,0:T(8,128)(2,1)S(1)}, u32[]{:S(2)}, u32[]{:S(2)}) collective-permute-start(bf16[7,256,128]{2,1,0:T(8,128)(2,1)S(1)} %get-tuple-element.47), channel_id=1, source_target_pairs={{0,3},{2,5},{4,7},{6,9},{8,11},{10,13},{12,15},{16,19},{18,21},{20... | collective-permute-start | bytes 1376264 | tf_op jit(solution)/shard_map/ppermute | solution.py:645
  38.1 0.0 collective-permute-done.5.refs_6_
  38.1 4.8 %layer_four.1 = (f32[6,128,256]{2,1,0:T(8,128)S(1)}, f32[6,128,256]{2,1,0:T(8,128)S(1)}, f32[128,256]{1,0:T(8,128)S(1)}) custom-call(s32[1]{0:T(128)} %bitcast.core_ref, bf16[4,12,128,256]{3,2,1,0:T(8,128)(2,1)S(1)} %get-tuple-element.36.refs_0_, f32[12,128,256]{2,1,0:T(8,128)S(1)} %get-tuple-element.37.refs_1_, ...), custom_call_target="tpu_custom_call" | custom-call | flops 4000000000 | bytes 4000000 | tf_op jit(solution)/shard_map/layer_four/pallas_call | solution.py:536
  43.0 2.0 %collective-permute-start.6 = (f32[6,128,256]{2,1,0:T(8,128)S(1)}, f32[6,128,256]{2,1,0:T(8,128)S(1)}, u32[]{:S(2)}, u32[]{:S(2)}) collective-permute-start(f32[6,128,256]{2,1,0:T(8,128)S(1)} %get-tuple-element.46), channel_id=1, source_target_pairs={{0,1},{1,0},{2,3},{3,2},{4,5},{5,4},{6,7},{7,6},{8,9},{9,8},{10,11... | collective-permute-start | bytes 2359304 | tf_op jit(solution)/shard_map/ppermute | solution.py:649
  45.0 8.3 %collective-permute-done.7.halo_ref = bf16[7,256,128]{2,1,0:T(8,128)(2,1)S(1)} collective-permute-done((bf16[7,256,128]{2,1,0:T(8,128)(2,1)S(1)}, bf16[7,256,128]{2,1,0:T(8,128)(2,1)S(1)}, u32[]{:S(2)}, u32[]{:S(2)}) %collective-permute-start.7) | collective-permute-done | bytes 458784 | tf_op jit(solution)/shard_map/ppermute | solution.py:645
  53.2 0.1 collective-permute-start.8
  53.3 1.7 %collective-permute-done.8.shares_ref = f32[6,128,128]{2,1,0:T(8,128)S(1)} collective-permute-done((f32[6,128,128]{2,1,0:T(8,128)S(1)}, f32[6,128,128]{2,1,0:T(8,128)S(1)}, u32[]{:S(2)}, u32[]{:S(2)}) %collective-permute-start.8) | collective-permute-done | bytes 393248 | tf_op jit(solution)/shard_map/ppermute | solution.py:649
  55.0 0.0 collective-permute-done.6.got_ref
  55.0 1.4 %assemble.1 = bf16[3072,128]{1,0:T(8,128)(2,1)} custom-call(s32[1]{0:T(128)} %bitcast.core_ref, f32[6,128,256]{2,1,0:T(8,128)S(1)} %get-tuple-element.45.own_ref, f32[6,128,256]{2,1,0:T(8,128)S(1)} %collective-permute-done.6.got_ref, bf16[7,256,128]{2,1,0:T(8,128)(2,1)S(1)} %collective-permute-done.7.halo_ref, f32[128,128]{1,0:T(8,128)S(1)} %get-tuple-element.50.fix_ref, ...), custom_call_target="tpu_custom_call" | custom-call | tf_op jit(solution)/shard_map/assemble/pallas_call | solution.py:631
  (1 shorter events, 0.0 us)
Async XLA Ops:
  0.0 7.2 %collective-permute-start.2 = (bf16[128,3456]{1,0:T(8,128)(2,1)}, bf16[128,3456]{1,0:T(8,128)(2,1)S(1)}, u32[]{:S(2)}, u32[]{:S(2)}) collective-permute-start(bf16[128,3456]{1,0:T(8,128)(2,1)} %own_ref.3), channel_id=1, source_target_pairs={{0,1},{1,0},{2,3},{3,2},{4,5},{5,4},{6,7},{7,6},{8,9},{9,8},{10,11... | collective-permute-start | bytes 2654216 | tf_op jit(solution)/shard_map/ppermute | solution.py:649
  0.7 6.5 %collective-permute-start = (bf16[64,1728]{1,0:T(8,128)(2,1)}, bf16[64,1728]{1,0:T(8,128)(2,1)S(1)}, u32[]{:S(2)}, u32[]{:S(2)}) collective-permute-start(bf16[64,1728]{1,0:T(8,128)(2,1)} %own_ref.2), channel_id=1, source_target_pairs={{0,1},{1,0},{2,3},{3,2},{4,5},{5,4},{6,7},{7,6},{8,9},{9,8},{10,11... | collective-permute-start | bytes 663560 | tf_op jit(solution)/shard_map/ppermute | solution.py:649
  1.5 5.7 %collective-permute-start.1 = (f32[3,128]{1,0:T(4,128)S(1)}, f32[3,128]{1,0:T(4,128)S(1)}, u32[]{:S(2)}, u32[]{:S(2)}) collective-permute-start(f32[3,128]{1,0:T(4,128)S(1)} %maximum_bitcast_fusion.own_scales_ref), channel_id=1, source_target_pairs={{0,1},{1,0},{2,3},{3,2},{4,5},{5,4},{6,7},{7,6},{8,9},{9,8},{10,11... | collective-permute-start | bytes 4616 | tf_op jit(solution)/shard_map/ppermute | solution.py:649
  2.0 5.2 %copy-start.2 = (bf16[64,1728]{1,0:T(8,128)(2,1)S(1)}, bf16[64,1728]{1,0:T(8,128)(2,1)}, u32[]{:S(2)}) copy-start(bf16[64,1728]{1,0:T(8,128)(2,1)} %own_ref.2) | copy-start | bytes 663556
  7.2 2.7 %copy-start.1 = (bf16[256,256]{1,0:T(8,128)(2,1)S(1)}, bf16[256,256]{1,0:T(8,128)(2,1)}, u32[]{:S(2)}) copy-start(bf16[256,256]{1,0:T(8,128)(2,1)} %constant.6.clone.place_ref.refs_8_.refs_9_) | copy-start | bytes 393220
  8.6 21.7 %collective-permute-start.3 = (bf16[12,128,256]{2,1,0:T(8,128)(2,1)S(1)}, bf16[12,128,256]{2,1,0:T(8,128)(2,1)S(1)}, u32[]{:S(2)}, u32[]{:S(2)}) collective-permute-start(bf16[12,128,256]{2,1,0:T(8,128)(2,1)S(1)} %get-tuple-element.39), channel_id=1, source_target_pairs={{0,3},{2,5},{4,7},{6,9},{8,11},{10,13},{12,15},{16,19},{18,21},{20... | collective-permute-start | bytes 2359304 | tf_op jit(solution)/shard_map/ppermute | solution.py:645
  9.9 20.4 %copy-start = (bf16[128,3456]{1,0:T(8,128)(2,1)S(1)}, bf16[128,3456]{1,0:T(8,128)(2,1)}, u32[]{:S(2)}) copy-start(bf16[128,3456]{1,0:T(8,128)(2,1)} %own_ref.3) | copy-start | bytes 2654212
  25.9 5.6 %collective-permute-start.4 = (bf16[12,128,256]{2,1,0:T(8,128)(2,1)S(1)}, bf16[12,128,256]{2,1,0:T(8,128)(2,1)S(1)}, u32[]{:S(2)}, u32[]{:S(2)}) collective-permute-start(bf16[12,128,256]{2,1,0:T(8,128)(2,1)S(1)} %get-tuple-element.42), channel_id=1, source_target_pairs={{0,1},{1,0},{2,3},{3,2},{4,5},{5,4},{6,7},{7,6},{8,9},{9,8},{10,11... | collective-permute-start | bytes 2359304 | tf_op jit(solution)/shard_map/ppermute | solution.py:649
  32.7 5.4 %collective-permute-start.5 = (bf16[4,128,256]{2,1,0:T(8,128)(2,1)S(1)}, bf16[4,128,256]{2,1,0:T(8,128)(2,1)S(1)}, u32[]{:S(2)}, u32[]{:S(2)}) collective-permute-start(bf16[4,128,256]{2,1,0:T(8,128)(2,1)S(1)} %get-tuple-element.44), channel_id=1, source_target_pairs={{1,0},{3,2},{5,4},{7,6},{9,8},{11,10},{13,12},{15,14},{17,16},{19,... | collective-permute-start | bytes 786440 | tf_op jit(solution)/shard_map/ppermute | solution.py:668
  36.8 16.4 %collective-permute-start.7 = (bf16[7,256,128]{2,1,0:T(8,128)(2,1)S(1)}, bf16[7,256,128]{2,1,0:T(8,128)(2,1)S(1)}, u32[]{:S(2)}, u32[]{:S(2)}) collective-permute-start(bf16[7,256,128]{2,1,0:T(8,128)(2,1)S(1)} %get-tuple-element.47), channel_id=1, source_target_pairs={{0,3},{2,5},{4,7},{6,9},{8,11},{10,13},{12,15},{16,19},{18,21},{20... | collective-permute-start | bytes 1376264 | tf_op jit(solution)/shard_map/ppermute | solution.py:645
  43.0 12.1 %collective-permute-start.6 = (f32[6,128,256]{2,1,0:T(8,128)S(1)}, f32[6,128,256]{2,1,0:T(8,128)S(1)}, u32[]{:S(2)}, u32[]{:S(2)}) collective-permute-start(f32[6,128,256]{2,1,0:T(8,128)S(1)} %get-tuple-element.46), channel_id=1, source_target_pairs={{0,1},{1,0},{2,3},{3,2},{4,5},{5,4},{6,7},{7,6},{8,9},{9,8},{10,11... | collective-permute-start | bytes 2359304 | tf_op jit(solution)/shard_map/ppermute | solution.py:649
  53.2 1.8 %collective-permute-start.8 = (f32[6,128,128]{2,1,0:T(8,128)S(1)}, f32[6,128,128]{2,1,0:T(8,128)S(1)}, u32[]{:S(2)}, u32[]{:S(2)}) collective-permute-start(f32[6,128,128]{2,1,0:T(8,128)S(1)} %get-tuple-element.52), channel_id=1, source_target_pairs={{0,1},{1,0},{2,3},{3,2},{4,5},{5,4},{6,7},{7,6},{8,9},{9,8},{10,11... | collective-permute-start | bytes 1179656 | tf_op jit(solution)/shard_map/ppermute | solution.py:649

commit v12 on v11

--- a/solution.py
+++ b/solution.py
@@ -158,7 +158,7 @@
             jnp.concatenate([part[at * chans : (at + 1) * chans] for part in parts], 0) for at in range(len(spots))
         ]
 
-    @pl.when(core == 0)
+    @pl.when((core == 0) & (step < last))
     def _():
         for plane, data in enumerate(picked([(plane, rim) for plane in range(block)])):
             picked_ref[step * block + plane] = data
@@ -166,8 +166,12 @@
     @pl.when((core == 0) & (step == last))
     def _():
         spots = [(plane, row) for plane in range(block - 3, block) for row in range(rim - 2, rim + 1)]
-        for index, data in enumerate(picked(spots)):
-            picked_ref[planes + index] = data
+        alone = [(plane, rim) for plane in range(block - 3)]
+        for index, ((plane, row), data) in enumerate(zip(spots + alone, picked(spots + alone))):
+            if index < len(spots):
+                picked_ref[planes + index] = data
+            if row == rim:
+                picked_ref[planes - block + plane] = data
         prior_ref[...] = jnp.zeros_like(prior_ref)
 
     @pl.when(core == 1)

time: 56.6 us -> 56.1 us (level)
  starting transfers between devices: 12.3 us -> 11 us
    ppermute x1, starting transfers between devices: 4.09 us -> 2.85 us  [shards(): rows = lax.ppermute(rows, 'fl', [(1, 0)])]
  transfers between devices with their start and end apart: 9 -> 9, of which waited for: 3 -> 3; matrix products, arithmetic and copies ran while one was open for 1% -> 1% of each run, Pallas kernels for 48% -> 49%
where the time goes in v12:
time: 56.1 us; the launch traced here: 55.9 us
  Pallas kernels  31.4 us (56%)
  waiting for transfers between devices  12.5 us (22%)
  starting transfers between devices  11 us (20%)
  other arithmetic  0.78 us (1%)
    pallas_call x1, Pallas kernels, layer_three(): pl.pallas_call(three_kernel, grid_spec=pltpu.PrefetchScalarGridSpec(num_s...  16 us
    ppermute x2, waiting for transfers between devices, handed_on(): return lax.ppermute(message, ('sp', 'fl'), pairs)  10.8 us
    ppermute x6, starting transfers between devices, swapped(): return lax.ppermute(value, 'fl', [(0, 1), (1, 0)])  5.57 us
    pallas_call x1, Pallas kernels, three_picks(): pl.pallas_call(three_picks_kernel, grid_spec=pltpu.PrefetchScalarGridSpec...  5.19 us
    pallas_call x1, Pallas kernels, layer_four(): pl.pallas_call(four_kernel, out_shape=[jax.ShapeDtypeStruct((out_rows, ou...  4.84 us
    ppermute x1, starting transfers between devices, shards(): rows = lax.ppermute(rows, 'fl', [(1, 0)])  2.85 us
    ppermute x2, starting transfers between devices, handed_on(): return lax.ppermute(message, ('sp', 'fl'), pairs)  2.58 us
    ppermute x6, waiting for transfers between devices, swapped(): return lax.ppermute(value, 'fl', [(0, 1), (1, 0)])  1.72 us
  transfers between devices with their start and end apart: 9, of which 3 were waited for; matrix products, arithmetic and copies ran while one was open for 1% of the time, Pallas kernels for 49%

profile of v12, /device:TPU:25, one launch (start us, length us, event | category | flops | bytes accessed | tf_op | source)
XLA Modules:
  0.0 55.9 jit_solution(14165685769562951466)
XLA Ops:
  0.0 0.7 %collective-permute-start.2 = (bf16[128,3456]{1,0:T(8,128)(2,1)}, bf16[128,3456]{1,0:T(8,128)(2,1)S(1)}, u32[]{:S(2)}, u32[]{:S(2)}) collective-permute-start(bf16[128,3456]{1,0:T(8,128)(2,1)} %own_ref.3), channel_id=1, source_target_pairs={{0,1},{1,0},{2,3},{3,2},{4,5},{5,4},{6,7},{7,6},{8,9},{9,8},{10,11... | collective-permute-start | bytes 2654216 | tf_op jit(solution)/shard_map/ppermute | solution.py:653
  0.7 0.0 collective-permute-start
  0.7 0.8 %maximum_bitcast_fusion.own_scales_ref = f32[3,128]{1,0:T(4,128)S(1)} fusion(f32[128]{0:T(128)} %param.17, f32[128]{0:T(128)} %param.16, f32[64]{0:T(128)} %param.14, f32[64]{0:T(128)} %param.13), kind=kLoop, calls=%fused_computation | loop fusion | flops 1152 | bytes 3072 | tf_op jit(solution)/shard_map/reshape | solution.py:658
  1.5 0.5 collective-permute-start.1
  2.0 0.0 copy-start.2
  2.0 5.2 %three_picks.1 = (bf16[25,192,256]{2,1,0:T(8,128)(2,1)S(1)}, bf16[25,192,256]{2,1,0:T(8,128)(2,1)S(1)}) custom-call(s32[1]{0:T(128)} %bitcast.core_ref, bf16[1,64,16,24,512]{4,3,2,1,0:T(8,128)(2,1)} %x_ref.1, bf16[1,64,16,24,512]{4,3,2,1,0:T(8,128)(2,1)} %x_ref.1, bf16[1,64,16,24,512]{4,3,2,1,0:T(8,128)(2,1)} %x_ref.1), custom_call_target="tpu_custom_call" | custom-call | flops 1000000000 | bytes 10000000 | tf_op jit(solution)/shard_map/three_picks/pallas_call | solution.py:200
  7.2 0.0 copy-start.1
  7.2 0.0 collective-permute-done.1.other_scales_ref
  7.2 0.0 collective-permute-done.other_ref
  7.2 0.0 collective-permute-done.2.other_ref
  7.2 0.0 copy-done.2
  7.2 1.3 %three_edges.1 = (bf16[12,128,256]{2,1,0:T(8,128)(2,1)S(1)}, bf16[128,1728]{1,0:T(8,128)(2,1)S(1)}, f32[128,1]{1,0:T(8,128)S(1)}, f32[128,1]{1,0:T(8,128)S(1)}, f32[128,128]{1,0:T(8,128)S(1)}) custom-call(s32[1]{0:T(128)} %bitcast.core_ref, bf16[25,192,256]{2,1,0:T(8,128)(2,1)S(1)} %get-tuple-element.30.picked_ref, bf16[64,1728]{1,0:T(8,128)(2,1)S(1)} %copy-done.2, ...), custom_call_target="tpu_custom_call" | custom-call | flops 1000000000 | bytes 1000000 | tf_op jit(solution)/shard_map/three_edges/pallas_call | solution.py:282
  8.6 1.3 %collective-permute-start.3 = (bf16[12,128,256]{2,1,0:T(8,128)(2,1)S(1)}, bf16[12,128,256]{2,1,0:T(8,128)(2,1)S(1)}, u32[]{:S(2)}, u32[]{:S(2)}) collective-permute-start(bf16[12,128,256]{2,1,0:T(8,128)(2,1)S(1)} %get-tuple-element.39), channel_id=1, source_target_pairs={{0,3},{2,5},{4,7},{6,9},{8,11},{10,13},{12,15},{16,19},{18,21},{20... | collective-permute-start | bytes 2359304 | tf_op jit(solution)/shard_map/ppermute | solution.py:649
  9.9 0.0 copy-done.1
  9.9 0.0 copy-start
  9.9 16.0 %layer_three.1 = (bf16[4,12,128,256]{3,2,1,0:T(8,128)(2,1)S(1)}, f32[12,128,256]{2,1,0:T(8,128)S(1)}, f32[4,128,256]{2,1,0:T(8,128)S(1)}, bf16[12,128,256]{2,1,0:T(8,128)(2,1)S(1)}) custom-call(s32[1]{0:T(128)} %bitcast.core_ref, bf16[1,64,16,24,512]{4,3,2,1,0:T(8,128)(2,1)} %x_ref.1, bf16[25,192,256]{2,1,0:T(8,128)(2,1)S(1)} %get-tuple-element.29.before_ref, ...), custom_call_target="tpu_custom_call" | custom-call | flops 10000000000 | bytes 20000000 | tf_op jit(solution)/shard_map/layer_three/pallas_call | solution.py:359
  25.9 2.3 %collective-permute-start.4 = (bf16[12,128,256]{2,1,0:T(8,128)(2,1)S(1)}, bf16[12,128,256]{2,1,0:T(8,128)(2,1)S(1)}, u32[]{:S(2)}, u32[]{:S(2)}) collective-permute-start(bf16[12,128,256]{2,1,0:T(8,128)(2,1)S(1)} %get-tuple-element.42), channel_id=1, source_target_pairs={{0,1},{1,0},{2,3},{3,2},{4,5},{5,4},{6,7},{7,6},{8,9},{9,8},{10,11... | collective-permute-start | bytes 2359304 | tf_op jit(solution)/shard_map/ppermute | solution.py:653
  28.3 2.5 %collective-permute-done.3.refs_3_ = bf16[12,128,256]{2,1,0:T(8,128)(2,1)S(1)} collective-permute-done((bf16[12,128,256]{2,1,0:T(8,128)(2,1)S(1)}, bf16[12,128,256]{2,1,0:T(8,128)(2,1)S(1)}, u32[]{:S(2)}, u32[]{:S(2)}) %collective-permute-start.3) | collective-permute-done | bytes 786464 | tf_op jit(solution)/shard_map/ppermute | solution.py:649
  30.8 0.0 copy-done
  30.8 1.2 %four_weights.1.refs_7_.refs_8_ = bf16[256,3456]{1,0:T(8,128)(2,1)S(1)} custom-call(s32[1]{0:T(128)} %bitcast.core_ref, bf16[128,3456]{1,0:T(8,128)(2,1)S(1)} %copy-done, bf16[128,3456]{1,0:T(8,128)(2,1)S(1)} %collective-permute-done.2.other_ref), custom_call_target="tpu_custom_call" | custom-call | flops 1000 | bytes 1000 | tf_op jit(solution)/shard_map/four_weights/pallas_call | solution.py:110
  32.0 0.0 collective-permute-done.4.refs_6_.refs_7_
  32.0 1.4 %four_edges.1 = (bf16[7,256,128]{2,1,0:T(8,128)(2,1)S(1)}, bf16[256,384]{1,0:T(8,128)(2,1)S(1)}, bf16[4,128,256]{2,1,0:T(8,128)(2,1)S(1)}) custom-call(s32[1]{0:T(128)} %bitcast.core_ref, bf16[4,12,128,256]{3,2,1,0:T(8,128)(2,1)S(1)} %get-tuple-element.36.refs_0_, f32[12,128,256]{2,1,0:T(8,128)S(1)} %get-tuple-element.37.refs_1_, ...), custom_call_target="tpu_custom_call" | custom-call | flops 1000000000 | bytes 1000000 | tf_op jit(solution)/shard_map/four_edges/pallas_call | solution.py:475
  33.4 2.8 %collective-permute-start.5 = (bf16[4,128,256]{2,1,0:T(8,128)(2,1)S(1)}, bf16[4,128,256]{2,1,0:T(8,128)(2,1)S(1)}, u32[]{:S(2)}, u32[]{:S(2)}) collective-permute-start(bf16[4,128,256]{2,1,0:T(8,128)(2,1)S(1)} %get-tuple-element.44), channel_id=1, source_target_pairs={{1,0},{3,2},{5,4},{7,6},{9,8},{11,10},{13,12},{15,14},{17,16},{19,... | collective-permute-start | bytes 786440 | tf_op jit(solution)/shard_map/ppermute | solution.py:672
  36.3 1.3 %collective-permute-start.7 = (bf16[7,256,128]{2,1,0:T(8,128)(2,1)S(1)}, bf16[7,256,128]{2,1,0:T(8,128)(2,1)S(1)}, u32[]{:S(2)}, u32[]{:S(2)}) collective-permute-start(bf16[7,256,128]{2,1,0:T(8,128)(2,1)S(1)} %get-tuple-element.47), channel_id=1, source_target_pairs={{0,3},{2,5},{4,7},{6,9},{8,11},{10,13},{12,15},{16,19},{18,21},{20... | collective-permute-start | bytes 1376264 | tf_op jit(solution)/shard_map/ppermute | solution.py:649
  37.6 0.0 collective-permute-done.5.refs_6_
  37.6 4.8 %layer_four.1 = (f32[6,128,256]{2,1,0:T(8,128)S(1)}, f32[6,128,256]{2,1,0:T(8,128)S(1)}, f32[128,256]{1,0:T(8,128)S(1)}) custom-call(s32[1]{0:T(128)} %bitcast.core_ref, bf16[4,12,128,256]{3,2,1,0:T(8,128)(2,1)S(1)} %get-tuple-element.36.refs_0_, f32[12,128,256]{2,1,0:T(8,128)S(1)} %get-tuple-element.37.refs_1_, ...), custom_call_target="tpu_custom_call" | custom-call | flops 4000000000 | bytes 4000000 | tf_op jit(solution)/shard_map/layer_four/pallas_call | solution.py:540
  42.5 2.0 %collective-permute-start.6 = (f32[6,128,256]{2,1,0:T(8,128)S(1)}, f32[6,128,256]{2,1,0:T(8,128)S(1)}, u32[]{:S(2)}, u32[]{:S(2)}) collective-permute-start(f32[6,128,256]{2,1,0:T(8,128)S(1)} %get-tuple-element.46), channel_id=1, source_target_pairs={{0,1},{1,0},{2,3},{3,2},{4,5},{5,4},{6,7},{7,6},{8,9},{9,8},{10,11... | collective-permute-start | bytes 2359304 | tf_op jit(solution)/shard_map/ppermute | solution.py:653
  44.4 8.2 %collective-permute-done.7.halo_ref = bf16[7,256,128]{2,1,0:T(8,128)(2,1)S(1)} collective-permute-done((bf16[7,256,128]{2,1,0:T(8,128)(2,1)S(1)}, bf16[7,256,128]{2,1,0:T(8,128)(2,1)S(1)}, u32[]{:S(2)}, u32[]{:S(2)}) %collective-permute-start.7) | collective-permute-done | bytes 458784 | tf_op jit(solution)/shard_map/ppermute | solution.py:649
  52.7 0.1 collective-permute-start.8
  52.8 1.7 %collective-permute-done.8.shares_ref = f32[6,128,128]{2,1,0:T(8,128)S(1)} collective-permute-done((f32[6,128,128]{2,1,0:T(8,128)S(1)}, f32[6,128,128]{2,1,0:T(8,128)S(1)}, u32[]{:S(2)}, u32[]{:S(2)}) %collective-permute-start.8) | collective-permute-done | bytes 393248 | tf_op jit(solution)/shard_map/ppermute | solution.py:653
  54.5 0.0 collective-permute-done.6.got_ref
  54.5 1.4 %assemble.1 = bf16[3072,128]{1,0:T(8,128)(2,1)} custom-call(s32[1]{0:T(128)} %bitcast.core_ref, f32[6,128,256]{2,1,0:T(8,128)S(1)} %get-tuple-element.45.own_ref, f32[6,128,256]{2,1,0:T(8,128)S(1)} %collective-permute-done.6.got_ref, bf16[7,256,128]{2,1,0:T(8,128)(2,1)S(1)} %collective-permute-done.7.halo_ref, f32[128,128]{1,0:T(8,128)S(1)} %get-tuple-element.50.fix_ref, ...), custom_call_target="tpu_custom_call" | custom-call | tf_op jit(solution)/shard_map/assemble/pallas_call | solution.py:635
  (1 shorter events, 0.0 us)
Async XLA Ops:
  0.0 7.2 %collective-permute-start.2 = (bf16[128,3456]{1,0:T(8,128)(2,1)}, bf16[128,3456]{1,0:T(8,128)(2,1)S(1)}, u32[]{:S(2)}, u32[]{:S(2)}) collective-permute-start(bf16[128,3456]{1,0:T(8,128)(2,1)} %own_ref.3), channel_id=1, source_target_pairs={{0,1},{1,0},{2,3},{3,2},{4,5},{5,4},{6,7},{7,6},{8,9},{9,8},{10,11... | collective-permute-start | bytes 2654216 | tf_op jit(solution)/shard_map/ppermute | solution.py:653
  0.7 6.5 %collective-permute-start = (bf16[64,1728]{1,0:T(8,128)(2,1)}, bf16[64,1728]{1,0:T(8,128)(2,1)S(1)}, u32[]{:S(2)}, u32[]{:S(2)}) collective-permute-start(bf16[64,1728]{1,0:T(8,128)(2,1)} %own_ref.2), channel_id=1, source_target_pairs={{0,1},{1,0},{2,3},{3,2},{4,5},{5,4},{6,7},{7,6},{8,9},{9,8},{10,11... | collective-permute-start | bytes 663560 | tf_op jit(solution)/shard_map/ppermute | solution.py:653
  1.5 5.7 %collective-permute-start.1 = (f32[3,128]{1,0:T(4,128)S(1)}, f32[3,128]{1,0:T(4,128)S(1)}, u32[]{:S(2)}, u32[]{:S(2)}) collective-permute-start(f32[3,128]{1,0:T(4,128)S(1)} %maximum_bitcast_fusion.own_scales_ref), channel_id=1, source_target_pairs={{0,1},{1,0},{2,3},{3,2},{4,5},{5,4},{6,7},{7,6},{8,9},{9,8},{10,11... | collective-permute-start | bytes 4616 | tf_op jit(solution)/shard_map/ppermute | solution.py:653
  2.0 5.3 %copy-start.2 = (bf16[64,1728]{1,0:T(8,128)(2,1)S(1)}, bf16[64,1728]{1,0:T(8,128)(2,1)}, u32[]{:S(2)}) copy-start(bf16[64,1728]{1,0:T(8,128)(2,1)} %own_ref.2) | copy-start | bytes 663556
  7.2 2.7 %copy-start.1 = (bf16[256,256]{1,0:T(8,128)(2,1)S(1)}, bf16[256,256]{1,0:T(8,128)(2,1)}, u32[]{:S(2)}) copy-start(bf16[256,256]{1,0:T(8,128)(2,1)} %constant.6.clone.place_ref.refs_8_.refs_9_) | copy-start | bytes 393220
  8.6 22.2 %collective-permute-start.3 = (bf16[12,128,256]{2,1,0:T(8,128)(2,1)S(1)}, bf16[12,128,256]{2,1,0:T(8,128)(2,1)S(1)}, u32[]{:S(2)}, u32[]{:S(2)}) collective-permute-start(bf16[12,128,256]{2,1,0:T(8,128)(2,1)S(1)} %get-tuple-element.39), channel_id=1, source_target_pairs={{0,3},{2,5},{4,7},{6,9},{8,11},{10,13},{12,15},{16,19},{18,21},{20... | collective-permute-start | bytes 2359304 | tf_op jit(solution)/shard_map/ppermute | solution.py:649
  9.9 20.9 %copy-start = (bf16[128,3456]{1,0:T(8,128)(2,1)S(1)}, bf16[128,3456]{1,0:T(8,128)(2,1)}, u32[]{:S(2)}) copy-start(bf16[128,3456]{1,0:T(8,128)(2,1)} %own_ref.3) | copy-start | bytes 2654212
  25.9 6.1 %collective-permute-start.4 = (bf16[12,128,256]{2,1,0:T(8,128)(2,1)S(1)}, bf16[12,128,256]{2,1,0:T(8,128)(2,1)S(1)}, u32[]{:S(2)}, u32[]{:S(2)}) collective-permute-start(bf16[12,128,256]{2,1,0:T(8,128)(2,1)S(1)} %get-tuple-element.42), channel_id=1, source_target_pairs={{0,1},{1,0},{2,3},{3,2},{4,5},{5,4},{6,7},{7,6},{8,9},{9,8},{10,11... | collective-permute-start | bytes 2359304 | tf_op jit(solution)/shard_map/ppermute | solution.py:653
  33.4 4.2 %collective-permute-start.5 = (bf16[4,128,256]{2,1,0:T(8,128)(2,1)S(1)}, bf16[4,128,256]{2,1,0:T(8,128)(2,1)S(1)}, u32[]{:S(2)}, u32[]{:S(2)}) collective-permute-start(bf16[4,128,256]{2,1,0:T(8,128)(2,1)S(1)} %get-tuple-element.44), channel_id=1, source_target_pairs={{1,0},{3,2},{5,4},{7,6},{9,8},{11,10},{13,12},{15,14},{17,16},{19,... | collective-permute-start | bytes 786440 | tf_op jit(solution)/shard_map/ppermute | solution.py:672
  36.3 16.4 %collective-permute-start.7 = (bf16[7,256,128]{2,1,0:T(8,128)(2,1)S(1)}, bf16[7,256,128]{2,1,0:T(8,128)(2,1)S(1)}, u32[]{:S(2)}, u32[]{:S(2)}) collective-permute-start(bf16[7,256,128]{2,1,0:T(8,128)(2,1)S(1)} %get-tuple-element.47), channel_id=1, source_target_pairs={{0,3},{2,5},{4,7},{6,9},{8,11},{10,13},{12,15},{16,19},{18,21},{20... | collective-permute-start | bytes 1376264 | tf_op jit(solution)/shard_map/ppermute | solution.py:649
  42.5 12.0 %collective-permute-start.6 = (f32[6,128,256]{2,1,0:T(8,128)S(1)}, f32[6,128,256]{2,1,0:T(8,128)S(1)}, u32[]{:S(2)}, u32[]{:S(2)}) collective-permute-start(f32[6,128,256]{2,1,0:T(8,128)S(1)} %get-tuple-element.46), channel_id=1, source_target_pairs={{0,1},{1,0},{2,3},{3,2},{4,5},{5,4},{6,7},{7,6},{8,9},{9,8},{10,11... | collective-permute-start | bytes 2359304 | tf_op jit(solution)/shard_map/ppermute | solution.py:653
  52.7 1.8 %collective-permute-start.8 = (f32[6,128,128]{2,1,0:T(8,128)S(1)}, f32[6,128,128]{2,1,0:T(8,128)S(1)}, u32[]{:S(2)}, u32[]{:S(2)}) collective-permute-start(f32[6,128,128]{2,1,0:T(8,128)S(1)} %get-tuple-element.52), channel_id=1, source_target_pairs={{0,1},{1,0},{2,3},{3,2},{4,5},{5,4},{6,7},{7,6},{8,9},{9,8},{10,11... | collective-permute-start | bytes 1179656 | tf_op jit(solution)/shard_map/ppermute | solution.py:653
